TPU v7x, 32 devices: a whole 2x2x4 slice. The times are simulated.
32 devices in a mesh: img: 16 (over z, y, core), ch: 2 (over x).
Axes of the slice: x: 2, y: 2, z: 4, core: 2. Of those that a mesh axis runs over, the one named last changes fastest.
Arguments:
- activations: bfloat16 [192, 56, 2048], P('img', None, 'ch'), may hold values from -6 to 6
- filters: bfloat16 [3, 3, 2048, 4096], P(None, None, 'img', 'ch'), may hold values from -0.046875 to 0.046875
- channel_bias: float32 [4096], P('ch'), may hold values from -3 to 3
Outputs:
- convolved: bfloat16 [192, 56, 4096], P('img', None, 'ch')
All inputs are finite; a program needn't handle non-finite values.
Results may differ from a plain program's by a relative error of at most 0.001.
Values may be sent and summed in bfloat16 or wider, within the bound.
No kernel may reach another device: no remote copies, remote signals or barrier semaphores. Data moves between devices by JAX's collectives and lax.ppermute only.
A program may use at most 192 MiB of HBM per device.

v0:
```python
import jax
import jax.numpy as jnp
from jax import lax
from jax.sharding import PartitionSpec as P

SIDE = 56


def with_halo(array, sides, width):
    for axis, dim in sides:
        size, length = (lax.axis_size(axis), array.shape[dim])
        up = [(i, (i + 1) % size) for i in range(size - 1)]
        down = [(j, i) for i, j in up]
        last = lax.slice_in_dim(array, length - width, length, axis=dim)
        first = lax.slice_in_dim(array, 0, width, axis=dim)
        before = lax.ppermute(last, axis, up)
        after = lax.ppermute(first, axis, down)
        array = jnp.concatenate([before, array, after], axis=dim)
    return array


def shift_views(padded, offset):
    row_count = padded.shape[0] - 2
    global_rows = offset + jnp.arange(row_count, dtype=jnp.int32)
    above_mask = (global_rows % SIDE != 0).astype(padded.dtype)
    below_mask = ((global_rows + 1) % SIDE != 0).astype(padded.dtype)
    padded_wide = jnp.pad(padded, ((0, 0), (1, 1), (0, 0)))
    return jnp.stack(
        [
            padded_wide[:row_count] * above_mask[:, None, None],
            padded_wide[1 : row_count + 1],
            padded_wide[2:] * below_mask[:, None, None],
        ]
    )


def add_taps(accumulated, shifted, weights):
    row_count = shifted.shape[1]
    width_count = shifted.shape[2] - 2
    for vertical in range(3):
        for horizontal in range(3):
            operand = shifted[vertical, :, horizontal : horizontal + width_count, :].reshape(
                row_count * width_count, -1
            )
            accumulated = accumulated + jnp.dot(
                operand, weights[vertical, horizontal], preferred_element_type=jnp.float32
            )
    return accumulated


def local(activations, filters, channel_bias):
    row_count = activations.shape[0]
    width_count = activations.shape[1]
    out_local = filters.shape[3]
    offset = lax.axis_index("img") * row_count
    initial = jnp.zeros((row_count * width_count, out_local), jnp.float32)
    full_channels = lax.all_gather(activations, "ch", axis=2, tiled=True)
    padded = with_halo(full_channels, (("img", 0),), 1)
    shifted = shift_views(padded, offset)
    accumulated = add_taps(initial, shifted, lax.all_gather(filters, "img", axis=2, tiled=True))
    output = accumulated + channel_bias[None, :]
    return output.astype(jnp.bfloat16).reshape(row_count, width_count, out_local)


def solution(mesh):
    placed = (P("img", None, "ch"), P(None, None, "img", "ch"), P("ch"))
    return jax.shard_map(
        local, mesh=mesh, in_specs=placed, out_specs=P("img", None, "ch"), check_vma=False
    )
```

profile of v0, /device:TPU:0, one launch (start us, length us, event | category | flops | bytes accessed | tf_op | source)
XLA Modules:
  0.0 530.6 jit_solution(4471491459070516271)
XLA Ops:
  6.5 0.0 all-gather.3.cloned.1.call-start
  6.5 0.7 all-gather.3.cloned.1.call-update
  7.3 0.0 all-gather.5.cloned.1.call-start
  7.3 0.7 all-gather.5.cloned.1.call-update
  8.0 44.1 %all-gather.3.cloned.1.call-done = bf16[12,56,2048]{2,1,0:T(8,128)(2,1)} async-done(((bf16[12,56,1024]{2,1,0:T(8,128)(2,1)}), bf16[12,56,2048]{2,1,0:T(8,128)(2,1)}) %all-gather.3.cloned.1.call-update) | async-done | bytes 2752528 | tf_op jit(solution)/shard_map/all_gather | solution.py:57
  52.1 1.1 fusion.20
  53.2 1.8 collective-permute-start
  55.0 1.3 collective-permute-start.1
  56.3 0.0 collective-permute-done
  56.3 3.3 collective-permute-done.1
  59.6 3.3 fusion.14
  63.0 0.8 fusion.16
  63.7 3.3 fusion.17
  67.0 3.6 fusion.18
  70.6 3.8 fusion.19
  74.4 347.4 %all-gather.5.cloned.1.call-done = bf16[3,3,2048,2048]{3,2,1,0:T(8,128)(2,1)} async-done(((bf16[3,3,128,2048]{3,2,1,0:T(8,128)(2,1)}), bf16[3,3,2048,2048]{3,2,1,0:T(8,128)(2,1)}) %all-gather.5.cloned.1.call-update) | async-done | bytes 75497488 | tf_op jit(solution)/shard_map/all_gather | solution.py:60
  421.8 0.0 copy-start.1
  421.8 10.8 %fusion.6 = f32[672,2048]{1,0:T(8,128)} fusion(bf16[672,2048]{1,0:T(8,128)(2,1)} %bitcast.59, bf16[3,3,2048,2048]{3,2,1,0:T(8,128)(2,1)} %all-gather.5.cloned.1.call-done), kind=kOutput, calls=%fused_computation.15 | convolution fusion | flops 5637144576 | bytes 16646144 | tf_op jit(solution)/shard_map/dot_general | solution.py:45
  432.6 0.0 copy-done.1
  432.6 0.0 copy-start.6
  432.6 10.0 %fusion.7 = f32[672,2048]{1,0:T(8,128)} fusion(bf16[672,2048]{1,0:T(8,128)(2,1)S(1)} %bitcast.56, bf16[3,3,2048,2048]{3,2,1,0:T(8,128)(2,1)} %all-gather.5.cloned.1.call-done), kind=kOutput, calls=%fused_computation.17 | convolution fusion | flops 5637144576 | bytes 16646144 | tf_op jit(solution)/shard_map/dot_general | solution.py:45
  442.6 0.0 copy-done.6
  442.6 0.0 copy-start.4
  442.6 10.0 %fusion.3 = f32[672,2048]{1,0:T(8,128)} fusion(bf16[672,2048]{1,0:T(8,128)(2,1)S(1)} %bitcast.62, bf16[3,3,2048,2048]{3,2,1,0:T(8,128)(2,1)} %all-gather.5.cloned.1.call-done), kind=kOutput, calls=%fused_computation.9 | convolution fusion | flops 5637144576 | bytes 16646144 | tf_op jit(solution)/shard_map/dot_general | solution.py:45
  452.6 0.0 copy-done.4
  452.6 0.0 copy-start.2
  452.6 10.0 %fusion.5 = f32[672,2048]{1,0:T(8,128)} fusion(bf16[672,2048]{1,0:T(8,128)(2,1)S(1)} %bitcast.60, bf16[3,3,2048,2048]{3,2,1,0:T(8,128)(2,1)} %all-gather.5.cloned.1.call-done), kind=kOutput, calls=%fused_computation.13 | convolution fusion | flops 5637144576 | bytes 16646144 | tf_op jit(solution)/shard_map/dot_general | solution.py:45
  462.6 0.0 copy-done.2
  462.6 0.0 copy-start.5
  462.6 9.9 %fusion.4 = f32[672,2048]{1,0:T(8,128)} fusion(bf16[672,2048]{1,0:T(8,128)(2,1)S(1)} %bitcast.57, bf16[3,3,2048,2048]{3,2,1,0:T(8,128)(2,1)} %all-gather.5.cloned.1.call-done), kind=kOutput, calls=%fused_computation.11 | convolution fusion | flops 5637144576 | bytes 16646144 | tf_op jit(solution)/shard_map/dot_general | solution.py:45
  472.5 0.0 copy-done.5
  472.5 0.0 copy-start.3
  472.5 10.0 %fusion = f32[672,2048]{1,0:T(8,128)} fusion(bf16[672,2048]{1,0:T(8,128)(2,1)S(1)} %bitcast.61, bf16[3,3,2048,2048]{3,2,1,0:T(8,128)(2,1)} %all-gather.5.cloned.1.call-done), kind=kOutput, calls=%fused_computation.3 | convolution fusion | flops 5637144576 | bytes 16646144 | tf_op jit(solution)/shard_map/dot_general | solution.py:45
  482.5 0.0 copy-done.3
  482.5 0.0 copy-start
  482.5 10.0 %fusion.2 = f32[672,2048]{1,0:T(8,128)} fusion(bf16[672,2048]{1,0:T(8,128)(2,1)S(1)} %bitcast.58, bf16[3,3,2048,2048]{3,2,1,0:T(8,128)(2,1)} %all-gather.5.cloned.1.call-done), kind=kOutput, calls=%fused_computation.7 | convolution fusion | flops 5637144576 | bytes 16646144 | tf_op jit(solution)/shard_map/dot_general | solution.py:45
  492.5 0.0 copy-done
  492.5 0.0 copy-start.7
  492.5 9.8 %fusion.1 = f32[672,2048]{1,0:T(8,128)} fusion(bf16[672,2048]{1,0:T(8,128)(2,1)S(1)} %bitcast.55, bf16[3,3,2048,2048]{3,2,1,0:T(8,128)(2,1)} %all-gather.5.cloned.1.call-done), kind=kOutput, calls=%fused_computation.5 | convolution fusion | flops 5637144576 | bytes 16646144 | tf_op jit(solution)/shard_map/dot_general | solution.py:45
  502.3 0.0 copy-done.7
  502.3 21.5 %add_convert_fusion = bf16[672,2048]{1,0:T(8,128)(2,1)} fusion(f32[672,2048]{1,0:T(8,128)} %fusion, f32[672,2048]{1,0:T(8,128)} %fusion.1, f32[672,2048]{1,0:T(8,128)} %fusion.2, f32[672,2048]{1,0:T(8,128)} %fusion.3, f32[672,2048]{1,0:T(8,128)} %fusion.4, f32[672,2048]{1,0:T(8,128)} %fusion.5, f32[672,2048]{1,0:T(8,128)} %fusion.6, ...), kind=kOutput, calls=%fused_computation.21 | convolution fusion | flops 5650907136 | bytes 57942016 | tf_op jit(solution)/shard_map/dot_general | solution.py:45
  (1 shorter events, 0.0 us)
Async XLA Ops:
  6.5 45.6 %all-gather.3.cloned.1.call-start = ((), (), s32[]{:S(2)}) async-start(), calls=%async_computation | async-start | bytes 4128768 | tf_op jit(solution)/shard_map/all_gather | solution.py:57
  7.3 414.5 %all-gather.5.cloned.1.call-start = ((), (), s32[]{:S(2)}) async-start(), calls=%async_computation.1 | async-start | bytes 80216064 | tf_op jit(solution)/shard_map/all_gather | solution.py:60
  53.2 3.1 collective-permute-start
  55.0 4.6 collective-permute-start.1
  421.8 10.8 %copy-start.1 = (bf16[1,12,56,2048]{3,2,1,0:T(8,128)(2,1)S(1)}, bf16[1,12,56,2048]{3,2,1,0:T(8,128)(2,1)}, u32[]{:S(2)}) copy-start(bf16[1,12,56,2048]{3,2,1,0:T(8,128)(2,1)} %get-tuple-element.10) | copy-start | bytes 8257540
  432.6 10.0 %copy-start.6 = (bf16[1,12,56,2048]{3,2,1,0:T(8,128)(2,1)S(1)}, bf16[1,12,56,2048]{3,2,1,0:T(8,128)(2,1)}, u32[]{:S(2)}) copy-start(bf16[1,12,56,2048]{3,2,1,0:T(8,128)(2,1)} %get-tuple-element.12) | copy-start | bytes 8257540
  442.6 10.0 %copy-start.4 = (bf16[1,12,56,2048]{3,2,1,0:T(8,128)(2,1)S(1)}, bf16[1,12,56,2048]{3,2,1,0:T(8,128)(2,1)}, u32[]{:S(2)}) copy-start(bf16[1,12,56,2048]{3,2,1,0:T(8,128)(2,1)} %get-tuple-element.11) | copy-start | bytes 8257540
  452.6 10.0 %copy-start.2 = (bf16[1,12,56,2048]{3,2,1,0:T(8,128)(2,1)S(1)}, bf16[1,12,56,2048]{3,2,1,0:T(8,128)(2,1)}, u32[]{:S(2)}) copy-start(bf16[1,12,56,2048]{3,2,1,0:T(8,128)(2,1)} %get-tuple-element.13) | copy-start | bytes 8257540
  462.6 9.9 %copy-start.5 = (bf16[1,12,56,2048]{3,2,1,0:T(8,128)(2,1)S(1)}, bf16[1,12,56,2048]{3,2,1,0:T(8,128)(2,1)}, u32[]{:S(2)}) copy-start(bf16[1,12,56,2048]{3,2,1,0:T(8,128)(2,1)} %get-tuple-element.15) | copy-start | bytes 8257540
  472.5 10.0 %copy-start.3 = (bf16[1,12,56,2048]{3,2,1,0:T(8,128)(2,1)S(1)}, bf16[1,12,56,2048]{3,2,1,0:T(8,128)(2,1)}, u32[]{:S(2)}) copy-start(bf16[1,12,56,2048]{3,2,1,0:T(8,128)(2,1)} %get-tuple-element.14) | copy-start | bytes 8257540
  482.5 10.0 %copy-start = (bf16[1,12,56,2048]{3,2,1,0:T(8,128)(2,1)S(1)}, bf16[1,12,56,2048]{3,2,1,0:T(8,128)(2,1)}, u32[]{:S(2)}) copy-start(bf16[1,12,56,2048]{3,2,1,0:T(8,128)(2,1)} %get-tuple-element.16) | copy-start | bytes 8257540
  492.5 9.8 %copy-start.7 = (f32[2048]{0:T(1024)S(1)}, f32[2048]{0:T(1024)}, u32[]{:S(2)}) copy-start(f32[2048]{0:T(1024)} %param.5) | copy-start | bytes 24580
Sparse Core Ops, SparseCore 0:
  8.9 43.1 all-gather.2
  53.7 368.0 all-gather.4
where the time goes:
time: 531 us
  waiting for transfers between devices  396 us (75%)
  matrix products  102 us (19%)
  between operations  13.5 us (3%)
  local copies, waits for them, and re-layouts  11.8 us (2%)
    all_gather x1, waiting for transfers between devices, local(): lax.all_gather(filters, 'img', axis=2, tiled=True)  347 us
    dot_general x9, matrix products, add_taps(): jnp.dot(operand, weights[vertical, horizontal], preferred_element_type=jn...  102 us
    all_gather x1, waiting for transfers between devices, local(): full_channels = lax.all_gather(activations, 'ch', axis=2, tiled=True)  44.1 us
    slice x3, local copies, waits for them, and re-layouts, add_taps(): shifted[vertical, :, horizontal:horizontal + width_count, :]  10.7 us
  transfers between devices with their start and end apart: 4, of which 3 were waited for; matrix products, arithmetic and copies ran while one was open for 3% of the time, Pallas kernels for 0%

commit v1 on v0

v1 whole, which is shorter than its diff:
```python
import functools

import jax
import jax.numpy as jnp
from jax import lax
from jax.experimental import pallas as pl
from jax.experimental.pallas import tpu as pltpu
from jax.sharding import PartitionSpec as P

SIDE = 56
GROUP = 8
TILE = 8


def swap(array, axis, bit):
    size = lax.axis_size(axis)
    return lax.ppermute(array, axis, [(i, i ^ bit) for i in range(size)])


def tap_kernel(shift, parts, last, scalars, image, *refs):
    weights, (acc_in, bias, out) = refs[:parts], refs[parts:]
    tile = pl.program_id(0)
    first_row, group = scalars[0], scalars[1]
    blocks, _, width, depth = image.shape
    per_part = blocks // parts
    rows = TILE
    row = first_row + tile * rows + lax.broadcasted_iota(jnp.int32, (rows, 1, 1), 0)
    total = None
    for vertical in range(3):
        part_sum = None
        for part in range(parts):
            for inner in range(per_part):
                block = (group ^ part) * per_part + inner
                operand = image[block, pl.ds(vertical, rows)].reshape(rows * width, depth)
                term = jnp.dot(
                    operand,
                    weights[part][vertical, pl.ds(inner * depth, depth), :],
                    preferred_element_type=jnp.float32,
                )
                part_sum = term if part_sum is None else part_sum + term
        part_sum = part_sum.reshape(rows, width, -1)
        if vertical == 0:
            part_sum = jnp.where(row % SIDE != 0, part_sum, 0.0)
        if vertical == 2:
            part_sum = jnp.where((row + 1) % SIDE != 0, part_sum, 0.0)
        total = part_sum if total is None else total + part_sum
    if shift:
        total = pltpu.roll(total, shift % width, 1)
    if acc_in is not None:
        total = total + acc_in[...]
    if last:
        total = total + bias[...].reshape(1, 1, -1)
    out[...] = total.astype(out.dtype)


def tap_call(shift, scalars, image, weights, acc, bias):
    blocks, padded_rows, width, depth = image.shape
    out_width = weights[0].shape[2]
    row_count = padded_rows - 2
    last = acc is not None and bias is not None
    parts = len(weights)

    def body(scalars_ref, image_ref, *refs):
        refs = list(refs)
        weight_refs, refs = refs[:parts], refs[parts:]
        acc_ref = refs.pop(0) if acc is not None else None
        bias_ref = refs.pop(0) if bias is not None else None
        tap_kernel(shift, parts, last, scalars_ref, image_ref, *weight_refs, acc_ref, bias_ref, refs[0])

    tile_spec = pl.BlockSpec((TILE, width, out_width), lambda t, s: (t, 0, 0))
    in_specs = [
        pl.BlockSpec(
            (pl.Element(blocks), pl.Element(TILE + 2), pl.Element(width), pl.Element(depth)),
            lambda t, s: (0, t * TILE, 0, 0),
        )
    ]
    operands = [image, *weights]
    for weight in weights:
        in_specs.append(pl.BlockSpec(weight.shape, lambda t, s: (0, 0, 0)))
    if acc is not None:
        in_specs.append(tile_spec)
        operands.append(acc)
    if bias is not None:
        in_specs.append(pl.BlockSpec((1, out_width), lambda t, s: (0, 0)))
        operands.append(bias)
    macs = row_count * width * 3 * blocks * depth * out_width
    return pl.pallas_call(
        body,
        grid_spec=pltpu.PrefetchScalarGridSpec(
            num_scalar_prefetch=1,
            grid=(row_count // TILE,),
            in_specs=in_specs,
            out_specs=tile_spec,
        ),
        out_shape=jax.ShapeDtypeStruct(
            (row_count, width, out_width), jnp.bfloat16 if last else jnp.float32
        ),
        compiler_params=pltpu.CompilerParams(vmem_limit_bytes=40 * 1024 * 1024),
        cost_estimate=pl.CostEstimate(
            flops=2 * macs, bytes_accessed=2 * image.size, transcendentals=0
        ),
    )(scalars, *operands)


def local(activations, filters, channel_bias):
    rows, side, depth = activations.shape
    out_local = filters.shape[3]
    size, chans = lax.axis_size("img"), lax.axis_size("ch")
    me, mine = lax.axis_index("img"), lax.axis_index("ch")
    parts = size // GROUP
    group, rank = me // GROUP, me % GROUP
    members = [[g * GROUP + r for r in range(GROUP)] for g in range(parts)]
    split = out_local // GROUP

    weights = []
    for horizontal in range(3):
        own = lax.all_to_all(
            filters[:, horizontal], "img", 2, 1, axis_index_groups=members, tiled=True
        )
        weights.append([own] + [swap(own, "img", GROUP * j) for j in range(1, parts)])

    edges = [(g * GROUP - 1, g * GROUP) for g in range(1, parts)]
    above = lax.ppermute(activations[-1:], "img", edges)
    below = lax.ppermute(activations[:1], "img", [(j, i) for i, j in edges])
    halo = jnp.where(rank == 0, above, below)
    piece = jnp.concatenate([activations, halo], axis=0)
    slots = {(0, 0): piece}
    slots[0, 4] = swap(piece, "img", 4)
    slots[0, 2] = swap(piece, "img", 2)
    slots[0, 6] = swap(slots[0, 4], "img", 2)
    for j in range(1, chans):
        for r in (0, 4, 2, 6):
            slots[j, r] = swap(slots[0, r], "ch", j)
    for (j, r), value in list(slots.items()):
        slots[j, r + 1] = swap(value, "img", 1)
    width = -(-side // 16) * 16
    image = jnp.zeros((chans, GROUP * rows + 2, width, depth), activations.dtype)
    for (j, r), value in slots.items():
        image = lax.dynamic_update_slice(
            image, value[None, :rows], (mine ^ j, (rank ^ r) * rows + 1, 0, 0)
        )
    for j in range(chans):
        stack = jnp.stack([slots[j, r][rows:] for r in range(GROUP)])
        top = lax.dynamic_index_in_dim(stack, rank, 0)
        bottom = lax.dynamic_index_in_dim(stack, rank ^ (GROUP - 1), 0)
        image = lax.dynamic_update_slice(image, top, (mine ^ j, 0, 0, 0))
        image = lax.dynamic_update_slice(image, bottom, (mine ^ j, GROUP * rows + 1, 0, 0))

    scalars = jnp.stack([group * GROUP * rows, group]).astype(jnp.int32)
    bias = lax.dynamic_slice_in_dim(channel_bias, rank * split, split)[None]
    acc = tap_call(1, scalars, image, weights[0], None, None)
    acc = tap_call(0, scalars, image, weights[1], acc, None)
    out = tap_call(-1, scalars, image, weights[2], acc, bias)[:, :side]
    return lax.all_to_all(out, "img", 0, 2, axis_index_groups=members, tiled=True)


def solution(mesh):
    placed = (P("img", None, "ch"), P(None, None, "img", "ch"), P("ch"))
    return jax.shard_map(
        local, mesh=mesh, in_specs=placed, out_specs=P("img", None, "ch"), check_vma=False
    )
```

time: 531 us -> 478 us (0.900)
  waiting for transfers between devices: 396 us -> 240 us
  matrix products: 102 us -> 0 us
  local copies, waits for them, and re-layouts: 11.8 us -> 87.2 us
  Pallas kernels: 0 us -> 73.2 us
  blocking collectives: 0 us -> 36.2 us
  starting transfers between devices: 3.09 us -> 37.3 us
  between operations: 13.5 us -> 0.28 us
    all_gather x2 -> x0, waiting for transfers between devices: 391 us -> none  [the longest x1 347 us: local(): lax.all_gather(filters, 'img', axis=2, tiled=True)]
    ppermute x2 -> x20, waiting for transfers between devices: 3.29 us -> 203 us  [the longest x18 203 us: swap(): return lax.ppermute(array, axis, [(i, i ^ bit) for i in range(size)])]
    dot_general x9 -> x0, matrix products: 102 us -> none  [add_taps(): jnp.dot(operand, weights[vertical, horizontal], preferred_element_type=jn...]
    pallas_call x0 -> x3, Pallas kernels: none -> 73.2 us  [tap_call(): pl.pallas_call(body, grid_spec=pltpu.PrefetchScalarGridSpec(num_scalar_pr...]
    all_to_all x0 -> x3, waiting for transfers between devices: none -> 37 us  [local(): lax.all_to_all(filters[:, horizontal], 'img', 2, 1, axis_index_groups=mem...]
    all_to_all x0 -> x1, blocking collectives: none -> 36.2 us  [local(): lax.all_to_all(out, 'img', 0, 2, axis_index_groups=members, tiled=True)]
    unnamed x16 -> x34, local copies, waits for them, and re-layouts: 0.03 us -> 34.2 us
    dynamic_update_slice x0 -> x20, local copies, waits for them, and re-layouts: none -> 31.7 us  [the longest x16 27.3 us: local(): lax.dynamic_update_slice(image, value[None, :rows], (mine ^ j, (rank ^ r)...]
  transfers between devices with their start and end apart: 4 -> 23, of which waited for: 3 -> 7; matrix products, arithmetic and copies ran while one was open for 3% -> 14% of each run, Pallas kernels for 0% -> 10%
where the time goes in v1:
time: 478 us; the launch traced here: 476 us
  waiting for transfers between devices  240 us (50%)
  local copies, waits for them, and re-layouts  87.2 us (18%)
  Pallas kernels  73.2 us (15%)
  starting transfers between devices  37.3 us (8%)
  blocking collectives  36.2 us (8%)
    ppermute x18, waiting for transfers between devices, swap(): return lax.ppermute(array, axis, [(i, i ^ bit) for i in range(size)])  203 us
    pallas_call x3, Pallas kernels, tap_call(): pl.pallas_call(body, grid_spec=pltpu.PrefetchScalarGridSpec(num_scalar_pr...  73.2 us
    all_to_all x3, waiting for transfers between devices, local(): lax.all_to_all(filters[:, horizontal], 'img', 2, 1, axis_index_groups=mem...  37 us
    all_to_all x1, blocking collectives, local(): lax.all_to_all(out, 'img', 0, 2, axis_index_groups=members, tiled=True)  36.2 us
    unnamed x34, local copies, waits for them, and re-layouts  34.2 us
    dynamic_update_slice x16, local copies, waits for them, and re-layouts, local(): lax.dynamic_update_slice(image, value[None, :rows], (mine ^ j, (rank ^ r)...  27.3 us
    ppermute x18, starting transfers between devices, swap(): return lax.ppermute(array, axis, [(i, i ^ bit) for i in range(size)])  22 us
    all_to_all x3, starting transfers between devices, local(): lax.all_to_all(filters[:, horizontal], 'img', 2, 1, axis_index_groups=mem...  13.9 us
  transfers between devices with their start and end apart: 23, of which 7 were waited for; matrix products, arithmetic and copies ran while one was open for 14% of the time, Pallas kernels for 10%

profile of v1, /device:TPU:0, one launch (start us, length us, event | category | flops | bytes accessed | tf_op | source)
XLA Modules:
  0.0 476.4 jit_solution(17741147073109919767)
XLA Ops:
  0.0 4.7 fusion.30
  4.7 2.5 copy.15
  7.2 5.3 %all-to-all-start = ((bf16[3,128,2048]{1,0,2:T(4,128)(2,1)}), bf16[3,128,2048]{1,0,2:T(4,128)(2,1)S(1)}, u32[]{:S(2)}, u32[]{:S(2)}) async-start(bf16[3,128,2048]{1,0,2:T(4,128)(2,1)} %bitcast.157), calls=%async_computation | async-start | bytes 4194304 | tf_op jit(solution)/shard_map/all_to_all | solution.py:117
  12.4 4.1 copy.16
  16.6 21.6 %all-to-all-done = bf16[3,128,2048]{1,0,2:T(4,128)(2,1)S(1)} async-done(((bf16[3,128,2048]{1,0,2:T(4,128)(2,1)}), bf16[3,128,2048]{1,0,2:T(4,128)(2,1)S(1)}, u32[]{:S(2)}, u32[]{:S(2)}) %all-to-all-start) | async-done | bytes 1572896 | tf_op jit(solution)/shard_map/all_to_all | solution.py:117
  39.4 4.3 all-to-all-start.1
  47.2 1.9 collective-permute-start.3
  50.5 1.5 collective-permute-start.5
  52.0 2.5 copy.17
  54.6 15.4 %all-to-all-done.1 = bf16[3,128,2048]{1,0,2:T(4,128)(2,1)} async-done(((bf16[3,128,2048]{1,0,2:T(4,128)(2,1)}), bf16[3,128,2048]{1,0,2:T(4,128)(2,1)}, u32[]{:S(2)}, u32[]{:S(2)}) %all-to-all-start.1) | async-done | bytes 1572896 | tf_op jit(solution)/shard_map/all_to_all | solution.py:117
  70.0 4.3 all-to-all-start.2
  75.5 26.4 %collective-permute-done.3 = bf16[13,56,1024]{2,1,0:T(8,128)(2,1)} collective-permute-done((bf16[13,56,1024]{2,1,0:T(8,128)(2,1)}, bf16[13,56,1024]{2,1,0:T(8,128)(2,1)}, u32[]{:S(2)}, u32[]{:S(2)}) %collective-permute-start.3) | collective-permute-done | bytes 1490976 | tf_op jit(solution)/shard_map/ppermute | solution.py:17
  101.9 3.3 broadcast_in_dim.54
  105.4 1.6 collective-permute-start.7
  107.2 1.6 fusion.22
  109.9 1.5 fusion.28
  111.5 1.5 fusion.14
  113.0 1.5 fusion.13
  114.5 8.5 %copy-done.2 = bf16[2,98,64,1024]{3,2,1,0:T(8,128)(2,1)} copy-done((bf16[2,98,64,1024]{3,2,1,0:T(8,128)(2,1)}, bf16[2,98,64,1024]{3,2,1,0:T(8,128)(2,1)S(1)}, u32[]{:S(2)}) %copy-start.2) | copy-done | bytes 25690136
  123.0 2.9 copy.9
  125.8 2.9 copy.11
  128.7 4.1 copy.13
  133.3 1.5 fusion.27
  134.9 1.5 fusion.26
  136.4 19.4 %collective-permute-done.4 = bf16[13,56,1024]{2,1,0:T(8,128)(2,1)} collective-permute-done((bf16[13,56,1024]{2,1,0:T(8,128)(2,1)}, bf16[13,56,1024]{2,1,0:T(8,128)(2,1)}, u32[]{:S(2)}, u32[]{:S(2)}) %collective-permute-start.4) | collective-permute-done | bytes 1490976 | tf_op jit(solution)/shard_map/ppermute | solution.py:17
  155.8 3.8 collective-permute-start.17
  159.7 1.5 collective-permute-start.8
  161.2 1.6 fusion.25
  162.7 1.5 fusion.24
  164.8 1.5 fusion.21
  166.3 2.6 fusion.12
  169.8 2.5 fusion.11
  173.0 4.1 collective-permute-start.18
  178.4 2.7 fusion.9
  181.1 23.5 %collective-permute-done.8 = bf16[13,56,1024]{2,1,0:T(8,128)(2,1)S(1)} collective-permute-done((bf16[13,56,1024]{2,1,0:T(8,128)(2,1)}, bf16[13,56,1024]{2,1,0:T(8,128)(2,1)S(1)}, u32[]{:S(2)}, u32[]{:S(2)}) %collective-permute-start.8) | collective-permute-done | bytes 1490976 | tf_op jit(solution)/shard_map/ppermute | solution.py:17
  204.6 4.1 collective-permute-start.19
  211.8 2.6 fusion.6
  214.3 2.6 fusion.5
  218.1 2.6 fusion.3
  224.4 1.5 dynamic-slice_dynamic-update-slice_fusion.3
  226.0 1.6 dynamic-slice_dynamic-update-slice_fusion.2
  228.9 133.3 %collective-permute-done.19.refs_1_ = bf16[3,1024,256]{2,1,0:T(8,128)(2,1)S(1)} collective-permute-done((bf16[3,1024,256]{2,1,0:T(8,128)(2,1)S(1)}, bf16[3,1024,256]{2,1,0:T(8,128)(2,1)S(1)}, u32[]{:S(2)}, u32[]{:S(2)}) %collective-permute-start.19) | collective-permute-done | bytes 1572896 | tf_op jit(solution)/shard_map/ppermute | solution.py:17
  362.1 24.1 %shard_map.37.refs_2_ = f32[96,64,256]{2,1,0:T(8,128)S(1)} custom-call(s32[2]{0:T(128)S(1)} %pad_add_fusion.scalars_ref, bf16[2,98,64,1024]{3,2,1,0:T(8,128)(2,1)} %dynamic-slice_dynamic-update-slice_fusion.image_ref, bf16[3,1024,256]{2,1,0:T(8,128)(2,1)S(1)} %bitcast.152, bf16[3,1024,256]{2,1,0:T(8,128)(2,1)S(1)} %collective-permute-done.19.refs_1_), custom_call_target="tpu_custom_call" | custom-call | flops 19327352832 | bytes 25690112 | tf_op jit(solution)/shard_map/pallas_call | solution.py:87
  386.2 2.7 copy-done.1
  388.9 24.6 %shard_map.38.refs_2_ = f32[96,64,256]{2,1,0:T(8,128)S(1)} custom-call(s32[2]{0:T(128)S(1)} %pad_add_fusion.scalars_ref, bf16[2,98,64,1024]{3,2,1,0:T(8,128)(2,1)} %dynamic-slice_dynamic-update-slice_fusion.image_ref, bf16[3,1024,256]{2,1,0:T(8,128)(2,1)S(1)} %bitcast.150, bf16[3,1024,256]{2,1,0:T(8,128)(2,1)S(1)} %collective-permute-done.18.refs_1_, ...), custom_call_target="tpu_custom_call" | custom-call | flops 19327352832 | bytes 25690112 | tf_op jit(solution)/shard_map/pallas_call | solution.py:87
  413.5 24.5 %shard_map.39 = bf16[96,64,256]{2,1,0:T(8,128)(2,1)S(1)} custom-call(s32[2]{0:T(128)S(1)} %pad_add_fusion.scalars_ref, bf16[2,98,64,1024]{3,2,1,0:T(8,128)(2,1)} %dynamic-slice_dynamic-update-slice_fusion.image_ref, bf16[3,1024,256]{2,1,0:T(8,128)(2,1)S(1)} %bitcast.148, bf16[3,1024,256]{2,1,0:T(8,128)(2,1)S(1)} %collective-permute-done.17.refs_1_, ...), custom_call_target="tpu_custom_call" | custom-call | flops 19327352832 | bytes 25690112 | tf_op jit(solution)/shard_map/pallas_call | solution.py:87
  438.3 36.2 %all_to_all.72 = bf16[96,56,256]{2,1,0:T(8,128)(2,1)S(1)} all-to-all(bf16[96,56,256]{2,1,0:T(8,128)(2,1)S(1)} %slice.174), channel_id=1, replica_groups={{0,2,4,6,8,10,12,14},{16,18,20,22,24,26,28,30},{1,3,5,7,9,11,13,15},{17..., dimensions={0} | all-to-all | bytes 5505024 | tf_op jit(solution)/shard_map/all_to_all | solution.py:154
  474.4 1.9 copy.18
  (70 shorter events, 22.4 us)
Async XLA Ops:
  7.2 31.0 %all-to-all-start = ((bf16[3,128,2048]{1,0,2:T(4,128)(2,1)}), bf16[3,128,2048]{1,0,2:T(4,128)(2,1)S(1)}, u32[]{:S(2)}, u32[]{:S(2)}) async-start(bf16[3,128,2048]{1,0,2:T(4,128)(2,1)} %bitcast.157), calls=%async_computation | async-start | bytes 4194304 | tf_op jit(solution)/shard_map/all_to_all | solution.py:117
  38.1 1.3 copy-start.3
  38.1 5.7 %copy-start.4 = (bf16[12,56,1024]{2,1,0:T(8,128)(2,1)S(1)}, bf16[12,56,1024]{2,1,0:T(8,128)(2,1)}, u32[]{:S(2)}) copy-start(bf16[12,56,1024]{2,1,0:T(8,128)(2,1)} %param.3) | copy-start | bytes 4128772
  39.4 30.5 %all-to-all-start.1 = ((bf16[3,128,2048]{1,0,2:T(4,128)(2,1)}), bf16[3,128,2048]{1,0,2:T(4,128)(2,1)}, u32[]{:S(2)}, u32[]{:S(2)}) async-start(bf16[3,128,2048]{1,0,2:T(4,128)(2,1)} %bitcast.156), calls=%async_computation.1 | async-start | bytes 4194304 | tf_op jit(solution)/shard_map/all_to_all | solution.py:117
  43.8 1.4 collective-permute-start
  44.5 0.7 collective-permute-start.1
  45.9 6.1 %copy-start.5 = (bf16[3,1,128,2048]{3,2,1,0:T(8,128)(2,1)S(1)}, bf16[3,1,128,2048]{3,2,1,0:T(8,128)(2,1)}, u32[]{:S(2)}) copy-start(bf16[3,1,128,2048]{3,2,1,0:T(8,128)(2,1)} %get-tuple-element.7) | copy-start | bytes 4718596
  47.2 54.7 %collective-permute-start.3 = (bf16[13,56,1024]{2,1,0:T(8,128)(2,1)}, bf16[13,56,1024]{2,1,0:T(8,128)(2,1)}, u32[]{:S(2)}, u32[]{:S(2)}) collective-permute-start(bf16[13,56,1024]{2,1,0:T(8,128)(2,1)} %pad_maximum_fusion), channel_id=1, source_target_pairs={{0,4},{2,6},{4,0},{6,2},{8,12},{10,14},{12,8},{14,10},{16,20},{18,... | collective-permute-start | bytes 4472840 | tf_op jit(solution)/shard_map/ppermute | solution.py:17
  49.1 57.9 %collective-permute-start.2 = (bf16[13,56,1024]{2,1,0:T(8,128)(2,1)}, bf16[13,56,1024]{2,1,0:T(8,128)(2,1)}, u32[]{:S(2)}, u32[]{:S(2)}) collective-permute-start(bf16[13,56,1024]{2,1,0:T(8,128)(2,1)} %pad_maximum_fusion), channel_id=1, source_target_pairs={{0,8},{2,10},{4,12},{6,14},{8,0},{10,2},{12,4},{14,6},{16,24},{18,... | collective-permute-start | bytes 4472840 | tf_op jit(solution)/shard_map/ppermute | solution.py:17
  50.5 56.5 %collective-permute-start.5 = (bf16[13,56,1024]{2,1,0:T(8,128)(2,1)}, bf16[13,56,1024]{2,1,0:T(8,128)(2,1)}, u32[]{:S(2)}, u32[]{:S(2)}) collective-permute-start(bf16[13,56,1024]{2,1,0:T(8,128)(2,1)} %pad_maximum_fusion), channel_id=1, source_target_pairs={{0,1},{1,0},{2,3},{3,2},{4,5},{5,4},{6,7},{7,6},{8,9},{9,8},{10,11... | collective-permute-start | bytes 4472840 | tf_op jit(solution)/shard_map/ppermute | solution.py:17
  70.0 58.8 %all-to-all-start.2 = ((bf16[3,128,2048]{1,0,2:T(4,128)(2,1)}), bf16[3,128,2048]{1,0,2:T(4,128)(2,1)}, u32[]{:S(2)}, u32[]{:S(2)}) async-start(bf16[3,128,2048]{1,0,2:T(4,128)(2,1)} %bitcast.44), calls=%async_computation.2 | async-start | bytes 4194304 | tf_op jit(solution)/shard_map/all_to_all | solution.py:117
  74.3 34.5 %collective-permute-start.9 = (bf16[13,56,1024]{2,1,0:T(8,128)(2,1)}, bf16[13,56,1024]{2,1,0:T(8,128)(2,1)S(1)}, u32[]{:S(2)}, u32[]{:S(2)}) collective-permute-start(bf16[13,56,1024]{2,1,0:T(8,128)(2,1)} %pad_maximum_fusion), channel_id=1, source_target_pairs={{0,2},{2,0},{4,6},{6,4},{8,10},{10,8},{12,14},{14,12},{16,18},{18,... | collective-permute-start | bytes 4472840 | tf_op jit(solution)/shard_map/ppermute | solution.py:17
  101.9 30.9 %collective-permute-start.11 = (bf16[13,56,1024]{2,1,0:T(8,128)(2,1)}, bf16[13,56,1024]{2,1,0:T(8,128)(2,1)}, u32[]{:S(2)}, u32[]{:S(2)}) collective-permute-start(bf16[13,56,1024]{2,1,0:T(8,128)(2,1)} %collective-permute-done.3), channel_id=1, source_target_pairs={{0,2},{2,0},{4,6},{6,4},{8,10},{10,8},{12,14},{14,12},{16,18},{18,... | collective-permute-start | bytes 4472840 | tf_op jit(solution)/shard_map/ppermute | solution.py:17
  105.4 58.9 %collective-permute-start.7 = (bf16[13,56,1024]{2,1,0:T(8,128)(2,1)}, bf16[13,56,1024]{2,1,0:T(8,128)(2,1)}, u32[]{:S(2)}, u32[]{:S(2)}) collective-permute-start(bf16[13,56,1024]{2,1,0:T(8,128)(2,1)} %collective-permute-done.3), channel_id=1, source_target_pairs={{0,1},{1,0},{2,3},{3,2},{4,5},{5,4},{6,7},{7,6},{8,9},{9,8},{10,11... | collective-permute-start | bytes 4472840 | tf_op jit(solution)/shard_map/ppermute | solution.py:17
  106.9 48.9 %collective-permute-start.4 = (bf16[13,56,1024]{2,1,0:T(8,128)(2,1)}, bf16[13,56,1024]{2,1,0:T(8,128)(2,1)}, u32[]{:S(2)}, u32[]{:S(2)}) collective-permute-start(bf16[13,56,1024]{2,1,0:T(8,128)(2,1)} %collective-permute-done.2), channel_id=1, source_target_pairs={{0,4},{2,6},{4,0},{6,2},{8,12},{10,14},{12,8},{14,10},{16,20},{18,... | collective-permute-start | bytes 4472840 | tf_op jit(solution)/shard_map/ppermute | solution.py:17
  107.0 52.6 %collective-permute-start.10 = (bf16[13,56,1024]{2,1,0:T(8,128)(2,1)}, bf16[13,56,1024]{2,1,0:T(8,128)(2,1)}, u32[]{:S(2)}, u32[]{:S(2)}) collective-permute-start(bf16[13,56,1024]{2,1,0:T(8,128)(2,1)} %collective-permute-done.2), channel_id=1, source_target_pairs={{0,2},{2,0},{4,6},{6,4},{8,10},{10,8},{12,14},{14,12},{16,18},{18,... | collective-permute-start | bytes 4472840 | tf_op jit(solution)/shard_map/ppermute | solution.py:17
  108.8 4.2 copy-start.6
  108.8 55.5 %collective-permute-start.13 = (bf16[13,56,1024]{2,1,0:T(8,128)(2,1)}, bf16[13,56,1024]{2,1,0:T(8,128)(2,1)}, u32[]{:S(2)}, u32[]{:S(2)}) collective-permute-start(bf16[13,56,1024]{2,1,0:T(8,128)(2,1)} %collective-permute-done.5), channel_id=1, source_target_pairs={{0,2},{2,0},{4,6},{6,4},{8,10},{10,8},{12,14},{14,12},{16,18},{18,... | collective-permute-start | bytes 4472840 | tf_op jit(solution)/shard_map/ppermute | solution.py:17
  114.5 8.5 %copy-start.2 = (bf16[2,98,64,1024]{3,2,1,0:T(8,128)(2,1)}, bf16[2,98,64,1024]{3,2,1,0:T(8,128)(2,1)S(1)}, u32[]{:S(2)}) copy-start(bf16[2,98,64,1024]{3,2,1,0:T(8,128)(2,1)S(1)} %fusion.13) | copy-start | bytes 77070336
  132.8 40.2 %collective-permute-start.6 = (bf16[13,56,1024]{2,1,0:T(8,128)(2,1)}, bf16[13,56,1024]{2,1,0:T(8,128)(2,1)S(1)}, u32[]{:S(2)}, u32[]{:S(2)}) collective-permute-start(bf16[13,56,1024]{2,1,0:T(8,128)(2,1)} %collective-permute-done.2), channel_id=1, source_target_pairs={{0,1},{1,0},{2,3},{3,2},{4,5},{5,4},{6,7},{7,6},{8,9},{9,8},{10,11... | collective-permute-start | bytes 4472840 | tf_op jit(solution)/shard_map/ppermute | solution.py:17
  155.8 257.6 %collective-permute-start.17 = (bf16[3,1024,256]{2,1,0:T(8,128)(2,1)S(1)}, bf16[3,1024,256]{2,1,0:T(8,128)(2,1)S(1)}, u32[]{:S(2)}, u32[]{:S(2)}) collective-permute-start(bf16[3,1024,256]{2,1,0:T(8,128)(2,1)S(1)} %bitcast.147), channel_id=1, source_target_pairs={{0,16},{2,18},{4,20},{6,22},{8,24},{10,26},{12,28},{14,30},{16,0},... | collective-permute-start | bytes 4718600 | tf_op jit(solution)/shard_map/ppermute | solution.py:17
  159.7 44.9 %collective-permute-start.8 = (bf16[13,56,1024]{2,1,0:T(8,128)(2,1)}, bf16[13,56,1024]{2,1,0:T(8,128)(2,1)S(1)}, u32[]{:S(2)}, u32[]{:S(2)}) collective-permute-start(bf16[13,56,1024]{2,1,0:T(8,128)(2,1)} %collective-permute-done.4), channel_id=1, source_target_pairs={{0,1},{1,0},{2,3},{3,2},{4,5},{5,4},{6,7},{7,6},{8,9},{9,8},{10,11... | collective-permute-start | bytes 4472840 | tf_op jit(solution)/shard_map/ppermute | solution.py:17
  164.2 44.5 %collective-permute-start.12 = (bf16[13,56,1024]{2,1,0:T(8,128)(2,1)}, bf16[13,56,1024]{2,1,0:T(8,128)(2,1)S(1)}, u32[]{:S(2)}, u32[]{:S(2)}) collective-permute-start(bf16[13,56,1024]{2,1,0:T(8,128)(2,1)} %collective-permute-done.4), channel_id=1, source_target_pairs={{0,2},{2,0},{4,6},{6,4},{8,10},{10,8},{12,14},{14,12},{16,18},{18,... | collective-permute-start | bytes 4472840 | tf_op jit(solution)/shard_map/ppermute | solution.py:17
  164.3 16.8 %collective-permute-start.15 = (bf16[13,56,1024]{2,1,0:T(8,128)(2,1)}, bf16[13,56,1024]{2,1,0:T(8,128)(2,1)S(1)}, u32[]{:S(2)}, u32[]{:S(2)}) collective-permute-start(bf16[13,56,1024]{2,1,0:T(8,128)(2,1)} %collective-permute-done.7), channel_id=1, source_target_pairs={{0,2},{2,0},{4,6},{6,4},{8,10},{10,8},{12,14},{14,12},{16,18},{18,... | collective-permute-start | bytes 4472840 | tf_op jit(solution)/shard_map/ppermute | solution.py:17
  166.3 2.6 copy-start.8
  173.0 215.9 %collective-permute-start.18 = (bf16[3,1024,256]{2,1,0:T(8,128)(2,1)S(1)}, bf16[3,1024,256]{2,1,0:T(8,128)(2,1)S(1)}, u32[]{:S(2)}, u32[]{:S(2)}) collective-permute-start(bf16[3,1024,256]{2,1,0:T(8,128)(2,1)S(1)} %bitcast.149), channel_id=1, source_target_pairs={{0,16},{2,18},{4,20},{6,22},{8,24},{10,26},{12,28},{14,30},{16,0},... | collective-permute-start | bytes 4718600 | tf_op jit(solution)/shard_map/ppermute | solution.py:17
  178.4 26.2 %copy-start = (bf16[3,128,8,256]{3,1,2,0:T(8,128)(2,1)S(1)}, bf16[3,128,8,256]{3,1,2,0:T(8,128)(2,1)}, u32[]{:S(2)}) copy-start(bf16[3,128,8,256]{3,1,2,0:T(8,128)(2,1)} %copy.13) | copy-start | bytes 4718596
  181.0 35.8 %collective-permute-start.14 = (bf16[13,56,1024]{2,1,0:T(8,128)(2,1)S(1)}, bf16[13,56,1024]{2,1,0:T(8,128)(2,1)S(1)}, u32[]{:S(2)}, u32[]{:S(2)}) collective-permute-start(bf16[13,56,1024]{2,1,0:T(8,128)(2,1)S(1)} %collective-permute-done.6), channel_id=1, source_target_pairs={{0,2},{2,0},{4,6},{6,4},{8,10},{10,8},{12,14},{14,12},{16,18},{18,... | collective-permute-start | bytes 4472840 | tf_op jit(solution)/shard_map/ppermute | solution.py:17
  181.1 29.5 %copy-start.7 = (bf16[13,56,1024]{2,1,0:T(8,128)(2,1)S(1)}, bf16[13,56,1024]{2,1,0:T(8,128)(2,1)}, u32[]{:S(2)}) copy-start(bf16[13,56,1024]{2,1,0:T(8,128)(2,1)} %copy-done.6) | copy-start | bytes 4472836
  204.6 157.6 %collective-permute-start.19 = (bf16[3,1024,256]{2,1,0:T(8,128)(2,1)S(1)}, bf16[3,1024,256]{2,1,0:T(8,128)(2,1)S(1)}, u32[]{:S(2)}, u32[]{:S(2)}) collective-permute-start(bf16[3,1024,256]{2,1,0:T(8,128)(2,1)S(1)} %bitcast.151), channel_id=1, source_target_pairs={{0,16},{2,18},{4,20},{6,22},{8,24},{10,26},{12,28},{14,30},{16,0},... | collective-permute-start | bytes 4718600 | tf_op jit(solution)/shard_map/ppermute | solution.py:17
  208.7 14.5 %collective-permute-start.16 = (bf16[13,56,1024]{2,1,0:T(8,128)(2,1)S(1)}, bf16[13,56,1024]{2,1,0:T(8,128)(2,1)S(1)}, u32[]{:S(2)}, u32[]{:S(2)}) collective-permute-start(bf16[13,56,1024]{2,1,0:T(8,128)(2,1)S(1)} %collective-permute-done.8), channel_id=1, source_target_pairs={{0,2},{2,0},{4,6},{6,4},{8,10},{10,8},{12,14},{14,12},{16,18},{18,... | collective-permute-start | bytes 4472840 | tf_op jit(solution)/shard_map/ppermute | solution.py:17
  386.2 2.7 copy-start.1

commit v2 on v1

v2 whole, which is shorter than its diff:
```python
import jax
import jax.numpy as jnp
from jax import lax
from jax.experimental import pallas as pl
from jax.experimental.pallas import tpu as pltpu
from jax.sharding import PartitionSpec as P

SIDE = 56
GROUP = 8
TILE = 8
CHUNKS = 4


def swap(array, axis, bit):
    size = lax.axis_size(axis)
    return lax.ppermute(array, axis, [(i, i ^ bit) for i in range(size)])


def after(array, *others):
    return lax.optimization_barrier((array, *others))[0]


def conv_call(taps, pieces, scalars, image, acc=None, bias=None):
    blocks, padded_rows, width, depth = image.shape
    shard, out_width = pieces[0][2].shape[2:]
    row_count = padded_rows - 2
    offsets = sorted({offset for offset, _, _ in pieces})
    per_group = GROUP * shard // depth
    first, count = min(taps), len(taps)
    final = bias is not None

    def body(scalars_ref, *refs):
        refs = list(refs)
        images = {offset: refs.pop(0) for offset in offsets}
        weights = [refs.pop(0) for _ in pieces]
        acc_ref = refs.pop(0) if acc is not None else None
        bias_ref = refs.pop(0) if final else None
        out = refs.pop(0)
        row = (
            scalars_ref[0]
            + pl.program_id(0) * TILE
            + lax.broadcasted_iota(jnp.int32, (TILE, 1, 1), 0)
        )
        total = None
        for horizontal in range(3):
            across = None
            for index, vertical in enumerate(taps):
                value = None
                for (offset, start, array), weight in zip(pieces, weights):
                    lanes = array.shape[0] * shard
                    flat = weight[:, 3 * index + horizontal].reshape(lanes, out_width)
                    low = start * shard
                    while low < start * shard + lanes:
                        inner, lane = divmod(low, depth)
                        size = min(depth - lane, start * shard + lanes - low)
                        operand = images[offset][
                            inner, pl.ds(vertical - first, TILE), :, pl.ds(lane, size)
                        ].reshape(TILE * width, size)
                        at = low - start * shard
                        term = jnp.dot(
                            operand, flat[at : at + size], preferred_element_type=jnp.float32
                        )
                        value = term if value is None else value + term
                        low += size
                value = value.reshape(TILE, width, out_width)
                if vertical == 0:
                    value = jnp.where(row % SIDE != 0, value, 0.0)
                if vertical == 2:
                    value = jnp.where((row + 1) % SIDE != 0, value, 0.0)
                across = value if across is None else across + value
            if horizontal != 1:
                across = pltpu.roll(across, (1 - horizontal) % width, 1)
            total = across if total is None else total + across
        if acc_ref is not None:
            total = total + acc_ref[...]
        if final:
            total = (total + bias_ref[...].reshape(1, 1, -1))[:, : out.shape[1]]
        out[...] = total.astype(out.dtype)

    def image_spec(offset):
        return pl.BlockSpec(
            (
                pl.Element(per_group),
                pl.Element(TILE + count - 1),
                pl.Element(width),
                pl.Element(depth),
            ),
            lambda t, s: ((s[1] ^ offset) * per_group, t * TILE + first, 0, 0),
        )

    out_cols = SIDE if final else width
    in_specs = [image_spec(offset) for offset in offsets]
    operands = [image] * len(offsets)
    for _, _, array in pieces:
        in_specs.append(pl.BlockSpec(array.shape, lambda t, s: (0, 0, 0, 0)))
        operands.append(array)
    if acc is not None:
        in_specs.append(pl.BlockSpec((TILE, width, out_width), lambda t, s: (t, 0, 0)))
        operands.append(acc)
    if final:
        in_specs.append(pl.BlockSpec((1, out_width), lambda t, s: (0, 0)))
        operands.append(bias)
    channels = sum(array.shape[0] for _, _, array in pieces) * shard
    return pl.pallas_call(
        body,
        grid_spec=pltpu.PrefetchScalarGridSpec(
            num_scalar_prefetch=1,
            grid=(row_count // TILE,),
            in_specs=in_specs,
            out_specs=pl.BlockSpec((TILE, out_cols, out_width), lambda t, s: (t, 0, 0)),
        ),
        out_shape=jax.ShapeDtypeStruct(
            (row_count, out_cols, out_width), jnp.bfloat16 if final else jnp.float32
        ),
        compiler_params=pltpu.CompilerParams(vmem_limit_bytes=40 * 1024 * 1024),
        cost_estimate=pl.CostEstimate(
            flops=2 * row_count * width * 3 * count * channels * out_width,
            bytes_accessed=2 * image.size,
            transcendentals=0,
        ),
    )(scalars, *operands)


def local(activations, filters, channel_bias):
    rows, side, depth = activations.shape
    shard, out_local = filters.shape[2:]
    size, chans = lax.axis_size("img"), lax.axis_size("ch")
    me, mine = lax.axis_index("img"), lax.axis_index("ch")
    parts = size // GROUP
    group, rank = me // GROUP, me % GROUP
    members = [[g * GROUP + r for r in range(GROUP)] for g in range(parts)]
    split = out_local // GROUP

    def share(taps):
        return lax.all_to_all(taps, "img", 0, 0, axis_index_groups=members, tiled=True)

    def by_member(array):
        return jnp.moveaxis(array.reshape(*array.shape[:-1], GROUP, split), -2, 0)

    raw = [by_member(filters[0, b]) for b in range(3)]
    chain = []
    others = {}
    for b in range(3):
        for j in range(1, parts):
            sent = raw[b] if len(chain) < 2 else after(raw[b], chain[-2])
            others[j, b] = swap(sent, "img", GROUP * j)
            chain.append(others[j, b])
    lower = share(by_member(filters[1:].reshape(6, shard, out_local)))
    step = GROUP // CHUNKS
    received = []
    for chunk in range(CHUNKS):
        for j in range(1, parts):
            sent = after(lower[chunk * step : (chunk + 1) * step], chain[-2])
            received.append((j, chunk * step, swap(sent, "img", GROUP * j)))
            chain.append(received[-1][2])
    stacked = [jnp.stack(raw, 1)] + [
        jnp.stack([others[j, b] for b in range(3)], 1) for j in range(1, parts)
    ]
    upper = [(j, 0, share(stacked[j])) for j in range(parts)]

    ups = [(i, i + 1) for i in range(size - 1)]
    above = lax.ppermute(activations[-1:], "img", ups)
    below = lax.ppermute(activations[:1], "img", [(j, i) for i, j in ups])
    late = rank >= GROUP // 2
    piece = jnp.where(
        late,
        jnp.concatenate([activations, below], axis=0),
        jnp.concatenate([above, activations], axis=0),
    )
    slots = {(0, 0): piece}
    slots[0, 4] = swap(piece, "img", 4)
    slots[0, 2] = swap(piece, "img", 2)
    slots[0, 6] = swap(slots[0, 4], "img", 2)
    sent = None
    for r in (0, 4, 2, 6):
        for j in range(1, chans):
            slots[j, r] = swap(slots[0, r] if sent is None else after(slots[0, r], sent), "ch", j)
        sent = slots[1, r]
    for (j, r), value in list(slots.items()):
        slots[j, r + 1] = swap(value, "img", 1)
    width = -(-side // 16) * 16
    image = jnp.zeros((chans, GROUP * rows + 2, width, depth), activations.dtype)
    for (j, r), value in slots.items():
        owner = rank ^ r
        start = owner * rows + (owner >= GROUP // 2).astype(jnp.int32)
        image = lax.dynamic_update_slice(image, value[None], (mine ^ j, start, 0, 0))

    scalars = jnp.stack([group * GROUP * rows, group]).astype(jnp.int32)
    bias = lax.dynamic_slice_in_dim(channel_bias, rank * split, split)[None]
    most = (CHUNKS - 1) * (parts - 1)
    acc = conv_call((1, 2), [(0, 0, lower)], scalars, image)
    acc = conv_call((0,), upper, scalars, image, acc)
    acc = conv_call((1, 2), received[:most], scalars, image, acc)
    out = conv_call((1, 2), received[most:], scalars, image, acc, bias)
    out = share(out).reshape(GROUP, rows, side, split)
    return jnp.moveaxis(out, 0, 2).reshape(rows, side, out_local)


def solution(mesh):
    placed = (P("img", None, "ch"), P(None, None, "img", "ch"), P("ch"))
    return jax.shard_map(
        local, mesh=mesh, in_specs=placed, out_specs=P("img", None, "ch"), check_vma=False
    )
```

time: 478 us -> 462 us (0.967)
  waiting for transfers between devices: 240 us -> 178 us
  starting transfers between devices: 37.3 us -> 68.1 us
  Pallas kernels: 73.2 us -> 81.7 us
  other arithmetic: 2.03 us -> 7.91 us
    all_to_all x3, waiting for transfers between devices: 37 us -> 0.01 us  [share(): lax.all_to_all(taps, 'img', 0, 0, axis_index_groups=members, tiled=True)]
    ppermute x18 -> x22, starting transfers between devices: 22 us -> 49.5 us  [swap(): return lax.ppermute(array, axis, [(i, i ^ bit) for i in range(size)])]
    ppermute x18 -> x22, waiting for transfers between devices: 203 us -> 177 us  [swap(): return lax.ppermute(array, axis, [(i, i ^ bit) for i in range(size)])]
    all_to_all x4 -> x0, local copies, waits for them, and re-layouts: 11.7 us -> none  [the longest x3 9.82 us: local(): lax.all_to_all(filters[:, horizontal], 'img', 2, 1, axis_index_groups=mem...]
    unnamed x34 -> x16, local copies, waits for them, and re-layouts: 34.2 us -> 24.2 us
    another operation x2 -> x5, local copies, waits for them, and re-layouts: 0.66 us -> 10.3 us  [the longest x4 9.03 us: by_member(): return jnp.moveaxis(array.reshape(*array.shape[:-1], GROUP, split), -2, 0)]
    pallas_call x3 -> x4, Pallas kernels: 73.2 us -> 81.7 us  [conv_call(): pl.pallas_call(body, grid_spec=pltpu.PrefetchScalarGridSpec(num_scalar_pr...]
    dynamic_update_slice x20 -> x15, local copies, waits for them, and re-layouts: 31.7 us -> 37.4 us  [local(): lax.dynamic_update_slice(image, value[None], (mine ^ j, start, 0, 0))]
  transfers between devices with their start and end apart: 23 -> 27, of which waited for: 7 -> 9; matrix products, arithmetic and copies ran while one was open for 14% -> 15% of each run, Pallas kernels for 10% -> 15%
where the time goes in v2:
time: 462 us; the launch traced here: 460 us
  waiting for transfers between devices  178 us (39%)
  local copies, waits for them, and re-layouts  87.7 us (19%)
  Pallas kernels  81.7 us (18%)
  starting transfers between devices  68.1 us (15%)
  blocking collectives  36.2 us (8%)
  other arithmetic  7.91 us (2%)
    ppermute x22, waiting for transfers between devices, swap(): return lax.ppermute(array, axis, [(i, i ^ bit) for i in range(size)])  177 us
    pallas_call x4, Pallas kernels, conv_call(): pl.pallas_call(body, grid_spec=pltpu.PrefetchScalarGridSpec(num_scalar_pr...  81.7 us
    ppermute x22, starting transfers between devices, swap(): return lax.ppermute(array, axis, [(i, i ^ bit) for i in range(size)])  49.5 us
    dynamic_update_slice x15, local copies, waits for them, and re-layouts, local(): lax.dynamic_update_slice(image, value[None], (mine ^ j, start, 0, 0))  37.4 us
    all_to_all x1, blocking collectives, share(): lax.all_to_all(taps, 'img', 0, 0, axis_index_groups=members, tiled=True)  36.2 us
    unnamed x16, local copies, waits for them, and re-layouts  24.2 us
    all_to_all x3, starting transfers between devices, share(): lax.all_to_all(taps, 'img', 0, 0, axis_index_groups=members, tiled=True)  14.3 us
  transfers between devices with their start and end apart: 27, of which 9 were waited for; matrix products, arithmetic and copies ran while one was open for 15% of the time, Pallas kernels for 15%

profile of v2, /device:TPU:0, one launch (start us, length us, event | category | flops | bytes accessed | tf_op | source)
XLA Modules:
  0.0 460.2 jit_solution(8634780211484283009)
XLA Ops:
  0.0 3.9 slice.32
  3.9 3.5 copy.32
  7.4 2.8 copy.21
  10.3 5.3 %all-to-all-start = ((bf16[8,6,128,256]{3,2,1,0:T(8,128)(2,1)}), bf16[8,6,128,256]{3,2,1,0:T(8,128)(2,1)S(1)}, u32[]{:S(2)}, u32[]{:S(2)}) async-start(bf16[8,6,128,256]{3,2,1,0:T(8,128)(2,1)} %bitcast.63), calls=%async_computation | async-start | bytes 6291456 | tf_op jit(solution)/shard_map/all_to_all | solution.py:135
  18.4 3.0 collective-permute-start.1
  22.4 3.2 maximum_select_fusion.1
  25.6 32.8 %collective-permute-start.2 = (bf16[13,56,1024]{2,1,0:T(8,128)(2,1)}, bf16[13,56,1024]{2,1,0:T(8,128)(2,1)}, u32[]{:S(2)}, u32[]{:S(2)}) collective-permute-start(bf16[13,56,1024]{2,1,0:T(8,128)(2,1)} %maximum_select_fusion.1), channel_id=1, source_target_pairs={{0,8},{2,10},{4,12},{6,14},{8,0},{10,2},{12,4},{14,6},{16,24},{18,... | collective-permute-start | bytes 4472840 | tf_op jit(solution)/shard_map/ppermute | solution.py:16
  61.6 30.4 %collective-permute-done.2 = bf16[13,56,1024]{2,1,0:T(8,128)(2,1)} collective-permute-done((bf16[13,56,1024]{2,1,0:T(8,128)(2,1)}, bf16[13,56,1024]{2,1,0:T(8,128)(2,1)}, u32[]{:S(2)}, u32[]{:S(2)}) %collective-permute-start.2) | collective-permute-done | bytes 1490976 | tf_op jit(solution)/shard_map/ppermute | solution.py:16
  95.5 2.5 fusion.1
  98.0 2.0 copy.34
  100.1 2.1 copy.25
  102.1 2.6 collective-permute-start.17
  104.7 23.9 %collective-permute-done.6 = bf16[13,56,1024]{2,1,0:T(8,128)(2,1)} collective-permute-done((bf16[13,56,1024]{2,1,0:T(8,128)(2,1)}, bf16[13,56,1024]{2,1,0:T(8,128)(2,1)}, u32[]{:S(2)}, u32[]{:S(2)}) %collective-permute-start.6) | collective-permute-done | bytes 1490976 | tf_op jit(solution)/shard_map/ppermute | solution.py:16
  130.1 2.1 copy.35
  132.2 2.0 copy.27
  134.3 2.6 collective-permute-start.21
  138.9 2.1 copy.23
  144.9 3.3 broadcast_in_dim.52
  148.7 22.3 %collective-permute-done.21 = bf16[8,128,256]{2,1,0:T(8,128)(2,1)} collective-permute-done((bf16[8,128,256]{2,1,0:T(8,128)(2,1)}, bf16[8,128,256]{2,1,0:T(8,128)(2,1)}, u32[]{:S(2)}, u32[]{:S(2)}) %collective-permute-start.21) | collective-permute-done | bytes 524320 | tf_op jit(solution)/shard_map/ppermute | solution.py:16
  170.9 10.7 %collective-permute-done.18 = bf16[8,128,256]{2,1,0:T(8,128)(2,1)} collective-permute-done((bf16[8,128,256]{2,1,0:T(8,128)(2,1)}, bf16[8,128,256]{2,1,0:T(8,128)(2,1)}, u32[]{:S(2)}, u32[]{:S(2)}) %collective-permute-start.18) | collective-permute-done | bytes 524320 | tf_op jit(solution)/shard_map/ppermute | solution.py:16
  181.7 2.7 pad_maximum_fusion.1
  188.1 8.4 %copy-done.4 = bf16[2,98,64,1024]{3,2,1,0:T(8,128)(2,1)} copy-done((bf16[2,98,64,1024]{3,2,1,0:T(8,128)(2,1)}, bf16[2,98,64,1024]{3,2,1,0:T(8,128)(2,1)S(1)}, u32[]{:S(2)}) %copy-start.4) | copy-done | bytes 25690136
  197.0 4.3 all-to-all-start.1
  201.3 2.6 bitcast_dynamic-update-slice_fusion.12
  204.0 2.6 bitcast_dynamic-update-slice_fusion.11
  206.6 2.7 bitcast_dynamic-update-slice_fusion.10
  209.2 2.6 bitcast_dynamic-update-slice_fusion.9
  213.6 17.8 %collective-permute-done.8 = bf16[13,56,1024]{2,1,0:T(8,128)(2,1)} collective-permute-done((bf16[13,56,1024]{2,1,0:T(8,128)(2,1)}, bf16[13,56,1024]{2,1,0:T(8,128)(2,1)}, u32[]{:S(2)}, u32[]{:S(2)}) %collective-permute-start.8) | collective-permute-done | bytes 1490976 | tf_op jit(solution)/shard_map/ppermute | solution.py:16
  231.3 2.6 bitcast_dynamic-update-slice_fusion.8
  234.5 2.6 bitcast_dynamic-update-slice_fusion.7
  237.1 2.6 bitcast_dynamic-update-slice_fusion.6
  240.3 2.7 bitcast_dynamic-update-slice_fusion.5
  243.0 2.7 bitcast_dynamic-update-slice_fusion.4
  245.7 4.8 %all-to-all-start.2 = ((bf16[8,3,128,256]{3,2,1,0:T(8,128)(2,1)}), bf16[8,3,128,256]{3,2,1,0:T(8,128)(2,1)}, u32[]{:S(2)}, u32[]{:S(2)}) async-start(bf16[8,3,128,256]{3,2,1,0:T(8,128)(2,1)} %pad_maximum_fusion.1), calls=%async_computation.2 | async-start | bytes 3145728 | tf_op jit(solution)/shard_map/all_to_all | solution.py:135
  250.5 2.7 collective-permute-start.22
  253.2 2.6 bitcast_dynamic-update-slice_fusion.3
  255.8 2.6 bitcast_dynamic-update-slice_fusion.2
  258.5 2.6 bitcast_dynamic-update-slice_fusion.1
  261.1 20.5 %collective-permute-done.19.refs_2_ = bf16[2,6,128,256]{3,2,1,0:T(8,128)(2,1)} collective-permute-done((bf16[2,6,128,256]{3,2,1,0:T(8,128)(2,1)}, bf16[2,6,128,256]{3,2,1,0:T(8,128)(2,1)}, u32[]{:S(2)}, u32[]{:S(2)}) %collective-permute-start.19) | collective-permute-done | bytes 786464 | tf_op jit(solution)/shard_map/ppermute | solution.py:16
  281.6 49.7 %collective-permute-done.22.refs_1_ = bf16[2,6,128,256]{3,2,1,0:T(8,128)(2,1)S(1)} collective-permute-done((bf16[2,6,128,256]{3,2,1,0:T(8,128)(2,1)}, bf16[2,6,128,256]{3,2,1,0:T(8,128)(2,1)S(1)}, u32[]{:S(2)}, u32[]{:S(2)}) %collective-permute-start.22) | collective-permute-done | bytes 786464 | tf_op jit(solution)/shard_map/ppermute | solution.py:16
  332.3 2.7 bitcast_dynamic-update-slice_fusion.refs_0_.refs_1_
  334.9 23.6 %shard_map.37.refs_4_ = f32[96,64,256]{2,1,0:T(8,128)S(1)} custom-call(s32[2]{0:T(128)S(1)} %pad_add_fusion.scalars_ref, bf16[2,98,64,1024]{3,2,1,0:T(8,128)(2,1)} %bitcast_dynamic-update-slice_fusion.refs_0_.refs_1_, bf16[8,6,128,256]{3,2,1,0:T(8,128)(2,1)S(1)} %all-to-all-done.refs_1_), custom_call_target="tpu_custom_call" | custom-call | flops 19327352832 | bytes 25690112 | tf_op jit(solution)/shard_map/pallas_call | solution.py:104
  358.5 2.7 copy-done.3
  361.2 25.6 %shard_map.38.refs_4_ = f32[96,64,256]{2,1,0:T(8,128)S(1)} custom-call(s32[2]{0:T(128)S(1)} %pad_add_fusion.scalars_ref, bf16[2,98,64,1024]{3,2,1,0:T(8,128)(2,1)} %bitcast_dynamic-update-slice_fusion.refs_0_.refs_1_, bf16[2,98,64,1024]{3,2,1,0:T(8,128)(2,1)} %bitcast_dynamic-update-slice_fusion.refs_0_.refs_1_, ...), custom_call_target="tpu_custom_call" | custom-call | flops 19327352832 | bytes 25690112 | tf_op jit(solution)/shard_map/pallas_call | solution.py:104
  386.8 2.7 copy-done.2
  389.5 19.6 %shard_map.39.refs_2_ = f32[96,64,256]{2,1,0:T(8,128)S(1)} custom-call(s32[2]{0:T(128)S(1)} %pad_add_fusion.scalars_ref, bf16[2,98,64,1024]{3,2,1,0:T(8,128)(2,1)} %bitcast_dynamic-update-slice_fusion.refs_0_.refs_1_, bf16[2,6,128,256]{3,2,1,0:T(8,128)(2,1)S(1)} %copy-done.1, bf16[2,6,128,256]{3,2,1,0:T(8,128)(2,1)} %collective-permute-done.19.refs_2_, ...), custom_call_target="tpu_custom_call" | custom-call | flops 14495514624 | bytes 25690112 | tf_op jit(solution)/shard_map/pallas_call | solution.py:104
  409.1 13.0 %shard_map.40 = bf16[96,56,256]{2,1,0:T(8,128)(2,1)S(1)} custom-call(s32[2]{0:T(128)S(1)} %pad_add_fusion.scalars_ref, bf16[2,98,64,1024]{3,2,1,0:T(8,128)(2,1)} %bitcast_dynamic-update-slice_fusion.refs_0_.refs_1_, bf16[2,6,128,256]{3,2,1,0:T(8,128)(2,1)} %collective-permute-done.20.refs_1_, f32[96,64,256]{2,1,0:T(8,128)S(1)} %shard_map.39.refs_2_, ...), custom_call_target="tpu_custom_call" | custom-call | flops 4831838208 | bytes 25690112 | tf_op jit(solution)/shard_map/pallas_call | solution.py:104
  422.1 36.2 %all_to_all.20 = bf16[96,56,256]{2,1,0:T(8,128)(2,1)S(1)} all-to-all(bf16[96,56,256]{2,1,0:T(8,128)(2,1)S(1)} %shard_map.40), channel_id=1, replica_groups={{0,2,4,6,8,10,12,14},{16,18,20,22,24,26,28,30},{1,3,5,7,9,11,13,15},{17..., dimensions={0} | all-to-all | bytes 5505024 | tf_op jit(solution)/shard_map/all_to_all | solution.py:135
  (59 shorter events, 28.3 us)
Async XLA Ops:
  10.3 186.7 %all-to-all-start = ((bf16[8,6,128,256]{3,2,1,0:T(8,128)(2,1)}), bf16[8,6,128,256]{3,2,1,0:T(8,128)(2,1)S(1)}, u32[]{:S(2)}, u32[]{:S(2)}) async-start(bf16[8,6,128,256]{3,2,1,0:T(8,128)(2,1)} %bitcast.63), calls=%async_computation | async-start | bytes 6291456 | tf_op jit(solution)/shard_map/all_to_all | solution.py:135
  17.1 4.4 collective-permute-start
  18.4 4.0 collective-permute-start.1
  25.6 66.4 %collective-permute-start.2 = (bf16[13,56,1024]{2,1,0:T(8,128)(2,1)}, bf16[13,56,1024]{2,1,0:T(8,128)(2,1)}, u32[]{:S(2)}, u32[]{:S(2)}) collective-permute-start(bf16[13,56,1024]{2,1,0:T(8,128)(2,1)} %maximum_select_fusion.1), channel_id=1, source_target_pairs={{0,8},{2,10},{4,12},{6,14},{8,0},{10,2},{12,4},{14,6},{16,24},{18,... | collective-permute-start | bytes 4472840 | tf_op jit(solution)/shard_map/ppermute | solution.py:16
  58.5 35.5 %collective-permute-start.5 = (bf16[13,56,1024]{2,1,0:T(8,128)(2,1)}, bf16[13,56,1024]{2,1,0:T(8,128)(2,1)}, u32[]{:S(2)}, u32[]{:S(2)}) collective-permute-start(bf16[13,56,1024]{2,1,0:T(8,128)(2,1)} %maximum_select_fusion.1), channel_id=1, source_target_pairs={{0,1},{1,0},{2,3},{3,2},{4,5},{5,4},{6,7},{7,6},{8,9},{9,8},{10,11... | collective-permute-start | bytes 4472840 | tf_op jit(solution)/shard_map/ppermute | solution.py:16
  59.9 44.8 %collective-permute-start.3 = (bf16[13,56,1024]{2,1,0:T(8,128)(2,1)}, bf16[13,56,1024]{2,1,0:T(8,128)(2,1)}, u32[]{:S(2)}, u32[]{:S(2)}) collective-permute-start(bf16[13,56,1024]{2,1,0:T(8,128)(2,1)} %maximum_select_fusion.1), channel_id=1, source_target_pairs={{0,4},{2,6},{4,0},{6,2},{8,12},{10,14},{12,8},{14,10},{16,20},{18,... | collective-permute-start | bytes 4472840 | tf_op jit(solution)/shard_map/ppermute | solution.py:16
  94.0 34.7 %collective-permute-start.6 = (bf16[13,56,1024]{2,1,0:T(8,128)(2,1)}, bf16[13,56,1024]{2,1,0:T(8,128)(2,1)}, u32[]{:S(2)}, u32[]{:S(2)}) collective-permute-start(bf16[13,56,1024]{2,1,0:T(8,128)(2,1)} %collective-permute-done.2), channel_id=1, source_target_pairs={{0,1},{1,0},{2,3},{3,2},{4,5},{5,4},{6,7},{7,6},{8,9},{9,8},{10,11... | collective-permute-start | bytes 4472840 | tf_op jit(solution)/shard_map/ppermute | solution.py:16
  102.1 38.8 %collective-permute-start.17 = (bf16[8,128,256]{2,1,0:T(8,128)(2,1)}, bf16[8,128,256]{2,1,0:T(8,128)(2,1)}, u32[]{:S(2)}, u32[]{:S(2)}) collective-permute-start(bf16[8,128,256]{2,1,0:T(8,128)(2,1)} %bitcast.74), channel_id=1, source_target_pairs={{0,16},{2,18},{4,20},{6,22},{8,24},{10,26},{12,28},{14,30},{16,0},... | collective-permute-start | bytes 1572872 | tf_op jit(solution)/shard_map/ppermute | solution.py:16
  104.7 83.3 %collective-permute-start.4 = (bf16[13,56,1024]{2,1,0:T(8,128)(2,1)}, bf16[13,56,1024]{2,1,0:T(8,128)(2,1)}, u32[]{:S(2)}, u32[]{:S(2)}) collective-permute-start(bf16[13,56,1024]{2,1,0:T(8,128)(2,1)} %collective-permute-done.2), channel_id=1, source_target_pairs={{0,4},{2,6},{4,0},{6,2},{8,12},{10,14},{12,8},{14,10},{16,20},{18,... | collective-permute-start | bytes 4472840 | tf_op jit(solution)/shard_map/ppermute | solution.py:16
  128.7 59.4 %collective-permute-start.7 = (bf16[13,56,1024]{2,1,0:T(8,128)(2,1)}, bf16[13,56,1024]{2,1,0:T(8,128)(2,1)}, u32[]{:S(2)}, u32[]{:S(2)}) collective-permute-start(bf16[13,56,1024]{2,1,0:T(8,128)(2,1)} %collective-permute-done.3), channel_id=1, source_target_pairs={{0,1},{1,0},{2,3},{3,2},{4,5},{5,4},{6,7},{7,6},{8,9},{9,8},{10,11... | collective-permute-start | bytes 4472840 | tf_op jit(solution)/shard_map/ppermute | solution.py:16
  134.3 36.7 %collective-permute-start.21 = (bf16[8,128,256]{2,1,0:T(8,128)(2,1)}, bf16[8,128,256]{2,1,0:T(8,128)(2,1)}, u32[]{:S(2)}, u32[]{:S(2)}) collective-permute-start(bf16[8,128,256]{2,1,0:T(8,128)(2,1)} %bitcast.70), channel_id=1, source_target_pairs={{0,16},{2,18},{4,20},{6,22},{8,24},{10,26},{12,28},{14,30},{16,0},... | collective-permute-start | bytes 1572872 | tf_op jit(solution)/shard_map/ppermute | solution.py:16
  141.0 40.7 %collective-permute-start.18 = (bf16[8,128,256]{2,1,0:T(8,128)(2,1)}, bf16[8,128,256]{2,1,0:T(8,128)(2,1)}, u32[]{:S(2)}, u32[]{:S(2)}) collective-permute-start(bf16[8,128,256]{2,1,0:T(8,128)(2,1)} %bitcast.72), channel_id=1, source_target_pairs={{0,16},{2,18},{4,20},{6,22},{8,24},{10,26},{12,28},{14,30},{16,0},... | collective-permute-start | bytes 1572872 | tf_op jit(solution)/shard_map/ppermute | solution.py:16
  144.9 89.0 %collective-permute-start.9 = (bf16[13,56,1024]{2,1,0:T(8,128)(2,1)}, bf16[13,56,1024]{2,1,0:T(8,128)(2,1)}, u32[]{:S(2)}, u32[]{:S(2)}) collective-permute-start(bf16[13,56,1024]{2,1,0:T(8,128)(2,1)} %maximum_select_fusion.1), channel_id=1, source_target_pairs={{0,2},{2,0},{4,6},{6,4},{8,10},{10,8},{12,14},{14,12},{16,18},{18,... | collective-permute-start | bytes 4472840 | tf_op jit(solution)/shard_map/ppermute | solution.py:16
  144.9 3.3 copy-start.5
  184.4 52.8 %collective-permute-start.10 = (bf16[13,56,1024]{2,1,0:T(8,128)(2,1)}, bf16[13,56,1024]{2,1,0:T(8,128)(2,1)}, u32[]{:S(2)}, u32[]{:S(2)}) collective-permute-start(bf16[13,56,1024]{2,1,0:T(8,128)(2,1)} %collective-permute-done.2), channel_id=1, source_target_pairs={{0,2},{2,0},{4,6},{6,4},{8,10},{10,8},{12,14},{14,12},{16,18},{18,... | collective-permute-start | bytes 4472840 | tf_op jit(solution)/shard_map/ppermute | solution.py:16
  184.4 55.4 %collective-permute-start.11 = (bf16[13,56,1024]{2,1,0:T(8,128)(2,1)}, bf16[13,56,1024]{2,1,0:T(8,128)(2,1)}, u32[]{:S(2)}, u32[]{:S(2)}) collective-permute-start(bf16[13,56,1024]{2,1,0:T(8,128)(2,1)} %collective-permute-done.3), channel_id=1, source_target_pairs={{0,2},{2,0},{4,6},{6,4},{8,10},{10,8},{12,14},{14,12},{16,18},{18,... | collective-permute-start | bytes 4472840 | tf_op jit(solution)/shard_map/ppermute | solution.py:16
  188.0 8.5 %copy-start.4 = (bf16[2,98,64,1024]{3,2,1,0:T(8,128)(2,1)}, bf16[2,98,64,1024]{3,2,1,0:T(8,128)(2,1)S(1)}, u32[]{:S(2)}) copy-start(bf16[2,98,64,1024]{3,2,1,0:T(8,128)(2,1)S(1)} %bitcast_dynamic-update-slice_fusion.13) | copy-start | bytes 77070336
  188.0 55.0 %collective-permute-start.12 = (bf16[13,56,1024]{2,1,0:T(8,128)(2,1)}, bf16[13,56,1024]{2,1,0:T(8,128)(2,1)}, u32[]{:S(2)}, u32[]{:S(2)}) collective-permute-start(bf16[13,56,1024]{2,1,0:T(8,128)(2,1)} %collective-permute-done.4), channel_id=1, source_target_pairs={{0,2},{2,0},{4,6},{6,4},{8,10},{10,8},{12,14},{14,12},{16,18},{18,... | collective-permute-start | bytes 4472840 | tf_op jit(solution)/shard_map/ppermute | solution.py:16
  196.5 34.9 %collective-permute-start.8 = (bf16[13,56,1024]{2,1,0:T(8,128)(2,1)}, bf16[13,56,1024]{2,1,0:T(8,128)(2,1)}, u32[]{:S(2)}, u32[]{:S(2)}) collective-permute-start(bf16[13,56,1024]{2,1,0:T(8,128)(2,1)} %collective-permute-done.4), channel_id=1, source_target_pairs={{0,1},{1,0},{2,3},{3,2},{4,5},{5,4},{6,7},{7,6},{8,9},{9,8},{10,11... | collective-permute-start | bytes 4472840 | tf_op jit(solution)/shard_map/ppermute | solution.py:16
  197.0 48.7 %all-to-all-start.1 = ((bf16[8,3,128,256]{3,2,1,0:T(8,128)(2,1)}), bf16[8,3,128,256]{3,2,1,0:T(8,128)(2,1)}, u32[]{:S(2)}, u32[]{:S(2)}) async-start(bf16[8,3,128,256]{3,2,1,0:T(8,128)(2,1)} %copy.28), calls=%async_computation.1 | async-start | bytes 3145728 | tf_op jit(solution)/shard_map/all_to_all | solution.py:135
  231.3 19.2 %collective-permute-start.13 = (bf16[13,56,1024]{2,1,0:T(8,128)(2,1)}, bf16[13,56,1024]{2,1,0:T(8,128)(2,1)}, u32[]{:S(2)}, u32[]{:S(2)}) collective-permute-start(bf16[13,56,1024]{2,1,0:T(8,128)(2,1)} %collective-permute-done.5), channel_id=1, source_target_pairs={{0,2},{2,0},{4,6},{6,4},{8,10},{10,8},{12,14},{14,12},{16,18},{18,... | collective-permute-start | bytes 4472840 | tf_op jit(solution)/shard_map/ppermute | solution.py:16
  233.9 21.9 %collective-permute-start.14 = (bf16[13,56,1024]{2,1,0:T(8,128)(2,1)}, bf16[13,56,1024]{2,1,0:T(8,128)(2,1)}, u32[]{:S(2)}, u32[]{:S(2)}) collective-permute-start(bf16[13,56,1024]{2,1,0:T(8,128)(2,1)} %collective-permute-done.6), channel_id=1, source_target_pairs={{0,2},{2,0},{4,6},{6,4},{8,10},{10,8},{12,14},{14,12},{16,18},{18,... | collective-permute-start | bytes 4472840 | tf_op jit(solution)/shard_map/ppermute | solution.py:16
  237.1 21.3 %collective-permute-start.15 = (bf16[13,56,1024]{2,1,0:T(8,128)(2,1)}, bf16[13,56,1024]{2,1,0:T(8,128)(2,1)}, u32[]{:S(2)}, u32[]{:S(2)}) collective-permute-start(bf16[13,56,1024]{2,1,0:T(8,128)(2,1)} %collective-permute-done.7), channel_id=1, source_target_pairs={{0,2},{2,0},{4,6},{6,4},{8,10},{10,8},{12,14},{14,12},{16,18},{18,... | collective-permute-start | bytes 4472840 | tf_op jit(solution)/shard_map/ppermute | solution.py:16
  239.8 92.5 %collective-permute-start.16 = (bf16[13,56,1024]{2,1,0:T(8,128)(2,1)}, bf16[13,56,1024]{2,1,0:T(8,128)(2,1)}, u32[]{:S(2)}, u32[]{:S(2)}) collective-permute-start(bf16[13,56,1024]{2,1,0:T(8,128)(2,1)} %collective-permute-done.8), channel_id=1, source_target_pairs={{0,2},{2,0},{4,6},{6,4},{8,10},{10,8},{12,14},{14,12},{16,18},{18,... | collective-permute-start | bytes 4472840 | tf_op jit(solution)/shard_map/ppermute | solution.py:16
  243.0 38.6 %collective-permute-start.19 = (bf16[2,6,128,256]{3,2,1,0:T(8,128)(2,1)}, bf16[2,6,128,256]{3,2,1,0:T(8,128)(2,1)}, u32[]{:S(2)}, u32[]{:S(2)}) collective-permute-start(bf16[2,6,128,256]{3,2,1,0:T(8,128)(2,1)} %get-tuple-element.17), channel_id=1, source_target_pairs={{0,16},{2,18},{4,20},{6,22},{8,24},{10,26},{12,28},{14,30},{16,0},... | collective-permute-start | bytes 2359304 | tf_op jit(solution)/shard_map/ppermute | solution.py:16
  245.7 115.5 %all-to-all-start.2 = ((bf16[8,3,128,256]{3,2,1,0:T(8,128)(2,1)}), bf16[8,3,128,256]{3,2,1,0:T(8,128)(2,1)}, u32[]{:S(2)}, u32[]{:S(2)}) async-start(bf16[8,3,128,256]{3,2,1,0:T(8,128)(2,1)} %pad_maximum_fusion.1), calls=%async_computation.2 | async-start | bytes 3145728 | tf_op jit(solution)/shard_map/all_to_all | solution.py:135
  250.5 80.9 %collective-permute-start.22 = (bf16[2,6,128,256]{3,2,1,0:T(8,128)(2,1)}, bf16[2,6,128,256]{3,2,1,0:T(8,128)(2,1)S(1)}, u32[]{:S(2)}, u32[]{:S(2)}) collective-permute-start(bf16[2,6,128,256]{3,2,1,0:T(8,128)(2,1)} %get-tuple-element.19), channel_id=1, source_target_pairs={{0,16},{2,18},{4,20},{6,22},{8,24},{10,26},{12,28},{14,30},{16,0},... | collective-permute-start | bytes 2359304 | tf_op jit(solution)/shard_map/ppermute | solution.py:16
  281.6 127.4 %collective-permute-start.20 = (bf16[2,6,128,256]{3,2,1,0:T(8,128)(2,1)}, bf16[2,6,128,256]{3,2,1,0:T(8,128)(2,1)}, u32[]{:S(2)}, u32[]{:S(2)}) collective-permute-start(bf16[2,6,128,256]{3,2,1,0:T(8,128)(2,1)} %get-tuple-element.18), channel_id=1, source_target_pairs={{0,16},{2,18},{4,20},{6,22},{8,24},{10,26},{12,28},{14,30},{16,0},... | collective-permute-start | bytes 2359304 | tf_op jit(solution)/shard_map/ppermute | solution.py:16
  331.4 0.9 copy-start
  332.3 57.2 %collective-permute-start.23 = (bf16[2,6,128,256]{3,2,1,0:T(8,128)(2,1)}, bf16[2,6,128,256]{3,2,1,0:T(8,128)(2,1)}, u32[]{:S(2)}, u32[]{:S(2)}) collective-permute-start(bf16[2,6,128,256]{3,2,1,0:T(8,128)(2,1)} %get-tuple-element.20), channel_id=1, source_target_pairs={{0,16},{2,18},{4,20},{6,22},{8,24},{10,26},{12,28},{14,30},{16,0},... | collective-permute-start | bytes 2359304 | tf_op jit(solution)/shard_map/ppermute | solution.py:16
  358.5 2.7 copy-start.3
  361.2 28.3 %copy-start.1 = (bf16[2,6,128,256]{3,2,1,0:T(8,128)(2,1)S(1)}, bf16[2,6,128,256]{3,2,1,0:T(8,128)(2,1)}, u32[]{:S(2)}) copy-start(bf16[2,6,128,256]{3,2,1,0:T(8,128)(2,1)} %copy-done) | copy-start | bytes 2359300
  386.8 2.7 copy-start.2

commit v3 on v2

v3 whole, which is shorter than its diff:
```python
import jax
import jax.numpy as jnp
from jax import lax
from jax.experimental import pallas as pl
from jax.experimental.pallas import tpu as pltpu
from jax.sharding import PartitionSpec as P

SIDE = 56
GROUP = 8
TILE = 8
CHUNKS = 4


def swap(array, axis, bit):
    size = lax.axis_size(axis)
    return lax.ppermute(array, axis, [(i, i ^ bit) for i in range(size)])


def after(array, *others):
    return lax.optimization_barrier((array, *others))[0]


def conv_call(taps, pieces, scalars, image, acc=None, bias=None):
    blocks, padded_rows, width, depth = image.shape
    shard, out_width = pieces[0][2].shape[2:]
    row_count = padded_rows - 3
    offsets = sorted({offset for offset, _, _ in pieces})
    per_group = GROUP * shard // depth
    final = bias is not None
    assert row_count % TILE == 0 and SIDE % TILE == 0

    windows = {}
    for offset in offsets:
        low = min(start for o, start, _ in pieces if o == offset) * shard
        high = max(start + a.shape[0] for o, start, a in pieces if o == offset) * shard
        if low // depth == (high - 1) // depth:
            windows[offset] = (1, low // depth, high - low, low % depth)
        else:
            windows[offset] = (per_group, 0, depth, 0)

    def body(scalars_ref, *refs):
        refs = list(refs)
        images = {}
        for offset in offsets:
            images[offset] = refs.pop(0), *(refs.pop(0) for v in taps if v != 1)
        weights = [refs.pop(0) for _ in pieces]
        acc_ref = refs.pop(0) if acc is not None else None
        bias_ref = refs.pop(0) if final else None
        out = refs.pop(0)

        operands, columns = [], []
        for (offset, start, array), weight in zip(pieces, weights):
            count, first_block, size, first_lane = windows[offset]
            main, *outer = images[offset]
            at, lanes = 0, array.shape[0] * shard
            while at < lanes:
                inner, lane = divmod(start * shard + at, depth)
                inner, lane = inner - first_block, lane - first_lane
                length = min(size - lane, lanes - at)
                window = pl.ds(lane, length)
                edges = list(outer)
                for index, vertical in enumerate(taps):
                    rows = main[inner, :, :, window]
                    if vertical == 0:
                        rows = jnp.concatenate(
                            [edges.pop(0)[inner, :, :, window], rows[:-1]], axis=0
                        )
                    if vertical == 2:
                        rows = jnp.concatenate(
                            [rows[1:], edges.pop(0)[inner, :, :, window]], axis=0
                        )
                    operands.append(rows.reshape(TILE * width, length))
                    members = pl.ds(at // shard, length // shard)
                    columns.append(
                        [
                            weight[members, 3 * index + b].reshape(length, out_width)
                            for b in range(3)
                        ]
                    )
                at += length
        operand = jnp.concatenate(operands, axis=1)
        total = None
        for horizontal in range(3):
            value = jnp.dot(
                operand,
                jnp.concatenate([c[horizontal] for c in columns], axis=0),
                preferred_element_type=jnp.float32,
            ).reshape(TILE, width, out_width)
            if horizontal != 1:
                value = pltpu.roll(value, (1 - horizontal) % width, 1)
            total = value if total is None else total + value
        if acc_ref is not None:
            total = total + acc_ref[...]
        if final:
            total = (total + bias_ref[...].reshape(1, 1, -1))[:, : out.shape[1]]
        out[...] = total.astype(out.dtype)

    def image_spec(offset, vertical):
        count, first_block, size, first_lane = windows[offset]
        rows = TILE if vertical == 1 else 1

        def place(t, s):
            row = t * TILE + 1
            if vertical == 0:
                row = jnp.where((s[0] + t * TILE) % SIDE == 0, row_count + 2, row - 1)
            if vertical == 2:
                row = jnp.where((s[0] + (t + 1) * TILE) % SIDE == 0, row_count + 2, row + TILE)
            return ((s[1] ^ offset) * per_group + first_block, row, 0, first_lane)

        return pl.BlockSpec(tuple(pl.Element(n) for n in (count, rows, width, size)), place)

    out_cols = SIDE if final else width
    in_specs, operands = [], []
    for offset in offsets:
        for vertical in [1] + [v for v in taps if v != 1]:
            in_specs.append(image_spec(offset, vertical))
            operands.append(image)
    for _, _, array in pieces:
        in_specs.append(pl.BlockSpec(array.shape, lambda t, s: (0, 0, 0, 0)))
        operands.append(array)
    if acc is not None:
        in_specs.append(pl.BlockSpec((TILE, width, out_width), lambda t, s: (t, 0, 0)))
        operands.append(acc)
    if final:
        in_specs.append(pl.BlockSpec((1, out_width), lambda t, s: (0, 0)))
        operands.append(bias)
    return pl.pallas_call(
        body,
        grid_spec=pltpu.PrefetchScalarGridSpec(
            num_scalar_prefetch=1,
            grid=(row_count // TILE,),
            in_specs=in_specs,
            out_specs=pl.BlockSpec((TILE, out_cols, out_width), lambda t, s: (t, 0, 0)),
        ),
        out_shape=jax.ShapeDtypeStruct(
            (row_count, out_cols, out_width), jnp.bfloat16 if final else jnp.float32
        ),
        compiler_params=pltpu.CompilerParams(vmem_limit_bytes=40 * 1024 * 1024),
        cost_estimate=pl.CostEstimate(flops=1024, bytes_accessed=1024, transcendentals=0),
    )(scalars, *operands)


def by_member(filters, first, count):
    _, across, shard, out_local = filters.shape
    split = out_local // GROUP
    if split % 128:
        taps = filters[first : first + count].reshape(count * across, shard, out_local)
        return jnp.stack([taps[..., r * split : (r + 1) * split] for r in range(GROUP)])

    def body(taps, out):
        out[...] = taps[...].reshape(out.shape)

    return pl.pallas_call(
        body,
        grid=(GROUP, count),
        in_specs=[
            pl.BlockSpec((1, across, shard, split), lambda r, v: (first + v, 0, 0, r))
        ],
        out_specs=pl.BlockSpec((1, across, shard, split), lambda r, v: (r, v, 0, 0)),
        out_shape=jax.ShapeDtypeStruct((GROUP, count * across, shard, split), filters.dtype),
    )(filters)


def local(activations, filters, channel_bias):
    rows, side, depth = activations.shape
    shard, out_local = filters.shape[2:]
    size, chans = lax.axis_size("img"), lax.axis_size("ch")
    me, mine = lax.axis_index("img"), lax.axis_index("ch")
    parts = size // GROUP
    group, rank = me // GROUP, me % GROUP
    members = [[g * GROUP + r for r in range(GROUP)] for g in range(parts)]
    split = out_local // GROUP

    def share(taps):
        return lax.all_to_all(taps, "img", 0, 0, axis_index_groups=members, tiled=True)

    raw = [swap(filters[0], "img", GROUP * j) for j in range(1, parts)]

    ups = [(i, i + 1) for i in range(size - 1)]
    above = lax.ppermute(activations[-1:], "img", ups)
    below = lax.ppermute(activations[:1], "img", [(j, i) for i, j in ups])
    piece = jnp.where(
        rank >= GROUP // 2,
        jnp.concatenate([activations, below], axis=0),
        jnp.concatenate([above, activations], axis=0),
    )
    slots = {(0, 0): piece}

    def cross(r, *others):
        sent = after(slots[0, r], *others) if others else slots[0, r]
        for j in range(1, chans):
            slots[j, r] = swap(sent, "ch", j)

    cross(0)
    slots[0, 4] = swap(piece, "img", 4)
    slots[0, 2] = swap(piece, "img", 2)
    cross(4, slots[1, 0])
    cross(2, slots[1, 4])

    lower = share(after(by_member(filters, 1, 2), slots[0, 4], slots[0, 2]))
    step = GROUP // CHUNKS
    received = []

    def exchange(chunk, *others):
        sent = after(lower[chunk * step : (chunk + 1) * step], *others)
        for j in range(1, parts):
            received.append((j, chunk * step, swap(sent, "img", GROUP * j)))

    exchange(0, *raw)
    exchange(1, *raw)
    slots[0, 6] = swap(after(slots[0, 4], lower), "img", 2)
    exchange(2, received[0][2])
    cross(6, slots[1, 2])
    upper = [
        (j, 0, share(by_member(after(taps, received[0][2]), 0, 1)))
        for j, taps in enumerate([filters] + [array[None] for array in raw])
    ]
    exchange(3, received[parts - 1][2])

    for (j, r), value in list(slots.items()):
        slots[j, r + 1] = swap(value, "img", 1)
    width = -(-side // 16) * 16
    image = jnp.zeros((chans, GROUP * rows + 3, width, depth), activations.dtype)
    for (j, r), value in slots.items():
        owner = rank ^ r
        start = owner * rows + (owner >= GROUP // 2).astype(jnp.int32)
        image = lax.dynamic_update_slice(image, value[None], (mine ^ j, start, 0, 0))

    scalars = jnp.stack([group * GROUP * rows, group]).astype(jnp.int32)
    bias = lax.dynamic_slice_in_dim(channel_bias, rank * split, split)[None]
    most = (CHUNKS - 1) * (parts - 1)
    acc = conv_call((1, 2), [(0, 0, lower)], scalars, image)
    acc = conv_call((0,), upper, scalars, image, acc)
    acc = conv_call((1, 2), received[:most], scalars, image, acc)
    out = conv_call((1, 2), received[most:], scalars, image, acc, bias)
    out = share(out).reshape(GROUP, rows, side, split)
    return jnp.moveaxis(out, 0, 2).reshape(rows, side, out_local)


def solution(mesh):
    placed = (P("img", None, "ch"), P(None, None, "img", "ch"), P("ch"))
    return jax.shard_map(
        local, mesh=mesh, in_specs=placed, out_specs=P("img", None, "ch"), check_vma=False
    )
```

time: 462 us -> 432 us (0.935)
  local copies, waits for them, and re-layouts: 87.7 us -> 46.8 us
  starting transfers between devices: 68.1 us -> 36.9 us
  waiting for transfers between devices: 178 us -> 207 us
  Pallas kernels: 81.7 us -> 101 us
  other arithmetic: 7.91 us -> 2.56 us
    all_to_all x3, waiting for transfers between devices: 0.01 us -> 30.4 us  [share(): lax.all_to_all(taps, 'img', 0, 0, axis_index_groups=members, tiled=True)]
    ppermute x22 -> x20, starting transfers between devices: 49.5 us -> 20.3 us  [swap(): return lax.ppermute(array, axis, [(i, i ^ bit) for i in range(size)])]
    pallas_call x0 -> x3, Pallas kernels: none -> 20.6 us  [by_member(): pl.pallas_call(body, grid=(GROUP, count), in_specs=[pl.BlockSpec((1, acro...]
    unnamed x16 -> x20, local copies, waits for them, and re-layouts: 24.2 us -> 6.97 us
    another operation x5 -> x0, local copies, waits for them, and re-layouts: 10.3 us -> none  [the longest x4 9.03 us: by_member(): return jnp.moveaxis(array.reshape(*array.shape[:-1], GROUP, split), -2, 0)]
    dynamic_update_slice x15, local copies, waits for them, and re-layouts: 37.4 us -> 28.7 us  [local(): lax.dynamic_update_slice(image, value[None], (mine ^ j, start, 0, 0))]
    slice x3 -> x1, local copies, waits for them, and re-layouts: 8.19 us -> 1.47 us  [exchange(): sent = after(lower[chunk * step:(chunk + 1) * step], *others)]
    ppermute x22 -> x20, waiting for transfers between devices: 177 us -> 176 us  [swap(): return lax.ppermute(array, axis, [(i, i ^ bit) for i in range(size)])]
  transfers between devices with their start and end apart: 27 -> 25, of which waited for: 9 -> 11; matrix products, arithmetic and copies ran while one was open for 15% -> 9% of each run, Pallas kernels for 15% -> 21%
where the time goes in v3:
time: 432 us; the launch traced here: 431 us
  waiting for transfers between devices  207 us (48%)
  Pallas kernels  101 us (23%)
  local copies, waits for them, and re-layouts  46.8 us (11%)
  starting transfers between devices  36.9 us (9%)
  blocking collectives  36.5 us (8%)
    ppermute x20, waiting for transfers between devices, swap(): return lax.ppermute(array, axis, [(i, i ^ bit) for i in range(size)])  176 us
    pallas_call x4, Pallas kernels, conv_call(): pl.pallas_call(body, grid_spec=pltpu.PrefetchScalarGridSpec(num_scalar_pr...  80 us
    all_to_all x1, blocking collectives, share(): lax.all_to_all(taps, 'img', 0, 0, axis_index_groups=members, tiled=True)  36.5 us
    all_to_all x3, waiting for transfers between devices, share(): lax.all_to_all(taps, 'img', 0, 0, axis_index_groups=members, tiled=True)  30.4 us
    dynamic_update_slice x15, local copies, waits for them, and re-layouts, local(): lax.dynamic_update_slice(image, value[None], (mine ^ j, start, 0, 0))  28.7 us
    pallas_call x3, Pallas kernels, by_member(): pl.pallas_call(body, grid=(GROUP, count), in_specs=[pl.BlockSpec((1, acro...  20.6 us
    ppermute x20, starting transfers between devices, swap(): return lax.ppermute(array, axis, [(i, i ^ bit) for i in range(size)])  20.3 us
    all_to_all x3, starting transfers between devices, share(): lax.all_to_all(taps, 'img', 0, 0, axis_index_groups=members, tiled=True)  12.2 us
  transfers between devices with their start and end apart: 25, of which 11 were waited for; matrix products, arithmetic and copies ran while one was open for 9% of the time, Pallas kernels for 21%

profile of v3, /device:TPU:0, one launch (start us, length us, event | category | flops | bytes accessed | tf_op | source)
XLA Modules:
  0.0 430.7 jit_solution(17748958865431146107)
XLA Ops:
  2.3 3.0 collective-permute-start.1
  6.3 2.1 maximum_select_fusion.1
  8.3 7.6 %collective-permute-start.3 = (bf16[13,56,1024]{2,1,0:T(8,128)(2,1)S(1)}, bf16[13,56,1024]{2,1,0:T(8,128)(2,1)}, u32[]{:S(2)}, u32[]{:S(2)}) collective-permute-start(bf16[13,56,1024]{2,1,0:T(8,128)(2,1)S(1)} %maximum_select_fusion.1), channel_id=1, source_target_pairs={{0,8},{2,10},{4,12},{6,14},{8,0},{10,2},{12,4},{14,6},{16,24},{18,... | collective-permute-start | bytes 4472840 | tf_op jit(solution)/shard_map/ppermute | solution.py:16
  15.9 9.8 %shard_map.37 = bf16[8,6,128,256]{3,2,1,0:T(8,128)(2,1)} custom-call(bf16[3,3,128,2048]{3,2,1,0:T(8,128)(2,1)} %taps.2), custom_call_target="tpu_custom_call" | custom-call | tf_op jit(solution)/shard_map/pallas_call | solution.py:153
  25.7 20.9 %collective-permute-done.3 = bf16[13,56,1024]{2,1,0:T(8,128)(2,1)} collective-permute-done((bf16[13,56,1024]{2,1,0:T(8,128)(2,1)S(1)}, bf16[13,56,1024]{2,1,0:T(8,128)(2,1)}, u32[]{:S(2)}, u32[]{:S(2)}) %collective-permute-start.3) | collective-permute-done | bytes 1490976 | tf_op jit(solution)/shard_map/ppermute | solution.py:16
  46.6 1.7 collective-permute-done.4
  48.4 3.6 all-to-all-start
  52.0 1.6 collective-permute-start.2
  53.6 2.7 slice_bitcast_fusion
  56.3 2.0 collective-permute-start.17
  58.3 29.0 %collective-permute-done.2 = bf16[13,56,1024]{2,1,0:T(8,128)(2,1)} collective-permute-done((bf16[13,56,1024]{2,1,0:T(8,128)(2,1)}, bf16[13,56,1024]{2,1,0:T(8,128)(2,1)}, u32[]{:S(2)}, u32[]{:S(2)}) %collective-permute-start.2) | collective-permute-done | bytes 1490976 | tf_op jit(solution)/shard_map/ppermute | solution.py:16
  87.3 1.5 collective-permute-start.5
  88.8 30.4 %all-to-all-done.refs_2_ = bf16[8,6,128,256]{3,2,1,0:T(8,128)(2,1)S(1)} async-done(((bf16[8,6,128,256]{3,2,1,0:T(8,128)(2,1)}), bf16[8,6,128,256]{3,2,1,0:T(8,128)(2,1)S(1)}, u32[]{:S(2)}, u32[]{:S(2)}) %all-to-all-start) | async-done | bytes 3145760 | tf_op jit(solution)/shard_map/all_to_all | solution.py:175
  119.2 1.5 fusion.1
  120.6 7.0 %collective-permute-done.17 = bf16[3,128,2048]{2,1,0:T(8,128)(2,1)} collective-permute-done((bf16[3,128,2048]{2,1,0:T(8,128)(2,1)}, bf16[3,128,2048]{2,1,0:T(8,128)(2,1)}, u32[]{:S(2)}, u32[]{:S(2)}) %collective-permute-start.17) | collective-permute-done | bytes 1572896 | tf_op jit(solution)/shard_map/ppermute | solution.py:16
  127.6 36.4 %collective-permute-done.20.refs_2_ = bf16[2,6,128,256]{3,2,1,0:T(8,128)(2,1)S(1)} collective-permute-done((bf16[2,6,128,256]{3,2,1,0:T(8,128)(2,1)S(1)}, bf16[2,6,128,256]{3,2,1,0:T(8,128)(2,1)S(1)}, u32[]{:S(2)}, u32[]{:S(2)}) %collective-permute-start.20) | collective-permute-done | bytes 786464 | tf_op jit(solution)/shard_map/ppermute | solution.py:16
  164.9 5.4 %shard_map.38 = bf16[8,3,128,256]{3,2,1,0:T(8,128)(2,1)} custom-call(bf16[3,3,128,2048]{3,2,1,0:T(8,128)(2,1)} %taps.2), custom_call_target="tpu_custom_call" | custom-call | tf_op jit(solution)/shard_map/pallas_call | solution.py:153
  170.3 4.3 %all-to-all-start.1 = ((bf16[8,3,128,256]{3,2,1,0:T(8,128)(2,1)}), bf16[8,3,128,256]{3,2,1,0:T(8,128)(2,1)}, u32[]{:S(2)}, u32[]{:S(2)}) async-start(bf16[8,3,128,256]{3,2,1,0:T(8,128)(2,1)} %shard_map.38), calls=%async_computation.1 | async-start | bytes 3145728 | tf_op jit(solution)/shard_map/all_to_all | solution.py:175
  175.3 1.8 collective-permute-start.7
  177.2 3.3 broadcast_in_dim.55
  181.6 1.6 bitcast_dynamic-update-slice_fusion.14
  183.1 26.8 %collective-permute-done.6 = bf16[13,56,1024]{2,1,0:T(8,128)(2,1)} collective-permute-done((bf16[13,56,1024]{2,1,0:T(8,128)(2,1)}, bf16[13,56,1024]{2,1,0:T(8,128)(2,1)}, u32[]{:S(2)}, u32[]{:S(2)}) %collective-permute-start.6) | collective-permute-done | bytes 1490976 | tf_op jit(solution)/shard_map/ppermute | solution.py:16
  209.9 16.8 %collective-permute-done.7 = bf16[13,56,1024]{2,1,0:T(8,128)(2,1)} collective-permute-done((bf16[13,56,1024]{2,1,0:T(8,128)(2,1)}, bf16[13,56,1024]{2,1,0:T(8,128)(2,1)}, u32[]{:S(2)}, u32[]{:S(2)}) %collective-permute-start.7) | collective-permute-done | bytes 1490976 | tf_op jit(solution)/shard_map/ppermute | solution.py:16
  227.2 1.6 bitcast_dynamic-update-slice_fusion.13
  228.8 1.6 bitcast_dynamic-update-slice_fusion.12
  230.4 1.6 bitcast_dynamic-update-slice_fusion.11
  232.0 1.6 bitcast_dynamic-update-slice_fusion.10
  233.6 31.8 %collective-permute-done.18.refs_3_ = bf16[2,6,128,256]{3,2,1,0:T(8,128)(2,1)S(1)} collective-permute-done((bf16[2,6,128,256]{3,2,1,0:T(8,128)(2,1)S(1)}, bf16[2,6,128,256]{3,2,1,0:T(8,128)(2,1)S(1)}, u32[]{:S(2)}, u32[]{:S(2)}) %collective-permute-start.18) | collective-permute-done | bytes 786464 | tf_op jit(solution)/shard_map/ppermute | solution.py:16
  266.3 5.4 %shard_map.39 = bf16[8,3,128,256]{3,2,1,0:T(8,128)(2,1)} custom-call(bf16[1,3,128,2048]{3,2,1,0:T(8,128)(2,1)} %bitcast.21.taps), custom_call_target="tpu_custom_call" | custom-call | tf_op jit(solution)/shard_map/pallas_call | solution.py:153
  271.7 4.3 all-to-all-start.2
  276.0 2.6 bitcast_dynamic-update-slice_fusion.9
  279.1 2.6 bitcast_dynamic-update-slice_fusion.8
  281.8 2.7 bitcast_dynamic-update-slice_fusion.7
  284.9 2.7 bitcast_dynamic-update-slice_fusion.6
  287.6 2.7 bitcast_dynamic-update-slice_fusion.5
  290.3 2.6 bitcast_dynamic-update-slice_fusion.4
  292.9 2.9 collective-permute-start.21
  297.1 1.3 bitcast_dynamic-update-slice_fusion.2
  299.7 1.3 bitcast_dynamic-update-slice_fusion.refs_0_.refs_1_.refs_2_.refs_3_
  301.8 23.7 %shard_map.40.refs_6_ = f32[96,64,256]{2,1,0:T(8,128)S(1)} custom-call(s32[2]{0:T(128)S(1)} %pad_add_fusion.scalars_ref, bf16[2,99,64,1024]{3,2,1,0:T(8,128)(2,1)} %bitcast_dynamic-update-slice_fusion.refs_0_.refs_1_.refs_2_.refs_3_, bf16[2,99,64,1024]{3,2,1,0:T(8,128)(2,1)} %bitcast_dynamic-update-slice_fusion.refs_0_.refs_1_.refs_2_.refs_3_, ...), custom_call_target="tpu_custom_call" | custom-call | flops 1024 | bytes 1024 | tf_op jit(solution)/shard_map/pallas_call | solution.py:127
  325.5 2.6 copy-done.1
  328.1 26.0 %shard_map.41.refs_5_ = f32[96,64,256]{2,1,0:T(8,128)S(1)} custom-call(s32[2]{0:T(128)S(1)} %pad_add_fusion.scalars_ref, bf16[2,99,64,1024]{3,2,1,0:T(8,128)(2,1)} %bitcast_dynamic-update-slice_fusion.refs_0_.refs_1_.refs_2_.refs_3_, bf16[2,99,64,1024]{3,2,1,0:T(8,128)(2,1)} %bitcast_dynamic-update-slice_fusion.refs_0_.refs_1_.refs_2_.refs_3_, ...), custom_call_target="tpu_custom_call" | custom-call | flops 1024 | bytes 1024 | tf_op jit(solution)/shard_map/pallas_call | solution.py:127
  354.0 2.6 copy-done
  356.6 5.3 %collective-permute-done.21.refs_4_ = bf16[2,6,128,256]{3,2,1,0:T(8,128)(2,1)} collective-permute-done((bf16[2,6,128,256]{3,2,1,0:T(8,128)(2,1)}, bf16[2,6,128,256]{3,2,1,0:T(8,128)(2,1)}, u32[]{:S(2)}, u32[]{:S(2)}) %collective-permute-start.21) | collective-permute-done | bytes 786464 | tf_op jit(solution)/shard_map/ppermute | solution.py:16
  361.9 19.4 %shard_map.42.refs_3_ = f32[96,64,256]{2,1,0:T(8,128)S(1)} custom-call(s32[2]{0:T(128)S(1)} %pad_add_fusion.scalars_ref, bf16[2,99,64,1024]{3,2,1,0:T(8,128)(2,1)} %bitcast_dynamic-update-slice_fusion.refs_0_.refs_1_.refs_2_.refs_3_, bf16[2,99,64,1024]{3,2,1,0:T(8,128)(2,1)} %bitcast_dynamic-update-slice_fusion.refs_0_.refs_1_.refs_2_.refs_3_, ...), custom_call_target="tpu_custom_call" | custom-call | flops 1024 | bytes 1024 | tf_op jit(solution)/shard_map/pallas_call | solution.py:127
  381.4 10.9 %shard_map.43 = bf16[96,56,256]{2,1,0:T(8,128)(2,1)S(1)} custom-call(s32[2]{0:T(128)S(1)} %pad_add_fusion.scalars_ref, bf16[2,99,64,1024]{3,2,1,0:T(8,128)(2,1)} %bitcast_dynamic-update-slice_fusion.refs_0_.refs_1_.refs_2_.refs_3_, bf16[2,99,64,1024]{3,2,1,0:T(8,128)(2,1)} %bitcast_dynamic-update-slice_fusion.refs_0_.refs_1_.refs_2_.refs_3_, ...), custom_call_target="tpu_custom_call" | custom-call | flops 1024 | bytes 1024 | tf_op jit(solution)/shard_map/pallas_call | solution.py:127
  392.3 36.5 %all_to_all.20 = bf16[96,56,256]{2,1,0:T(8,128)(2,1)S(1)} all-to-all(bf16[96,56,256]{2,1,0:T(8,128)(2,1)S(1)} %shard_map.43), channel_id=1, replica_groups={{0,2,4,6,8,10,12,14},{16,18,20,22,24,26,28,30},{1,3,5,7,9,11,13,15},{17..., dimensions={0} | all-to-all | bytes 5505024 | tf_op jit(solution)/shard_map/all_to_all | solution.py:175
  428.8 1.9 copy.5
  (54 shorter events, 11.7 us)
Async XLA Ops:
  1.0 4.4 %collective-permute-start = (bf16[1,56,1024]{2,1,0:T(8,128)(2,1)S(1)}, bf16[1,56,1024]{2,1,0:T(8,128)(2,1)S(1)}, u32[]{:S(2)}, u32[]{:S(2)}) collective-permute-start(bf16[1,56,1024]{2,1,0:T(8,128)(2,1)S(1)} %get-tuple-element.32), channel_id=1, source_target_pairs={{2,0},{4,2},{6,4},{8,6},{10,8},{12,10},{14,12},{16,14},{18,16},{20... | collective-permute-start | bytes 344072 | tf_op jit(solution)/shard_map/ppermute | solution.py:181
  2.3 4.0 collective-permute-start.1
  8.3 17.4 %copy-start.8 = (bf16[13,56,1024]{2,1,0:T(8,128)(2,1)}, bf16[13,56,1024]{2,1,0:T(8,128)(2,1)S(1)}, u32[]{:S(2)}) copy-start(bf16[13,56,1024]{2,1,0:T(8,128)(2,1)S(1)} %maximum_select_fusion.1) | copy-start | bytes 4472836
  8.3 38.3 %collective-permute-start.3 = (bf16[13,56,1024]{2,1,0:T(8,128)(2,1)S(1)}, bf16[13,56,1024]{2,1,0:T(8,128)(2,1)}, u32[]{:S(2)}, u32[]{:S(2)}) collective-permute-start(bf16[13,56,1024]{2,1,0:T(8,128)(2,1)S(1)} %maximum_select_fusion.1), channel_id=1, source_target_pairs={{0,8},{2,10},{4,12},{6,14},{8,0},{10,2},{12,4},{14,6},{16,24},{18,... | collective-permute-start | bytes 4472840 | tf_op jit(solution)/shard_map/ppermute | solution.py:16
  15.9 32.5 %collective-permute-start.4 = (bf16[13,56,1024]{2,1,0:T(8,128)(2,1)S(1)}, bf16[13,56,1024]{2,1,0:T(8,128)(2,1)}, u32[]{:S(2)}, u32[]{:S(2)}) collective-permute-start(bf16[13,56,1024]{2,1,0:T(8,128)(2,1)S(1)} %maximum_select_fusion.1), channel_id=1, source_target_pairs={{0,4},{2,6},{4,0},{6,2},{8,12},{10,14},{12,8},{14,10},{16,20},{18,... | collective-permute-start | bytes 4472840 | tf_op jit(solution)/shard_map/ppermute | solution.py:16
  48.4 70.8 %all-to-all-start = ((bf16[8,6,128,256]{3,2,1,0:T(8,128)(2,1)}), bf16[8,6,128,256]{3,2,1,0:T(8,128)(2,1)S(1)}, u32[]{:S(2)}, u32[]{:S(2)}) async-start(bf16[8,6,128,256]{3,2,1,0:T(8,128)(2,1)} %shard_map.37), calls=%async_computation | async-start | bytes 6291456 | tf_op jit(solution)/shard_map/all_to_all | solution.py:175
  52.0 35.3 %collective-permute-start.2 = (bf16[13,56,1024]{2,1,0:T(8,128)(2,1)}, bf16[13,56,1024]{2,1,0:T(8,128)(2,1)}, u32[]{:S(2)}, u32[]{:S(2)}) collective-permute-start(bf16[13,56,1024]{2,1,0:T(8,128)(2,1)} %copy-done.8), channel_id=1, source_target_pairs={{0,1},{1,0},{2,3},{3,2},{4,5},{5,4},{6,7},{7,6},{8,9},{9,8},{10,11... | collective-permute-start | bytes 4472840 | tf_op jit(solution)/shard_map/ppermute | solution.py:16
  56.3 71.3 %collective-permute-start.17 = (bf16[3,128,2048]{2,1,0:T(8,128)(2,1)}, bf16[3,128,2048]{2,1,0:T(8,128)(2,1)}, u32[]{:S(2)}, u32[]{:S(2)}) collective-permute-start(bf16[3,128,2048]{2,1,0:T(8,128)(2,1)} %slice_bitcast_fusion), channel_id=1, source_target_pairs={{0,16},{2,18},{4,20},{6,22},{8,24},{10,26},{12,28},{14,30},{16,0},... | collective-permute-start | bytes 4718600 | tf_op jit(solution)/shard_map/ppermute | solution.py:16
  87.3 87.4 %collective-permute-start.5 = (bf16[13,56,1024]{2,1,0:T(8,128)(2,1)}, bf16[13,56,1024]{2,1,0:T(8,128)(2,1)}, u32[]{:S(2)}, u32[]{:S(2)}) collective-permute-start(bf16[13,56,1024]{2,1,0:T(8,128)(2,1)} %collective-permute-done.3), channel_id=1, source_target_pairs={{0,1},{1,0},{2,3},{3,2},{4,5},{5,4},{6,7},{7,6},{8,9},{9,8},{10,11... | collective-permute-start | bytes 4472840 | tf_op jit(solution)/shard_map/ppermute | solution.py:16
  127.6 36.4 %collective-permute-start.20 = (bf16[2,6,128,256]{3,2,1,0:T(8,128)(2,1)S(1)}, bf16[2,6,128,256]{3,2,1,0:T(8,128)(2,1)S(1)}, u32[]{:S(2)}, u32[]{:S(2)}) collective-permute-start(bf16[2,6,128,256]{3,2,1,0:T(8,128)(2,1)S(1)} %get-tuple-element.23), channel_id=1, source_target_pairs={{0,16},{2,18},{4,20},{6,22},{8,24},{10,26},{12,28},{14,30},{16,0},... | collective-permute-start | bytes 2359304 | tf_op jit(solution)/shard_map/ppermute | solution.py:16
  164.1 0.9 copy-start.2
  170.3 101.4 %all-to-all-start.1 = ((bf16[8,3,128,256]{3,2,1,0:T(8,128)(2,1)}), bf16[8,3,128,256]{3,2,1,0:T(8,128)(2,1)}, u32[]{:S(2)}, u32[]{:S(2)}) async-start(bf16[8,3,128,256]{3,2,1,0:T(8,128)(2,1)} %shard_map.38), calls=%async_computation.1 | async-start | bytes 3145728 | tf_op jit(solution)/shard_map/all_to_all | solution.py:175
  174.7 35.2 %collective-permute-start.6 = (bf16[13,56,1024]{2,1,0:T(8,128)(2,1)}, bf16[13,56,1024]{2,1,0:T(8,128)(2,1)}, u32[]{:S(2)}, u32[]{:S(2)}) collective-permute-start(bf16[13,56,1024]{2,1,0:T(8,128)(2,1)} %collective-permute-done.4), channel_id=1, source_target_pairs={{0,1},{1,0},{2,3},{3,2},{4,5},{5,4},{6,7},{7,6},{8,9},{9,8},{10,11... | collective-permute-start | bytes 4472840 | tf_op jit(solution)/shard_map/ppermute | solution.py:16
  175.3 51.4 %collective-permute-start.7 = (bf16[13,56,1024]{2,1,0:T(8,128)(2,1)}, bf16[13,56,1024]{2,1,0:T(8,128)(2,1)}, u32[]{:S(2)}, u32[]{:S(2)}) collective-permute-start(bf16[13,56,1024]{2,1,0:T(8,128)(2,1)} %collective-permute-done.3), channel_id=1, source_target_pairs={{0,4},{2,6},{4,0},{6,2},{8,12},{10,14},{12,8},{14,10},{16,20},{18,... | collective-permute-start | bytes 4472840 | tf_op jit(solution)/shard_map/ppermute | solution.py:16
  177.2 104.5 %collective-permute-start.9 = (bf16[13,56,1024]{2,1,0:T(8,128)(2,1)}, bf16[13,56,1024]{2,1,0:T(8,128)(2,1)}, u32[]{:S(2)}, u32[]{:S(2)}) collective-permute-start(bf16[13,56,1024]{2,1,0:T(8,128)(2,1)} %copy-done.8), channel_id=1, source_target_pairs={{0,2},{2,0},{4,6},{6,4},{8,10},{10,8},{12,14},{14,12},{16,18},{18,... | collective-permute-start | bytes 4472840 | tf_op jit(solution)/shard_map/ppermute | solution.py:16
  177.2 3.3 copy-start.7
  180.9 47.8 %copy-start.9 = (bf16[2,6,128,256]{3,2,1,0:T(8,128)(2,1)S(1)}, bf16[2,6,128,256]{3,2,1,0:T(8,128)(2,1)}, u32[]{:S(2)}) copy-start(bf16[2,6,128,256]{3,2,1,0:T(8,128)(2,1)} %get-tuple-element.21) | copy-start | bytes 2359300
  180.9 103.6 %collective-permute-start.10 = (bf16[13,56,1024]{2,1,0:T(8,128)(2,1)}, bf16[13,56,1024]{2,1,0:T(8,128)(2,1)}, u32[]{:S(2)}, u32[]{:S(2)}) collective-permute-start(bf16[13,56,1024]{2,1,0:T(8,128)(2,1)} %collective-permute-done.2), channel_id=1, source_target_pairs={{0,2},{2,0},{4,6},{6,4},{8,10},{10,8},{12,14},{14,12},{16,18},{18,... | collective-permute-start | bytes 4472840 | tf_op jit(solution)/shard_map/ppermute | solution.py:16
  181.5 106.0 %collective-permute-start.11 = (bf16[13,56,1024]{2,1,0:T(8,128)(2,1)}, bf16[13,56,1024]{2,1,0:T(8,128)(2,1)}, u32[]{:S(2)}, u32[]{:S(2)}) collective-permute-start(bf16[13,56,1024]{2,1,0:T(8,128)(2,1)} %collective-permute-done.3), channel_id=1, source_target_pairs={{0,2},{2,0},{4,6},{6,4},{8,10},{10,8},{12,14},{14,12},{16,18},{18,... | collective-permute-start | bytes 4472840 | tf_op jit(solution)/shard_map/ppermute | solution.py:16
  226.7 52.0 %collective-permute-start.8 = (bf16[13,56,1024]{2,1,0:T(8,128)(2,1)}, bf16[13,56,1024]{2,1,0:T(8,128)(2,1)}, u32[]{:S(2)}, u32[]{:S(2)}) collective-permute-start(bf16[13,56,1024]{2,1,0:T(8,128)(2,1)} %collective-permute-done.7), channel_id=1, source_target_pairs={{0,1},{1,0},{2,3},{3,2},{4,5},{5,4},{6,7},{7,6},{8,9},{9,8},{10,11... | collective-permute-start | bytes 4472840 | tf_op jit(solution)/shard_map/ppermute | solution.py:16
  228.8 36.6 %collective-permute-start.18 = (bf16[2,6,128,256]{3,2,1,0:T(8,128)(2,1)S(1)}, bf16[2,6,128,256]{3,2,1,0:T(8,128)(2,1)S(1)}, u32[]{:S(2)}, u32[]{:S(2)}) collective-permute-start(bf16[2,6,128,256]{3,2,1,0:T(8,128)(2,1)S(1)} %copy-done.9), channel_id=1, source_target_pairs={{0,16},{2,18},{4,20},{6,22},{8,24},{10,26},{12,28},{14,30},{16,0},... | collective-permute-start | bytes 2359304 | tf_op jit(solution)/shard_map/ppermute | solution.py:16
  233.5 31.8 %copy-start.6 = (bf16[2,99,64,1024]{3,2,1,0:T(8,128)(2,1)}, bf16[2,99,64,1024]{3,2,1,0:T(8,128)(2,1)S(1)}, u32[]{:S(2)}) copy-start(bf16[2,99,64,1024]{3,2,1,0:T(8,128)(2,1)S(1)} %bitcast_dynamic-update-slice_fusion.10) | copy-start | bytes 77856768
  265.4 0.9 copy-start.4
  266.3 24.0 %collective-permute-start.12 = (bf16[13,56,1024]{2,1,0:T(8,128)(2,1)}, bf16[13,56,1024]{2,1,0:T(8,128)(2,1)}, u32[]{:S(2)}, u32[]{:S(2)}) collective-permute-start(bf16[13,56,1024]{2,1,0:T(8,128)(2,1)} %collective-permute-done.4), channel_id=1, source_target_pairs={{0,2},{2,0},{4,6},{6,4},{8,10},{10,8},{12,14},{14,12},{16,18},{18,... | collective-permute-start | bytes 4472840 | tf_op jit(solution)/shard_map/ppermute | solution.py:16
  271.7 56.3 %all-to-all-start.2 = ((bf16[8,3,128,256]{3,2,1,0:T(8,128)(2,1)}), bf16[8,3,128,256]{3,2,1,0:T(8,128)(2,1)}, u32[]{:S(2)}, u32[]{:S(2)}) async-start(bf16[8,3,128,256]{3,2,1,0:T(8,128)(2,1)} %shard_map.39), calls=%async_computation.2 | async-start | bytes 3145728 | tf_op jit(solution)/shard_map/all_to_all | solution.py:175
  278.6 14.3 %collective-permute-start.13 = (bf16[13,56,1024]{2,1,0:T(8,128)(2,1)}, bf16[13,56,1024]{2,1,0:T(8,128)(2,1)S(1)}, u32[]{:S(2)}, u32[]{:S(2)}) collective-permute-start(bf16[13,56,1024]{2,1,0:T(8,128)(2,1)} %collective-permute-done.5), channel_id=1, source_target_pairs={{0,2},{2,0},{4,6},{6,4},{8,10},{10,8},{12,14},{14,12},{16,18},{18,... | collective-permute-start | bytes 4472840 | tf_op jit(solution)/shard_map/ppermute | solution.py:16
  281.7 15.4 %collective-permute-start.14 = (bf16[13,56,1024]{2,1,0:T(8,128)(2,1)}, bf16[13,56,1024]{2,1,0:T(8,128)(2,1)S(1)}, u32[]{:S(2)}, u32[]{:S(2)}) collective-permute-start(bf16[13,56,1024]{2,1,0:T(8,128)(2,1)} %collective-permute-done.6), channel_id=1, source_target_pairs={{0,2},{2,0},{4,6},{6,4},{8,10},{10,8},{12,14},{14,12},{16,18},{18,... | collective-permute-start | bytes 4472840 | tf_op jit(solution)/shard_map/ppermute | solution.py:16
  284.5 14.0 %collective-permute-start.15 = (bf16[13,56,1024]{2,1,0:T(8,128)(2,1)}, bf16[13,56,1024]{2,1,0:T(8,128)(2,1)S(1)}, u32[]{:S(2)}, u32[]{:S(2)}) collective-permute-start(bf16[13,56,1024]{2,1,0:T(8,128)(2,1)} %collective-permute-done.7), channel_id=1, source_target_pairs={{0,2},{2,0},{4,6},{6,4},{8,10},{10,8},{12,14},{14,12},{16,18},{18,... | collective-permute-start | bytes 4472840 | tf_op jit(solution)/shard_map/ppermute | solution.py:16
  287.5 12.2 %collective-permute-start.16 = (bf16[13,56,1024]{2,1,0:T(8,128)(2,1)}, bf16[13,56,1024]{2,1,0:T(8,128)(2,1)S(1)}, u32[]{:S(2)}, u32[]{:S(2)}) collective-permute-start(bf16[13,56,1024]{2,1,0:T(8,128)(2,1)} %collective-permute-done.8), channel_id=1, source_target_pairs={{0,2},{2,0},{4,6},{6,4},{8,10},{10,8},{12,14},{14,12},{16,18},{18,... | collective-permute-start | bytes 4472840 | tf_op jit(solution)/shard_map/ppermute | solution.py:16
  290.3 91.1 %collective-permute-start.19 = (bf16[2,6,128,256]{3,2,1,0:T(8,128)(2,1)}, bf16[2,6,128,256]{3,2,1,0:T(8,128)(2,1)}, u32[]{:S(2)}, u32[]{:S(2)}) collective-permute-start(bf16[2,6,128,256]{3,2,1,0:T(8,128)(2,1)} %get-tuple-element.22), channel_id=1, source_target_pairs={{0,16},{2,18},{4,20},{6,22},{8,24},{10,26},{12,28},{14,30},{16,0},... | collective-permute-start | bytes 2359304 | tf_op jit(solution)/shard_map/ppermute | solution.py:16
  292.9 69.0 %collective-permute-start.21 = (bf16[2,6,128,256]{3,2,1,0:T(8,128)(2,1)}, bf16[2,6,128,256]{3,2,1,0:T(8,128)(2,1)}, u32[]{:S(2)}, u32[]{:S(2)}) collective-permute-start(bf16[2,6,128,256]{3,2,1,0:T(8,128)(2,1)} %get-tuple-element.24), channel_id=1, source_target_pairs={{0,16},{2,18},{4,20},{6,22},{8,24},{10,26},{12,28},{14,30},{16,0},... | collective-permute-start | bytes 2359304 | tf_op jit(solution)/shard_map/ppermute | solution.py:16
  325.5 2.6 copy-start.1
  328.1 33.9 %copy-start.3 = (bf16[2,6,128,256]{3,2,1,0:T(8,128)(2,1)S(1)}, bf16[2,6,128,256]{3,2,1,0:T(8,128)(2,1)}, u32[]{:S(2)}) copy-start(bf16[2,6,128,256]{3,2,1,0:T(8,128)(2,1)} %copy-done.2) | copy-start | bytes 2359300
  328.1 33.9 %copy-start.5 = (bf16[2,6,128,256]{3,2,1,0:T(8,128)(2,1)S(1)}, bf16[2,6,128,256]{3,2,1,0:T(8,128)(2,1)}, u32[]{:S(2)}) copy-start(bf16[2,6,128,256]{3,2,1,0:T(8,128)(2,1)} %copy-done.4) | copy-start | bytes 2359300
  354.0 2.6 copy-start

commit v4 on v3

--- a/solution.py
+++ b/solution.py
@@ -22,17 +22,17 @@
 
 def conv_call(taps, pieces, scalars, image, acc=None, bias=None):
     blocks, padded_rows, width, depth = image.shape
-    shard, out_width = pieces[0][2].shape[2:]
+    shard, out_width = pieces[0][2].shape[-2:]
     row_count = padded_rows - 3
-    offsets = sorted({offset for offset, _, _ in pieces})
+    offsets = list(dict.fromkeys(piece[0] for piece in pieces))
     per_group = GROUP * shard // depth
     final = bias is not None
     assert row_count % TILE == 0 and SIDE % TILE == 0
 
     windows = {}
     for offset in offsets:
-        low = min(start for o, start, _ in pieces if o == offset) * shard
-        high = max(start + a.shape[0] for o, start, a in pieces if o == offset) * shard
+        ranges = [(start, start + block[-4]) for o, start, _, block, _ in pieces if o == offset]
+        low, high = min(a for a, _ in ranges) * shard, max(b for _, b in ranges) * shard
         if low // depth == (high - 1) // depth:
             windows[offset] = (1, low // depth, high - low, low % depth)
         else:
@@ -49,10 +49,10 @@
         out = refs.pop(0)
 
         operands, columns = [], []
-        for (offset, start, array), weight in zip(pieces, weights):
+        for (offset, start, _, block, _), weight in zip(pieces, weights):
             count, first_block, size, first_lane = windows[offset]
             main, *outer = images[offset]
-            at, lanes = 0, array.shape[0] * shard
+            at, lanes = 0, block[-4] * shard
             while at < lanes:
                 inner, lane = divmod(start * shard + at, depth)
                 inner, lane = inner - first_block, lane - first_lane
@@ -105,7 +105,7 @@
                 row = jnp.where((s[0] + t * TILE) % SIDE == 0, row_count + 2, row - 1)
             if vertical == 2:
                 row = jnp.where((s[0] + (t + 1) * TILE) % SIDE == 0, row_count + 2, row + TILE)
-            return ((s[1] ^ offset) * per_group + first_block, row, 0, first_lane)
+            return (offset(s) * per_group + first_block, row, 0, first_lane)
 
         return pl.BlockSpec(tuple(pl.Element(n) for n in (count, rows, width, size)), place)
 
@@ -115,8 +115,8 @@
         for vertical in [1] + [v for v in taps if v != 1]:
             in_specs.append(image_spec(offset, vertical))
             operands.append(image)
-    for _, _, array in pieces:
-        in_specs.append(pl.BlockSpec(array.shape, lambda t, s: (0, 0, 0, 0)))
+    for _, _, array, block, place in pieces:
+        in_specs.append(pl.BlockSpec(block, lambda t, s, place=place: place(s)))
         operands.append(array)
     if acc is not None:
         in_specs.append(pl.BlockSpec((TILE, width, out_width), lambda t, s: (t, 0, 0)))
@@ -174,7 +174,11 @@
     def share(taps):
         return lax.all_to_all(taps, "img", 0, 0, axis_index_groups=members, tiled=True)
 
-    raw = [swap(filters[0], "img", GROUP * j) for j in range(1, parts)]
+    def exchange(array):
+        groups = [[g * GROUP + r for g in range(parts)] for r in range(GROUP)]
+        return lax.all_gather(array, "img", axis_index_groups=groups)
+
+    raw = exchange(filters[0])
 
     ups = [(i, i + 1) for i in range(size - 1)]
     above = lax.ppermute(activations[-1:], "img", ups)
@@ -197,25 +201,13 @@
     cross(4, slots[1, 0])
     cross(2, slots[1, 4])
 
-    lower = share(after(by_member(filters, 1, 2), slots[0, 4], slots[0, 2]))
-    step = GROUP // CHUNKS
-    received = []
-
-    def exchange(chunk, *others):
-        sent = after(lower[chunk * step : (chunk + 1) * step], *others)
-        for j in range(1, parts):
-            received.append((j, chunk * step, swap(sent, "img", GROUP * j)))
-
-    exchange(0, *raw)
-    exchange(1, *raw)
-    slots[0, 6] = swap(after(slots[0, 4], lower), "img", 2)
-    exchange(2, received[0][2])
+    lower = share(after(by_member(filters, 1, 2), slots[0, 4], slots[0, 2], slots[1, 0]))
+    cut = GROUP - GROUP // CHUNKS
+    most = exchange(lower[:cut])
+    rest = exchange(lower[cut:])
+    slots[0, 6] = swap(after(slots[0, 4], lower, slots[1, 4]), "img", 2)
     cross(6, slots[1, 2])
-    upper = [
-        (j, 0, share(by_member(after(taps, received[0][2]), 0, 1)))
-        for j, taps in enumerate([filters] + [array[None] for array in raw])
-    ]
-    exchange(3, received[parts - 1][2])
+    upper = share(by_member(after(raw, slots[0, 6], slots[1, 2]), 0, parts))
 
     for (j, r), value in list(slots.items()):
         slots[j, r + 1] = swap(value, "img", 1)
@@ -228,11 +220,30 @@
 
     scalars = jnp.stack([group * GROUP * rows, group]).astype(jnp.int32)
     bias = lax.dynamic_slice_in_dim(channel_bias, rank * split, split)[None]
-    most = (CHUNKS - 1) * (parts - 1)
-    acc = conv_call((1, 2), [(0, 0, lower)], scalars, image)
-    acc = conv_call((0,), upper, scalars, image, acc)
-    acc = conv_call((1, 2), received[:most], scalars, image, acc)
-    out = conv_call((1, 2), received[most:], scalars, image, acc, bias)
+    own = lambda s: s[1]
+    mine_first = [(own, 0, lower, lower.shape, lambda s: (0, 0, 0, 0))]
+    every = [
+        (lambda s, p=p: p, 0, upper, (GROUP, 3, shard, split), lambda s, p=p: (0, p, 0, 0))
+        for p in range(parts)
+    ]
+
+    def foreign(array, start):
+        block = (None, *array.shape[1:])
+        return [
+            (
+                lambda s, j=j: s[1] ^ j,
+                start,
+                array,
+                block,
+                lambda s, j=j: (s[1] ^ j, 0, 0, 0, 0),
+            )
+            for j in range(1, parts)
+        ]
+
+    acc = conv_call((1, 2), mine_first, scalars, image)
+    acc = conv_call((0,), every, scalars, image, acc)
+    acc = conv_call((1, 2), foreign(most, 0), scalars, image, acc)
+    out = conv_call((1, 2), foreign(rest, cut), scalars, image, acc, bias)
     out = share(out).reshape(GROUP, rows, side, split)
     return jnp.moveaxis(out, 0, 2).reshape(rows, side, out_local)
 

time: 432 us -> 381 us (0.88)
  waiting for transfers between devices: 207 us -> 131 us
  local copies, waits for them, and re-layouts: 46.8 us -> 66.4 us
  between operations: 0.29 us -> 13.4 us
  starting transfers between devices: 36.9 us -> 27.5 us
    ppermute x20 -> x15, waiting for transfers between devices: 176 us -> 54.6 us  [swap(): return lax.ppermute(array, axis, [(i, i ^ bit) for i in range(size)])]
    all_to_all x3 -> x2, waiting for transfers between devices: 30.4 us -> 56.2 us  [share(): lax.all_to_all(taps, 'img', 0, 0, axis_index_groups=members, tiled=True)]
    all_gather x0 -> x3, waiting for transfers between devices: none -> 19.6 us  [exchange(): return lax.all_gather(array, 'img', axis_index_groups=groups)]
    unnamed x20 -> x16, local copies, waits for them, and re-layouts: 6.97 us -> 14.5 us
    broadcast_in_dim x1, local copies, waits for them, and re-layouts: 3.29 us -> 8.84 us  [local(): jnp.zeros((chans, GROUP * rows + 3, width, depth), activations.dtype)]
    ppermute x20 -> x15, starting transfers between devices: 20.3 us -> 15 us  [swap(): return lax.ppermute(array, axis, [(i, i ^ bit) for i in range(size)])]
    dynamic_update_slice x15, local copies, waits for them, and re-layouts: 28.7 us -> 34 us  [local(): lax.dynamic_update_slice(image, value[None], (mine ^ j, start, 0, 0))]
    all_to_all x3 -> x2, starting transfers between devices: 12.2 us -> 8.11 us  [share(): lax.all_to_all(taps, 'img', 0, 0, axis_index_groups=members, tiled=True)]
  transfers between devices with their start and end apart: 25 -> 22, of which waited for: 11 -> 9; matrix products, arithmetic and copies ran while one was open for 9% -> 13% of each run, Pallas kernels for 21% -> 23%
where the time goes in v4:
time: 381 us; the launch traced here: 379 us
  waiting for transfers between devices  131 us (34%)
  Pallas kernels  99.1 us (26%)
  local copies, waits for them, and re-layouts  66.4 us (17%)
  blocking collectives  37.4 us (10%)
  starting transfers between devices  27.5 us (7%)
  between operations  13.4 us (4%)
    pallas_call x4, Pallas kernels, conv_call(): pl.pallas_call(body, grid_spec=pltpu.PrefetchScalarGridSpec(num_scalar_pr...  79.5 us
    all_to_all x2, waiting for transfers between devices, share(): lax.all_to_all(taps, 'img', 0, 0, axis_index_groups=members, tiled=True)  56.2 us
    ppermute x15, waiting for transfers between devices, swap(): return lax.ppermute(array, axis, [(i, i ^ bit) for i in range(size)])  54.6 us
    all_to_all x1, blocking collectives, share(): lax.all_to_all(taps, 'img', 0, 0, axis_index_groups=members, tiled=True)  37.4 us
    dynamic_update_slice x15, local copies, waits for them, and re-layouts, local(): lax.dynamic_update_slice(image, value[None], (mine ^ j, start, 0, 0))  34 us
    pallas_call x2, Pallas kernels, by_member(): pl.pallas_call(body, grid=(GROUP, count), in_specs=[pl.BlockSpec((1, acro...  19.6 us
    all_gather x3, waiting for transfers between devices, exchange(): return lax.all_gather(array, 'img', axis_index_groups=groups)  19.6 us
    ppermute x15, starting transfers between devices, swap(): return lax.ppermute(array, axis, [(i, i ^ bit) for i in range(size)])  15 us
  transfers between devices with their start and end apart: 22, of which 9 were waited for; matrix products, arithmetic and copies ran while one was open for 13% of the time, Pallas kernels for 23%

profile of v4, /device:TPU:0, one launch (start us, length us, event | category | flops | bytes accessed | tf_op | source)
XLA Modules:
  0.0 378.9 jit_solution(3178757595127261923)
XLA Ops:
  7.5 1.3 collective-permute-start
  8.8 3.0 collective-permute-start.1
  12.8 2.0 maximum_select_fusion.1
  14.8 3.0 collective-permute-start.2
  17.8 6.1 %collective-permute-start.3 = (bf16[13,56,1024]{2,1,0:T(8,128)(2,1)S(1)}, bf16[13,56,1024]{2,1,0:T(8,128)(2,1)}, u32[]{:S(2)}, u32[]{:S(2)}) collective-permute-start(bf16[13,56,1024]{2,1,0:T(8,128)(2,1)S(1)} %maximum_select_fusion.1), channel_id=1, source_target_pairs={{0,8},{2,10},{4,12},{6,14},{8,0},{10,2},{12,4},{14,6},{16,24},{18,... | collective-permute-start | bytes 4472840 | tf_op jit(solution)/shard_map/ppermute | solution.py:16
  23.9 9.8 %shard_map.37 = bf16[8,6,128,256]{3,2,1,0:T(8,128)(2,1)} custom-call(bf16[3,3,128,2048]{3,2,1,0:T(8,128)(2,1)} %taps.1), custom_call_target="tpu_custom_call" | custom-call | tf_op jit(solution)/shard_map/pallas_call | solution.py:153
  33.7 16.0 %collective-permute-done.2 = bf16[13,56,1024]{2,1,0:T(8,128)(2,1)} collective-permute-done((bf16[13,56,1024]{2,1,0:T(8,128)(2,1)S(1)}, bf16[13,56,1024]{2,1,0:T(8,128)(2,1)}, u32[]{:S(2)}, u32[]{:S(2)}) %collective-permute-start.2) | collective-permute-done | bytes 1490976 | tf_op jit(solution)/shard_map/ppermute | solution.py:16
  49.7 4.6 %collective-permute-done.3 = bf16[13,56,1024]{2,1,0:T(8,128)(2,1)} collective-permute-done((bf16[13,56,1024]{2,1,0:T(8,128)(2,1)S(1)}, bf16[13,56,1024]{2,1,0:T(8,128)(2,1)}, u32[]{:S(2)}, u32[]{:S(2)}) %collective-permute-start.3) | collective-permute-done | bytes 1490976 | tf_op jit(solution)/shard_map/ppermute | solution.py:16
  54.3 1.7 collective-permute-done.4
  56.1 3.6 all-to-all-start
  59.8 2.8 slice.19
  63.3 56.2 %all-to-all-done.refs_2_ = bf16[8,6,128,256]{3,2,1,0:T(8,128)(2,1)S(1)} async-done(((bf16[8,6,128,256]{3,2,1,0:T(8,128)(2,1)}), bf16[8,6,128,256]{3,2,1,0:T(8,128)(2,1)S(1)}, u32[]{:S(2)}, u32[]{:S(2)}) %all-to-all-start) | async-done | bytes 3145760 | tf_op jit(solution)/shard_map/all_to_all | solution.py:175
  119.5 1.7 slice.21
  121.2 1.5 collective-permute-start.7
  122.8 19.6 %all-gather.6.cloned.1.call-done.taps = bf16[2,3,128,2048]{3,2,1,0:T(8,128)(2,1)} async-done(((bf16[1,3,128,2048]{3,2,1,0:T(8,128)(2,1)}), bf16[2,3,128,2048]{3,2,1,0:T(8,128)(2,1)}) %all-gather.6.cloned.1.call-update) | async-done | bytes 3145744 | tf_op jit(solution)/shard_map/all_gather | solution.py:179
  142.4 13.0 %collective-permute-done.6 = bf16[13,56,1024]{2,1,0:T(8,128)(2,1)} collective-permute-done((bf16[13,56,1024]{2,1,0:T(8,128)(2,1)}, bf16[13,56,1024]{2,1,0:T(8,128)(2,1)}, u32[]{:S(2)}, u32[]{:S(2)}) %collective-permute-start.6) | collective-permute-done | bytes 1490976 | tf_op jit(solution)/shard_map/ppermute | solution.py:16
  155.4 9.8 %shard_map.38 = bf16[8,6,128,256]{3,2,1,0:T(8,128)(2,1)} custom-call(bf16[2,3,128,2048]{3,2,1,0:T(8,128)(2,1)} %all-gather.6.cloned.1.call-done.taps), custom_call_target="tpu_custom_call" | custom-call | tf_op jit(solution)/shard_map/pallas_call | solution.py:153
  165.3 4.5 %all-to-all-start.1 = ((bf16[8,6,128,256]{3,2,1,0:T(8,128)(2,1)}), bf16[8,6,128,256]{3,2,1,0:T(8,128)(2,1)}, u32[]{:S(2)}, u32[]{:S(2)}) async-start(bf16[8,6,128,256]{3,2,1,0:T(8,128)(2,1)} %shard_map.38), calls=%async_computation.1 | async-start | bytes 6291456 | tf_op jit(solution)/shard_map/all_to_all | solution.py:175
  170.2 8.8 %broadcast_in_dim.52 = bf16[2,99,64,1024]{3,2,1,0:T(8,128)(2,1)} broadcast(bf16[]{:T(256)} %constant.48.clone.1), dimensions={} | broadcast | bytes 25952258 | tf_op jit(solution)/shard_map/broadcast_in_dim | solution.py:215
  179.0 1.6 fusion
  181.4 2.6 bitcast_dynamic-update-slice_fusion.14
  184.0 1.7 collective-permute-start.8
  185.7 2.7 bitcast_dynamic-update-slice_fusion.13
  188.5 2.6 bitcast_dynamic-update-slice_fusion.12
  191.1 2.7 bitcast_dynamic-update-slice_fusion.11
  193.8 2.6 bitcast_dynamic-update-slice_fusion.10
  197.4 2.6 bitcast_dynamic-update-slice_fusion.9
  200.0 19.2 %collective-permute-done.8 = bf16[13,56,1024]{2,1,0:T(8,128)(2,1)} collective-permute-done((bf16[13,56,1024]{2,1,0:T(8,128)(2,1)}, bf16[13,56,1024]{2,1,0:T(8,128)(2,1)}, u32[]{:S(2)}, u32[]{:S(2)}) %collective-permute-start.8) | collective-permute-done | bytes 1490976 | tf_op jit(solution)/shard_map/ppermute | solution.py:16
  219.2 2.7 bitcast_dynamic-update-slice_fusion.8
  222.3 2.6 bitcast_dynamic-update-slice_fusion.7
  225.0 2.7 bitcast_dynamic-update-slice_fusion.6
  228.1 2.6 bitcast_dynamic-update-slice_fusion.5
  230.7 2.6 bitcast_dynamic-update-slice_fusion.4
  233.3 1.2 bitcast_dynamic-update-slice_fusion.3
  235.8 1.2 bitcast_dynamic-update-slice_fusion.1
  237.0 1.2 bitcast_dynamic-update-slice_fusion.refs_0_.refs_1_.refs_2_.refs_3_
  239.0 23.7 %shard_map.39.refs_6_ = f32[96,64,256]{2,1,0:T(8,128)S(1)} custom-call(s32[2]{0:T(128)S(1)} %pad_add_fusion.scalars_ref, bf16[2,99,64,1024]{3,2,1,0:T(8,128)(2,1)} %bitcast_dynamic-update-slice_fusion.refs_0_.refs_1_.refs_2_.refs_3_, bf16[2,99,64,1024]{3,2,1,0:T(8,128)(2,1)} %bitcast_dynamic-update-slice_fusion.refs_0_.refs_1_.refs_2_.refs_3_, ...), custom_call_target="tpu_custom_call" | custom-call | flops 1024 | bytes 1024 | tf_op jit(solution)/shard_map/pallas_call | solution.py:127
  262.7 2.6 copy-done
  265.3 26.1 %shard_map.40.refs_3_ = f32[96,64,256]{2,1,0:T(8,128)S(1)} custom-call(s32[2]{0:T(128)S(1)} %pad_add_fusion.scalars_ref, bf16[2,99,64,1024]{3,2,1,0:T(8,128)(2,1)} %bitcast_dynamic-update-slice_fusion.refs_0_.refs_1_.refs_2_.refs_3_, bf16[2,99,64,1024]{3,2,1,0:T(8,128)(2,1)} %bitcast_dynamic-update-slice_fusion.refs_0_.refs_1_.refs_2_.refs_3_, ...), custom_call_target="tpu_custom_call" | custom-call | flops 1024 | bytes 1024 | tf_op jit(solution)/shard_map/pallas_call | solution.py:127
  291.4 2.7 copy-done.1
  294.1 2.3 copy-done.4
  296.4 19.2 %shard_map.41.refs_3_ = f32[96,64,256]{2,1,0:T(8,128)S(1)} custom-call(s32[2]{0:T(128)S(1)} %pad_add_fusion.scalars_ref, bf16[2,99,64,1024]{3,2,1,0:T(8,128)(2,1)} %bitcast_dynamic-update-slice_fusion.refs_0_.refs_1_.refs_2_.refs_3_, bf16[2,99,64,1024]{3,2,1,0:T(8,128)(2,1)} %bitcast_dynamic-update-slice_fusion.refs_0_.refs_1_.refs_2_.refs_3_, ...), custom_call_target="tpu_custom_call" | custom-call | flops 1024 | bytes 1024 | tf_op jit(solution)/shard_map/pallas_call | solution.py:127
  315.6 2.7 copy-done.2
  318.3 2.8 copy-done.3
  321.1 1.4 copy-done.5
  322.5 10.6 %shard_map.42 = bf16[96,56,256]{2,1,0:T(8,128)(2,1)S(1)} custom-call(s32[2]{0:T(128)S(1)} %pad_add_fusion.scalars_ref, bf16[2,99,64,1024]{3,2,1,0:T(8,128)(2,1)} %bitcast_dynamic-update-slice_fusion.refs_0_.refs_1_.refs_2_.refs_3_, bf16[2,99,64,1024]{3,2,1,0:T(8,128)(2,1)} %bitcast_dynamic-update-slice_fusion.refs_0_.refs_1_.refs_2_.refs_3_, ...), custom_call_target="tpu_custom_call" | custom-call | flops 1024 | bytes 1024 | tf_op jit(solution)/shard_map/pallas_call | solution.py:127
  333.1 37.4 %all_to_all.15 = bf16[96,56,256]{2,1,0:T(8,128)(2,1)S(1)} all-to-all(bf16[96,56,256]{2,1,0:T(8,128)(2,1)S(1)} %shard_map.42), channel_id=1, replica_groups={{0,2,4,6,8,10,12,14},{16,18,20,22,24,26,28,30},{1,3,5,7,9,11,13,15},{17..., dimensions={0} | all-to-all | bytes 5505024 | tf_op jit(solution)/shard_map/all_to_all | solution.py:175
  370.5 1.9 copy.6
  (47 shorter events, 7.8 us)
Async XLA Ops:
  7.5 4.4 %collective-permute-start = (bf16[1,56,1024]{2,1,0:T(8,128)(2,1)S(1)}, bf16[1,56,1024]{2,1,0:T(8,128)(2,1)S(1)}, u32[]{:S(2)}, u32[]{:S(2)}) collective-permute-start(bf16[1,56,1024]{2,1,0:T(8,128)(2,1)S(1)} %get-tuple-element.18), channel_id=1, source_target_pairs={{2,0},{4,2},{6,4},{8,6},{10,8},{12,10},{14,12},{16,14},{18,16},{20... | collective-permute-start | bytes 344072 | tf_op jit(solution)/shard_map/ppermute | solution.py:185
  8.8 4.0 %collective-permute-start.1 = (bf16[1,56,1024]{2,1,0:T(8,128)(2,1)S(1)}, bf16[1,56,1024]{2,1,0:T(8,128)(2,1)S(1)}, u32[]{:S(2)}, u32[]{:S(2)}) collective-permute-start(bf16[1,56,1024]{2,1,0:T(8,128)(2,1)S(1)} %get-tuple-element.17), channel_id=1, source_target_pairs={{0,2},{2,4},{4,6},{6,8},{8,10},{10,12},{12,14},{14,16},{16,18},{18... | collective-permute-start | bytes 344072 | tf_op jit(solution)/shard_map/ppermute | solution.py:184
  14.8 18.9 %copy-start.7 = (bf16[13,56,1024]{2,1,0:T(8,128)(2,1)}, bf16[13,56,1024]{2,1,0:T(8,128)(2,1)S(1)}, u32[]{:S(2)}) copy-start(bf16[13,56,1024]{2,1,0:T(8,128)(2,1)S(1)} %maximum_select_fusion.1) | copy-start | bytes 4472836
  14.8 34.9 %collective-permute-start.2 = (bf16[13,56,1024]{2,1,0:T(8,128)(2,1)S(1)}, bf16[13,56,1024]{2,1,0:T(8,128)(2,1)}, u32[]{:S(2)}, u32[]{:S(2)}) collective-permute-start(bf16[13,56,1024]{2,1,0:T(8,128)(2,1)S(1)} %maximum_select_fusion.1), channel_id=1, source_target_pairs={{0,1},{1,0},{2,3},{3,2},{4,5},{5,4},{6,7},{7,6},{8,9},{9,8},{10,11... | collective-permute-start | bytes 4472840 | tf_op jit(solution)/shard_map/ppermute | solution.py:16
  17.8 36.5 %collective-permute-start.3 = (bf16[13,56,1024]{2,1,0:T(8,128)(2,1)S(1)}, bf16[13,56,1024]{2,1,0:T(8,128)(2,1)}, u32[]{:S(2)}, u32[]{:S(2)}) collective-permute-start(bf16[13,56,1024]{2,1,0:T(8,128)(2,1)S(1)} %maximum_select_fusion.1), channel_id=1, source_target_pairs={{0,8},{2,10},{4,12},{6,14},{8,0},{10,2},{12,4},{14,6},{16,24},{18,... | collective-permute-start | bytes 4472840 | tf_op jit(solution)/shard_map/ppermute | solution.py:16
  23.9 32.2 %collective-permute-start.4 = (bf16[13,56,1024]{2,1,0:T(8,128)(2,1)S(1)}, bf16[13,56,1024]{2,1,0:T(8,128)(2,1)}, u32[]{:S(2)}, u32[]{:S(2)}) collective-permute-start(bf16[13,56,1024]{2,1,0:T(8,128)(2,1)S(1)} %maximum_select_fusion.1), channel_id=1, source_target_pairs={{0,4},{2,6},{4,0},{6,2},{8,12},{10,14},{12,8},{14,10},{16,20},{18,... | collective-permute-start | bytes 4472840 | tf_op jit(solution)/shard_map/ppermute | solution.py:16
  56.1 63.4 %all-to-all-start = ((bf16[8,6,128,256]{3,2,1,0:T(8,128)(2,1)}), bf16[8,6,128,256]{3,2,1,0:T(8,128)(2,1)S(1)}, u32[]{:S(2)}, u32[]{:S(2)}) async-start(bf16[8,6,128,256]{3,2,1,0:T(8,128)(2,1)} %shard_map.37), calls=%async_computation | async-start | bytes 6291456 | tf_op jit(solution)/shard_map/all_to_all | solution.py:175
  59.7 82.6 %all-gather.6.cloned.1.call-start = ((), (), s32[]{:S(2)}) async-start(), calls=%async_computation.3 | async-start | bytes 4718592 | tf_op jit(solution)/shard_map/all_gather | solution.py:179
  62.6 231.5 %all-gather.10.cloned.1.call-start = ((), (), s32[]{:S(2)}) async-start(), calls=%async_computation.5 | async-start | bytes 7077888 | tf_op jit(solution)/shard_map/all_gather | solution.py:179
  62.7 58.5 %collective-permute-start.5 = (bf16[13,56,1024]{2,1,0:T(8,128)(2,1)}, bf16[13,56,1024]{2,1,0:T(8,128)(2,1)}, u32[]{:S(2)}, u32[]{:S(2)}) collective-permute-start(bf16[13,56,1024]{2,1,0:T(8,128)(2,1)} %collective-permute-done.3), channel_id=1, source_target_pairs={{0,1},{1,0},{2,3},{3,2},{4,5},{5,4},{6,7},{7,6},{8,9},{9,8},{10,11... | collective-permute-start | bytes 4472840 | tf_op jit(solution)/shard_map/ppermute | solution.py:16
  121.1 34.2 %collective-permute-start.6 = (bf16[13,56,1024]{2,1,0:T(8,128)(2,1)}, bf16[13,56,1024]{2,1,0:T(8,128)(2,1)}, u32[]{:S(2)}, u32[]{:S(2)}) collective-permute-start(bf16[13,56,1024]{2,1,0:T(8,128)(2,1)} %collective-permute-done.4), channel_id=1, source_target_pairs={{0,1},{1,0},{2,3},{3,2},{4,5},{5,4},{6,7},{7,6},{8,9},{9,8},{10,11... | collective-permute-start | bytes 4472840 | tf_op jit(solution)/shard_map/ppermute | solution.py:16
  121.2 34.2 %collective-permute-start.7 = (bf16[13,56,1024]{2,1,0:T(8,128)(2,1)}, bf16[13,56,1024]{2,1,0:T(8,128)(2,1)}, u32[]{:S(2)}, u32[]{:S(2)}) collective-permute-start(bf16[13,56,1024]{2,1,0:T(8,128)(2,1)} %collective-permute-done.3), channel_id=1, source_target_pairs={{0,4},{2,6},{4,0},{6,2},{8,12},{10,14},{12,8},{14,10},{16,20},{18,... | collective-permute-start | bytes 4472840 | tf_op jit(solution)/shard_map/ppermute | solution.py:16
  165.3 100.1 %all-to-all-start.1 = ((bf16[8,6,128,256]{3,2,1,0:T(8,128)(2,1)}), bf16[8,6,128,256]{3,2,1,0:T(8,128)(2,1)}, u32[]{:S(2)}, u32[]{:S(2)}) async-start(bf16[8,6,128,256]{3,2,1,0:T(8,128)(2,1)} %shard_map.38), calls=%async_computation.1 | async-start | bytes 6291456 | tf_op jit(solution)/shard_map/all_to_all | solution.py:175
  169.7 148.6 %all-gather.8.cloned.1.call-start = ((), (), s32[]{:S(2)}) async-start(), calls=%async_computation.4 | async-start | bytes 2359296 | tf_op jit(solution)/shard_map/all_gather | solution.py:179
  170.0 51.9 %collective-permute-start.9 = (bf16[13,56,1024]{2,1,0:T(8,128)(2,1)}, bf16[13,56,1024]{2,1,0:T(8,128)(2,1)}, u32[]{:S(2)}, u32[]{:S(2)}) collective-permute-start(bf16[13,56,1024]{2,1,0:T(8,128)(2,1)} %copy-done.7), channel_id=1, source_target_pairs={{0,2},{2,0},{4,6},{6,4},{8,10},{10,8},{12,14},{14,12},{16,18},{18,... | collective-permute-start | bytes 4472840 | tf_op jit(solution)/shard_map/ppermute | solution.py:16
  170.2 8.8 %copy-start.6 = (bf16[12,56,1024]{2,1,0:T(8,128)(2,1)S(1)}, bf16[12,56,1024]{2,1,0:T(8,128)(2,1)}, u32[]{:S(2)}) copy-start(bf16[12,56,1024]{2,1,0:T(8,128)(2,1)} %param.3) | copy-start | bytes 4128772
  180.6 44.3 %collective-permute-start.10 = (bf16[13,56,1024]{2,1,0:T(8,128)(2,1)}, bf16[13,56,1024]{2,1,0:T(8,128)(2,1)}, u32[]{:S(2)}, u32[]{:S(2)}) collective-permute-start(bf16[13,56,1024]{2,1,0:T(8,128)(2,1)} %collective-permute-done.2), channel_id=1, source_target_pairs={{0,2},{2,0},{4,6},{6,4},{8,10},{10,8},{12,14},{14,12},{16,18},{18,... | collective-permute-start | bytes 4472840 | tf_op jit(solution)/shard_map/ppermute | solution.py:16
  180.9 46.8 %collective-permute-start.11 = (bf16[13,56,1024]{2,1,0:T(8,128)(2,1)}, bf16[13,56,1024]{2,1,0:T(8,128)(2,1)}, u32[]{:S(2)}, u32[]{:S(2)}) collective-permute-start(bf16[13,56,1024]{2,1,0:T(8,128)(2,1)} %collective-permute-done.3), channel_id=1, source_target_pairs={{0,2},{2,0},{4,6},{6,4},{8,10},{10,8},{12,14},{14,12},{16,18},{18,... | collective-permute-start | bytes 4472840 | tf_op jit(solution)/shard_map/ppermute | solution.py:16
  181.1 49.6 %collective-permute-start.12 = (bf16[13,56,1024]{2,1,0:T(8,128)(2,1)}, bf16[13,56,1024]{2,1,0:T(8,128)(2,1)}, u32[]{:S(2)}, u32[]{:S(2)}) collective-permute-start(bf16[13,56,1024]{2,1,0:T(8,128)(2,1)} %collective-permute-done.4), channel_id=1, source_target_pairs={{0,2},{2,0},{4,6},{6,4},{8,10},{10,8},{12,14},{14,12},{16,18},{18,... | collective-permute-start | bytes 4472840 | tf_op jit(solution)/shard_map/ppermute | solution.py:16
  184.0 35.2 %collective-permute-start.8 = (bf16[13,56,1024]{2,1,0:T(8,128)(2,1)}, bf16[13,56,1024]{2,1,0:T(8,128)(2,1)}, u32[]{:S(2)}, u32[]{:S(2)}) collective-permute-start(bf16[13,56,1024]{2,1,0:T(8,128)(2,1)} %collective-permute-done.7), channel_id=1, source_target_pairs={{0,1},{1,0},{2,3},{3,2},{4,5},{5,4},{6,7},{7,6},{8,9},{9,8},{10,11... | collective-permute-start | bytes 4472840 | tf_op jit(solution)/shard_map/ppermute | solution.py:16
  219.2 14.2 %collective-permute-start.13 = (bf16[13,56,1024]{2,1,0:T(8,128)(2,1)}, bf16[13,56,1024]{2,1,0:T(8,128)(2,1)S(1)}, u32[]{:S(2)}, u32[]{:S(2)}) collective-permute-start(bf16[13,56,1024]{2,1,0:T(8,128)(2,1)} %collective-permute-done.5), channel_id=1, source_target_pairs={{0,2},{2,0},{4,6},{6,4},{8,10},{10,8},{12,14},{14,12},{16,18},{18,... | collective-permute-start | bytes 4472840 | tf_op jit(solution)/shard_map/ppermute | solution.py:16
  221.8 12.7 %collective-permute-start.14 = (bf16[13,56,1024]{2,1,0:T(8,128)(2,1)}, bf16[13,56,1024]{2,1,0:T(8,128)(2,1)S(1)}, u32[]{:S(2)}, u32[]{:S(2)}) collective-permute-start(bf16[13,56,1024]{2,1,0:T(8,128)(2,1)} %collective-permute-done.6), channel_id=1, source_target_pairs={{0,2},{2,0},{4,6},{6,4},{8,10},{10,8},{12,14},{14,12},{16,18},{18,... | collective-permute-start | bytes 4472840 | tf_op jit(solution)/shard_map/ppermute | solution.py:16
  224.9 10.8 %collective-permute-start.15 = (bf16[13,56,1024]{2,1,0:T(8,128)(2,1)}, bf16[13,56,1024]{2,1,0:T(8,128)(2,1)S(1)}, u32[]{:S(2)}, u32[]{:S(2)}) collective-permute-start(bf16[13,56,1024]{2,1,0:T(8,128)(2,1)} %collective-permute-done.7), channel_id=1, source_target_pairs={{0,2},{2,0},{4,6},{6,4},{8,10},{10,8},{12,14},{14,12},{16,18},{18,... | collective-permute-start | bytes 4472840 | tf_op jit(solution)/shard_map/ppermute | solution.py:16
  227.7 9.3 %collective-permute-start.16 = (bf16[13,56,1024]{2,1,0:T(8,128)(2,1)}, bf16[13,56,1024]{2,1,0:T(8,128)(2,1)S(1)}, u32[]{:S(2)}, u32[]{:S(2)}) collective-permute-start(bf16[13,56,1024]{2,1,0:T(8,128)(2,1)} %collective-permute-done.8), channel_id=1, source_target_pairs={{0,2},{2,0},{4,6},{6,4},{8,10},{10,8},{12,14},{14,12},{16,18},{18,... | collective-permute-start | bytes 4472840 | tf_op jit(solution)/shard_map/ppermute | solution.py:16
  262.7 2.6 copy-start
  291.4 2.7 copy-start.1
  294.1 2.3 copy-start.4
  315.6 2.7 copy-start.2
  318.3 2.8 copy-start.3
  321.1 1.4 copy-start.5
Sparse Core Ops, SparseCore 0:
  62.7 79.5 all-gather.5
  143.9 113.1 all-gather.9
  258.6 44.0 all-gather.7

commit v5 on v4

--- a/solution.py
+++ b/solution.py
@@ -148,15 +148,16 @@
         return jnp.stack([taps[..., r * split : (r + 1) * split] for r in range(GROUP)])
 
     def body(taps, out):
-        out[...] = taps[...].reshape(out.shape)
+        for r in range(GROUP):
+            out[r, 0] = taps[0, 0, :, r * split : (r + 1) * split]
 
     return pl.pallas_call(
         body,
-        grid=(GROUP, count),
-        in_specs=[
-            pl.BlockSpec((1, across, shard, split), lambda r, v: (first + v, 0, 0, r))
-        ],
-        out_specs=pl.BlockSpec((1, across, shard, split), lambda r, v: (r, v, 0, 0)),
+        grid=(count, across),
+        in_specs=[pl.BlockSpec((1, 1, shard, out_local), lambda v, b: (first + v, b, 0, 0))],
+        out_specs=pl.BlockSpec(
+            (GROUP, 1, shard, split), lambda v, b: (0, v * across + b, 0, 0)
+        ),
         out_shape=jax.ShapeDtypeStruct((GROUP, count * across, shard, split), filters.dtype),
     )(filters)
 
@@ -178,7 +179,8 @@
         groups = [[g * GROUP + r for g in range(parts)] for r in range(GROUP)]
         return lax.all_gather(array, "img", axis_index_groups=groups)
 
-    raw = exchange(filters[0])
+    first, activations = lax.optimization_barrier((filters[0], activations))
+    raw = exchange(first)
 
     ups = [(i, i + 1) for i in range(size - 1)]
     above = lax.ppermute(activations[-1:], "img", ups)
@@ -198,19 +200,30 @@
     cross(0)
     slots[0, 4] = swap(piece, "img", 4)
     slots[0, 2] = swap(piece, "img", 2)
-    cross(4, slots[1, 0])
-    cross(2, slots[1, 4])
-
-    lower = share(after(by_member(filters, 1, 2), slots[0, 4], slots[0, 2], slots[1, 0]))
-    cut = GROUP - GROUP // CHUNKS
-    most = exchange(lower[:cut])
-    rest = exchange(lower[cut:])
-    slots[0, 6] = swap(after(slots[0, 4], lower, slots[1, 4]), "img", 2)
-    cross(6, slots[1, 2])
-    upper = share(by_member(after(raw, slots[0, 6], slots[1, 2]), 0, parts))
-
+
+    ready = slots[0, 4], slots[0, 2], slots[1, 0]
+    lower = share(after(by_member(filters, 1, 2), *ready))
+    cross(4, *ready)
+    cross(2, *ready)
+    slots[0, 6] = swap(after(slots[0, 4], *ready), "img", 2)
+    ready = lower, raw, slots[1, 4], slots[1, 2], slots[0, 6]
+    step = GROUP // CHUNKS
+    received = []
+
+    def exchange_chunks(chunks, *others):
+        for chunk in chunks:
+            sent = after(lower[chunk * step : (chunk + 1) * step], *others)
+            for j in range(1, parts):
+                received.append((j, chunk * step, swap(sent, "img", GROUP * j)))
+
+    exchange_chunks(range(CHUNKS // 2), *ready)
+    cross(6, *ready)
+    upper = share(by_member(after(raw, *ready), 0, parts))
     for (j, r), value in list(slots.items()):
         slots[j, r + 1] = swap(value, "img", 1)
+    ready = [array for _, _, array in received] + list(slots.values())
+    exchange_chunks(range(CHUNKS // 2, CHUNKS), *ready)
+
     width = -(-side // 16) * 16
     image = jnp.zeros((chans, GROUP * rows + 3, width, depth), activations.dtype)
     for (j, r), value in slots.items():
@@ -221,29 +234,23 @@
     scalars = jnp.stack([group * GROUP * rows, group]).astype(jnp.int32)
     bias = lax.dynamic_slice_in_dim(channel_bias, rank * split, split)[None]
     own = lambda s: s[1]
+    half = len(received) // 2
     mine_first = [(own, 0, lower, lower.shape, lambda s: (0, 0, 0, 0))]
     every = [
         (lambda s, p=p: p, 0, upper, (GROUP, 3, shard, split), lambda s, p=p: (0, p, 0, 0))
         for p in range(parts)
     ]
 
-    def foreign(array, start):
-        block = (None, *array.shape[1:])
+    def foreign(arrays):
         return [
-            (
-                lambda s, j=j: s[1] ^ j,
-                start,
-                array,
-                block,
-                lambda s, j=j: (s[1] ^ j, 0, 0, 0, 0),
-            )
-            for j in range(1, parts)
+            (lambda s, j=j: s[1] ^ j, start, array, array.shape, lambda s: (0, 0, 0, 0))
+            for j, start, array in arrays
         ]
 
     acc = conv_call((1, 2), mine_first, scalars, image)
     acc = conv_call((0,), every, scalars, image, acc)
-    acc = conv_call((1, 2), foreign(most, 0), scalars, image, acc)
-    out = conv_call((1, 2), foreign(rest, cut), scalars, image, acc, bias)
+    acc = conv_call((1, 2), foreign(received[:half]), scalars, image, acc)
+    out = conv_call((1, 2), foreign(received[half:]), scalars, image, acc, bias)
     out = share(out).reshape(GROUP, rows, side, split)
     return jnp.moveaxis(out, 0, 2).reshape(rows, side, out_local)
 

time: 381 us -> 414 us (1.087)
  waiting for transfers between devices: 131 us -> 190 us
  local copies, waits for them, and re-layouts: 66.4 us -> 47.6 us
  Pallas kernels: 99.1 us -> 89.3 us
  starting transfers between devices: 27.5 us -> 35.1 us
    ppermute x15 -> x19, waiting for transfers between devices: 54.6 us -> 175 us  [swap(): return lax.ppermute(array, axis, [(i, i ^ bit) for i in range(size)])]
    all_to_all x2, waiting for transfers between devices: 56.2 us -> 0.01 us  [share(): lax.all_to_all(taps, 'img', 0, 0, axis_index_groups=members, tiled=True)]
    unnamed x16, local copies, waits for them, and re-layouts: 14.5 us -> 4.51 us
    pallas_call x2, Pallas kernels: 19.6 us -> 10.6 us  [by_member(): pl.pallas_call(body, grid=(count, across), in_specs=[pl.BlockSpec((1, 1,...]
    ppermute x15 -> x19, starting transfers between devices: 15 us -> 22.6 us  [swap(): return lax.ppermute(array, axis, [(i, i ^ bit) for i in range(size)])]
    dynamic_update_slice x15, local copies, waits for them, and re-layouts: 34 us -> 27.2 us  [local(): lax.dynamic_update_slice(image, value[None], (mine ^ j, start, 0, 0))]
    all_gather x3 -> x1, waiting for transfers between devices: 19.6 us -> 13.2 us  [exchange(): return lax.all_gather(array, 'img', axis_index_groups=groups)]
  transfers between devices with their start and end apart: 22 -> 24, of which waited for: 9 -> 11; matrix products, arithmetic and copies ran while one was open for 13% -> 10% of each run, Pallas kernels for 23% -> 17%
where the time goes in v5:
time: 414 us; the launch traced here: 413 us
  waiting for transfers between devices  190 us (46%)
  Pallas kernels  89.3 us (22%)
  local copies, waits for them, and re-layouts  47.6 us (11%)
  blocking collectives  36.2 us (9%)
  starting transfers between devices  35.1 us (8%)
  between operations  13.7 us (3%)
    ppermute x19, waiting for transfers between devices, swap(): return lax.ppermute(array, axis, [(i, i ^ bit) for i in range(size)])  175 us
    pallas_call x4, Pallas kernels, conv_call(): pl.pallas_call(body, grid_spec=pltpu.PrefetchScalarGridSpec(num_scalar_pr...  78.7 us
    all_to_all x1, blocking collectives, share(): lax.all_to_all(taps, 'img', 0, 0, axis_index_groups=members, tiled=True)  36.2 us
    dynamic_update_slice x15, local copies, waits for them, and re-layouts, local(): lax.dynamic_update_slice(image, value[None], (mine ^ j, start, 0, 0))  27.2 us
    ppermute x19, starting transfers between devices, swap(): return lax.ppermute(array, axis, [(i, i ^ bit) for i in range(size)])  22.6 us
    all_gather x1, waiting for transfers between devices, exchange(): return lax.all_gather(array, 'img', axis_index_groups=groups)  13.2 us
    pallas_call x2, Pallas kernels, by_member(): pl.pallas_call(body, grid=(count, across), in_specs=[pl.BlockSpec((1, 1,...  10.6 us
    broadcast_in_dim x1, local copies, waits for them, and re-layouts, local(): jnp.zeros((chans, GROUP * rows + 3, width, depth), activations.dtype)  8.85 us
  transfers between devices with their start and end apart: 24, of which 11 were waited for; matrix products, arithmetic and copies ran while one was open for 10% of the time, Pallas kernels for 17%

profile of v5, /device:TPU:0, one launch (start us, length us, event | category | flops | bytes accessed | tf_op | source)
XLA Modules:
  0.0 413.3 jit_solution(13854561577055581086)
XLA Ops:
  6.5 2.8 slice_bitcast_fusion
  9.4 1.3 collective-permute-start
  10.7 3.0 collective-permute-start.1
  14.9 3.0 collective-permute-start.2
  17.9 6.1 %collective-permute-start.3 = (bf16[13,56,1024]{2,1,0:T(8,128)(2,1)S(1)}, bf16[13,56,1024]{2,1,0:T(8,128)(2,1)}, u32[]{:S(2)}, u32[]{:S(2)}) collective-permute-start(bf16[13,56,1024]{2,1,0:T(8,128)(2,1)S(1)} %maximum_select_fusion.1), channel_id=1, source_target_pairs={{0,8},{2,10},{4,12},{6,14},{8,0},{10,2},{12,4},{14,6},{16,24},{18,... | collective-permute-start | bytes 4472840 | tf_op jit(solution)/shard_map/ppermute | solution.py:16
  24.0 5.3 %shard_map.37 = bf16[8,6,128,256]{3,2,1,0:T(8,128)(2,1)} custom-call(bf16[3,3,128,2048]{3,2,1,0:T(8,128)(2,1)} %taps.1), custom_call_target="tpu_custom_call" | custom-call | tf_op jit(solution)/shard_map/pallas_call | solution.py:154
  29.3 20.5 %collective-permute-done.2 = bf16[13,56,1024]{2,1,0:T(8,128)(2,1)} collective-permute-done((bf16[13,56,1024]{2,1,0:T(8,128)(2,1)S(1)}, bf16[13,56,1024]{2,1,0:T(8,128)(2,1)}, u32[]{:S(2)}, u32[]{:S(2)}) %collective-permute-start.2) | collective-permute-done | bytes 1490976 | tf_op jit(solution)/shard_map/ppermute | solution.py:16
  49.8 4.6 %collective-permute-done.3 = bf16[13,56,1024]{2,1,0:T(8,128)(2,1)} collective-permute-done((bf16[13,56,1024]{2,1,0:T(8,128)(2,1)S(1)}, bf16[13,56,1024]{2,1,0:T(8,128)(2,1)}, u32[]{:S(2)}, u32[]{:S(2)}) %collective-permute-start.3) | collective-permute-done | bytes 1490976 | tf_op jit(solution)/shard_map/ppermute | solution.py:16
  54.4 1.7 collective-permute-done.4
  56.2 3.6 all-to-all-start
  61.2 1.5 collective-permute-start.6
  62.7 1.9 collective-permute-start.7
  64.6 31.9 %collective-permute-done.5 = bf16[13,56,1024]{2,1,0:T(8,128)(2,1)} collective-permute-done((bf16[13,56,1024]{2,1,0:T(8,128)(2,1)}, bf16[13,56,1024]{2,1,0:T(8,128)(2,1)}, u32[]{:S(2)}, u32[]{:S(2)}) %collective-permute-start.5) | collective-permute-done | bytes 1490976 | tf_op jit(solution)/shard_map/ppermute | solution.py:16
  96.4 31.4 %collective-permute-done.6 = bf16[13,56,1024]{2,1,0:T(8,128)(2,1)} collective-permute-done((bf16[13,56,1024]{2,1,0:T(8,128)(2,1)}, bf16[13,56,1024]{2,1,0:T(8,128)(2,1)}, u32[]{:S(2)}, u32[]{:S(2)}) %collective-permute-start.6) | collective-permute-done | bytes 1490976 | tf_op jit(solution)/shard_map/ppermute | solution.py:16
  128.7 13.2 %all-gather.3.cloned.1.call-done = bf16[6,128,2048]{2,1,0:T(8,128)(2,1)} async-done(((bf16[3,128,2048]{2,1,0:T(8,128)(2,1)}), bf16[6,128,2048]{2,1,0:T(8,128)(2,1)}) %all-gather.3.cloned.1.call-update) | async-done | bytes 3145744 | tf_op jit(solution)/shard_map/all_gather | solution.py:180
  141.9 5.3 %shard_map.38 = bf16[8,6,128,256]{3,2,1,0:T(8,128)(2,1)} custom-call(bf16[2,3,128,2048]{3,2,1,0:T(8,128)(2,1)} %bitcast.47), custom_call_target="tpu_custom_call" | custom-call | tf_op jit(solution)/shard_map/pallas_call | solution.py:154
  147.2 4.5 %all-to-all-start.1 = ((bf16[8,6,128,256]{3,2,1,0:T(8,128)(2,1)}), bf16[8,6,128,256]{3,2,1,0:T(8,128)(2,1)}, u32[]{:S(2)}, u32[]{:S(2)}) async-start(bf16[8,6,128,256]{3,2,1,0:T(8,128)(2,1)} %shard_map.38), calls=%async_computation.1 | async-start | bytes 6291456 | tf_op jit(solution)/shard_map/all_to_all | solution.py:176
  152.1 8.9 %broadcast_in_dim.52 = bf16[2,99,64,1024]{3,2,1,0:T(8,128)(2,1)} broadcast(bf16[]{:T(256)} %constant.48.clone.1), dimensions={} | broadcast | bytes 25952258 | tf_op jit(solution)/shard_map/broadcast_in_dim | solution.py:228
  161.0 1.5 fusion
  163.2 1.5 collective-permute-start.8
  164.7 2.6 bitcast_dynamic-update-slice_fusion.14
  167.3 2.7 bitcast_dynamic-update-slice_fusion.13
  170.0 2.6 bitcast_dynamic-update-slice_fusion.12
  172.6 2.6 bitcast_dynamic-update-slice_fusion.11
  175.2 2.6 bitcast_dynamic-update-slice_fusion.10
  177.9 20.4 %collective-permute-done.8 = bf16[13,56,1024]{2,1,0:T(8,128)(2,1)S(1)} collective-permute-done((bf16[13,56,1024]{2,1,0:T(8,128)(2,1)}, bf16[13,56,1024]{2,1,0:T(8,128)(2,1)S(1)}, u32[]{:S(2)}, u32[]{:S(2)}) %collective-permute-start.8) | collective-permute-done | bytes 1490976 | tf_op jit(solution)/shard_map/ppermute | solution.py:16
  198.3 2.6 bitcast_dynamic-update-slice_fusion.9
  200.9 1.5 fusion.1
  202.4 1.3 bitcast_dynamic-update-slice_fusion.8
  204.9 1.2 bitcast_dynamic-update-slice_fusion.7
  206.1 1.2 bitcast_dynamic-update-slice_fusion.6
  207.4 2.9 collective-permute-start.18
  210.3 1.3 bitcast_dynamic-update-slice_fusion.5
  211.6 1.3 bitcast_dynamic-update-slice_fusion.4
  212.9 1.3 bitcast_dynamic-update-slice_fusion.3
  214.1 48.3 %collective-permute-done.17.refs_4_ = bf16[2,6,128,256]{3,2,1,0:T(8,128)(2,1)S(1)} collective-permute-done((bf16[2,6,128,256]{3,2,1,0:T(8,128)(2,1)S(1)}, bf16[2,6,128,256]{3,2,1,0:T(8,128)(2,1)S(1)}, u32[]{:S(2)}, u32[]{:S(2)}) %collective-permute-start.17) | collective-permute-done | bytes 786464 | tf_op jit(solution)/shard_map/ppermute | solution.py:16
  263.3 15.1 %collective-permute-done.18.refs_5_ = bf16[2,6,128,256]{3,2,1,0:T(8,128)(2,1)S(1)} collective-permute-done((bf16[2,6,128,256]{3,2,1,0:T(8,128)(2,1)S(1)}, bf16[2,6,128,256]{3,2,1,0:T(8,128)(2,1)S(1)}, u32[]{:S(2)}, u32[]{:S(2)}) %collective-permute-start.18) | collective-permute-done | bytes 786464 | tf_op jit(solution)/shard_map/ppermute | solution.py:16
  279.3 2.9 collective-permute-start.20
  282.2 1.2 bitcast_dynamic-update-slice_fusion.2
  283.5 1.3 bitcast_dynamic-update-slice_fusion.1
  284.8 1.3 bitcast_dynamic-update-slice_fusion.refs_0_.refs_1_.refs_2_.refs_3_
  286.1 23.7 %shard_map.39.refs_6_ = f32[96,64,256]{2,1,0:T(8,128)S(1)} custom-call(s32[2]{0:T(128)S(1)} %pad_add_fusion.scalars_ref, bf16[2,99,64,1024]{3,2,1,0:T(8,128)(2,1)} %bitcast_dynamic-update-slice_fusion.refs_0_.refs_1_.refs_2_.refs_3_, bf16[2,99,64,1024]{3,2,1,0:T(8,128)(2,1)} %bitcast_dynamic-update-slice_fusion.refs_0_.refs_1_.refs_2_.refs_3_, ...), custom_call_target="tpu_custom_call" | custom-call | flops 1024 | bytes 1024 | tf_op jit(solution)/shard_map/pallas_call | solution.py:127
  309.8 2.7 copy-done
  312.5 25.9 %shard_map.40.refs_6_ = f32[96,64,256]{2,1,0:T(8,128)S(1)} custom-call(s32[2]{0:T(128)S(1)} %pad_add_fusion.scalars_ref, bf16[2,99,64,1024]{3,2,1,0:T(8,128)(2,1)} %bitcast_dynamic-update-slice_fusion.refs_0_.refs_1_.refs_2_.refs_3_, bf16[2,99,64,1024]{3,2,1,0:T(8,128)(2,1)} %bitcast_dynamic-update-slice_fusion.refs_0_.refs_1_.refs_2_.refs_3_, ...), custom_call_target="tpu_custom_call" | custom-call | flops 1024 | bytes 1024 | tf_op jit(solution)/shard_map/pallas_call | solution.py:127
  339.2 14.3 %shard_map.41.refs_6_ = f32[96,64,256]{2,1,0:T(8,128)S(1)} custom-call(s32[2]{0:T(128)S(1)} %pad_add_fusion.scalars_ref, bf16[2,99,64,1024]{3,2,1,0:T(8,128)(2,1)} %bitcast_dynamic-update-slice_fusion.refs_0_.refs_1_.refs_2_.refs_3_, bf16[2,99,64,1024]{3,2,1,0:T(8,128)(2,1)} %bitcast_dynamic-update-slice_fusion.refs_0_.refs_1_.refs_2_.refs_3_, ...), custom_call_target="tpu_custom_call" | custom-call | flops 1024 | bytes 1024 | tf_op jit(solution)/shard_map/pallas_call | solution.py:127
  353.5 14.8 %shard_map.42 = bf16[96,56,256]{2,1,0:T(8,128)(2,1)S(1)} custom-call(s32[2]{0:T(128)S(1)} %pad_add_fusion.scalars_ref, bf16[2,99,64,1024]{3,2,1,0:T(8,128)(2,1)} %bitcast_dynamic-update-slice_fusion.refs_0_.refs_1_.refs_2_.refs_3_, bf16[2,99,64,1024]{3,2,1,0:T(8,128)(2,1)} %bitcast_dynamic-update-slice_fusion.refs_0_.refs_1_.refs_2_.refs_3_, ...), custom_call_target="tpu_custom_call" | custom-call | flops 1024 | bytes 1024 | tf_op jit(solution)/shard_map/pallas_call | solution.py:127
  368.4 36.2 %all_to_all.15 = bf16[96,56,256]{2,1,0:T(8,128)(2,1)S(1)} all-to-all(bf16[96,56,256]{2,1,0:T(8,128)(2,1)S(1)} %shard_map.42), channel_id=1, replica_groups={{0,2,4,6,8,10,12,14},{16,18,20,22,24,26,28,30},{1,3,5,7,9,11,13,15},{17..., dimensions={0} | all-to-all | bytes 5505024 | tf_op jit(solution)/shard_map/all_to_all | solution.py:176
  404.6 1.9 copy.6
  (48 shorter events, 8.3 us)
Async XLA Ops:
  6.5 2.8 copy-start.5
  9.4 4.4 %collective-permute-start = (bf16[1,56,1024]{2,1,0:T(8,128)(2,1)S(1)}, bf16[1,56,1024]{2,1,0:T(8,128)(2,1)S(1)}, u32[]{:S(2)}, u32[]{:S(2)}) collective-permute-start(bf16[1,56,1024]{2,1,0:T(8,128)(2,1)S(1)} %get-tuple-element.32), channel_id=1, source_target_pairs={{2,0},{4,2},{6,4},{8,6},{10,8},{12,10},{14,12},{16,14},{18,16},{20... | collective-permute-start | bytes 344072 | tf_op jit(solution)/shard_map/ppermute | solution.py:187
  10.7 4.0 collective-permute-start.1
  14.9 14.4 %copy-start.7 = (bf16[13,56,1024]{2,1,0:T(8,128)(2,1)}, bf16[13,56,1024]{2,1,0:T(8,128)(2,1)S(1)}, u32[]{:S(2)}) copy-start(bf16[13,56,1024]{2,1,0:T(8,128)(2,1)S(1)} %maximum_select_fusion.1) | copy-start | bytes 4472836
  14.9 34.9 %collective-permute-start.2 = (bf16[13,56,1024]{2,1,0:T(8,128)(2,1)S(1)}, bf16[13,56,1024]{2,1,0:T(8,128)(2,1)}, u32[]{:S(2)}, u32[]{:S(2)}) collective-permute-start(bf16[13,56,1024]{2,1,0:T(8,128)(2,1)S(1)} %maximum_select_fusion.1), channel_id=1, source_target_pairs={{0,1},{1,0},{2,3},{3,2},{4,5},{5,4},{6,7},{7,6},{8,9},{9,8},{10,11... | collective-permute-start | bytes 4472840 | tf_op jit(solution)/shard_map/ppermute | solution.py:16
  17.9 36.5 %collective-permute-start.3 = (bf16[13,56,1024]{2,1,0:T(8,128)(2,1)S(1)}, bf16[13,56,1024]{2,1,0:T(8,128)(2,1)}, u32[]{:S(2)}, u32[]{:S(2)}) collective-permute-start(bf16[13,56,1024]{2,1,0:T(8,128)(2,1)S(1)} %maximum_select_fusion.1), channel_id=1, source_target_pairs={{0,8},{2,10},{4,12},{6,14},{8,0},{10,2},{12,4},{14,6},{16,24},{18,... | collective-permute-start | bytes 4472840 | tf_op jit(solution)/shard_map/ppermute | solution.py:16
  24.0 32.2 %collective-permute-start.4 = (bf16[13,56,1024]{2,1,0:T(8,128)(2,1)S(1)}, bf16[13,56,1024]{2,1,0:T(8,128)(2,1)}, u32[]{:S(2)}, u32[]{:S(2)}) collective-permute-start(bf16[13,56,1024]{2,1,0:T(8,128)(2,1)S(1)} %maximum_select_fusion.1), channel_id=1, source_target_pairs={{0,4},{2,6},{4,0},{6,2},{8,12},{10,14},{12,8},{14,10},{16,20},{18,... | collective-permute-start | bytes 4472840 | tf_op jit(solution)/shard_map/ppermute | solution.py:16
  56.2 85.7 %all-to-all-start = ((bf16[8,6,128,256]{3,2,1,0:T(8,128)(2,1)}), bf16[8,6,128,256]{3,2,1,0:T(8,128)(2,1)S(1)}, u32[]{:S(2)}, u32[]{:S(2)}) async-start(bf16[8,6,128,256]{3,2,1,0:T(8,128)(2,1)} %shard_map.37), calls=%async_computation | async-start | bytes 6291456 | tf_op jit(solution)/shard_map/all_to_all | solution.py:176
  59.8 82.1 %all-gather.3.cloned.1.call-start = ((), (), s32[]{:S(2)}) async-start(), calls=%async_computation.3 | async-start | bytes 4718592 | tf_op jit(solution)/shard_map/all_gather | solution.py:180
  60.6 35.9 %collective-permute-start.5 = (bf16[13,56,1024]{2,1,0:T(8,128)(2,1)}, bf16[13,56,1024]{2,1,0:T(8,128)(2,1)}, u32[]{:S(2)}, u32[]{:S(2)}) collective-permute-start(bf16[13,56,1024]{2,1,0:T(8,128)(2,1)} %collective-permute-done.3), channel_id=1, source_target_pairs={{0,1},{1,0},{2,3},{3,2},{4,5},{5,4},{6,7},{7,6},{8,9},{9,8},{10,11... | collective-permute-start | bytes 4472840 | tf_op jit(solution)/shard_map/ppermute | solution.py:16
  61.2 66.6 %collective-permute-start.6 = (bf16[13,56,1024]{2,1,0:T(8,128)(2,1)}, bf16[13,56,1024]{2,1,0:T(8,128)(2,1)}, u32[]{:S(2)}, u32[]{:S(2)}) collective-permute-start(bf16[13,56,1024]{2,1,0:T(8,128)(2,1)} %collective-permute-done.4), channel_id=1, source_target_pairs={{0,1},{1,0},{2,3},{3,2},{4,5},{5,4},{6,7},{7,6},{8,9},{9,8},{10,11... | collective-permute-start | bytes 4472840 | tf_op jit(solution)/shard_map/ppermute | solution.py:16
  62.7 66.0 %collective-permute-start.7 = (bf16[13,56,1024]{2,1,0:T(8,128)(2,1)}, bf16[13,56,1024]{2,1,0:T(8,128)(2,1)}, u32[]{:S(2)}, u32[]{:S(2)}) collective-permute-start(bf16[13,56,1024]{2,1,0:T(8,128)(2,1)} %collective-permute-done.3), channel_id=1, source_target_pairs={{0,4},{2,6},{4,0},{6,2},{8,12},{10,14},{12,8},{14,10},{16,20},{18,... | collective-permute-start | bytes 4472840 | tf_op jit(solution)/shard_map/ppermute | solution.py:16
  147.2 165.3 %all-to-all-start.1 = ((bf16[8,6,128,256]{3,2,1,0:T(8,128)(2,1)}), bf16[8,6,128,256]{3,2,1,0:T(8,128)(2,1)}, u32[]{:S(2)}, u32[]{:S(2)}) async-start(bf16[8,6,128,256]{3,2,1,0:T(8,128)(2,1)} %shard_map.38), calls=%async_computation.1 | async-start | bytes 6291456 | tf_op jit(solution)/shard_map/all_to_all | solution.py:176
  151.8 51.9 %collective-permute-start.9 = (bf16[13,56,1024]{2,1,0:T(8,128)(2,1)}, bf16[13,56,1024]{2,1,0:T(8,128)(2,1)S(1)}, u32[]{:S(2)}, u32[]{:S(2)}) collective-permute-start(bf16[13,56,1024]{2,1,0:T(8,128)(2,1)} %copy-done.7), channel_id=1, source_target_pairs={{0,2},{2,0},{4,6},{6,4},{8,10},{10,8},{12,14},{14,12},{16,18},{18,... | collective-permute-start | bytes 4472840 | tf_op jit(solution)/shard_map/ppermute | solution.py:16
  152.1 8.9 %copy-start.6 = (bf16[12,56,1024]{2,1,0:T(8,128)(2,1)S(1)}, bf16[12,56,1024]{2,1,0:T(8,128)(2,1)}, u32[]{:S(2)}) copy-start(bf16[12,56,1024]{2,1,0:T(8,128)(2,1)} %param.3) | copy-start | bytes 4128772
  162.5 41.9 %collective-permute-start.10 = (bf16[13,56,1024]{2,1,0:T(8,128)(2,1)}, bf16[13,56,1024]{2,1,0:T(8,128)(2,1)S(1)}, u32[]{:S(2)}, u32[]{:S(2)}) collective-permute-start(bf16[13,56,1024]{2,1,0:T(8,128)(2,1)} %collective-permute-done.2), channel_id=1, source_target_pairs={{0,2},{2,0},{4,6},{6,4},{8,10},{10,8},{12,14},{14,12},{16,18},{18,... | collective-permute-start | bytes 4472840 | tf_op jit(solution)/shard_map/ppermute | solution.py:16
  162.7 41.7 %collective-permute-start.11 = (bf16[13,56,1024]{2,1,0:T(8,128)(2,1)}, bf16[13,56,1024]{2,1,0:T(8,128)(2,1)S(1)}, u32[]{:S(2)}, u32[]{:S(2)}) collective-permute-start(bf16[13,56,1024]{2,1,0:T(8,128)(2,1)} %collective-permute-done.3), channel_id=1, source_target_pairs={{0,2},{2,0},{4,6},{6,4},{8,10},{10,8},{12,14},{14,12},{16,18},{18,... | collective-permute-start | bytes 4472840 | tf_op jit(solution)/shard_map/ppermute | solution.py:16
  163.0 44.4 %collective-permute-start.12 = (bf16[13,56,1024]{2,1,0:T(8,128)(2,1)}, bf16[13,56,1024]{2,1,0:T(8,128)(2,1)S(1)}, u32[]{:S(2)}, u32[]{:S(2)}) collective-permute-start(bf16[13,56,1024]{2,1,0:T(8,128)(2,1)} %collective-permute-done.4), channel_id=1, source_target_pairs={{0,2},{2,0},{4,6},{6,4},{8,10},{10,8},{12,14},{14,12},{16,18},{18,... | collective-permute-start | bytes 4472840 | tf_op jit(solution)/shard_map/ppermute | solution.py:16
  163.2 35.1 %collective-permute-start.8 = (bf16[13,56,1024]{2,1,0:T(8,128)(2,1)}, bf16[13,56,1024]{2,1,0:T(8,128)(2,1)S(1)}, u32[]{:S(2)}, u32[]{:S(2)}) collective-permute-start(bf16[13,56,1024]{2,1,0:T(8,128)(2,1)} %collective-permute-done.7), channel_id=1, source_target_pairs={{0,1},{1,0},{2,3},{3,2},{4,5},{5,4},{6,7},{7,6},{8,9},{9,8},{10,11... | collective-permute-start | bytes 4472840 | tf_op jit(solution)/shard_map/ppermute | solution.py:16
  198.3 9.1 %collective-permute-start.13 = (bf16[13,56,1024]{2,1,0:T(8,128)(2,1)}, bf16[13,56,1024]{2,1,0:T(8,128)(2,1)S(1)}, u32[]{:S(2)}, u32[]{:S(2)}) collective-permute-start(bf16[13,56,1024]{2,1,0:T(8,128)(2,1)} %collective-permute-done.5), channel_id=1, source_target_pairs={{0,2},{2,0},{4,6},{6,4},{8,10},{10,8},{12,14},{14,12},{16,18},{18,... | collective-permute-start | bytes 4472840 | tf_op jit(solution)/shard_map/ppermute | solution.py:16
  203.7 10.4 %collective-permute-start.14 = (bf16[13,56,1024]{2,1,0:T(8,128)(2,1)}, bf16[13,56,1024]{2,1,0:T(8,128)(2,1)S(1)}, u32[]{:S(2)}, u32[]{:S(2)}) collective-permute-start(bf16[13,56,1024]{2,1,0:T(8,128)(2,1)} %collective-permute-done.6), channel_id=1, source_target_pairs={{0,2},{2,0},{4,6},{6,4},{8,10},{10,8},{12,14},{14,12},{16,18},{18,... | collective-permute-start | bytes 4472840 | tf_op jit(solution)/shard_map/ppermute | solution.py:16
  204.4 9.8 %collective-permute-start.15 = (bf16[13,56,1024]{2,1,0:T(8,128)(2,1)}, bf16[13,56,1024]{2,1,0:T(8,128)(2,1)S(1)}, u32[]{:S(2)}, u32[]{:S(2)}) collective-permute-start(bf16[13,56,1024]{2,1,0:T(8,128)(2,1)} %collective-permute-done.7), channel_id=1, source_target_pairs={{0,2},{2,0},{4,6},{6,4},{8,10},{10,8},{12,14},{14,12},{16,18},{18,... | collective-permute-start | bytes 4472840 | tf_op jit(solution)/shard_map/ppermute | solution.py:16
  204.4 74.8 %collective-permute-start.16 = (bf16[13,56,1024]{2,1,0:T(8,128)(2,1)S(1)}, bf16[13,56,1024]{2,1,0:T(8,128)(2,1)S(1)}, u32[]{:S(2)}, u32[]{:S(2)}) collective-permute-start(bf16[13,56,1024]{2,1,0:T(8,128)(2,1)S(1)} %collective-permute-done.8), channel_id=1, source_target_pairs={{0,2},{2,0},{4,6},{6,4},{8,10},{10,8},{12,14},{14,12},{16,18},{18,... | collective-permute-start | bytes 4472840 | tf_op jit(solution)/shard_map/ppermute | solution.py:16
  207.4 55.0 %collective-permute-start.17 = (bf16[2,6,128,256]{3,2,1,0:T(8,128)(2,1)S(1)}, bf16[2,6,128,256]{3,2,1,0:T(8,128)(2,1)S(1)}, u32[]{:S(2)}, u32[]{:S(2)}) collective-permute-start(bf16[2,6,128,256]{3,2,1,0:T(8,128)(2,1)S(1)} %get-tuple-element.22), channel_id=1, source_target_pairs={{0,16},{2,18},{4,20},{6,22},{8,24},{10,26},{12,28},{14,30},{16,0},... | collective-permute-start | bytes 2359304 | tf_op jit(solution)/shard_map/ppermute | solution.py:16
  207.4 71.0 %collective-permute-start.18 = (bf16[2,6,128,256]{3,2,1,0:T(8,128)(2,1)S(1)}, bf16[2,6,128,256]{3,2,1,0:T(8,128)(2,1)S(1)}, u32[]{:S(2)}, u32[]{:S(2)}) collective-permute-start(bf16[2,6,128,256]{3,2,1,0:T(8,128)(2,1)S(1)} %get-tuple-element.23), channel_id=1, source_target_pairs={{0,16},{2,18},{4,20},{6,22},{8,24},{10,26},{12,28},{14,30},{16,0},... | collective-permute-start | bytes 2359304 | tf_op jit(solution)/shard_map/ppermute | solution.py:16
  262.4 0.9 copy-start.1
  278.4 0.9 copy-start.3
  279.3 74.2 %collective-permute-start.19 = (bf16[2,6,128,256]{3,2,1,0:T(8,128)(2,1)}, bf16[2,6,128,256]{3,2,1,0:T(8,128)(2,1)}, u32[]{:S(2)}, u32[]{:S(2)}) collective-permute-start(bf16[2,6,128,256]{3,2,1,0:T(8,128)(2,1)} %get-tuple-element.24), channel_id=1, source_target_pairs={{0,16},{2,18},{4,20},{6,22},{8,24},{10,26},{12,28},{14,30},{16,0},... | collective-permute-start | bytes 2359304 | tf_op jit(solution)/shard_map/ppermute | solution.py:16
  279.3 74.2 %collective-permute-start.20 = (bf16[2,6,128,256]{3,2,1,0:T(8,128)(2,1)}, bf16[2,6,128,256]{3,2,1,0:T(8,128)(2,1)}, u32[]{:S(2)}, u32[]{:S(2)}) collective-permute-start(bf16[2,6,128,256]{3,2,1,0:T(8,128)(2,1)} %get-tuple-element.25), channel_id=1, source_target_pairs={{0,16},{2,18},{4,20},{6,22},{8,24},{10,26},{12,28},{14,30},{16,0},... | collective-permute-start | bytes 2359304 | tf_op jit(solution)/shard_map/ppermute | solution.py:16
  309.8 2.7 copy-start
  312.5 26.7 %copy-start.2 = (bf16[2,6,128,256]{3,2,1,0:T(8,128)(2,1)S(1)}, bf16[2,6,128,256]{3,2,1,0:T(8,128)(2,1)}, u32[]{:S(2)}) copy-start(bf16[2,6,128,256]{3,2,1,0:T(8,128)(2,1)} %copy-done.1) | copy-start | bytes 2359300
  312.5 26.7 %copy-start.4 = (bf16[2,6,128,256]{3,2,1,0:T(8,128)(2,1)S(1)}, bf16[2,6,128,256]{3,2,1,0:T(8,128)(2,1)}, u32[]{:S(2)}) copy-start(bf16[2,6,128,256]{3,2,1,0:T(8,128)(2,1)} %copy-done.3) | copy-start | bytes 2359300
Sparse Core Ops, SparseCore 0:
  62.2 79.6 all-gather.2

commit v6 on v5

--- a/solution.py
+++ b/solution.py
@@ -176,12 +176,14 @@
         return lax.all_to_all(taps, "img", 0, 0, axis_index_groups=members, tiled=True)
 
     def exchange(array):
-        groups = [[g * GROUP + r for g in range(parts)] for r in range(GROUP)]
-        return lax.all_gather(array, "img", axis_index_groups=groups)
-
-    first, activations = lax.optimization_barrier((filters[0], activations))
-    raw = exchange(first)
-
+        return [swap(array, "img", GROUP * j) for j in range(1, parts)]
+
+    ready = []
+
+    def step(array):
+        return after(array, *ready) if ready else array
+
+    first, second = filters[0, :2], filters[0, 2:]
     ups = [(i, i + 1) for i in range(size - 1)]
     above = lax.ppermute(activations[-1:], "img", ups)
     below = lax.ppermute(activations[:1], "img", [(j, i) for i, j in ups])
@@ -191,66 +193,96 @@
         jnp.concatenate([above, activations], axis=0),
     )
     slots = {(0, 0): piece}
-
-    def cross(r, *others):
-        sent = after(slots[0, r], *others) if others else slots[0, r]
+    width = -(-side // 16) * 16
+    image = jnp.zeros((chans, GROUP * rows + 3, width, depth), activations.dtype)
+
+    def over_ch(r):
+        sent = step(slots[0, r])
         for j in range(1, chans):
             slots[j, r] = swap(sent, "ch", j)
 
-    cross(0)
+    def over_core(keys):
+        for j, r in keys:
+            slots[j, r + 1] = swap(step(slots[j, r]), "img", 1)
+
+    def place(image, keys):
+        for j, r in keys:
+            owner = rank ^ r
+            start = owner * rows + (owner >= GROUP // 2).astype(jnp.int32)
+            image = lax.dynamic_update_slice(image, slots[j, r][None], (mine ^ j, start, 0, 0))
+        return image
+
+    others = range(1, chans)
+
+    taken = exchange(first)
+    by_rank = by_member(filters, 1, 2)
+    over_ch(0)
     slots[0, 4] = swap(piece, "img", 4)
     slots[0, 2] = swap(piece, "img", 2)
-
-    ready = slots[0, 4], slots[0, 2], slots[1, 0]
-    lower = share(after(by_member(filters, 1, 2), *ready))
-    cross(4, *ready)
-    cross(2, *ready)
-    slots[0, 6] = swap(after(slots[0, 4], *ready), "img", 2)
-    ready = lower, raw, slots[1, 4], slots[1, 2], slots[0, 6]
-    step = GROUP // CHUNKS
-    received = []
-
-    def exchange_chunks(chunks, *others):
-        for chunk in chunks:
-            sent = after(lower[chunk * step : (chunk + 1) * step], *others)
-            for j in range(1, parts):
-                received.append((j, chunk * step, swap(sent, "img", GROUP * j)))
-
-    exchange_chunks(range(CHUNKS // 2), *ready)
-    cross(6, *ready)
-    upper = share(by_member(after(raw, *ready), 0, parts))
-    for (j, r), value in list(slots.items()):
-        slots[j, r + 1] = swap(value, "img", 1)
-    ready = [array for _, _, array in received] + list(slots.values())
-    exchange_chunks(range(CHUNKS // 2, CHUNKS), *ready)
-
-    width = -(-side // 16) * 16
-    image = jnp.zeros((chans, GROUP * rows + 3, width, depth), activations.dtype)
-    for (j, r), value in slots.items():
-        owner = rank ^ r
-        start = owner * rows + (owner >= GROUP // 2).astype(jnp.int32)
-        image = lax.dynamic_update_slice(image, value[None], (mine ^ j, start, 0, 0))
+    ready = [*taken, slots[0, 4], slots[0, 2], *(slots[j, 0] for j in others), by_rank]
+
+    lower = share(step(by_rank))
+    over_ch(4)
+    taken_last = exchange(step(second))
+    keys = [(0, 0), (0, 4), (0, 2)] + [(j, 0) for j in others]
+    over_core(keys)
+    image = place(image, keys)
+    ready = [lower, *(slots[j, 4] for j in others), *taken_last, image]
+    ready += [slots[j, r + 1] for j, r in keys]
+
+    span = GROUP // CHUNKS
+    chunks = [lower[c * span : (c + 1) * span] for c in range(CHUNKS)]
+    received = [exchange(step(chunks[0]))]
+    over_ch(2)
+    slots[0, 6] = swap(step(slots[0, 4]), "img", 2)
+    image = place(image, [(j, r + 1) for j, r in keys])
+    keys = [(j, 4) for j in others]
+    over_core(keys)
+    image = place(image, keys)
+    raw = [filters[0]] + [jnp.concatenate(pair) for pair in zip(taken, taken_last)]
+    by_rank = by_member(step(jnp.stack(raw)), 0, parts)
+    ready = [*received[0], slots[0, 6], *(slots[j, 2] for j in others), image, by_rank]
+    ready += [slots[j, r + 1] for j, r in keys]
+
+    received.append(exchange(step(chunks[1])))
+    over_ch(6)
+    upper = share(step(by_rank))
+    image = place(image, [(j, r + 1) for j, r in keys])
+    keys = [(0, 6)] + [(j, 2) for j in others]
+    over_core(keys)
+    image = place(image, keys)
+    image = place(image, [(j, r + 1) for j, r in keys])
+    ready = [*received[1], upper, *(slots[j, 6] for j in others), image]
+
+    received.append(exchange(step(chunks[2])))
+    keys = [(j, 6) for j in others]
+    over_core(keys)
+    image = place(image, keys)
+    image = place(image, [(j, r + 1) for j, r in keys])
 
     scalars = jnp.stack([group * GROUP * rows, group]).astype(jnp.int32)
     bias = lax.dynamic_slice_in_dim(channel_bias, rank * split, split)[None]
     own = lambda s: s[1]
-    half = len(received) // 2
-    mine_first = [(own, 0, lower, lower.shape, lambda s: (0, 0, 0, 0))]
+    at_start = lambda s: (0, 0, 0, 0)
     every = [
-        (lambda s, p=p: p, 0, upper, (GROUP, 3, shard, split), lambda s, p=p: (0, p, 0, 0))
-        for p in range(parts)
+        (lambda s, j=j: s[1] ^ j, 0, upper, (GROUP, 3, shard, split), lambda s, j=j: (0, j, 0, 0))
+        for j in range(parts)
     ]
-
-    def foreign(arrays):
+    foreign = [lambda s, j=j: s[1] ^ j for j in range(1, parts)]
+
+    def pieces(chosen):
         return [
-            (lambda s, j=j: s[1] ^ j, start, array, array.shape, lambda s: (0, 0, 0, 0))
-            for j, start, array in arrays
+            (foreign[j], c * span, array, array.shape, at_start)
+            for c in chosen
+            for j, array in enumerate(received[c])
         ]
 
-    acc = conv_call((1, 2), mine_first, scalars, image)
+    acc = conv_call((1, 2), [(own, 0, lower, lower.shape, at_start)], scalars, image)
+
+    received.append(exchange(after(chunks[3], acc, *received[2])))
     acc = conv_call((0,), every, scalars, image, acc)
-    acc = conv_call((1, 2), foreign(received[:half]), scalars, image, acc)
-    out = conv_call((1, 2), foreign(received[half:]), scalars, image, acc, bias)
+    acc = conv_call((1, 2), pieces((0, 1, 2)), scalars, image, acc)
+    out = conv_call((1, 2), pieces((3,)), scalars, image, acc, bias)
     out = share(out).reshape(GROUP, rows, side, split)
     return jnp.moveaxis(out, 0, 2).reshape(rows, side, out_local)
 

time: 414 us -> 373 us (0.901)
  waiting for transfers between devices: 190 us -> 131 us
  local copies, waits for them, and re-layouts: 47.6 us -> 63.5 us
  between operations: 13.7 us -> 0.19 us
  other arithmetic: 1.85 us -> 7.89 us
  starting transfers between devices: 35.1 us -> 40.6 us
    ppermute x19 -> x21, waiting for transfers between devices: 175 us -> 129 us  [swap(): return lax.ppermute(array, axis, [(i, i ^ bit) for i in range(size)])]
    all_gather x1 -> x0, waiting for transfers between devices: 13.2 us -> none  [exchange(): return lax.all_gather(array, 'img', axis_index_groups=groups)]
    dynamic_update_slice x15, local copies, waits for them, and re-layouts: 27.2 us -> 39.8 us  [place(): lax.dynamic_update_slice(image, slots[j, r][None], (mine ^ j, start, 0, 0))]
    ppermute x19 -> x21, starting transfers between devices: 22.6 us -> 25.4 us  [swap(): return lax.ppermute(array, axis, [(i, i ^ bit) for i in range(size)])]
  transfers between devices with their start and end apart: 24 -> 25, of which waited for: 11 -> 9; matrix products, arithmetic and copies ran while one was open for 10% -> 16% of each run, Pallas kernels for 17% -> 22%
where the time goes in v6:
time: 373 us; the launch traced here: 371 us
  waiting for transfers between devices  131 us (35%)
  Pallas kernels  90.8 us (24%)
  local copies, waits for them, and re-layouts  63.5 us (17%)
  starting transfers between devices  40.6 us (11%)
  blocking collectives  37.1 us (10%)
  other arithmetic  7.89 us (2%)
    ppermute x21, waiting for transfers between devices, swap(): return lax.ppermute(array, axis, [(i, i ^ bit) for i in range(size)])  129 us
    pallas_call x4, Pallas kernels, conv_call(): pl.pallas_call(body, grid_spec=pltpu.PrefetchScalarGridSpec(num_scalar_pr...  80.2 us
    dynamic_update_slice x15, local copies, waits for them, and re-layouts, place(): lax.dynamic_update_slice(image, slots[j, r][None], (mine ^ j, start, 0, 0))  39.8 us
    all_to_all x1, blocking collectives, share(): lax.all_to_all(taps, 'img', 0, 0, axis_index_groups=members, tiled=True)  37.1 us
    ppermute x21, starting transfers between devices, swap(): return lax.ppermute(array, axis, [(i, i ^ bit) for i in range(size)])  25.4 us
    all_to_all x2, starting transfers between devices, share(): lax.all_to_all(taps, 'img', 0, 0, axis_index_groups=members, tiled=True)  10.8 us
    pallas_call x2, Pallas kernels, by_member(): pl.pallas_call(body, grid=(count, across), in_specs=[pl.BlockSpec((1, 1,...  10.6 us
    broadcast_in_dim x1, local copies, waits for them, and re-layouts, local(): jnp.zeros((chans, GROUP * rows + 3, width, depth), activations.dtype)  8.85 us
  transfers between devices with their start and end apart: 25, of which 9 were waited for; matrix products, arithmetic and copies ran while one was open for 16% of the time, Pallas kernels for 22%

profile of v6, /device:TPU:0, one launch (start us, length us, event | category | flops | bytes accessed | tf_op | source)
XLA Modules:
  0.0 371.1 jit_solution(13365699213253099864)
XLA Ops:
  2.3 3.0 collective-permute-start.1
  6.3 3.2 maximum_select_fusion.1
  9.5 7.5 %collective-permute-start.2 = (bf16[13,56,1024]{2,1,0:T(8,128)(2,1)}, bf16[13,56,1024]{2,1,0:T(8,128)(2,1)}, u32[]{:S(2)}, u32[]{:S(2)}) collective-permute-start(bf16[13,56,1024]{2,1,0:T(8,128)(2,1)} %maximum_select_fusion.1), channel_id=1, source_target_pairs={{0,8},{2,10},{4,12},{6,14},{8,0},{10,2},{12,4},{14,6},{16,24},{18,... | collective-permute-start | bytes 4472840 | tf_op jit(solution)/shard_map/ppermute | solution.py:16
  17.0 1.5 collective-permute-start.4
  19.8 2.7 collective-permute-start.5
  22.4 5.3 %shard_map.37 = bf16[8,6,128,256]{3,2,1,0:T(8,128)(2,1)} custom-call(bf16[3,3,128,2048]{3,2,1,0:T(8,128)(2,1)} %taps.1), custom_call_target="tpu_custom_call" | custom-call | tf_op jit(solution)/shard_map/pallas_call | solution.py:154
  27.7 41.6 %collective-permute-done.5 = bf16[2,128,2048]{2,1,0:T(8,128)(2,1)S(1)} collective-permute-done((bf16[2,128,2048]{2,1,0:T(8,128)(2,1)S(1)}, bf16[2,128,2048]{2,1,0:T(8,128)(2,1)S(1)}, u32[]{:S(2)}, u32[]{:S(2)}) %collective-permute-start.5) | collective-permute-done | bytes 1048608 | tf_op jit(solution)/shard_map/ppermute | solution.py:16
  70.4 6.3 %all-to-all-start = ((bf16[8,6,128,256]{3,2,1,0:T(8,128)(2,1)}), bf16[8,6,128,256]{3,2,1,0:T(8,128)(2,1)S(1)}, u32[]{:S(2)}, u32[]{:S(2)}) async-start(bf16[8,6,128,256]{3,2,1,0:T(8,128)(2,1)} %shard_map.37), calls=%async_computation | async-start | bytes 6291456 | tf_op jit(solution)/shard_map/all_to_all | solution.py:176
  76.7 1.9 slice_bitcast_fusion.1
  79.3 8.9 %broadcast_in_dim.52 = bf16[2,99,64,1024]{3,2,1,0:T(8,128)(2,1)} broadcast(bf16[]{:T(256)} %constant.48.clone.1), dimensions={} | broadcast | bytes 25952258 | tf_op jit(solution)/shard_map/broadcast_in_dim | solution.py:197
  88.1 1.5 fusion
  89.7 1.5 collective-permute-start.10
  91.6 31.3 %collective-permute-done.11 = bf16[1,128,2048]{2,1,0:T(8,128)(2,1)} collective-permute-done((bf16[1,128,2048]{2,1,0:T(8,128)(2,1)}, bf16[1,128,2048]{2,1,0:T(8,128)(2,1)}, u32[]{:S(2)}, u32[]{:S(2)}) %collective-permute-start.11) | collective-permute-done | bytes 524320 | tf_op jit(solution)/shard_map/ppermute | solution.py:16
  122.9 2.7 bitcast_dynamic-update-slice_fusion.14
  125.6 2.7 bitcast_dynamic-update-slice_fusion.13
  128.3 2.7 bitcast_dynamic-update-slice_fusion.12
  132.2 1.9 pad_maximum_fusion.taps
  134.1 1.7 fusion.1
  135.9 3.4 collective-permute-start.15
  139.3 1.6 collective-permute-start.13
  140.9 1.5 collective-permute-start.14
  142.4 5.3 %shard_map.38 = bf16[8,6,128,256]{3,2,1,0:T(8,128)(2,1)} custom-call(bf16[2,3,128,2048]{3,2,1,0:T(8,128)(2,1)} %pad_maximum_fusion.taps), custom_call_target="tpu_custom_call" | custom-call | tf_op jit(solution)/shard_map/pallas_call | solution.py:154
  147.7 2.6 bitcast_dynamic-update-slice_fusion.11
  150.3 2.7 bitcast_dynamic-update-slice_fusion.10
  153.0 2.6 bitcast_dynamic-update-slice_fusion.9
  155.6 2.6 bitcast_dynamic-update-slice_fusion.8
  158.2 2.6 bitcast_dynamic-update-slice_fusion.7
  160.9 13.9 %collective-permute-done.15.refs_2_ = bf16[2,6,128,256]{3,2,1,0:T(8,128)(2,1)} collective-permute-done((bf16[2,6,128,256]{3,2,1,0:T(8,128)(2,1)}, bf16[2,6,128,256]{3,2,1,0:T(8,128)(2,1)}, u32[]{:S(2)}, u32[]{:S(2)}) %collective-permute-start.15) | collective-permute-done | bytes 786464 | tf_op jit(solution)/shard_map/ppermute | solution.py:16
  175.8 4.5 %all-to-all-start.1 = ((bf16[8,6,128,256]{3,2,1,0:T(8,128)(2,1)}), bf16[8,6,128,256]{3,2,1,0:T(8,128)(2,1)}, u32[]{:S(2)}, u32[]{:S(2)}) async-start(bf16[8,6,128,256]{3,2,1,0:T(8,128)(2,1)} %shard_map.38), calls=%async_computation.1 | async-start | bytes 6291456 | tf_op jit(solution)/shard_map/all_to_all | solution.py:176
  180.8 1.5 collective-permute-start.18
  182.7 2.6 bitcast_dynamic-update-slice_fusion.6
  185.4 2.6 bitcast_dynamic-update-slice_fusion.5
  188.0 2.6 bitcast_dynamic-update-slice_fusion.4
  190.7 2.7 bitcast_dynamic-update-slice_fusion.3
  193.4 2.6 bitcast_dynamic-update-slice_fusion.2
  196.0 36.0 %collective-permute-done.19.refs_3_ = bf16[2,6,128,256]{3,2,1,0:T(8,128)(2,1)S(1)} collective-permute-done((bf16[2,6,128,256]{3,2,1,0:T(8,128)(2,1)}, bf16[2,6,128,256]{3,2,1,0:T(8,128)(2,1)S(1)}, u32[]{:S(2)}, u32[]{:S(2)}) %collective-permute-start.19) | collective-permute-done | bytes 786464 | tf_op jit(solution)/shard_map/ppermute | solution.py:16
  234.0 2.1 collective-permute-start.21
  236.3 2.6 bitcast_dynamic-update-slice_fusion.1
  238.9 2.7 bitcast_dynamic-update-slice_fusion.refs_0_.refs_1_.refs_2_.refs_3_
  241.6 23.7 %shard_map.39.refs_6_ = f32[96,64,256]{2,1,0:T(8,128)S(1)} custom-call(s32[2]{0:T(128)S(1)} %pad_add_fusion.scalars_ref, bf16[2,99,64,1024]{3,2,1,0:T(8,128)(2,1)} %bitcast_dynamic-update-slice_fusion.refs_0_.refs_1_.refs_2_.refs_3_, bf16[2,99,64,1024]{3,2,1,0:T(8,128)(2,1)} %bitcast_dynamic-update-slice_fusion.refs_0_.refs_1_.refs_2_.refs_3_, ...), custom_call_target="tpu_custom_call" | custom-call | flops 1024 | bytes 1024 | tf_op jit(solution)/shard_map/pallas_call | solution.py:127
  265.3 2.7 copy-done
  268.0 4.1 %collective-permute-done.21.refs_4_ = bf16[2,6,128,256]{3,2,1,0:T(8,128)(2,1)} collective-permute-done((bf16[2,6,128,256]{3,2,1,0:T(8,128)(2,1)}, bf16[2,6,128,256]{3,2,1,0:T(8,128)(2,1)}, u32[]{:S(2)}, u32[]{:S(2)}) %collective-permute-start.21) | collective-permute-done | bytes 786464 | tf_op jit(solution)/shard_map/ppermute | solution.py:16
  272.1 26.2 %shard_map.40.refs_5_ = f32[96,64,256]{2,1,0:T(8,128)S(1)} custom-call(s32[2]{0:T(128)S(1)} %pad_add_fusion.scalars_ref, bf16[2,99,64,1024]{3,2,1,0:T(8,128)(2,1)} %bitcast_dynamic-update-slice_fusion.refs_0_.refs_1_.refs_2_.refs_3_, bf16[2,99,64,1024]{3,2,1,0:T(8,128)(2,1)} %bitcast_dynamic-update-slice_fusion.refs_0_.refs_1_.refs_2_.refs_3_, ...), custom_call_target="tpu_custom_call" | custom-call | flops 1024 | bytes 1024 | tf_op jit(solution)/shard_map/pallas_call | solution.py:127
  298.3 2.7 copy-done.1
  301.7 19.8 %shard_map.41.refs_3_ = f32[96,64,256]{2,1,0:T(8,128)S(1)} custom-call(s32[2]{0:T(128)S(1)} %pad_add_fusion.scalars_ref, bf16[2,99,64,1024]{3,2,1,0:T(8,128)(2,1)} %bitcast_dynamic-update-slice_fusion.refs_0_.refs_1_.refs_2_.refs_3_, bf16[2,99,64,1024]{3,2,1,0:T(8,128)(2,1)} %bitcast_dynamic-update-slice_fusion.refs_0_.refs_1_.refs_2_.refs_3_, ...), custom_call_target="tpu_custom_call" | custom-call | flops 1024 | bytes 1024 | tf_op jit(solution)/shard_map/pallas_call | solution.py:127
  321.5 10.5 %shard_map.42 = bf16[96,56,256]{2,1,0:T(8,128)(2,1)S(1)} custom-call(s32[2]{0:T(128)S(1)} %pad_add_fusion.scalars_ref, bf16[2,99,64,1024]{3,2,1,0:T(8,128)(2,1)} %bitcast_dynamic-update-slice_fusion.refs_0_.refs_1_.refs_2_.refs_3_, bf16[2,99,64,1024]{3,2,1,0:T(8,128)(2,1)} %bitcast_dynamic-update-slice_fusion.refs_0_.refs_1_.refs_2_.refs_3_, ...), custom_call_target="tpu_custom_call" | custom-call | flops 1024 | bytes 1024 | tf_op jit(solution)/shard_map/pallas_call | solution.py:127
  332.1 37.1 %all_to_all.15 = bf16[96,56,256]{2,1,0:T(8,128)(2,1)S(1)} all-to-all(bf16[96,56,256]{2,1,0:T(8,128)(2,1)S(1)} %shard_map.42), channel_id=1, replica_groups={{0,2,4,6,8,10,12,14},{16,18,20,22,24,26,28,30},{1,3,5,7,9,11,13,15},{17..., dimensions={0} | all-to-all | bytes 5505024 | tf_op jit(solution)/shard_map/all_to_all | solution.py:176
  369.2 1.9 copy.5
  (52 shorter events, 12.8 us)
Async XLA Ops:
  1.0 4.4 %collective-permute-start = (bf16[1,56,1024]{2,1,0:T(8,128)(2,1)S(1)}, bf16[1,56,1024]{2,1,0:T(8,128)(2,1)S(1)}, u32[]{:S(2)}, u32[]{:S(2)}) collective-permute-start(bf16[1,56,1024]{2,1,0:T(8,128)(2,1)S(1)} %get-tuple-element.46), channel_id=1, source_target_pairs={{2,0},{4,2},{6,4},{8,6},{10,8},{12,10},{14,12},{16,14},{18,16},{20... | collective-permute-start | bytes 344072 | tf_op jit(solution)/shard_map/ppermute | solution.py:189
  2.3 4.0 %collective-permute-start.1 = (bf16[1,56,1024]{2,1,0:T(8,128)(2,1)S(1)}, bf16[1,56,1024]{2,1,0:T(8,128)(2,1)S(1)}, u32[]{:S(2)}, u32[]{:S(2)}) collective-permute-start(bf16[1,56,1024]{2,1,0:T(8,128)(2,1)S(1)} %get-tuple-element.45), channel_id=1, source_target_pairs={{0,2},{2,4},{4,6},{6,8},{8,10},{10,12},{12,14},{14,16},{16,18},{18... | collective-permute-start | bytes 344072 | tf_op jit(solution)/shard_map/ppermute | solution.py:188
  9.5 60.9 %collective-permute-start.2 = (bf16[13,56,1024]{2,1,0:T(8,128)(2,1)}, bf16[13,56,1024]{2,1,0:T(8,128)(2,1)}, u32[]{:S(2)}, u32[]{:S(2)}) collective-permute-start(bf16[13,56,1024]{2,1,0:T(8,128)(2,1)} %maximum_select_fusion.1), channel_id=1, source_target_pairs={{0,8},{2,10},{4,12},{6,14},{8,0},{10,2},{12,4},{14,6},{16,24},{18,... | collective-permute-start | bytes 4472840 | tf_op jit(solution)/shard_map/ppermute | solution.py:16
  17.0 53.4 %collective-permute-start.3 = (bf16[13,56,1024]{2,1,0:T(8,128)(2,1)}, bf16[13,56,1024]{2,1,0:T(8,128)(2,1)}, u32[]{:S(2)}, u32[]{:S(2)}) collective-permute-start(bf16[13,56,1024]{2,1,0:T(8,128)(2,1)} %maximum_select_fusion.1), channel_id=1, source_target_pairs={{0,4},{2,6},{4,0},{6,2},{8,12},{10,14},{12,8},{14,10},{16,20},{18,... | collective-permute-start | bytes 4472840 | tf_op jit(solution)/shard_map/ppermute | solution.py:16
  17.0 53.4 %collective-permute-start.4 = (bf16[13,56,1024]{2,1,0:T(8,128)(2,1)}, bf16[13,56,1024]{2,1,0:T(8,128)(2,1)}, u32[]{:S(2)}, u32[]{:S(2)}) collective-permute-start(bf16[13,56,1024]{2,1,0:T(8,128)(2,1)} %maximum_select_fusion.1), channel_id=1, source_target_pairs={{0,1},{1,0},{2,3},{3,2},{4,5},{5,4},{6,7},{7,6},{8,9},{9,8},{10,11... | collective-permute-start | bytes 4472840 | tf_op jit(solution)/shard_map/ppermute | solution.py:16
  19.8 49.6 %collective-permute-start.5 = (bf16[2,128,2048]{2,1,0:T(8,128)(2,1)S(1)}, bf16[2,128,2048]{2,1,0:T(8,128)(2,1)S(1)}, u32[]{:S(2)}, u32[]{:S(2)}) collective-permute-start(bf16[2,128,2048]{2,1,0:T(8,128)(2,1)S(1)} %slice_bitcast_fusion), channel_id=1, source_target_pairs={{0,16},{2,18},{4,20},{6,22},{8,24},{10,26},{12,28},{14,30},{16,0},... | collective-permute-start | bytes 3145736 | tf_op jit(solution)/shard_map/ppermute | solution.py:16
  69.3 1.0 copy-start.5
  70.4 63.8 %all-to-all-start = ((bf16[8,6,128,256]{3,2,1,0:T(8,128)(2,1)}), bf16[8,6,128,256]{3,2,1,0:T(8,128)(2,1)S(1)}, u32[]{:S(2)}, u32[]{:S(2)}) async-start(bf16[8,6,128,256]{3,2,1,0:T(8,128)(2,1)} %shard_map.37), calls=%async_computation | async-start | bytes 6291456 | tf_op jit(solution)/shard_map/all_to_all | solution.py:176
  78.6 44.3 %collective-permute-start.11 = (bf16[1,128,2048]{2,1,0:T(8,128)(2,1)}, bf16[1,128,2048]{2,1,0:T(8,128)(2,1)}, u32[]{:S(2)}, u32[]{:S(2)}) collective-permute-start(bf16[1,128,2048]{2,1,0:T(8,128)(2,1)} %slice_bitcast_fusion.1), channel_id=1, source_target_pairs={{0,16},{2,18},{4,20},{6,22},{8,24},{10,26},{12,28},{14,30},{16,0},... | collective-permute-start | bytes 1572872 | tf_op jit(solution)/shard_map/ppermute | solution.py:16
  79.3 8.9 %copy-start.4 = (bf16[12,56,1024]{2,1,0:T(8,128)(2,1)S(1)}, bf16[12,56,1024]{2,1,0:T(8,128)(2,1)}, u32[]{:S(2)}) copy-start(bf16[12,56,1024]{2,1,0:T(8,128)(2,1)} %param.3) | copy-start | bytes 4128772
  89.7 46.2 %collective-permute-start.10 = (bf16[13,56,1024]{2,1,0:T(8,128)(2,1)}, bf16[13,56,1024]{2,1,0:T(8,128)(2,1)}, u32[]{:S(2)}, u32[]{:S(2)}) collective-permute-start(bf16[13,56,1024]{2,1,0:T(8,128)(2,1)} %collective-permute-done.2), channel_id=1, source_target_pairs={{0,1},{1,0},{2,3},{3,2},{4,5},{5,4},{6,7},{7,6},{8,9},{9,8},{10,11... | collective-permute-start | bytes 4472840 | tf_op jit(solution)/shard_map/ppermute | solution.py:16
  91.1 44.7 %collective-permute-start.7 = (bf16[13,56,1024]{2,1,0:T(8,128)(2,1)}, bf16[13,56,1024]{2,1,0:T(8,128)(2,1)}, u32[]{:S(2)}, u32[]{:S(2)}) collective-permute-start(bf16[13,56,1024]{2,1,0:T(8,128)(2,1)} %collective-permute-done.2), channel_id=1, source_target_pairs={{0,2},{2,0},{4,6},{6,4},{8,10},{10,8},{12,14},{14,12},{16,18},{18,... | collective-permute-start | bytes 4472840 | tf_op jit(solution)/shard_map/ppermute | solution.py:16
  91.1 44.7 %collective-permute-start.6 = (bf16[13,56,1024]{2,1,0:T(8,128)(2,1)}, bf16[13,56,1024]{2,1,0:T(8,128)(2,1)}, u32[]{:S(2)}, u32[]{:S(2)}) collective-permute-start(bf16[13,56,1024]{2,1,0:T(8,128)(2,1)} %maximum_select_fusion.1), channel_id=1, source_target_pairs={{0,2},{2,0},{4,6},{6,4},{8,10},{10,8},{12,14},{14,12},{16,18},{18,... | collective-permute-start | bytes 4472840 | tf_op jit(solution)/shard_map/ppermute | solution.py:16
  91.6 44.2 %collective-permute-start.8 = (bf16[13,56,1024]{2,1,0:T(8,128)(2,1)}, bf16[13,56,1024]{2,1,0:T(8,128)(2,1)}, u32[]{:S(2)}, u32[]{:S(2)}) collective-permute-start(bf16[13,56,1024]{2,1,0:T(8,128)(2,1)} %collective-permute-done.3), channel_id=1, source_target_pairs={{0,2},{2,0},{4,6},{6,4},{8,10},{10,8},{12,14},{14,12},{16,18},{18,... | collective-permute-start | bytes 4472840 | tf_op jit(solution)/shard_map/ppermute | solution.py:16
  122.9 12.9 %collective-permute-start.9 = (bf16[13,56,1024]{2,1,0:T(8,128)(2,1)}, bf16[13,56,1024]{2,1,0:T(8,128)(2,1)}, u32[]{:S(2)}, u32[]{:S(2)}) collective-permute-start(bf16[13,56,1024]{2,1,0:T(8,128)(2,1)} %collective-permute-done.4), channel_id=1, source_target_pairs={{0,2},{2,0},{4,6},{6,4},{8,10},{10,8},{12,14},{14,12},{16,18},{18,... | collective-permute-start | bytes 4472840 | tf_op jit(solution)/shard_map/ppermute | solution.py:16
  125.6 5.4 %copy-start.6 = (bf16[2,128,2048]{2,1,0:T(8,128)(2,1)S(1)}, bf16[2,128,2048]{2,1,0:T(8,128)(2,1)}, u32[]{:S(2)}) copy-start(bf16[2,128,2048]{2,1,0:T(8,128)(2,1)} %copy-done.5) | copy-start | bytes 3145732
  128.3 3.9 %slice-start = ((bf16[3,3,128,2048]{3,2,1,0:T(8,128)(2,1)}), bf16[1,3,128,2048]{3,2,1,0:T(8,128)(2,1)S(1)}, s32[]{:S(2)}) async-start(bf16[3,3,128,2048]{3,2,1,0:T(8,128)(2,1)} %taps.1), calls=%async_computation.3 | async-start | bytes 3145728 | tf_op jit(solution)/shard_map/slice | solution.py:242
  135.9 38.9 %collective-permute-start.15 = (bf16[2,6,128,256]{3,2,1,0:T(8,128)(2,1)}, bf16[2,6,128,256]{3,2,1,0:T(8,128)(2,1)}, u32[]{:S(2)}, u32[]{:S(2)}) collective-permute-start(bf16[2,6,128,256]{3,2,1,0:T(8,128)(2,1)} %get-tuple-element.32), channel_id=1, source_target_pairs={{0,16},{2,18},{4,20},{6,22},{8,24},{10,26},{12,28},{14,30},{16,0},... | collective-permute-start | bytes 2359304 | tf_op jit(solution)/shard_map/ppermute | solution.py:16
  139.3 35.4 %collective-permute-start.13 = (bf16[13,56,1024]{2,1,0:T(8,128)(2,1)}, bf16[13,56,1024]{2,1,0:T(8,128)(2,1)}, u32[]{:S(2)}, u32[]{:S(2)}) collective-permute-start(bf16[13,56,1024]{2,1,0:T(8,128)(2,1)} %collective-permute-done.2), channel_id=1, source_target_pairs={{0,4},{2,6},{4,0},{6,2},{8,12},{10,14},{12,8},{14,10},{16,20},{18,... | collective-permute-start | bytes 4472840 | tf_op jit(solution)/shard_map/ppermute | solution.py:16
  140.9 34.8 %collective-permute-start.14 = (bf16[13,56,1024]{2,1,0:T(8,128)(2,1)}, bf16[13,56,1024]{2,1,0:T(8,128)(2,1)}, u32[]{:S(2)}, u32[]{:S(2)}) collective-permute-start(bf16[13,56,1024]{2,1,0:T(8,128)(2,1)} %collective-permute-done.3), channel_id=1, source_target_pairs={{0,1},{1,0},{2,3},{3,2},{4,5},{5,4},{6,7},{7,6},{8,9},{9,8},{10,11... | collective-permute-start | bytes 4472840 | tf_op jit(solution)/shard_map/ppermute | solution.py:16
  147.7 28.1 %collective-permute-start.12 = (bf16[13,56,1024]{2,1,0:T(8,128)(2,1)}, bf16[13,56,1024]{2,1,0:T(8,128)(2,1)}, u32[]{:S(2)}, u32[]{:S(2)}) collective-permute-start(bf16[13,56,1024]{2,1,0:T(8,128)(2,1)} %collective-permute-done.10), channel_id=1, source_target_pairs={{0,2},{2,0},{4,6},{6,4},{8,10},{10,8},{12,14},{14,12},{16,18},{18,... | collective-permute-start | bytes 4472840 | tf_op jit(solution)/shard_map/ppermute | solution.py:16
  175.8 58.3 %all-to-all-start.1 = ((bf16[8,6,128,256]{3,2,1,0:T(8,128)(2,1)}), bf16[8,6,128,256]{3,2,1,0:T(8,128)(2,1)}, u32[]{:S(2)}, u32[]{:S(2)}) async-start(bf16[8,6,128,256]{3,2,1,0:T(8,128)(2,1)} %shard_map.38), calls=%async_computation.1 | async-start | bytes 6291456 | tf_op jit(solution)/shard_map/all_to_all | solution.py:176
  180.3 10.4 %collective-permute-start.16 = (bf16[13,56,1024]{2,1,0:T(8,128)(2,1)}, bf16[13,56,1024]{2,1,0:T(8,128)(2,1)}, u32[]{:S(2)}, u32[]{:S(2)}) collective-permute-start(bf16[13,56,1024]{2,1,0:T(8,128)(2,1)} %collective-permute-done.13), channel_id=1, source_target_pairs={{0,2},{2,0},{4,6},{6,4},{8,10},{10,8},{12,14},{14,12},{16,18},{18,... | collective-permute-start | bytes 4472840 | tf_op jit(solution)/shard_map/ppermute | solution.py:16
  180.6 12.7 %collective-permute-start.17 = (bf16[13,56,1024]{2,1,0:T(8,128)(2,1)}, bf16[13,56,1024]{2,1,0:T(8,128)(2,1)}, u32[]{:S(2)}, u32[]{:S(2)}) collective-permute-start(bf16[13,56,1024]{2,1,0:T(8,128)(2,1)} %collective-permute-done.14), channel_id=1, source_target_pairs={{0,2},{2,0},{4,6},{6,4},{8,10},{10,8},{12,14},{14,12},{16,18},{18,... | collective-permute-start | bytes 4472840 | tf_op jit(solution)/shard_map/ppermute | solution.py:16
  180.8 52.0 %collective-permute-start.18 = (bf16[13,56,1024]{2,1,0:T(8,128)(2,1)}, bf16[13,56,1024]{2,1,0:T(8,128)(2,1)}, u32[]{:S(2)}, u32[]{:S(2)}) collective-permute-start(bf16[13,56,1024]{2,1,0:T(8,128)(2,1)} %collective-permute-done.13), channel_id=1, source_target_pairs={{0,1},{1,0},{2,3},{3,2},{4,5},{5,4},{6,7},{7,6},{8,9},{9,8},{10,11... | collective-permute-start | bytes 4472840 | tf_op jit(solution)/shard_map/ppermute | solution.py:16
  182.4 49.6 %collective-permute-start.19 = (bf16[2,6,128,256]{3,2,1,0:T(8,128)(2,1)}, bf16[2,6,128,256]{3,2,1,0:T(8,128)(2,1)S(1)}, u32[]{:S(2)}, u32[]{:S(2)}) collective-permute-start(bf16[2,6,128,256]{3,2,1,0:T(8,128)(2,1)} %get-tuple-element.36), channel_id=1, source_target_pairs={{0,16},{2,18},{4,20},{6,22},{8,24},{10,26},{12,28},{14,30},{16,0},... | collective-permute-start | bytes 2359304 | tf_op jit(solution)/shard_map/ppermute | solution.py:16
  231.9 0.9 copy-start.2
  234.0 4.9 %collective-permute-start.20 = (bf16[13,56,1024]{2,1,0:T(8,128)(2,1)}, bf16[13,56,1024]{2,1,0:T(8,128)(2,1)}, u32[]{:S(2)}, u32[]{:S(2)}) collective-permute-start(bf16[13,56,1024]{2,1,0:T(8,128)(2,1)} %collective-permute-done.18), channel_id=1, source_target_pairs={{0,2},{2,0},{4,6},{6,4},{8,10},{10,8},{12,14},{14,12},{16,18},{18,... | collective-permute-start | bytes 4472840 | tf_op jit(solution)/shard_map/ppermute | solution.py:16
  234.0 38.0 %collective-permute-start.21 = (bf16[2,6,128,256]{3,2,1,0:T(8,128)(2,1)}, bf16[2,6,128,256]{3,2,1,0:T(8,128)(2,1)}, u32[]{:S(2)}, u32[]{:S(2)}) collective-permute-start(bf16[2,6,128,256]{3,2,1,0:T(8,128)(2,1)} %get-tuple-element.39), channel_id=1, source_target_pairs={{0,16},{2,18},{4,20},{6,22},{8,24},{10,26},{12,28},{14,30},{16,0},... | collective-permute-start | bytes 2359304 | tf_op jit(solution)/shard_map/ppermute | solution.py:16
  265.3 2.7 copy-start
  272.1 49.5 %collective-permute-start.22 = (bf16[2,6,128,256]{3,2,1,0:T(8,128)(2,1)}, bf16[2,6,128,256]{3,2,1,0:T(8,128)(2,1)S(1)}, u32[]{:S(2)}, u32[]{:S(2)}) collective-permute-start(bf16[2,6,128,256]{3,2,1,0:T(8,128)(2,1)} %get-tuple-element.40), channel_id=1, source_target_pairs={{0,16},{2,18},{4,20},{6,22},{8,24},{10,26},{12,28},{14,30},{16,0},... | collective-permute-start | bytes 2359304 | tf_op jit(solution)/shard_map/ppermute | solution.py:16
  272.1 29.6 %copy-start.3 = (bf16[2,6,128,256]{3,2,1,0:T(8,128)(2,1)S(1)}, bf16[2,6,128,256]{3,2,1,0:T(8,128)(2,1)}, u32[]{:S(2)}) copy-start(bf16[2,6,128,256]{3,2,1,0:T(8,128)(2,1)} %copy-done.2) | copy-start | bytes 2359300
  298.3 2.7 copy-start.1

commit v7 on v6

--- a/solution.py
+++ b/solution.py
@@ -8,7 +8,6 @@
 SIDE = 56
 GROUP = 8
 TILE = 8
-CHUNKS = 4
 
 
 def swap(array, axis, bit):
@@ -20,18 +19,22 @@
     return lax.optimization_barrier((array, *others))[0]
 
 
-def conv_call(taps, pieces, scalars, image, acc=None, bias=None):
+def conv_call(pieces, scalars, image, acc=None, bias=None):
     blocks, padded_rows, width, depth = image.shape
-    shard, out_width = pieces[0][2].shape[-2:]
+    shard, out_width = pieces[0][3][-2:]
     row_count = padded_rows - 3
     offsets = list(dict.fromkeys(piece[0] for piece in pieces))
     per_group = GROUP * shard // depth
     final = bias is not None
     assert row_count % TILE == 0 and SIDE % TILE == 0
 
+    edges_of = {
+        offset: sorted({v for o, *_, taps in pieces if o == offset for v in taps if v != 1})
+        for offset in offsets
+    }
     windows = {}
     for offset in offsets:
-        ranges = [(start, start + block[-4]) for o, start, _, block, _ in pieces if o == offset]
+        ranges = [(start, start + block[-4]) for o, start, _, block, *_ in pieces if o == offset]
         low, high = min(a for a, _ in ranges) * shard, max(b for _, b in ranges) * shard
         if low // depth == (high - 1) // depth:
             windows[offset] = (1, low // depth, high - low, low % depth)
@@ -42,32 +45,31 @@
         refs = list(refs)
         images = {}
         for offset in offsets:
-            images[offset] = refs.pop(0), *(refs.pop(0) for v in taps if v != 1)
+            images[offset] = refs.pop(0), {v: refs.pop(0) for v in edges_of[offset]}
         weights = [refs.pop(0) for _ in pieces]
         acc_ref = refs.pop(0) if acc is not None else None
         bias_ref = refs.pop(0) if final else None
         out = refs.pop(0)
 
         operands, columns = [], []
-        for (offset, start, _, block, _), weight in zip(pieces, weights):
+        for (offset, start, _, block, _, taps), weight in zip(pieces, weights):
             count, first_block, size, first_lane = windows[offset]
-            main, *outer = images[offset]
+            main, edges = images[offset]
             at, lanes = 0, block[-4] * shard
             while at < lanes:
                 inner, lane = divmod(start * shard + at, depth)
                 inner, lane = inner - first_block, lane - first_lane
                 length = min(size - lane, lanes - at)
                 window = pl.ds(lane, length)
-                edges = list(outer)
                 for index, vertical in enumerate(taps):
                     rows = main[inner, :, :, window]
                     if vertical == 0:
                         rows = jnp.concatenate(
-                            [edges.pop(0)[inner, :, :, window], rows[:-1]], axis=0
+                            [edges[0][inner, :, :, window], rows[:-1]], axis=0
                         )
                     if vertical == 2:
                         rows = jnp.concatenate(
-                            [rows[1:], edges.pop(0)[inner, :, :, window]], axis=0
+                            [rows[1:], edges[2][inner, :, :, window]], axis=0
                         )
                     operands.append(rows.reshape(TILE * width, length))
                     members = pl.ds(at // shard, length // shard)
@@ -112,10 +114,10 @@
     out_cols = SIDE if final else width
     in_specs, operands = [], []
     for offset in offsets:
-        for vertical in [1] + [v for v in taps if v != 1]:
+        for vertical in [1] + edges_of[offset]:
             in_specs.append(image_spec(offset, vertical))
             operands.append(image)
-    for _, _, array, block, place in pieces:
+    for _, _, array, block, place, _ in pieces:
         in_specs.append(pl.BlockSpec(block, lambda t, s, place=place: place(s)))
         operands.append(array)
     if acc is not None:
@@ -183,7 +185,8 @@
     def step(array):
         return after(array, *ready) if ready else array
 
-    first, second = filters[0, :2], filters[0, 2:]
+    first, activations = lax.optimization_barrier((filters[0, :2], activations))
+    second = filters[0, 2:]
     ups = [(i, i + 1) for i in range(size - 1)]
     above = lax.ppermute(activations[-1:], "img", ups)
     below = lax.ppermute(activations[:1], "img", [(j, i) for i, j in ups])
@@ -227,11 +230,11 @@
     keys = [(0, 0), (0, 4), (0, 2)] + [(j, 0) for j in others]
     over_core(keys)
     image = place(image, keys)
-    ready = [lower, *(slots[j, 4] for j in others), *taken_last, image]
+    ready = [lower, *(slots[j, 4] for j in others), *taken_last]
     ready += [slots[j, r + 1] for j, r in keys]
 
-    span = GROUP // CHUNKS
-    chunks = [lower[c * span : (c + 1) * span] for c in range(CHUNKS)]
+    cuts = (0, GROUP // 4, GROUP // 2, GROUP)
+    chunks = [lower[a:b] for a, b in zip(cuts, cuts[1:])]
     received = [exchange(step(chunks[0]))]
     over_ch(2)
     slots[0, 6] = swap(step(slots[0, 4]), "img", 2)
@@ -239,8 +242,10 @@
     keys = [(j, 4) for j in others]
     over_core(keys)
     image = place(image, keys)
-    raw = [filters[0]] + [jnp.concatenate(pair) for pair in zip(taken, taken_last)]
-    by_rank = by_member(step(jnp.stack(raw)), 0, parts)
+    raw = [filters[0]] + [
+        jnp.concatenate([step(a), step(b)]) for a, b in zip(taken, taken_last)
+    ]
+    by_rank = by_member(jnp.stack(raw), 0, parts)
     ready = [*received[0], slots[0, 6], *(slots[j, 2] for j in others), image, by_rank]
     ready += [slots[j, r + 1] for j, r in keys]
 
@@ -252,7 +257,7 @@
     over_core(keys)
     image = place(image, keys)
     image = place(image, [(j, r + 1) for j, r in keys])
-    ready = [*received[1], upper, *(slots[j, 6] for j in others), image]
+    ready = [*received[1], *(slots[j, 6] for j in others), image]
 
     received.append(exchange(step(chunks[2])))
     keys = [(j, 6) for j in others]
@@ -262,27 +267,23 @@
 
     scalars = jnp.stack([group * GROUP * rows, group]).astype(jnp.int32)
     bias = lax.dynamic_slice_in_dim(channel_bias, rank * split, split)[None]
-    own = lambda s: s[1]
+    which = [lambda s, j=j: s[1] ^ j for j in range(parts)]
     at_start = lambda s: (0, 0, 0, 0)
     every = [
-        (lambda s, j=j: s[1] ^ j, 0, upper, (GROUP, 3, shard, split), lambda s, j=j: (0, j, 0, 0))
+        (which[j], 0, upper, (GROUP, 3, shard, split), lambda s, j=j: (0, j, 0, 0), (0,))
         for j in range(parts)
     ]
-    foreign = [lambda s, j=j: s[1] ^ j for j in range(1, parts)]
 
     def pieces(chosen):
         return [
-            (foreign[j], c * span, array, array.shape, at_start)
+            (which[j], cuts[c], array, array.shape, at_start, (1, 2))
             for c in chosen
-            for j, array in enumerate(received[c])
+            for j, array in enumerate(received[c], 1)
         ]
 
-    acc = conv_call((1, 2), [(own, 0, lower, lower.shape, at_start)], scalars, image)
-
-    received.append(exchange(after(chunks[3], acc, *received[2])))
-    acc = conv_call((0,), every, scalars, image, acc)
-    acc = conv_call((1, 2), pieces((0, 1, 2)), scalars, image, acc)
-    out = conv_call((1, 2), pieces((3,)), scalars, image, acc, bias)
+    acc = conv_call([(which[0], 0, lower, lower.shape, at_start, (1, 2))], scalars, image)
+    acc = conv_call(every + pieces((0, 1)), scalars, image, acc)
+    out = conv_call(pieces((2,)), scalars, image, acc, bias)
     out = share(out).reshape(GROUP, rows, side, split)
     return jnp.moveaxis(out, 0, 2).reshape(rows, side, out_local)
 

time: 373 us -> 357 us (0.957)
  local copies, waits for them, and re-layouts: 63.5 us -> 54.1 us
  Pallas kernels: 90.8 us -> 85.3 us
  other arithmetic: 7.89 us -> 2.81 us
  waiting for transfers between devices: 131 us -> 136 us
    dynamic_update_slice x15, local copies, waits for them, and re-layouts: 39.8 us -> 33 us  [place(): lax.dynamic_update_slice(image, slots[j, r][None], (mine ^ j, start, 0, 0))]
    ppermute x21 -> x20, waiting for transfers between devices: 129 us -> 135 us  [swap(): return lax.ppermute(array, axis, [(i, i ^ bit) for i in range(size)])]
    pallas_call x4 -> x3, Pallas kernels: 80.2 us -> 74.6 us  [conv_call(): pl.pallas_call(body, grid_spec=pltpu.PrefetchScalarGridSpec(num_scalar_pr...]
    broadcast_in_dim x1, local copies, waits for them, and re-layouts: 8.85 us -> 3.28 us  [local(): jnp.zeros((chans, GROUP * rows + 3, width, depth), activations.dtype)]
    ppermute x21 -> x20, starting transfers between devices: 25.4 us -> 26.1 us  [swap(): return lax.ppermute(array, axis, [(i, i ^ bit) for i in range(size)])]
  transfers between devices with their start and end apart: 25 -> 24, of which waited for: 9 -> 6; matrix products, arithmetic and copies ran while one was open for 16% -> 12% of each run, Pallas kernels for 22% -> 20%
where the time goes in v7:
time: 357 us; the launch traced here: 356 us
  waiting for transfers between devices  136 us (38%)
  Pallas kernels  85.3 us (24%)
  local copies, waits for them, and re-layouts  54.1 us (15%)
  starting transfers between devices  41.2 us (12%)
  blocking collectives  36.4 us (10%)
    ppermute x20, waiting for transfers between devices, swap(): return lax.ppermute(array, axis, [(i, i ^ bit) for i in range(size)])  135 us
    pallas_call x3, Pallas kernels, conv_call(): pl.pallas_call(body, grid_spec=pltpu.PrefetchScalarGridSpec(num_scalar_pr...  74.6 us
    all_to_all x1, blocking collectives, share(): lax.all_to_all(taps, 'img', 0, 0, axis_index_groups=members, tiled=True)  36.4 us
    dynamic_update_slice x15, local copies, waits for them, and re-layouts, place(): lax.dynamic_update_slice(image, slots[j, r][None], (mine ^ j, start, 0, 0))  33 us
    ppermute x20, starting transfers between devices, swap(): return lax.ppermute(array, axis, [(i, i ^ bit) for i in range(size)])  26.1 us
    all_to_all x2, starting transfers between devices, share(): lax.all_to_all(taps, 'img', 0, 0, axis_index_groups=members, tiled=True)  10.8 us
    pallas_call x2, Pallas kernels, by_member(): pl.pallas_call(body, grid=(count, across), in_specs=[pl.BlockSpec((1, 1,...  10.7 us
    unnamed x30, local copies, waits for them, and re-layouts  7.17 us
  transfers between devices with their start and end apart: 24, of which 6 were waited for; matrix products, arithmetic and copies ran while one was open for 12% of the time, Pallas kernels for 20%

profile of v7, /device:TPU:0, one launch (start us, length us, event | category | flops | bytes accessed | tf_op | source)
XLA Modules:
  0.0 355.7 jit_solution(2199542662592009481)
XLA Ops:
  0.0 2.4 slice_bitcast_fusion
  2.4 1.0 fusion.2
  3.4 1.3 collective-permute-start
  4.7 3.0 collective-permute-start.1
  9.0 7.6 %collective-permute-start.2 = (bf16[13,56,1024]{2,1,0:T(8,128)(2,1)S(1)}, bf16[13,56,1024]{2,1,0:T(8,128)(2,1)}, u32[]{:S(2)}, u32[]{:S(2)}) collective-permute-start(bf16[13,56,1024]{2,1,0:T(8,128)(2,1)S(1)} %maximum_select_fusion.1), channel_id=1, source_target_pairs={{0,8},{2,10},{4,12},{6,14},{8,0},{10,2},{12,4},{14,6},{16,24},{18,... | collective-permute-start | bytes 4472840 | tf_op jit(solution)/shard_map/ppermute | solution.py:15
  16.5 1.5 collective-permute-start.4
  18.0 2.6 collective-permute-start.5
  20.6 5.3 %shard_map.37 = bf16[8,6,128,256]{3,2,1,0:T(8,128)(2,1)} custom-call(bf16[3,3,128,2048]{3,2,1,0:T(8,128)(2,1)} %taps.1), custom_call_target="tpu_custom_call" | custom-call | tf_op jit(solution)/shard_map/pallas_call | solution.py:156
  26.0 42.8 %collective-permute-done.5 = bf16[2,128,2048]{2,1,0:T(8,128)(2,1)S(1)} collective-permute-done((bf16[2,128,2048]{2,1,0:T(8,128)(2,1)}, bf16[2,128,2048]{2,1,0:T(8,128)(2,1)S(1)}, u32[]{:S(2)}, u32[]{:S(2)}) %collective-permute-start.5) | collective-permute-done | bytes 1048608 | tf_op jit(solution)/shard_map/ppermute | solution.py:15
  69.8 6.3 %all-to-all-start = ((bf16[8,6,128,256]{3,2,1,0:T(8,128)(2,1)}), bf16[8,6,128,256]{3,2,1,0:T(8,128)(2,1)S(1)}, u32[]{:S(2)}, u32[]{:S(2)}) async-start(bf16[8,6,128,256]{3,2,1,0:T(8,128)(2,1)} %shard_map.37), calls=%async_computation | async-start | bytes 6291456 | tf_op jit(solution)/shard_map/all_to_all | solution.py:178
  76.6 1.9 slice_bitcast_fusion.1
  78.5 3.3 broadcast_in_dim.52
  82.2 1.6 collective-permute-start.10
  84.3 1.6 bitcast_dynamic-update-slice_fusion.14
  85.8 1.6 bitcast_dynamic-update-slice_fusion.13
  87.4 1.6 bitcast_dynamic-update-slice_fusion.12
  89.8 1.6 bitcast_dynamic-update-slice_fusion.11
  91.4 1.6 bitcast_dynamic-update-slice_fusion.10
  92.9 29.2 %collective-permute-done.11 = bf16[1,128,2048]{2,1,0:T(8,128)(2,1)S(1)} collective-permute-done((bf16[1,128,2048]{2,1,0:T(8,128)(2,1)S(1)}, bf16[1,128,2048]{2,1,0:T(8,128)(2,1)S(1)}, u32[]{:S(2)}, u32[]{:S(2)}) %collective-permute-start.11) | collective-permute-done | bytes 524320 | tf_op jit(solution)/shard_map/ppermute | solution.py:15
  123.5 1.1 copy-done.8
  124.7 1.6 collective-permute-start.14
  126.2 1.6 collective-permute-start.13
  127.9 2.7 bitcast_dynamic-update-slice_fusion.9
  130.5 1.3 bitcast_dynamic-update-slice_fusion.8
  131.8 1.3 fusion.1
  133.1 3.4 collective-permute-start.15
  136.5 2.6 bitcast_dynamic-update-slice_fusion.7
  139.3 1.9 pad_maximum_fusion.taps
  141.2 5.3 %shard_map.38 = bf16[8,6,128,256]{3,2,1,0:T(8,128)(2,1)} custom-call(bf16[2,3,128,2048]{3,2,1,0:T(8,128)(2,1)} %pad_maximum_fusion.taps), custom_call_target="tpu_custom_call" | custom-call | tf_op jit(solution)/shard_map/pallas_call | solution.py:156
  146.5 24.6 %collective-permute-done.15.refs_7_ = bf16[2,6,128,256]{3,2,1,0:T(8,128)(2,1)} collective-permute-done((bf16[2,6,128,256]{3,2,1,0:T(8,128)(2,1)}, bf16[2,6,128,256]{3,2,1,0:T(8,128)(2,1)}, u32[]{:S(2)}, u32[]{:S(2)}) %collective-permute-start.15) | collective-permute-done | bytes 786464 | tf_op jit(solution)/shard_map/ppermute | solution.py:15
  171.2 4.5 %all-to-all-start.1 = ((bf16[8,6,128,256]{3,2,1,0:T(8,128)(2,1)}), bf16[8,6,128,256]{3,2,1,0:T(8,128)(2,1)}, u32[]{:S(2)}, u32[]{:S(2)}) async-start(bf16[8,6,128,256]{3,2,1,0:T(8,128)(2,1)} %shard_map.38), calls=%async_computation.1 | async-start | bytes 6291456 | tf_op jit(solution)/shard_map/all_to_all | solution.py:178
  176.8 2.7 bitcast_dynamic-update-slice_fusion.6
  179.5 2.6 bitcast_dynamic-update-slice_fusion.5
  182.1 2.7 bitcast_dynamic-update-slice_fusion.4
  184.8 2.7 bitcast_dynamic-update-slice_fusion.3
  187.5 2.7 bitcast_dynamic-update-slice_fusion.2
  190.2 37.1 %collective-permute-done.19.refs_8_ = bf16[2,6,128,256]{3,2,1,0:T(8,128)(2,1)S(1)} collective-permute-done((bf16[2,6,128,256]{3,2,1,0:T(8,128)(2,1)}, bf16[2,6,128,256]{3,2,1,0:T(8,128)(2,1)S(1)}, u32[]{:S(2)}, u32[]{:S(2)}) %collective-permute-start.19) | collective-permute-done | bytes 786464 | tf_op jit(solution)/shard_map/ppermute | solution.py:15
  228.2 1.3 slice.34
  229.5 3.3 collective-permute-start.21
  232.9 2.6 bitcast_dynamic-update-slice_fusion.1
  235.5 2.7 bitcast_dynamic-update-slice_fusion.refs_0_.refs_1_.refs_2_.refs_3_.refs_4_
  239.0 23.7 %shard_map.39.refs_9_ = f32[96,64,256]{2,1,0:T(8,128)S(1)} custom-call(s32[2]{0:T(128)S(1)} %pad_add_fusion.scalars_ref, bf16[2,99,64,1024]{3,2,1,0:T(8,128)(2,1)} %bitcast_dynamic-update-slice_fusion.refs_0_.refs_1_.refs_2_.refs_3_.refs_4_, bf16[2,99,64,1024]{3,2,1,0:T(8,128)(2,1)} %bitcast_dynamic-update-slice_fusion.refs_0_.refs_1_.refs_2_.refs_3_.refs_4_, ...), custom_call_target="tpu_custom_call" | custom-call | flops 1024 | bytes 1024 | tf_op jit(solution)/shard_map/pallas_call | solution.py:129
  262.6 2.6 copy-done
  265.3 1.1 copy-done.2
  266.4 36.5 %shard_map.40.refs_3_ = f32[96,64,256]{2,1,0:T(8,128)S(1)} custom-call(s32[2]{0:T(128)S(1)} %pad_add_fusion.scalars_ref, bf16[2,99,64,1024]{3,2,1,0:T(8,128)(2,1)} %bitcast_dynamic-update-slice_fusion.refs_0_.refs_1_.refs_2_.refs_3_.refs_4_, bf16[2,99,64,1024]{3,2,1,0:T(8,128)(2,1)} %bitcast_dynamic-update-slice_fusion.refs_0_.refs_1_.refs_2_.refs_3_.refs_4_, ...), custom_call_target="tpu_custom_call" | custom-call | flops 1024 | bytes 1024 | tf_op jit(solution)/shard_map/pallas_call | solution.py:129
  302.9 14.5 %shard_map.41 = bf16[96,56,256]{2,1,0:T(8,128)(2,1)S(1)} custom-call(s32[2]{0:T(128)S(1)} %pad_add_fusion.scalars_ref, bf16[2,99,64,1024]{3,2,1,0:T(8,128)(2,1)} %bitcast_dynamic-update-slice_fusion.refs_0_.refs_1_.refs_2_.refs_3_.refs_4_, bf16[2,99,64,1024]{3,2,1,0:T(8,128)(2,1)} %bitcast_dynamic-update-slice_fusion.refs_0_.refs_1_.refs_2_.refs_3_.refs_4_, ...), custom_call_target="tpu_custom_call" | custom-call | flops 1024 | bytes 1024 | tf_op jit(solution)/shard_map/pallas_call | solution.py:129
  317.4 36.4 %all_to_all.15 = bf16[96,56,256]{2,1,0:T(8,128)(2,1)S(1)} all-to-all(bf16[96,56,256]{2,1,0:T(8,128)(2,1)S(1)} %shard_map.41), channel_id=1, replica_groups={{0,2,4,6,8,10,12,14},{16,18,20,22,24,26,28,30},{1,3,5,7,9,11,13,15},{17..., dimensions={0} | all-to-all | bytes 5505024 | tf_op jit(solution)/shard_map/all_to_all | solution.py:178
  353.8 1.9 copy.5
  (66 shorter events, 8.8 us)
Async XLA Ops:
  0.0 8.7 %copy-start.4 = (bf16[12,56,1024]{2,1,0:T(8,128)(2,1)S(1)}, bf16[12,56,1024]{2,1,0:T(8,128)(2,1)}, u32[]{:S(2)}) copy-start(bf16[12,56,1024]{2,1,0:T(8,128)(2,1)} %param.3) | copy-start | bytes 4128772
  3.4 4.4 %collective-permute-start = (bf16[1,56,1024]{2,1,0:T(8,128)(2,1)S(1)}, bf16[1,56,1024]{2,1,0:T(8,128)(2,1)S(1)}, u32[]{:S(2)}, u32[]{:S(2)}) collective-permute-start(bf16[1,56,1024]{2,1,0:T(8,128)(2,1)S(1)} %get-tuple-element.48), channel_id=1, source_target_pairs={{2,0},{4,2},{6,4},{8,6},{10,8},{12,10},{14,12},{16,14},{18,16},{20... | collective-permute-start | bytes 344072 | tf_op jit(solution)/shard_map/ppermute | solution.py:192
  4.7 4.0 %collective-permute-start.1 = (bf16[1,56,1024]{2,1,0:T(8,128)(2,1)S(1)}, bf16[1,56,1024]{2,1,0:T(8,128)(2,1)S(1)}, u32[]{:S(2)}, u32[]{:S(2)}) collective-permute-start(bf16[1,56,1024]{2,1,0:T(8,128)(2,1)S(1)} %get-tuple-element.47), channel_id=1, source_target_pairs={{0,2},{2,4},{4,6},{6,8},{8,10},{10,12},{12,14},{14,16},{16,18},{18... | collective-permute-start | bytes 344072 | tf_op jit(solution)/shard_map/ppermute | solution.py:191
  8.9 17.0 %copy-start.6 = (bf16[13,56,1024]{2,1,0:T(8,128)(2,1)}, bf16[13,56,1024]{2,1,0:T(8,128)(2,1)S(1)}, u32[]{:S(2)}) copy-start(bf16[13,56,1024]{2,1,0:T(8,128)(2,1)S(1)} %maximum_select_fusion.1) | copy-start | bytes 4472836
  9.0 60.8 %collective-permute-start.2 = (bf16[13,56,1024]{2,1,0:T(8,128)(2,1)S(1)}, bf16[13,56,1024]{2,1,0:T(8,128)(2,1)}, u32[]{:S(2)}, u32[]{:S(2)}) collective-permute-start(bf16[13,56,1024]{2,1,0:T(8,128)(2,1)S(1)} %maximum_select_fusion.1), channel_id=1, source_target_pairs={{0,8},{2,10},{4,12},{6,14},{8,0},{10,2},{12,4},{14,6},{16,24},{18,... | collective-permute-start | bytes 4472840 | tf_op jit(solution)/shard_map/ppermute | solution.py:15
  16.5 53.2 %collective-permute-start.3 = (bf16[13,56,1024]{2,1,0:T(8,128)(2,1)S(1)}, bf16[13,56,1024]{2,1,0:T(8,128)(2,1)}, u32[]{:S(2)}, u32[]{:S(2)}) collective-permute-start(bf16[13,56,1024]{2,1,0:T(8,128)(2,1)S(1)} %maximum_select_fusion.1), channel_id=1, source_target_pairs={{0,4},{2,6},{4,0},{6,2},{8,12},{10,14},{12,8},{14,10},{16,20},{18,... | collective-permute-start | bytes 4472840 | tf_op jit(solution)/shard_map/ppermute | solution.py:15
  16.5 53.2 %collective-permute-start.4 = (bf16[13,56,1024]{2,1,0:T(8,128)(2,1)S(1)}, bf16[13,56,1024]{2,1,0:T(8,128)(2,1)}, u32[]{:S(2)}, u32[]{:S(2)}) collective-permute-start(bf16[13,56,1024]{2,1,0:T(8,128)(2,1)S(1)} %maximum_select_fusion.1), channel_id=1, source_target_pairs={{0,1},{1,0},{2,3},{3,2},{4,5},{5,4},{6,7},{7,6},{8,9},{9,8},{10,11... | collective-permute-start | bytes 4472840 | tf_op jit(solution)/shard_map/ppermute | solution.py:15
  18.0 50.8 %collective-permute-start.5 = (bf16[2,128,2048]{2,1,0:T(8,128)(2,1)}, bf16[2,128,2048]{2,1,0:T(8,128)(2,1)S(1)}, u32[]{:S(2)}, u32[]{:S(2)}) collective-permute-start(bf16[2,128,2048]{2,1,0:T(8,128)(2,1)} %slice_bitcast_fusion), channel_id=1, source_target_pairs={{0,16},{2,18},{4,20},{6,22},{8,24},{10,26},{12,28},{14,30},{16,0},... | collective-permute-start | bytes 3145736 | tf_op jit(solution)/shard_map/ppermute | solution.py:15
  68.8 1.0 copy-start.10
  69.8 54.8 %all-to-all-start = ((bf16[8,6,128,256]{3,2,1,0:T(8,128)(2,1)}), bf16[8,6,128,256]{3,2,1,0:T(8,128)(2,1)S(1)}, u32[]{:S(2)}, u32[]{:S(2)}) async-start(bf16[8,6,128,256]{3,2,1,0:T(8,128)(2,1)} %shard_map.37), calls=%async_computation | async-start | bytes 6291456 | tf_op jit(solution)/shard_map/all_to_all | solution.py:178
  76.1 12.9 %collective-permute-start.6 = (bf16[13,56,1024]{2,1,0:T(8,128)(2,1)}, bf16[13,56,1024]{2,1,0:T(8,128)(2,1)}, u32[]{:S(2)}, u32[]{:S(2)}) collective-permute-start(bf16[13,56,1024]{2,1,0:T(8,128)(2,1)} %copy-done.6), channel_id=1, source_target_pairs={{0,2},{2,0},{4,6},{6,4},{8,10},{10,8},{12,14},{14,12},{16,18},{18,... | collective-permute-start | bytes 4472840 | tf_op jit(solution)/shard_map/ppermute | solution.py:15
  76.6 14.8 %collective-permute-start.7 = (bf16[13,56,1024]{2,1,0:T(8,128)(2,1)}, bf16[13,56,1024]{2,1,0:T(8,128)(2,1)}, u32[]{:S(2)}, u32[]{:S(2)}) collective-permute-start(bf16[13,56,1024]{2,1,0:T(8,128)(2,1)} %collective-permute-done.2), channel_id=1, source_target_pairs={{0,2},{2,0},{4,6},{6,4},{8,10},{10,8},{12,14},{14,12},{16,18},{18,... | collective-permute-start | bytes 4472840 | tf_op jit(solution)/shard_map/ppermute | solution.py:15
  78.5 3.3 copy-start.5
  82.2 42.4 %collective-permute-start.10 = (bf16[13,56,1024]{2,1,0:T(8,128)(2,1)}, bf16[13,56,1024]{2,1,0:T(8,128)(2,1)}, u32[]{:S(2)}, u32[]{:S(2)}) collective-permute-start(bf16[13,56,1024]{2,1,0:T(8,128)(2,1)} %collective-permute-done.2), channel_id=1, source_target_pairs={{0,1},{1,0},{2,3},{3,2},{4,5},{5,4},{6,7},{7,6},{8,9},{9,8},{10,11... | collective-permute-start | bytes 4472840 | tf_op jit(solution)/shard_map/ppermute | solution.py:15
  83.7 38.4 %collective-permute-start.8 = (bf16[13,56,1024]{2,1,0:T(8,128)(2,1)}, bf16[13,56,1024]{2,1,0:T(8,128)(2,1)S(1)}, u32[]{:S(2)}, u32[]{:S(2)}) collective-permute-start(bf16[13,56,1024]{2,1,0:T(8,128)(2,1)} %collective-permute-done.3), channel_id=1, source_target_pairs={{0,2},{2,0},{4,6},{6,4},{8,10},{10,8},{12,14},{14,12},{16,18},{18,... | collective-permute-start | bytes 4472840 | tf_op jit(solution)/shard_map/ppermute | solution.py:15
  84.0 38.2 %collective-permute-start.9 = (bf16[13,56,1024]{2,1,0:T(8,128)(2,1)}, bf16[13,56,1024]{2,1,0:T(8,128)(2,1)S(1)}, u32[]{:S(2)}, u32[]{:S(2)}) collective-permute-start(bf16[13,56,1024]{2,1,0:T(8,128)(2,1)} %collective-permute-done.4), channel_id=1, source_target_pairs={{0,2},{2,0},{4,6},{6,4},{8,10},{10,8},{12,14},{14,12},{16,18},{18,... | collective-permute-start | bytes 4472840 | tf_op jit(solution)/shard_map/ppermute | solution.py:15
  85.8 3.2 copy-start.12
  89.0 33.1 %collective-permute-start.11 = (bf16[1,128,2048]{2,1,0:T(8,128)(2,1)S(1)}, bf16[1,128,2048]{2,1,0:T(8,128)(2,1)S(1)}, u32[]{:S(2)}, u32[]{:S(2)}) collective-permute-start(bf16[1,128,2048]{2,1,0:T(8,128)(2,1)S(1)} %copy-done.12), channel_id=1, source_target_pairs={{0,16},{2,18},{4,20},{6,22},{8,24},{10,26},{12,28},{14,30},{16,0},... | collective-permute-start | bytes 1572872 | tf_op jit(solution)/shard_map/ppermute | solution.py:15
  92.9 29.2 %copy-start.3 = (bf16[2,99,64,1024]{3,2,1,0:T(8,128)(2,1)}, bf16[2,99,64,1024]{3,2,1,0:T(8,128)(2,1)S(1)}, u32[]{:S(2)}) copy-start(bf16[2,99,64,1024]{3,2,1,0:T(8,128)(2,1)S(1)} %bitcast_dynamic-update-slice_fusion.10) | copy-start | bytes 77856768
  122.2 0.8 copy-start.13
  122.2 1.3 copy-start.7
  123.5 1.1 copy-start.8
  124.6 5.9 %copy-start.9 = (bf16[13,56,1024]{2,1,0:T(8,128)(2,1)S(1)}, bf16[13,56,1024]{2,1,0:T(8,128)(2,1)}, u32[]{:S(2)}) copy-start(bf16[13,56,1024]{2,1,0:T(8,128)(2,1)} %copy-done.8) | copy-start | bytes 4472836
  124.6 46.5 %collective-permute-start.12 = (bf16[13,56,1024]{2,1,0:T(8,128)(2,1)}, bf16[13,56,1024]{2,1,0:T(8,128)(2,1)}, u32[]{:S(2)}, u32[]{:S(2)}) collective-permute-start(bf16[13,56,1024]{2,1,0:T(8,128)(2,1)} %collective-permute-done.10), channel_id=1, source_target_pairs={{0,2},{2,0},{4,6},{6,4},{8,10},{10,8},{12,14},{14,12},{16,18},{18,... | collective-permute-start | bytes 4472840 | tf_op jit(solution)/shard_map/ppermute | solution.py:15
  124.7 46.5 %collective-permute-start.14 = (bf16[13,56,1024]{2,1,0:T(8,128)(2,1)}, bf16[13,56,1024]{2,1,0:T(8,128)(2,1)}, u32[]{:S(2)}, u32[]{:S(2)}) collective-permute-start(bf16[13,56,1024]{2,1,0:T(8,128)(2,1)} %collective-permute-done.3), channel_id=1, source_target_pairs={{0,1},{1,0},{2,3},{3,2},{4,5},{5,4},{6,7},{7,6},{8,9},{9,8},{10,11... | collective-permute-start | bytes 4472840 | tf_op jit(solution)/shard_map/ppermute | solution.py:15
  126.2 44.9 %collective-permute-start.13 = (bf16[13,56,1024]{2,1,0:T(8,128)(2,1)}, bf16[13,56,1024]{2,1,0:T(8,128)(2,1)}, u32[]{:S(2)}, u32[]{:S(2)}) collective-permute-start(bf16[13,56,1024]{2,1,0:T(8,128)(2,1)} %collective-permute-done.2), channel_id=1, source_target_pairs={{0,4},{2,6},{4,0},{6,2},{8,12},{10,14},{12,8},{14,10},{16,20},{18,... | collective-permute-start | bytes 4472840 | tf_op jit(solution)/shard_map/ppermute | solution.py:15
  131.8 7.3 %copy-start.11 = (bf16[2,128,2048]{2,1,0:T(8,128)(2,1)S(1)}, bf16[2,128,2048]{2,1,0:T(8,128)(2,1)}, u32[]{:S(2)}) copy-start(bf16[2,128,2048]{2,1,0:T(8,128)(2,1)} %copy-done.10) | copy-start | bytes 3145732
  131.8 7.3 %copy-start.14 = (bf16[1,128,2048]{2,1,0:T(8,128)(2,1)S(1)}, bf16[1,128,2048]{2,1,0:T(8,128)(2,1)}, u32[]{:S(2)}) copy-start(bf16[1,128,2048]{2,1,0:T(8,128)(2,1)} %copy-done.13) | copy-start | bytes 1572868
  133.1 6.2 %slice-start = ((bf16[3,3,128,2048]{3,2,1,0:T(8,128)(2,1)}), bf16[1,3,128,2048]{3,2,1,0:T(8,128)(2,1)S(1)}, s32[]{:S(2)}) async-start(bf16[3,3,128,2048]{3,2,1,0:T(8,128)(2,1)} %taps.1), calls=%async_computation.3 | async-start | bytes 3145728 | tf_op jit(solution)/shard_map/slice | solution.py:245
  133.1 38.1 %collective-permute-start.15 = (bf16[2,6,128,256]{3,2,1,0:T(8,128)(2,1)}, bf16[2,6,128,256]{3,2,1,0:T(8,128)(2,1)}, u32[]{:S(2)}, u32[]{:S(2)}) collective-permute-start(bf16[2,6,128,256]{3,2,1,0:T(8,128)(2,1)} %get-tuple-element.36), channel_id=1, source_target_pairs={{0,16},{2,18},{4,20},{6,22},{8,24},{10,26},{12,28},{14,30},{16,0},... | collective-permute-start | bytes 2359304 | tf_op jit(solution)/shard_map/ppermute | solution.py:15
  171.2 94.1 %all-to-all-start.1 = ((bf16[8,6,128,256]{3,2,1,0:T(8,128)(2,1)}), bf16[8,6,128,256]{3,2,1,0:T(8,128)(2,1)}, u32[]{:S(2)}, u32[]{:S(2)}) async-start(bf16[8,6,128,256]{3,2,1,0:T(8,128)(2,1)} %shard_map.38), calls=%async_computation.1 | async-start | bytes 6291456 | tf_op jit(solution)/shard_map/all_to_all | solution.py:178
  175.6 9.2 %collective-permute-start.16 = (bf16[13,56,1024]{2,1,0:T(8,128)(2,1)}, bf16[13,56,1024]{2,1,0:T(8,128)(2,1)}, u32[]{:S(2)}, u32[]{:S(2)}) collective-permute-start(bf16[13,56,1024]{2,1,0:T(8,128)(2,1)} %collective-permute-done.13), channel_id=1, source_target_pairs={{0,2},{2,0},{4,6},{6,4},{8,10},{10,8},{12,14},{14,12},{16,18},{18,... | collective-permute-start | bytes 4472840 | tf_op jit(solution)/shard_map/ppermute | solution.py:15
  176.0 11.5 %collective-permute-start.17 = (bf16[13,56,1024]{2,1,0:T(8,128)(2,1)}, bf16[13,56,1024]{2,1,0:T(8,128)(2,1)}, u32[]{:S(2)}, u32[]{:S(2)}) collective-permute-start(bf16[13,56,1024]{2,1,0:T(8,128)(2,1)} %collective-permute-done.14), channel_id=1, source_target_pairs={{0,2},{2,0},{4,6},{6,4},{8,10},{10,8},{12,14},{14,12},{16,18},{18,... | collective-permute-start | bytes 4472840 | tf_op jit(solution)/shard_map/ppermute | solution.py:15
  176.2 52.0 %collective-permute-start.18 = (bf16[13,56,1024]{2,1,0:T(8,128)(2,1)}, bf16[13,56,1024]{2,1,0:T(8,128)(2,1)}, u32[]{:S(2)}, u32[]{:S(2)}) collective-permute-start(bf16[13,56,1024]{2,1,0:T(8,128)(2,1)} %collective-permute-done.13), channel_id=1, source_target_pairs={{0,1},{1,0},{2,3},{3,2},{4,5},{5,4},{6,7},{7,6},{8,9},{9,8},{10,11... | collective-permute-start | bytes 4472840 | tf_op jit(solution)/shard_map/ppermute | solution.py:15
  176.8 50.5 %collective-permute-start.19 = (bf16[2,6,128,256]{3,2,1,0:T(8,128)(2,1)}, bf16[2,6,128,256]{3,2,1,0:T(8,128)(2,1)S(1)}, u32[]{:S(2)}, u32[]{:S(2)}) collective-permute-start(bf16[2,6,128,256]{3,2,1,0:T(8,128)(2,1)} %get-tuple-element.41), channel_id=1, source_target_pairs={{0,16},{2,18},{4,20},{6,22},{8,24},{10,26},{12,28},{14,30},{16,0},... | collective-permute-start | bytes 2359304 | tf_op jit(solution)/shard_map/ppermute | solution.py:15
  227.3 0.9 copy-start.1
  228.2 7.3 %collective-permute-start.20 = (bf16[13,56,1024]{2,1,0:T(8,128)(2,1)}, bf16[13,56,1024]{2,1,0:T(8,128)(2,1)}, u32[]{:S(2)}, u32[]{:S(2)}) collective-permute-start(bf16[13,56,1024]{2,1,0:T(8,128)(2,1)} %collective-permute-done.18), channel_id=1, source_target_pairs={{0,2},{2,0},{4,6},{6,4},{8,10},{10,8},{12,14},{14,12},{16,18},{18,... | collective-permute-start | bytes 4472840 | tf_op jit(solution)/shard_map/ppermute | solution.py:15
  229.5 73.4 %collective-permute-start.21 = (bf16[4,6,128,256]{3,2,1,0:T(8,128)(2,1)}, bf16[4,6,128,256]{3,2,1,0:T(8,128)(2,1)}, u32[]{:S(2)}, u32[]{:S(2)}) collective-permute-start(bf16[4,6,128,256]{3,2,1,0:T(8,128)(2,1)} %slice.34), channel_id=1, source_target_pairs={{0,16},{2,18},{4,20},{6,22},{8,24},{10,26},{12,28},{14,30},{16,0},... | collective-permute-start | bytes 4718600 | tf_op jit(solution)/shard_map/ppermute | solution.py:15
  262.6 2.7 copy-start
  265.3 1.1 copy-start.2

commit v8 on v7

--- a/solution.py
+++ b/solution.py
@@ -185,8 +185,10 @@
     def step(array):
         return after(array, *ready) if ready else array
 
-    first, activations = lax.optimization_barrier((filters[0, :2], activations))
-    second = filters[0, 2:]
+    first, activations = lax.optimization_barrier((filters[0, :1], activations))
+    taken_first = exchange(first)
+    taken = exchange(after(filters[0, 1:], *taken_first))
+
     ups = [(i, i + 1) for i in range(size - 1)]
     above = lax.ppermute(activations[-1:], "img", ups)
     below = lax.ppermute(activations[:1], "img", [(j, i) for i, j in ups])
@@ -217,73 +219,58 @@
 
     others = range(1, chans)
 
-    taken = exchange(first)
-    by_rank = by_member(filters, 1, 2)
+    by_rank = by_member(filters, 2, 1)
+    own_mid = share(by_member(filters, 1, 1))
     over_ch(0)
     slots[0, 4] = swap(piece, "img", 4)
     slots[0, 2] = swap(piece, "img", 2)
-    ready = [*taken, slots[0, 4], slots[0, 2], *(slots[j, 0] for j in others), by_rank]
-
-    lower = share(step(by_rank))
+    ready = [*taken, own_mid, slots[0, 4], slots[0, 2], *(slots[j, 0] for j in others), by_rank]
+
+    taken_mid = exchange(step(own_mid))
+    own_low = share(step(by_rank))
     over_ch(4)
-    taken_last = exchange(step(second))
+    over_ch(2)
+    slots[0, 6] = swap(step(slots[0, 4]), "img", 2)
     keys = [(0, 0), (0, 4), (0, 2)] + [(j, 0) for j in others]
     over_core(keys)
     image = place(image, keys)
-    ready = [lower, *(slots[j, 4] for j in others), *taken_last]
-    ready += [slots[j, r + 1] for j, r in keys]
-
-    cuts = (0, GROUP // 4, GROUP // 2, GROUP)
-    chunks = [lower[a:b] for a, b in zip(cuts, cuts[1:])]
-    received = [exchange(step(chunks[0]))]
-    over_ch(2)
-    slots[0, 6] = swap(step(slots[0, 4]), "img", 2)
-    image = place(image, [(j, r + 1) for j, r in keys])
-    keys = [(j, 4) for j in others]
-    over_core(keys)
-    image = place(image, keys)
     raw = [filters[0]] + [
-        jnp.concatenate([step(a), step(b)]) for a, b in zip(taken, taken_last)
+        jnp.concatenate([step(a), step(b)]) for a, b in zip(taken_first, taken)
     ]
     by_rank = by_member(jnp.stack(raw), 0, parts)
-    ready = [*received[0], slots[0, 6], *(slots[j, 2] for j in others), image, by_rank]
+    ready = [*taken_mid, own_low, slots[0, 6], by_rank, image]
+    ready += [slots[j, r] for j in others for r in (4, 2)]
     ready += [slots[j, r + 1] for j, r in keys]
 
-    received.append(exchange(step(chunks[1])))
+    taken_low = exchange(step(own_low))
     over_ch(6)
     upper = share(step(by_rank))
     image = place(image, [(j, r + 1) for j, r in keys])
-    keys = [(0, 6)] + [(j, 2) for j in others]
+    keys = [(0, 6)] + [(j, r) for j in others for r in (4, 2)]
     over_core(keys)
-    image = place(image, keys)
-    image = place(image, [(j, r + 1) for j, r in keys])
-    ready = [*received[1], *(slots[j, 6] for j in others), image]
-
-    received.append(exchange(step(chunks[2])))
+    image = place(image, keys + [(j, r + 1) for j, r in keys])
     keys = [(j, 6) for j in others]
+    ready = []
     over_core(keys)
-    image = place(image, keys)
-    image = place(image, [(j, r + 1) for j, r in keys])
+    image = place(image, keys + [(j, r + 1) for j, r in keys])
 
     scalars = jnp.stack([group * GROUP * rows, group]).astype(jnp.int32)
     bias = lax.dynamic_slice_in_dim(channel_bias, rank * split, split)[None]
     which = [lambda s, j=j: s[1] ^ j for j in range(parts)]
-    at_start = lambda s: (0, 0, 0, 0)
+
+    def pieces(arrays, vertical):
+        return [
+            (which[j], 0, array, array.shape, lambda s: (0, 0, 0, 0), (vertical,))
+            for j, array in arrays
+        ]
+
     every = [
         (which[j], 0, upper, (GROUP, 3, shard, split), lambda s, j=j: (0, j, 0, 0), (0,))
         for j in range(parts)
     ]
-
-    def pieces(chosen):
-        return [
-            (which[j], cuts[c], array, array.shape, at_start, (1, 2))
-            for c in chosen
-            for j, array in enumerate(received[c], 1)
-        ]
-
-    acc = conv_call([(which[0], 0, lower, lower.shape, at_start, (1, 2))], scalars, image)
-    acc = conv_call(every + pieces((0, 1)), scalars, image, acc)
-    out = conv_call(pieces((2,)), scalars, image, acc, bias)
+    early = pieces([(0, own_mid), *enumerate(taken_mid, 1)], 1) + pieces([(0, own_low)], 2)
+    acc = conv_call(early, scalars, image)
+    out = conv_call(every + pieces(enumerate(taken_low, 1), 2), scalars, image, acc, bias)
     out = share(out).reshape(GROUP, rows, side, split)
     return jnp.moveaxis(out, 0, 2).reshape(rows, side, out_local)
 

time: 357 us -> 376 us (1.053)
  starting transfers between devices: 41.2 us -> 58.7 us
  Pallas kernels: 85.3 us -> 81.5 us
    ppermute x20 -> x19, starting transfers between devices: 26.1 us -> 39.9 us  [swap(): return lax.ppermute(array, axis, [(i, i ^ bit) for i in range(size)])]
    broadcast_in_dim x1, local copies, waits for them, and re-layouts: 3.28 us -> 8.85 us  [local(): jnp.zeros((chans, GROUP * rows + 3, width, depth), activations.dtype)]
    pallas_call x3 -> x2, Pallas kernels: 74.6 us -> 69.4 us  [conv_call(): pl.pallas_call(body, grid_spec=pltpu.PrefetchScalarGridSpec(num_scalar_pr...]
    all_to_all x2 -> x3, starting transfers between devices: 10.8 us -> 14.5 us  [share(): lax.all_to_all(taps, 'img', 0, 0, axis_index_groups=members, tiled=True)]
    unnamed x30 -> x24, local copies, waits for them, and re-layouts: 7.17 us -> 9.15 us
    pallas_call x2 -> x3, Pallas kernels: 10.7 us -> 12 us  [by_member(): pl.pallas_call(body, grid=(count, across), in_specs=[pl.BlockSpec((1, 1,...]
    ppermute x20 -> x19, waiting for transfers between devices: 135 us -> 134 us  [swap(): return lax.ppermute(array, axis, [(i, i ^ bit) for i in range(size)])]
  transfers between devices with their start and end apart: 24 -> 24, of which waited for: 6 -> 6; matrix products, arithmetic and copies ran while one was open for 12% -> 14% of each run, Pallas kernels for 20% -> 11%
where the time goes in v8:
time: 376 us; the launch traced here: 375 us
  waiting for transfers between devices  134 us (36%)
  Pallas kernels  81.5 us (22%)
  starting transfers between devices  58.7 us (16%)
  local copies, waits for them, and re-layouts  56.5 us (15%)
  blocking collectives  37.6 us (10%)
  other arithmetic  6.42 us (2%)
    ppermute x19, waiting for transfers between devices, swap(): return lax.ppermute(array, axis, [(i, i ^ bit) for i in range(size)])  134 us
    pallas_call x2, Pallas kernels, conv_call(): pl.pallas_call(body, grid_spec=pltpu.PrefetchScalarGridSpec(num_scalar_pr...  69.4 us
    ppermute x19, starting transfers between devices, swap(): return lax.ppermute(array, axis, [(i, i ^ bit) for i in range(size)])  39.9 us
    all_to_all x1, blocking collectives, share(): lax.all_to_all(taps, 'img', 0, 0, axis_index_groups=members, tiled=True)  37.6 us
    dynamic_update_slice x15, local copies, waits for them, and re-layouts, place(): lax.dynamic_update_slice(image, slots[j, r][None], (mine ^ j, start, 0, 0))  31.7 us
    all_to_all x3, starting transfers between devices, share(): lax.all_to_all(taps, 'img', 0, 0, axis_index_groups=members, tiled=True)  14.5 us
    pallas_call x3, Pallas kernels, by_member(): pl.pallas_call(body, grid=(count, across), in_specs=[pl.BlockSpec((1, 1,...  12 us
    unnamed x24, local copies, waits for them, and re-layouts  9.15 us
  transfers between devices with their start and end apart: 24, of which 6 were waited for; matrix products, arithmetic and copies ran while one was open for 14% of the time, Pallas kernels for 11%

profile of v8, /device:TPU:0, one launch (start us, length us, event | category | flops | bytes accessed | tf_op | source)
XLA Modules:
  0.0 375.3 jit_solution(6783298612294285716)
XLA Ops:
  0.0 3.4 shard_map.37
  3.4 5.4 %all-to-all-start = ((bf16[8,3,128,256]{3,2,1,0:T(8,128)(2,1)}), bf16[8,3,128,256]{3,2,1,0:T(8,128)(2,1)S(1)}, u32[]{:S(2)}, u32[]{:S(2)}) async-start(bf16[8,3,128,256]{3,2,1,0:T(8,128)(2,1)} %shard_map.37), calls=%async_computation | async-start | bytes 3145728 | tf_op jit(solution)/shard_map/all_to_all | solution.py:178
  8.8 1.9 slice_bitcast_fusion.1
  10.7 1.3 collective-permute-start
  12.0 3.0 collective-permute-start.1
  15.0 3.7 collective-permute-start.5
  18.8 1.3 maximum_select_fusion.1
  20.1 23.8 %collective-permute-start.2 = (bf16[13,56,1024]{2,1,0:T(8,128)(2,1)}, bf16[13,56,1024]{2,1,0:T(8,128)(2,1)}, u32[]{:S(2)}, u32[]{:S(2)}) collective-permute-start(bf16[13,56,1024]{2,1,0:T(8,128)(2,1)} %maximum_select_fusion.1), channel_id=1, source_target_pairs={{0,8},{2,10},{4,12},{6,14},{8,0},{10,2},{12,4},{14,6},{16,24},{18,... | collective-permute-start | bytes 4472840 | tf_op jit(solution)/shard_map/ppermute | solution.py:15
  43.9 1.5 collective-permute-start.4
  45.4 2.3 slice_bitcast_fusion
  48.6 3.4 shard_map.38
  52.0 41.8 %collective-permute-done.6 = bf16[2,128,2048]{2,1,0:T(8,128)(2,1)} collective-permute-done((bf16[2,128,2048]{2,1,0:T(8,128)(2,1)}, bf16[2,128,2048]{2,1,0:T(8,128)(2,1)}, u32[]{:S(2)}, u32[]{:S(2)}) %collective-permute-start.6) | collective-permute-done | bytes 1048608 | tf_op jit(solution)/shard_map/ppermute | solution.py:15
  93.8 2.0 collective-permute-done.2
  96.0 1.6 collective-permute-start.12
  98.1 5.3 %all-to-all-start.1 = ((bf16[8,3,128,256]{3,2,1,0:T(8,128)(2,1)}), bf16[8,3,128,256]{3,2,1,0:T(8,128)(2,1)S(1)}, u32[]{:S(2)}, u32[]{:S(2)}) async-start(bf16[8,3,128,256]{3,2,1,0:T(8,128)(2,1)} %shard_map.38), calls=%async_computation.1 | async-start | bytes 3145728 | tf_op jit(solution)/shard_map/all_to_all | solution.py:178
  103.8 36.4 %collective-permute-done.11 = bf16[13,56,1024]{2,1,0:T(8,128)(2,1)} collective-permute-done((bf16[13,56,1024]{2,1,0:T(8,128)(2,1)}, bf16[13,56,1024]{2,1,0:T(8,128)(2,1)}, u32[]{:S(2)}, u32[]{:S(2)}) %collective-permute-start.11) | collective-permute-done | bytes 1490976 | tf_op jit(solution)/shard_map/ppermute | solution.py:15
  140.3 1.3 collective-permute-start.14
  141.6 20.9 %collective-permute-done.13 = bf16[13,56,1024]{2,1,0:T(8,128)(2,1)} collective-permute-done((bf16[13,56,1024]{2,1,0:T(8,128)(2,1)}, bf16[13,56,1024]{2,1,0:T(8,128)(2,1)}, u32[]{:S(2)}, u32[]{:S(2)}) %collective-permute-start.13) | collective-permute-done | bytes 1490976 | tf_op jit(solution)/shard_map/ppermute | solution.py:15
  162.6 8.8 %broadcast_in_dim.52 = bf16[2,99,64,1024]{3,2,1,0:T(8,128)(2,1)} broadcast(bf16[]{:T(256)} %constant.48.clone.1), dimensions={} | broadcast | bytes 25952258 | tf_op jit(solution)/shard_map/broadcast_in_dim | solution.py:202
  171.4 1.6 fusion
  173.0 2.8 bitcast_dynamic-update-slice_fusion.14
  175.8 2.6 bitcast_dynamic-update-slice_fusion.13
  179.7 1.5 maximum_bitcast_fusion
  181.2 1.9 pad_maximum_fusion.taps
  183.1 5.3 %shard_map.39 = bf16[8,6,128,256]{3,2,1,0:T(8,128)(2,1)} custom-call(bf16[2,3,128,2048]{3,2,1,0:T(8,128)(2,1)} %pad_maximum_fusion.taps), custom_call_target="tpu_custom_call" | custom-call | tf_op jit(solution)/shard_map/pallas_call | solution.py:156
  188.4 19.5 %collective-permute-done.14.refs_4_ = bf16[8,3,128,256]{3,2,1,0:T(8,128)(2,1)} collective-permute-done((bf16[8,3,128,256]{3,2,1,0:T(8,128)(2,1)S(1)}, bf16[8,3,128,256]{3,2,1,0:T(8,128)(2,1)}, u32[]{:S(2)}, u32[]{:S(2)}) %collective-permute-start.14) | collective-permute-done | bytes 1572896 | tf_op jit(solution)/shard_map/ppermute | solution.py:15
  209.1 3.8 %all-to-all-start.2 = ((bf16[8,6,128,256]{3,2,1,0:T(8,128)(2,1)}), bf16[8,6,128,256]{3,2,1,0:T(8,128)(2,1)S(1)}, u32[]{:S(2)}, u32[]{:S(2)}) async-start(bf16[8,6,128,256]{3,2,1,0:T(8,128)(2,1)} %shard_map.39), calls=%async_computation.2 | async-start | bytes 6291456 | tf_op jit(solution)/shard_map/all_to_all | solution.py:178
  213.5 1.5 collective-permute-start.18
  215.5 3.5 collective-permute-start.20
  219.0 2.6 bitcast_dynamic-update-slice_fusion.11
  221.6 2.6 bitcast_dynamic-update-slice_fusion.10
  224.2 2.7 bitcast_dynamic-update-slice_fusion.9
  226.9 2.6 bitcast_dynamic-update-slice_fusion.8
  229.5 2.7 bitcast_dynamic-update-slice_fusion.7
  232.2 2.6 bitcast_dynamic-update-slice_fusion.6
  234.8 13.6 %collective-permute-done.18 = bf16[13,56,1024]{2,1,0:T(8,128)(2,1)S(1)} collective-permute-done((bf16[13,56,1024]{2,1,0:T(8,128)(2,1)}, bf16[13,56,1024]{2,1,0:T(8,128)(2,1)S(1)}, u32[]{:S(2)}, u32[]{:S(2)}) %collective-permute-start.18) | collective-permute-done | bytes 1490976 | tf_op jit(solution)/shard_map/ppermute | solution.py:15
  248.4 2.7 bitcast_dynamic-update-slice_fusion.5
  251.0 1.4 bitcast_dynamic-update-slice_fusion.4
  252.4 1.3 bitcast_dynamic-update-slice_fusion.3
  253.7 1.3 bitcast_dynamic-update-slice_fusion.2
  256.3 1.3 bitcast_dynamic-update-slice_fusion.refs_0_.refs_1_.refs_2_.refs_3_.refs_4_
  258.3 34.5 %shard_map.40.refs_8_ = f32[96,64,256]{2,1,0:T(8,128)S(1)} custom-call(s32[2]{0:T(128)S(1)} %pad_add_fusion.scalars_ref, bf16[2,99,64,1024]{3,2,1,0:T(8,128)(2,1)} %bitcast_dynamic-update-slice_fusion.refs_0_.refs_1_.refs_2_.refs_3_.refs_4_, bf16[2,99,64,1024]{3,2,1,0:T(8,128)(2,1)} %bitcast_dynamic-update-slice_fusion.refs_0_.refs_1_.refs_2_.refs_3_.refs_4_, ...), custom_call_target="tpu_custom_call" | custom-call | flops 1024 | bytes 1024 | tf_op jit(solution)/shard_map/pallas_call | solution.py:129
  292.8 2.6 copy-done
  296.6 2.8 copy-done.1
  299.4 1.4 copy-done.7
  300.8 35.0 %shard_map.41 = bf16[96,56,256]{2,1,0:T(8,128)(2,1)S(1)} custom-call(s32[2]{0:T(128)S(1)} %pad_add_fusion.scalars_ref, bf16[2,99,64,1024]{3,2,1,0:T(8,128)(2,1)} %bitcast_dynamic-update-slice_fusion.refs_0_.refs_1_.refs_2_.refs_3_.refs_4_, bf16[2,99,64,1024]{3,2,1,0:T(8,128)(2,1)} %bitcast_dynamic-update-slice_fusion.refs_0_.refs_1_.refs_2_.refs_3_.refs_4_, ...), custom_call_target="tpu_custom_call" | custom-call | flops 1024 | bytes 1024 | tf_op jit(solution)/shard_map/pallas_call | solution.py:129
  335.7 37.6 %all_to_all.20 = bf16[96,56,256]{2,1,0:T(8,128)(2,1)S(1)} all-to-all(bf16[96,56,256]{2,1,0:T(8,128)(2,1)S(1)} %shard_map.41), channel_id=1, replica_groups={{0,2,4,6,8,10,12,14},{16,18,20,22,24,26,28,30},{1,3,5,7,9,11,13,15},{17..., dimensions={0} | all-to-all | bytes 5505024 | tf_op jit(solution)/shard_map/all_to_all | solution.py:178
  373.3 1.9 copy.5
  (58 shorter events, 8.8 us)
Async XLA Ops:
  3.4 7.3 %copy-start.8 = (bf16[12,56,1024]{2,1,0:T(8,128)(2,1)S(1)}, bf16[12,56,1024]{2,1,0:T(8,128)(2,1)}, u32[]{:S(2)}) copy-start(bf16[12,56,1024]{2,1,0:T(8,128)(2,1)} %param.3) | copy-start | bytes 4128772
  3.4 92.5 %all-to-all-start = ((bf16[8,3,128,256]{3,2,1,0:T(8,128)(2,1)}), bf16[8,3,128,256]{3,2,1,0:T(8,128)(2,1)S(1)}, u32[]{:S(2)}, u32[]{:S(2)}) async-start(bf16[8,3,128,256]{3,2,1,0:T(8,128)(2,1)} %shard_map.37), calls=%async_computation | async-start | bytes 3145728 | tf_op jit(solution)/shard_map/all_to_all | solution.py:178
  10.7 8.1 %collective-permute-start = (bf16[1,56,1024]{2,1,0:T(8,128)(2,1)S(1)}, bf16[1,56,1024]{2,1,0:T(8,128)(2,1)S(1)}, u32[]{:S(2)}, u32[]{:S(2)}) collective-permute-start(bf16[1,56,1024]{2,1,0:T(8,128)(2,1)S(1)} %get-tuple-element.38), channel_id=1, source_target_pairs={{2,0},{4,2},{6,4},{8,6},{10,8},{12,10},{14,12},{16,14},{18,16},{20... | collective-permute-start | bytes 344072 | tf_op jit(solution)/shard_map/ppermute | solution.py:194
  12.0 6.8 %collective-permute-start.1 = (bf16[1,56,1024]{2,1,0:T(8,128)(2,1)S(1)}, bf16[1,56,1024]{2,1,0:T(8,128)(2,1)S(1)}, u32[]{:S(2)}, u32[]{:S(2)}) collective-permute-start(bf16[1,56,1024]{2,1,0:T(8,128)(2,1)S(1)} %get-tuple-element.37), channel_id=1, source_target_pairs={{0,2},{2,4},{4,6},{6,8},{8,10},{10,12},{12,14},{14,16},{16,18},{18... | collective-permute-start | bytes 344072 | tf_op jit(solution)/shard_map/ppermute | solution.py:193
  15.0 32.7 %collective-permute-start.5 = (bf16[1,128,2048]{2,1,0:T(8,128)(2,1)}, bf16[1,128,2048]{2,1,0:T(8,128)(2,1)}, u32[]{:S(2)}, u32[]{:S(2)}) collective-permute-start(bf16[1,128,2048]{2,1,0:T(8,128)(2,1)} %slice_bitcast_fusion.1), channel_id=1, source_target_pairs={{0,16},{2,18},{4,20},{6,22},{8,24},{10,26},{12,28},{14,30},{16,0},... | collective-permute-start | bytes 1572872 | tf_op jit(solution)/shard_map/ppermute | solution.py:15
  20.1 75.8 %collective-permute-start.2 = (bf16[13,56,1024]{2,1,0:T(8,128)(2,1)}, bf16[13,56,1024]{2,1,0:T(8,128)(2,1)}, u32[]{:S(2)}, u32[]{:S(2)}) collective-permute-start(bf16[13,56,1024]{2,1,0:T(8,128)(2,1)} %maximum_select_fusion.1), channel_id=1, source_target_pairs={{0,8},{2,10},{4,12},{6,14},{8,0},{10,2},{12,4},{14,6},{16,24},{18,... | collective-permute-start | bytes 4472840 | tf_op jit(solution)/shard_map/ppermute | solution.py:15
  43.9 51.9 %collective-permute-start.3 = (bf16[13,56,1024]{2,1,0:T(8,128)(2,1)}, bf16[13,56,1024]{2,1,0:T(8,128)(2,1)}, u32[]{:S(2)}, u32[]{:S(2)}) collective-permute-start(bf16[13,56,1024]{2,1,0:T(8,128)(2,1)} %maximum_select_fusion.1), channel_id=1, source_target_pairs={{0,4},{2,6},{4,0},{6,2},{8,12},{10,14},{12,8},{14,10},{16,20},{18,... | collective-permute-start | bytes 4472840 | tf_op jit(solution)/shard_map/ppermute | solution.py:15
  43.9 51.9 %collective-permute-start.4 = (bf16[13,56,1024]{2,1,0:T(8,128)(2,1)}, bf16[13,56,1024]{2,1,0:T(8,128)(2,1)S(1)}, u32[]{:S(2)}, u32[]{:S(2)}) collective-permute-start(bf16[13,56,1024]{2,1,0:T(8,128)(2,1)} %maximum_select_fusion.1), channel_id=1, source_target_pairs={{0,1},{1,0},{2,3},{3,2},{4,5},{5,4},{6,7},{7,6},{8,9},{9,8},{10,11... | collective-permute-start | bytes 4472840 | tf_op jit(solution)/shard_map/ppermute | solution.py:15
  47.8 46.1 %collective-permute-start.6 = (bf16[2,128,2048]{2,1,0:T(8,128)(2,1)}, bf16[2,128,2048]{2,1,0:T(8,128)(2,1)}, u32[]{:S(2)}, u32[]{:S(2)}) collective-permute-start(bf16[2,128,2048]{2,1,0:T(8,128)(2,1)} %slice_bitcast_fusion), channel_id=1, source_target_pairs={{0,16},{2,18},{4,20},{6,22},{8,24},{10,26},{12,28},{14,30},{16,0},... | collective-permute-start | bytes 3145736 | tf_op jit(solution)/shard_map/ppermute | solution.py:15
  95.9 2.2 copy-start.10
  95.9 44.4 %copy-start.2 = (bf16[8,3,128,256]{3,2,1,0:T(8,128)(2,1)}, bf16[8,3,128,256]{3,2,1,0:T(8,128)(2,1)S(1)}, u32[]{:S(2)}) copy-start(bf16[8,3,128,256]{3,2,1,0:T(8,128)(2,1)S(1)} %all-to-all-done.refs_3_) | copy-start | bytes 4718596
  95.9 44.4 %collective-permute-start.11 = (bf16[13,56,1024]{2,1,0:T(8,128)(2,1)}, bf16[13,56,1024]{2,1,0:T(8,128)(2,1)}, u32[]{:S(2)}, u32[]{:S(2)}) collective-permute-start(bf16[13,56,1024]{2,1,0:T(8,128)(2,1)} %collective-permute-done.2), channel_id=1, source_target_pairs={{0,4},{2,6},{4,0},{6,2},{8,12},{10,14},{12,8},{14,10},{16,20},{18,... | collective-permute-start | bytes 4472840 | tf_op jit(solution)/shard_map/ppermute | solution.py:15
  96.0 45.6 %collective-permute-start.12 = (bf16[13,56,1024]{2,1,0:T(8,128)(2,1)}, bf16[13,56,1024]{2,1,0:T(8,128)(2,1)}, u32[]{:S(2)}, u32[]{:S(2)}) collective-permute-start(bf16[13,56,1024]{2,1,0:T(8,128)(2,1)} %collective-permute-done.2), channel_id=1, source_target_pairs={{0,1},{1,0},{2,3},{3,2},{4,5},{5,4},{6,7},{7,6},{8,9},{9,8},{10,11... | collective-permute-start | bytes 4472840 | tf_op jit(solution)/shard_map/ppermute | solution.py:15
  97.5 65.0 %collective-permute-start.13 = (bf16[13,56,1024]{2,1,0:T(8,128)(2,1)}, bf16[13,56,1024]{2,1,0:T(8,128)(2,1)}, u32[]{:S(2)}, u32[]{:S(2)}) collective-permute-start(bf16[13,56,1024]{2,1,0:T(8,128)(2,1)} %collective-permute-done.3), channel_id=1, source_target_pairs={{0,1},{1,0},{2,3},{3,2},{4,5},{5,4},{6,7},{7,6},{8,9},{9,8},{10,11... | collective-permute-start | bytes 4472840 | tf_op jit(solution)/shard_map/ppermute | solution.py:15
  98.1 109.9 %all-to-all-start.1 = ((bf16[8,3,128,256]{3,2,1,0:T(8,128)(2,1)}), bf16[8,3,128,256]{3,2,1,0:T(8,128)(2,1)S(1)}, u32[]{:S(2)}, u32[]{:S(2)}) async-start(bf16[8,3,128,256]{3,2,1,0:T(8,128)(2,1)} %shard_map.38), calls=%async_computation.1 | async-start | bytes 3145728 | tf_op jit(solution)/shard_map/all_to_all | solution.py:178
  103.3 85.1 %collective-permute-start.8 = (bf16[13,56,1024]{2,1,0:T(8,128)(2,1)}, bf16[13,56,1024]{2,1,0:T(8,128)(2,1)}, u32[]{:S(2)}, u32[]{:S(2)}) collective-permute-start(bf16[13,56,1024]{2,1,0:T(8,128)(2,1)} %collective-permute-done.2), channel_id=1, source_target_pairs={{0,2},{2,0},{4,6},{6,4},{8,10},{10,8},{12,14},{14,12},{16,18},{18,... | collective-permute-start | bytes 4472840 | tf_op jit(solution)/shard_map/ppermute | solution.py:15
  103.8 84.6 %collective-permute-start.9 = (bf16[13,56,1024]{2,1,0:T(8,128)(2,1)}, bf16[13,56,1024]{2,1,0:T(8,128)(2,1)}, u32[]{:S(2)}, u32[]{:S(2)}) collective-permute-start(bf16[13,56,1024]{2,1,0:T(8,128)(2,1)} %collective-permute-done.3), channel_id=1, source_target_pairs={{0,2},{2,0},{4,6},{6,4},{8,10},{10,8},{12,14},{14,12},{16,18},{18,... | collective-permute-start | bytes 4472840 | tf_op jit(solution)/shard_map/ppermute | solution.py:15
  140.3 67.7 %collective-permute-start.14 = (bf16[8,3,128,256]{3,2,1,0:T(8,128)(2,1)S(1)}, bf16[8,3,128,256]{3,2,1,0:T(8,128)(2,1)}, u32[]{:S(2)}, u32[]{:S(2)}) collective-permute-start(bf16[8,3,128,256]{3,2,1,0:T(8,128)(2,1)S(1)} %all-to-all-done.refs_3_), channel_id=1, source_target_pairs={{0,16},{2,18},{4,20},{6,22},{8,24},{10,26},{12,28},{14,30},{16,0},... | collective-permute-start | bytes 4718600 | tf_op jit(solution)/shard_map/ppermute | solution.py:15
  141.6 46.8 %collective-permute-start.7 = (bf16[13,56,1024]{2,1,0:T(8,128)(2,1)}, bf16[13,56,1024]{2,1,0:T(8,128)(2,1)}, u32[]{:S(2)}, u32[]{:S(2)}) collective-permute-start(bf16[13,56,1024]{2,1,0:T(8,128)(2,1)} %maximum_select_fusion.1), channel_id=1, source_target_pairs={{0,2},{2,0},{4,6},{6,4},{8,10},{10,8},{12,14},{14,12},{16,18},{18,... | collective-permute-start | bytes 4472840 | tf_op jit(solution)/shard_map/ppermute | solution.py:15
  162.5 25.9 %collective-permute-start.10 = (bf16[13,56,1024]{2,1,0:T(8,128)(2,1)}, bf16[13,56,1024]{2,1,0:T(8,128)(2,1)}, u32[]{:S(2)}, u32[]{:S(2)}) collective-permute-start(bf16[13,56,1024]{2,1,0:T(8,128)(2,1)} %copy-done.10), channel_id=1, source_target_pairs={{0,2},{2,0},{4,6},{6,4},{8,10},{10,8},{12,14},{14,12},{16,18},{18,... | collective-permute-start | bytes 4472840 | tf_op jit(solution)/shard_map/ppermute | solution.py:15
  162.6 8.9 %copy-start.9 = (bf16[12,56,1024]{2,1,0:T(8,128)(2,1)S(1)}, bf16[12,56,1024]{2,1,0:T(8,128)(2,1)}, u32[]{:S(2)}) copy-start(bf16[12,56,1024]{2,1,0:T(8,128)(2,1)} %param.3) | copy-start | bytes 4128772
  173.0 5.4 %copy-start.11 = (bf16[13,56,1024]{2,1,0:T(8,128)(2,1)S(1)}, bf16[13,56,1024]{2,1,0:T(8,128)(2,1)}, u32[]{:S(2)}) copy-start(bf16[13,56,1024]{2,1,0:T(8,128)(2,1)} %copy-done.10) | copy-start | bytes 4472836
  178.4 2.8 slice-start
  208.0 1.1 copy-start.4
  209.1 87.5 %all-to-all-start.2 = ((bf16[8,6,128,256]{3,2,1,0:T(8,128)(2,1)}), bf16[8,6,128,256]{3,2,1,0:T(8,128)(2,1)S(1)}, u32[]{:S(2)}, u32[]{:S(2)}) async-start(bf16[8,6,128,256]{3,2,1,0:T(8,128)(2,1)} %shard_map.39), calls=%async_computation.2 | async-start | bytes 6291456 | tf_op jit(solution)/shard_map/all_to_all | solution.py:178
  213.0 38.0 %collective-permute-start.15 = (bf16[13,56,1024]{2,1,0:T(8,128)(2,1)}, bf16[13,56,1024]{2,1,0:T(8,128)(2,1)S(1)}, u32[]{:S(2)}, u32[]{:S(2)}) collective-permute-start(bf16[13,56,1024]{2,1,0:T(8,128)(2,1)} %collective-permute-done.11), channel_id=1, source_target_pairs={{0,2},{2,0},{4,6},{6,4},{8,10},{10,8},{12,14},{14,12},{16,18},{18,... | collective-permute-start | bytes 4472840 | tf_op jit(solution)/shard_map/ppermute | solution.py:15
  213.5 34.8 %collective-permute-start.18 = (bf16[13,56,1024]{2,1,0:T(8,128)(2,1)}, bf16[13,56,1024]{2,1,0:T(8,128)(2,1)S(1)}, u32[]{:S(2)}, u32[]{:S(2)}) collective-permute-start(bf16[13,56,1024]{2,1,0:T(8,128)(2,1)} %collective-permute-done.11), channel_id=1, source_target_pairs={{0,1},{1,0},{2,3},{3,2},{4,5},{5,4},{6,7},{7,6},{8,9},{9,8},{10,11... | collective-permute-start | bytes 4472840 | tf_op jit(solution)/shard_map/ppermute | solution.py:15
  215.0 37.4 %collective-permute-start.16 = (bf16[13,56,1024]{2,1,0:T(8,128)(2,1)}, bf16[13,56,1024]{2,1,0:T(8,128)(2,1)S(1)}, u32[]{:S(2)}, u32[]{:S(2)}) collective-permute-start(bf16[13,56,1024]{2,1,0:T(8,128)(2,1)} %collective-permute-done.12), channel_id=1, source_target_pairs={{0,2},{2,0},{4,6},{6,4},{8,10},{10,8},{12,14},{14,12},{16,18},{18,... | collective-permute-start | bytes 4472840 | tf_op jit(solution)/shard_map/ppermute | solution.py:15
  215.0 38.7 %collective-permute-start.17 = (bf16[13,56,1024]{2,1,0:T(8,128)(2,1)}, bf16[13,56,1024]{2,1,0:T(8,128)(2,1)S(1)}, u32[]{:S(2)}, u32[]{:S(2)}) collective-permute-start(bf16[13,56,1024]{2,1,0:T(8,128)(2,1)} %collective-permute-done.13), channel_id=1, source_target_pairs={{0,2},{2,0},{4,6},{6,4},{8,10},{10,8},{12,14},{14,12},{16,18},{18,... | collective-permute-start | bytes 4472840 | tf_op jit(solution)/shard_map/ppermute | solution.py:15
  215.5 79.9 %collective-permute-start.20 = (bf16[8,3,128,256]{3,2,1,0:T(8,128)(2,1)}, bf16[8,3,128,256]{3,2,1,0:T(8,128)(2,1)S(1)}, u32[]{:S(2)}, u32[]{:S(2)}) collective-permute-start(bf16[8,3,128,256]{3,2,1,0:T(8,128)(2,1)} %copy-done.4), channel_id=1, source_target_pairs={{0,16},{2,18},{4,20},{6,22},{8,24},{10,26},{12,28},{14,30},{16,0},... | collective-permute-start | bytes 4718600 | tf_op jit(solution)/shard_map/ppermute | solution.py:15
  248.4 7.9 %collective-permute-start.19 = (bf16[13,56,1024]{2,1,0:T(8,128)(2,1)S(1)}, bf16[13,56,1024]{2,1,0:T(8,128)(2,1)S(1)}, u32[]{:S(2)}, u32[]{:S(2)}) collective-permute-start(bf16[13,56,1024]{2,1,0:T(8,128)(2,1)S(1)} %collective-permute-done.18), channel_id=1, source_target_pairs={{0,2},{2,0},{4,6},{6,4},{8,10},{10,8},{12,14},{14,12},{16,18},{18,... | collective-permute-start | bytes 4472840 | tf_op jit(solution)/shard_map/ppermute | solution.py:15
  255.0 3.3 copy-start.3
  255.0 3.3 copy-start.5
  292.8 2.7 copy-start
  295.4 1.1 copy-start.6
  296.6 2.8 copy-start.1
  299.4 1.4 copy-start.7

commit v9 on v8

--- a/solution.py
+++ b/solution.py
@@ -186,8 +186,8 @@
         return after(array, *ready) if ready else array
 
     first, activations = lax.optimization_barrier((filters[0, :1], activations))
-    taken_first = exchange(first)
-    taken = exchange(after(filters[0, 1:], *taken_first))
+    taken = [exchange(first)]
+    taken.append(exchange(after(filters[0, 1:2], *taken[0])))
 
     ups = [(i, i + 1) for i in range(size - 1)]
     above = lax.ppermute(activations[-1:], "img", ups)
@@ -219,58 +219,55 @@
 
     others = range(1, chans)
 
-    by_rank = by_member(filters, 2, 1)
-    own_mid = share(by_member(filters, 1, 1))
+    by_rank = by_member(filters, 1, 2)
     over_ch(0)
     slots[0, 4] = swap(piece, "img", 4)
     slots[0, 2] = swap(piece, "img", 2)
-    ready = [*taken, own_mid, slots[0, 4], slots[0, 2], *(slots[j, 0] for j in others), by_rank]
-
-    taken_mid = exchange(step(own_mid))
-    own_low = share(step(by_rank))
+    ready = [*taken[1], slots[0, 4], slots[0, 2], *(slots[j, 0] for j in others), by_rank]
+
+    lower = share(step(by_rank))
     over_ch(4)
     over_ch(2)
     slots[0, 6] = swap(step(slots[0, 4]), "img", 2)
-    keys = [(0, 0), (0, 4), (0, 2)] + [(j, 0) for j in others]
-    over_core(keys)
-    image = place(image, keys)
+    taken.append(exchange(step(filters[0, 2:])))
+    ready = [lower, *taken[2], slots[0, 6], *(slots[j, r] for j in others for r in (4, 2))]
+
+    half = GROUP // 2
+    received = [exchange(step(lower[:half]))]
+    over_ch(6)
     raw = [filters[0]] + [
-        jnp.concatenate([step(a), step(b)]) for a, b in zip(taken_first, taken)
+        jnp.concatenate([step(array) for array in arrays]) for arrays in zip(*taken)
     ]
-    by_rank = by_member(jnp.stack(raw), 0, parts)
-    ready = [*taken_mid, own_low, slots[0, 6], by_rank, image]
-    ready += [slots[j, r] for j in others for r in (4, 2)]
-    ready += [slots[j, r + 1] for j, r in keys]
-
-    taken_low = exchange(step(own_low))
-    over_ch(6)
-    upper = share(step(by_rank))
-    image = place(image, [(j, r + 1) for j, r in keys])
-    keys = [(0, 6)] + [(j, r) for j in others for r in (4, 2)]
+    upper = share(by_member(jnp.stack(raw), 0, parts))
+    late = [(j, 6) for j in others]
+    keys = [key for key in slots if key not in late]
     over_core(keys)
     image = place(image, keys + [(j, r + 1) for j, r in keys])
-    keys = [(j, 6) for j in others]
     ready = []
-    over_core(keys)
-    image = place(image, keys + [(j, r + 1) for j, r in keys])
+    over_core(late)
+    image = place(image, late + [(j, r + 1) for j, r in late])
 
     scalars = jnp.stack([group * GROUP * rows, group]).astype(jnp.int32)
     bias = lax.dynamic_slice_in_dim(channel_bias, rank * split, split)[None]
     which = [lambda s, j=j: s[1] ^ j for j in range(parts)]
 
-    def pieces(arrays, vertical):
+    at_start = lambda s: (0, 0, 0, 0)
+
+    def pieces(start, arrays):
         return [
-            (which[j], 0, array, array.shape, lambda s: (0, 0, 0, 0), (vertical,))
-            for j, array in arrays
+            (which[j], start, array, array.shape, at_start, (1, 2))
+            for j, array in enumerate(arrays, 1)
         ]
 
     every = [
         (which[j], 0, upper, (GROUP, 3, shard, split), lambda s, j=j: (0, j, 0, 0), (0,))
         for j in range(parts)
     ]
-    early = pieces([(0, own_mid), *enumerate(taken_mid, 1)], 1) + pieces([(0, own_low)], 2)
-    acc = conv_call(early, scalars, image)
-    out = conv_call(every + pieces(enumerate(taken_low, 1), 2), scalars, image, acc, bias)
+    own = [(which[0], 0, lower, lower.shape, at_start, (1, 2))]
+    acc = conv_call(own, scalars, image)
+    received.append(exchange(after(lower[half:], *received[0], acc, upper)))
+    acc = conv_call(every + pieces(0, received[0]), scalars, image, acc)
+    out = conv_call(pieces(half, received[1]), scalars, image, acc, bias)
     out = share(out).reshape(GROUP, rows, side, split)
     return jnp.moveaxis(out, 0, 2).reshape(rows, side, out_local)
 

time: 376 us -> 392 us (1.043)
  waiting for transfers between devices: 134 us -> 184 us
  starting transfers between devices: 58.7 us -> 39 us
  local copies, waits for them, and re-layouts: 56.5 us -> 42.5 us
    ppermute x19 -> x20, waiting for transfers between devices: 134 us -> 183 us  [swap(): return lax.ppermute(array, axis, [(i, i ^ bit) for i in range(size)])]
    dynamic_update_slice x15, local copies, waits for them, and re-layouts: 31.7 us -> 16.4 us  [place(): lax.dynamic_update_slice(image, slots[j, r][None], (mine ^ j, start, 0, 0))]
    ppermute x19 -> x20, starting transfers between devices: 39.9 us -> 26.6 us  [swap(): return lax.ppermute(array, axis, [(i, i ^ bit) for i in range(size)])]
    unnamed x24 -> x32, local copies, waits for them, and re-layouts: 9.15 us -> 15.8 us
    all_to_all x3 -> x2, starting transfers between devices: 14.5 us -> 8.08 us  [share(): lax.all_to_all(taps, 'img', 0, 0, axis_index_groups=members, tiled=True)]
    broadcast_in_dim x1, local copies, waits for them, and re-layouts: 8.85 us -> 3.28 us  [local(): jnp.zeros((chans, GROUP * rows + 3, width, depth), activations.dtype)]
    pallas_call x2 -> x3, Pallas kernels: 69.4 us -> 73.8 us  [conv_call(): pl.pallas_call(body, grid_spec=pltpu.PrefetchScalarGridSpec(num_scalar_pr...]
    pallas_call x3 -> x2, Pallas kernels: 12 us -> 10.6 us  [by_member(): pl.pallas_call(body, grid=(count, across), in_specs=[pl.BlockSpec((1, 1,...]
  transfers between devices with their start and end apart: 24 -> 24, of which waited for: 6 -> 9; matrix products, arithmetic and copies ran while one was open for 14% -> 6% of each run, Pallas kernels for 11% -> 17%
where the time goes in v9:
time: 392 us; the launch traced here: 391 us
  waiting for transfers between devices  184 us (47%)
  Pallas kernels  84.4 us (22%)
  local copies, waits for them, and re-layouts  42.5 us (11%)
  starting transfers between devices  39 us (10%)
  blocking collectives  36.5 us (9%)
  other arithmetic  4.3 us (1%)
    ppermute x20, waiting for transfers between devices, swap(): return lax.ppermute(array, axis, [(i, i ^ bit) for i in range(size)])  183 us
    pallas_call x3, Pallas kernels, conv_call(): pl.pallas_call(body, grid_spec=pltpu.PrefetchScalarGridSpec(num_scalar_pr...  73.8 us
    all_to_all x1, blocking collectives, share(): lax.all_to_all(taps, 'img', 0, 0, axis_index_groups=members, tiled=True)  36.5 us
    ppermute x20, starting transfers between devices, swap(): return lax.ppermute(array, axis, [(i, i ^ bit) for i in range(size)])  26.6 us
    dynamic_update_slice x15, local copies, waits for them, and re-layouts, place(): lax.dynamic_update_slice(image, slots[j, r][None], (mine ^ j, start, 0, 0))  16.4 us
    unnamed x32, local copies, waits for them, and re-layouts  15.8 us
    pallas_call x2, Pallas kernels, by_member(): pl.pallas_call(body, grid=(count, across), in_specs=[pl.BlockSpec((1, 1,...  10.6 us
    all_to_all x2, starting transfers between devices, share(): lax.all_to_all(taps, 'img', 0, 0, axis_index_groups=members, tiled=True)  8.08 us
  transfers between devices with their start and end apart: 24, of which 9 were waited for; matrix products, arithmetic and copies ran while one was open for 6% of the time, Pallas kernels for 17%

profile of v9, /device:TPU:0, one launch (start us, length us, event | category | flops | bytes accessed | tf_op | source)
XLA Modules:
  0.0 391.4 jit_solution(10772183725319740756)
XLA Ops:
  0.0 2.7 slice_bitcast_fusion
  2.7 1.3 collective-permute-start
  4.0 3.0 collective-permute-start.1
  7.1 0.9 collective-permute-done.1
  8.2 3.0 collective-permute-start.2
  11.2 6.1 %collective-permute-start.3 = (bf16[13,56,1024]{2,1,0:T(8,128)(2,1)S(1)}, bf16[13,56,1024]{2,1,0:T(8,128)(2,1)}, u32[]{:S(2)}, u32[]{:S(2)}) collective-permute-start(bf16[13,56,1024]{2,1,0:T(8,128)(2,1)S(1)} %maximum_select_fusion.1), channel_id=1, source_target_pairs={{0,8},{2,10},{4,12},{6,14},{8,0},{10,2},{12,4},{14,6},{16,24},{18,... | collective-permute-start | bytes 4472840 | tf_op jit(solution)/shard_map/ppermute | solution.py:15
  17.3 2.6 collective-permute-start.5
  19.9 38.1 %collective-permute-done.5 = bf16[1,128,2048]{2,1,0:T(8,128)(2,1)S(1)} collective-permute-done((bf16[1,128,2048]{2,1,0:T(8,128)(2,1)S(1)}, bf16[1,128,2048]{2,1,0:T(8,128)(2,1)S(1)}, u32[]{:S(2)}, u32[]{:S(2)}) %collective-permute-start.5) | collective-permute-done | bytes 524320 | tf_op jit(solution)/shard_map/ppermute | solution.py:15
  57.9 3.5 collective-permute-start.6
  61.4 5.3 %shard_map.37 = bf16[8,6,128,256]{3,2,1,0:T(8,128)(2,1)} custom-call(bf16[3,3,128,2048]{3,2,1,0:T(8,128)(2,1)} %taps.1), custom_call_target="tpu_custom_call" | custom-call | tf_op jit(solution)/shard_map/pallas_call | solution.py:156
  66.8 16.6 %collective-permute-done.6 = bf16[1,128,2048]{2,1,0:T(8,128)(2,1)S(1)} collective-permute-done((bf16[1,128,2048]{2,1,0:T(8,128)(2,1)}, bf16[1,128,2048]{2,1,0:T(8,128)(2,1)S(1)}, u32[]{:S(2)}, u32[]{:S(2)}) %collective-permute-start.6) | collective-permute-done | bytes 524320 | tf_op jit(solution)/shard_map/ppermute | solution.py:15
  84.1 3.6 all-to-all-start
  88.4 1.5 collective-permute-start.8
  89.9 2.3 collective-permute-start.9
  92.2 2.1 collective-permute-start.10
  94.3 39.7 %collective-permute-done.10 = bf16[1,128,2048]{2,1,0:T(8,128)(2,1)S(1)} collective-permute-done((bf16[1,128,2048]{2,1,0:T(8,128)(2,1)}, bf16[1,128,2048]{2,1,0:T(8,128)(2,1)S(1)}, u32[]{:S(2)}, u32[]{:S(2)}) %collective-permute-start.10) | collective-permute-done | bytes 524320 | tf_op jit(solution)/shard_map/ppermute | solution.py:15
  133.9 21.0 %collective-permute-done.8 = bf16[13,56,1024]{2,1,0:T(8,128)(2,1)S(1)} collective-permute-done((bf16[13,56,1024]{2,1,0:T(8,128)(2,1)}, bf16[13,56,1024]{2,1,0:T(8,128)(2,1)S(1)}, u32[]{:S(2)}, u32[]{:S(2)}) %collective-permute-start.8) | collective-permute-done | bytes 1490976 | tf_op jit(solution)/shard_map/ppermute | solution.py:15
  155.0 1.2 copy-done.8
  156.7 1.6 maximum_bitcast_fusion
  158.6 1.9 pad_maximum_fusion.taps
  160.5 5.3 %shard_map.39 = bf16[8,6,128,256]{3,2,1,0:T(8,128)(2,1)} custom-call(bf16[2,3,128,2048]{3,2,1,0:T(8,128)(2,1)} %pad_maximum_fusion.taps), custom_call_target="tpu_custom_call" | custom-call | tf_op jit(solution)/shard_map/pallas_call | solution.py:156
  165.8 4.4 %all-to-all-start.1 = ((bf16[8,6,128,256]{3,2,1,0:T(8,128)(2,1)}), bf16[8,6,128,256]{3,2,1,0:T(8,128)(2,1)}, u32[]{:S(2)}, u32[]{:S(2)}) async-start(bf16[8,6,128,256]{3,2,1,0:T(8,128)(2,1)} %shard_map.39), calls=%async_computation.1 | async-start | bytes 6291456 | tf_op jit(solution)/shard_map/all_to_all | solution.py:178
  170.4 3.3 broadcast_in_dim.52
  174.2 1.6 bitcast_dynamic-update-slice_fusion.14
  176.1 1.6 bitcast_dynamic-update-slice_fusion.13
  178.1 1.6 bitcast_dynamic-update-slice_fusion.12
  181.4 1.6 bitcast_dynamic-update-slice_fusion.9
  183.1 1.5 fusion.1
  185.1 1.6 bitcast_dynamic-update-slice_fusion.8
  187.1 8.6 %copy-done.3 = bf16[2,99,64,1024]{3,2,1,0:T(8,128)(2,1)} copy-done((bf16[2,99,64,1024]{3,2,1,0:T(8,128)(2,1)}, bf16[2,99,64,1024]{3,2,1,0:T(8,128)(2,1)S(1)}, u32[]{:S(2)}) %copy-start.3) | copy-done | bytes 25952280
  195.7 2.5 collective-permute-start.20
  198.2 17.7 %collective-permute-done.18 = bf16[13,56,1024]{2,1,0:T(8,128)(2,1)S(1)} collective-permute-done((bf16[13,56,1024]{2,1,0:T(8,128)(2,1)}, bf16[13,56,1024]{2,1,0:T(8,128)(2,1)S(1)}, u32[]{:S(2)}, u32[]{:S(2)}) %collective-permute-start.18) | collective-permute-done | bytes 1490976 | tf_op jit(solution)/shard_map/ppermute | solution.py:15
  215.9 1.3 bitcast_dynamic-update-slice_fusion.5
  217.1 1.3 bitcast_dynamic-update-slice_fusion.4
  218.4 1.2 bitcast_dynamic-update-slice_fusion.3
  219.7 1.3 bitcast_dynamic-update-slice_fusion.2
  221.0 1.2 bitcast_dynamic-update-slice_fusion.1
  222.2 1.3 bitcast_dynamic-update-slice_fusion.refs_0_.refs_1_.refs_2_.refs_3_.refs_4_
  223.6 23.7 %shard_map.38.refs_8_ = f32[96,64,256]{2,1,0:T(8,128)S(1)} custom-call(s32[2]{0:T(128)S(1)} %pad_add_fusion.scalars_ref, bf16[2,99,64,1024]{3,2,1,0:T(8,128)(2,1)} %bitcast_dynamic-update-slice_fusion.refs_0_.refs_1_.refs_2_.refs_3_.refs_4_, bf16[2,99,64,1024]{3,2,1,0:T(8,128)(2,1)} %bitcast_dynamic-update-slice_fusion.refs_0_.refs_1_.refs_2_.refs_3_.refs_4_, ...), custom_call_target="tpu_custom_call" | custom-call | flops 1024 | bytes 1024 | tf_op jit(solution)/shard_map/pallas_call | solution.py:129
  247.2 2.6 copy-done
  249.9 17.3 %collective-permute-done.20.refs_7_ = bf16[4,6,128,256]{3,2,1,0:T(8,128)(2,1)S(1)} collective-permute-done((bf16[4,6,128,256]{3,2,1,0:T(8,128)(2,1)S(1)}, bf16[4,6,128,256]{3,2,1,0:T(8,128)(2,1)S(1)}, u32[]{:S(2)}, u32[]{:S(2)}) %collective-permute-start.20) | collective-permute-done | bytes 1572896 | tf_op jit(solution)/shard_map/ppermute | solution.py:15
  267.1 1.2 copy-done.1
  269.1 1.4 copy-done.2
  270.5 36.3 %shard_map.40.refs_3_ = f32[96,64,256]{2,1,0:T(8,128)S(1)} custom-call(s32[2]{0:T(128)S(1)} %pad_add_fusion.scalars_ref, bf16[2,99,64,1024]{3,2,1,0:T(8,128)(2,1)} %bitcast_dynamic-update-slice_fusion.refs_0_.refs_1_.refs_2_.refs_3_.refs_4_, bf16[2,99,64,1024]{3,2,1,0:T(8,128)(2,1)} %bitcast_dynamic-update-slice_fusion.refs_0_.refs_1_.refs_2_.refs_3_.refs_4_, ...), custom_call_target="tpu_custom_call" | custom-call | flops 1024 | bytes 1024 | tf_op jit(solution)/shard_map/pallas_call | solution.py:129
  306.7 32.4 %collective-permute-done.21.refs_2_ = bf16[4,6,128,256]{3,2,1,0:T(8,128)(2,1)S(1)} collective-permute-done((bf16[4,6,128,256]{3,2,1,0:T(8,128)(2,1)}, bf16[4,6,128,256]{3,2,1,0:T(8,128)(2,1)S(1)}, u32[]{:S(2)}, u32[]{:S(2)}) %collective-permute-start.21) | collective-permute-done | bytes 1572896 | tf_op jit(solution)/shard_map/ppermute | solution.py:15
  339.1 13.9 %shard_map.41 = bf16[96,56,256]{2,1,0:T(8,128)(2,1)S(1)} custom-call(s32[2]{0:T(128)S(1)} %pad_add_fusion.scalars_ref, bf16[2,99,64,1024]{3,2,1,0:T(8,128)(2,1)} %bitcast_dynamic-update-slice_fusion.refs_0_.refs_1_.refs_2_.refs_3_.refs_4_, bf16[2,99,64,1024]{3,2,1,0:T(8,128)(2,1)} %bitcast_dynamic-update-slice_fusion.refs_0_.refs_1_.refs_2_.refs_3_.refs_4_, ...), custom_call_target="tpu_custom_call" | custom-call | flops 1024 | bytes 1024 | tf_op jit(solution)/shard_map/pallas_call | solution.py:129
  353.0 36.5 %all_to_all.15 = bf16[96,56,256]{2,1,0:T(8,128)(2,1)S(1)} all-to-all(bf16[96,56,256]{2,1,0:T(8,128)(2,1)S(1)} %shard_map.41), channel_id=1, replica_groups={{0,2,4,6,8,10,12,14},{16,18,20,22,24,26,28,30},{1,3,5,7,9,11,13,15},{17..., dimensions={0} | all-to-all | bytes 5505024 | tf_op jit(solution)/shard_map/all_to_all | solution.py:178
  389.5 1.9 copy.5
  (66 shorter events, 7.0 us)
Async XLA Ops:
  0.0 2.7 copy-start.4
  2.7 4.4 %collective-permute-start = (bf16[1,56,1024]{2,1,0:T(8,128)(2,1)S(1)}, bf16[1,56,1024]{2,1,0:T(8,128)(2,1)S(1)}, u32[]{:S(2)}, u32[]{:S(2)}) collective-permute-start(bf16[1,56,1024]{2,1,0:T(8,128)(2,1)S(1)} %get-tuple-element.49), channel_id=1, source_target_pairs={{2,0},{4,2},{6,4},{8,6},{10,8},{12,10},{14,12},{16,14},{18,16},{20... | collective-permute-start | bytes 344072 | tf_op jit(solution)/shard_map/ppermute | solution.py:194
  4.0 4.0 %collective-permute-start.1 = (bf16[1,56,1024]{2,1,0:T(8,128)(2,1)S(1)}, bf16[1,56,1024]{2,1,0:T(8,128)(2,1)S(1)}, u32[]{:S(2)}, u32[]{:S(2)}) collective-permute-start(bf16[1,56,1024]{2,1,0:T(8,128)(2,1)S(1)} %get-tuple-element.48), channel_id=1, source_target_pairs={{0,2},{2,4},{4,6},{6,8},{8,10},{10,12},{12,14},{14,16},{16,18},{18... | collective-permute-start | bytes 344072 | tf_op jit(solution)/shard_map/ppermute | solution.py:193
  7.0 10.2 %copy-start.12 = (bf16[1,128,2048]{2,1,0:T(8,128)(2,1)S(1)}, bf16[1,128,2048]{2,1,0:T(8,128)(2,1)}, u32[]{:S(2)}) copy-start(bf16[1,128,2048]{2,1,0:T(8,128)(2,1)} %get-tuple-element.25) | copy-start | bytes 1572868
  8.2 58.5 %copy-start.6 = (bf16[13,56,1024]{2,1,0:T(8,128)(2,1)}, bf16[13,56,1024]{2,1,0:T(8,128)(2,1)S(1)}, u32[]{:S(2)}) copy-start(bf16[13,56,1024]{2,1,0:T(8,128)(2,1)S(1)} %maximum_select_fusion.1) | copy-start | bytes 4472836
  8.2 75.1 %collective-permute-start.2 = (bf16[13,56,1024]{2,1,0:T(8,128)(2,1)S(1)}, bf16[13,56,1024]{2,1,0:T(8,128)(2,1)}, u32[]{:S(2)}, u32[]{:S(2)}) collective-permute-start(bf16[13,56,1024]{2,1,0:T(8,128)(2,1)S(1)} %maximum_select_fusion.1), channel_id=1, source_target_pairs={{0,1},{1,0},{2,3},{3,2},{4,5},{5,4},{6,7},{7,6},{8,9},{9,8},{10,11... | collective-permute-start | bytes 4472840 | tf_op jit(solution)/shard_map/ppermute | solution.py:15
  11.2 72.1 %collective-permute-start.3 = (bf16[13,56,1024]{2,1,0:T(8,128)(2,1)S(1)}, bf16[13,56,1024]{2,1,0:T(8,128)(2,1)}, u32[]{:S(2)}, u32[]{:S(2)}) collective-permute-start(bf16[13,56,1024]{2,1,0:T(8,128)(2,1)S(1)} %maximum_select_fusion.1), channel_id=1, source_target_pairs={{0,8},{2,10},{4,12},{6,14},{8,0},{10,2},{12,4},{14,6},{16,24},{18,... | collective-permute-start | bytes 4472840 | tf_op jit(solution)/shard_map/ppermute | solution.py:15
  17.3 66.1 %collective-permute-start.4 = (bf16[13,56,1024]{2,1,0:T(8,128)(2,1)S(1)}, bf16[13,56,1024]{2,1,0:T(8,128)(2,1)}, u32[]{:S(2)}, u32[]{:S(2)}) collective-permute-start(bf16[13,56,1024]{2,1,0:T(8,128)(2,1)S(1)} %maximum_select_fusion.1), channel_id=1, source_target_pairs={{0,4},{2,6},{4,0},{6,2},{8,12},{10,14},{12,8},{14,10},{16,20},{18,... | collective-permute-start | bytes 4472840 | tf_op jit(solution)/shard_map/ppermute | solution.py:15
  17.3 40.6 %collective-permute-start.5 = (bf16[1,128,2048]{2,1,0:T(8,128)(2,1)S(1)}, bf16[1,128,2048]{2,1,0:T(8,128)(2,1)S(1)}, u32[]{:S(2)}, u32[]{:S(2)}) collective-permute-start(bf16[1,128,2048]{2,1,0:T(8,128)(2,1)S(1)} %copy-done.12), channel_id=1, source_target_pairs={{0,16},{2,18},{4,20},{6,22},{8,24},{10,26},{12,28},{14,30},{16,0},... | collective-permute-start | bytes 1572872 | tf_op jit(solution)/shard_map/ppermute | solution.py:15
  57.9 8.8 %copy-start.13 = (bf16[1,128,2048]{2,1,0:T(8,128)(2,1)}, bf16[1,128,2048]{2,1,0:T(8,128)(2,1)S(1)}, u32[]{:S(2)}) copy-start(bf16[1,128,2048]{2,1,0:T(8,128)(2,1)S(1)} %collective-permute-done.5) | copy-start | bytes 1572868
  57.9 25.4 %collective-permute-start.6 = (bf16[1,128,2048]{2,1,0:T(8,128)(2,1)}, bf16[1,128,2048]{2,1,0:T(8,128)(2,1)S(1)}, u32[]{:S(2)}, u32[]{:S(2)}) collective-permute-start(bf16[1,128,2048]{2,1,0:T(8,128)(2,1)} %get-tuple-element.26), channel_id=1, source_target_pairs={{0,16},{2,18},{4,20},{6,22},{8,24},{10,26},{12,28},{14,30},{16,0},... | collective-permute-start | bytes 1572872 | tf_op jit(solution)/shard_map/ppermute | solution.py:15
  83.3 0.8 copy-start.14
  84.1 72.6 %all-to-all-start = ((bf16[8,6,128,256]{3,2,1,0:T(8,128)(2,1)}), bf16[8,6,128,256]{3,2,1,0:T(8,128)(2,1)S(1)}, u32[]{:S(2)}, u32[]{:S(2)}) async-start(bf16[8,6,128,256]{3,2,1,0:T(8,128)(2,1)} %shard_map.37), calls=%async_computation | async-start | bytes 6291456 | tf_op jit(solution)/shard_map/all_to_all | solution.py:178
  87.8 46.2 %collective-permute-start.7 = (bf16[13,56,1024]{2,1,0:T(8,128)(2,1)}, bf16[13,56,1024]{2,1,0:T(8,128)(2,1)S(1)}, u32[]{:S(2)}, u32[]{:S(2)}) collective-permute-start(bf16[13,56,1024]{2,1,0:T(8,128)(2,1)} %collective-permute-done.3), channel_id=1, source_target_pairs={{0,1},{1,0},{2,3},{3,2},{4,5},{5,4},{6,7},{7,6},{8,9},{9,8},{10,11... | collective-permute-start | bytes 4472840 | tf_op jit(solution)/shard_map/ppermute | solution.py:15
  88.4 66.6 %collective-permute-start.8 = (bf16[13,56,1024]{2,1,0:T(8,128)(2,1)}, bf16[13,56,1024]{2,1,0:T(8,128)(2,1)S(1)}, u32[]{:S(2)}, u32[]{:S(2)}) collective-permute-start(bf16[13,56,1024]{2,1,0:T(8,128)(2,1)} %collective-permute-done.4), channel_id=1, source_target_pairs={{0,1},{1,0},{2,3},{3,2},{4,5},{5,4},{6,7},{7,6},{8,9},{9,8},{10,11... | collective-permute-start | bytes 4472840 | tf_op jit(solution)/shard_map/ppermute | solution.py:15
  89.9 66.9 %collective-permute-start.9 = (bf16[13,56,1024]{2,1,0:T(8,128)(2,1)}, bf16[13,56,1024]{2,1,0:T(8,128)(2,1)}, u32[]{:S(2)}, u32[]{:S(2)}) collective-permute-start(bf16[13,56,1024]{2,1,0:T(8,128)(2,1)} %collective-permute-done.3), channel_id=1, source_target_pairs={{0,4},{2,6},{4,0},{6,2},{8,12},{10,14},{12,8},{14,10},{16,20},{18,... | collective-permute-start | bytes 4472840 | tf_op jit(solution)/shard_map/ppermute | solution.py:15
  92.2 41.8 %collective-permute-start.10 = (bf16[1,128,2048]{2,1,0:T(8,128)(2,1)}, bf16[1,128,2048]{2,1,0:T(8,128)(2,1)S(1)}, u32[]{:S(2)}, u32[]{:S(2)}) collective-permute-start(bf16[1,128,2048]{2,1,0:T(8,128)(2,1)} %get-tuple-element.30), channel_id=1, source_target_pairs={{0,16},{2,18},{4,20},{6,22},{8,24},{10,26},{12,28},{14,30},{16,0},... | collective-permute-start | bytes 1572872 | tf_op jit(solution)/shard_map/ppermute | solution.py:15
  133.9 21.0 %copy-start.15 = (bf16[1,128,2048]{2,1,0:T(8,128)(2,1)}, bf16[1,128,2048]{2,1,0:T(8,128)(2,1)S(1)}, u32[]{:S(2)}) copy-start(bf16[1,128,2048]{2,1,0:T(8,128)(2,1)S(1)} %collective-permute-done.10) | copy-start | bytes 1572868
  133.9 21.0 %copy-start.10 = (bf16[13,56,1024]{2,1,0:T(8,128)(2,1)}, bf16[13,56,1024]{2,1,0:T(8,128)(2,1)S(1)}, u32[]{:S(2)}) copy-start(bf16[13,56,1024]{2,1,0:T(8,128)(2,1)S(1)} %collective-permute-done.7) | copy-start | bytes 4472836
  155.0 1.2 copy-start.8
  156.7 1.9 slice-start
  165.8 102.5 %all-to-all-start.1 = ((bf16[8,6,128,256]{3,2,1,0:T(8,128)(2,1)}), bf16[8,6,128,256]{3,2,1,0:T(8,128)(2,1)}, u32[]{:S(2)}, u32[]{:S(2)}) async-start(bf16[8,6,128,256]{3,2,1,0:T(8,128)(2,1)} %shard_map.39), calls=%async_computation.1 | async-start | bytes 6291456 | tf_op jit(solution)/shard_map/all_to_all | solution.py:178
  170.4 3.3 copy-start.5
  173.7 2.0 copy-start.7
  175.8 4.4 %copy-start.11 = (bf16[13,56,1024]{2,1,0:T(8,128)(2,1)S(1)}, bf16[13,56,1024]{2,1,0:T(8,128)(2,1)}, u32[]{:S(2)}) copy-start(bf16[13,56,1024]{2,1,0:T(8,128)(2,1)} %copy-done.10) | copy-start | bytes 4472836
  175.8 7.2 %collective-permute-start.11 = (bf16[13,56,1024]{2,1,0:T(8,128)(2,1)S(1)}, bf16[13,56,1024]{2,1,0:T(8,128)(2,1)}, u32[]{:S(2)}, u32[]{:S(2)}) collective-permute-start(bf16[13,56,1024]{2,1,0:T(8,128)(2,1)S(1)} %copy-done.7), channel_id=1, source_target_pairs={{0,2},{2,0},{4,6},{6,4},{8,10},{10,8},{12,14},{14,12},{16,18},{18,... | collective-permute-start | bytes 4472840 | tf_op jit(solution)/shard_map/ppermute | solution.py:15
  177.8 2.6 copy-start.9
  177.8 6.8 %collective-permute-start.12 = (bf16[13,56,1024]{2,1,0:T(8,128)(2,1)}, bf16[13,56,1024]{2,1,0:T(8,128)(2,1)S(1)}, u32[]{:S(2)}, u32[]{:S(2)}) collective-permute-start(bf16[13,56,1024]{2,1,0:T(8,128)(2,1)} %collective-permute-done.2), channel_id=1, source_target_pairs={{0,2},{2,0},{4,6},{6,4},{8,10},{10,8},{12,14},{14,12},{16,18},{18,... | collective-permute-start | bytes 4472840 | tf_op jit(solution)/shard_map/ppermute | solution.py:15
  179.8 6.8 %collective-permute-start.13 = (bf16[13,56,1024]{2,1,0:T(8,128)(2,1)}, bf16[13,56,1024]{2,1,0:T(8,128)(2,1)S(1)}, u32[]{:S(2)}, u32[]{:S(2)}) collective-permute-start(bf16[13,56,1024]{2,1,0:T(8,128)(2,1)} %collective-permute-done.3), channel_id=1, source_target_pairs={{0,2},{2,0},{4,6},{6,4},{8,10},{10,8},{12,14},{14,12},{16,18},{18,... | collective-permute-start | bytes 4472840 | tf_op jit(solution)/shard_map/ppermute | solution.py:15
  180.5 15.2 %collective-permute-start.14 = (bf16[13,56,1024]{2,1,0:T(8,128)(2,1)}, bf16[13,56,1024]{2,1,0:T(8,128)(2,1)S(1)}, u32[]{:S(2)}, u32[]{:S(2)}) collective-permute-start(bf16[13,56,1024]{2,1,0:T(8,128)(2,1)} %collective-permute-done.4), channel_id=1, source_target_pairs={{0,2},{2,0},{4,6},{6,4},{8,10},{10,8},{12,14},{14,12},{16,18},{18,... | collective-permute-start | bytes 4472840 | tf_op jit(solution)/shard_map/ppermute | solution.py:15
  180.8 35.0 %collective-permute-start.18 = (bf16[13,56,1024]{2,1,0:T(8,128)(2,1)}, bf16[13,56,1024]{2,1,0:T(8,128)(2,1)S(1)}, u32[]{:S(2)}, u32[]{:S(2)}) collective-permute-start(bf16[13,56,1024]{2,1,0:T(8,128)(2,1)} %collective-permute-done.9), channel_id=1, source_target_pairs={{0,1},{1,0},{2,3},{3,2},{4,5},{5,4},{6,7},{7,6},{8,9},{9,8},{10,11... | collective-permute-start | bytes 4472840 | tf_op jit(solution)/shard_map/ppermute | solution.py:15
  183.0 34.2 %collective-permute-start.15 = (bf16[13,56,1024]{2,1,0:T(8,128)(2,1)S(1)}, bf16[13,56,1024]{2,1,0:T(8,128)(2,1)S(1)}, u32[]{:S(2)}, u32[]{:S(2)}) collective-permute-start(bf16[13,56,1024]{2,1,0:T(8,128)(2,1)S(1)} %copy-done.11), channel_id=1, source_target_pairs={{0,2},{2,0},{4,6},{6,4},{8,10},{10,8},{12,14},{14,12},{16,18},{18,... | collective-permute-start | bytes 4472840 | tf_op jit(solution)/shard_map/ppermute | solution.py:15
  184.6 33.9 %collective-permute-start.16 = (bf16[13,56,1024]{2,1,0:T(8,128)(2,1)S(1)}, bf16[13,56,1024]{2,1,0:T(8,128)(2,1)S(1)}, u32[]{:S(2)}, u32[]{:S(2)}) collective-permute-start(bf16[13,56,1024]{2,1,0:T(8,128)(2,1)S(1)} %copy-done.9), channel_id=1, source_target_pairs={{0,2},{2,0},{4,6},{6,4},{8,10},{10,8},{12,14},{14,12},{16,18},{18,... | collective-permute-start | bytes 4472840 | tf_op jit(solution)/shard_map/ppermute | solution.py:15
  186.6 33.0 %collective-permute-start.17 = (bf16[13,56,1024]{2,1,0:T(8,128)(2,1)}, bf16[13,56,1024]{2,1,0:T(8,128)(2,1)S(1)}, u32[]{:S(2)}, u32[]{:S(2)}) collective-permute-start(bf16[13,56,1024]{2,1,0:T(8,128)(2,1)} %collective-permute-done.9), channel_id=1, source_target_pairs={{0,2},{2,0},{4,6},{6,4},{8,10},{10,8},{12,14},{14,12},{16,18},{18,... | collective-permute-start | bytes 4472840 | tf_op jit(solution)/shard_map/ppermute | solution.py:15
  187.1 8.6 %copy-start.3 = (bf16[2,99,64,1024]{3,2,1,0:T(8,128)(2,1)}, bf16[2,99,64,1024]{3,2,1,0:T(8,128)(2,1)S(1)}, u32[]{:S(2)}) copy-start(bf16[2,99,64,1024]{3,2,1,0:T(8,128)(2,1)S(1)} %bitcast_dynamic-update-slice_fusion.6) | copy-start | bytes 77856768
  195.7 71.4 %collective-permute-start.20 = (bf16[4,6,128,256]{3,2,1,0:T(8,128)(2,1)S(1)}, bf16[4,6,128,256]{3,2,1,0:T(8,128)(2,1)S(1)}, u32[]{:S(2)}, u32[]{:S(2)}) collective-permute-start(bf16[4,6,128,256]{3,2,1,0:T(8,128)(2,1)S(1)} %get-tuple-element.38), channel_id=1, source_target_pairs={{0,16},{2,18},{4,20},{6,22},{8,24},{10,26},{12,28},{14,30},{16,0},... | collective-permute-start | bytes 4718600 | tf_op jit(solution)/shard_map/ppermute | solution.py:15
  215.9 6.4 %collective-permute-start.19 = (bf16[13,56,1024]{2,1,0:T(8,128)(2,1)S(1)}, bf16[13,56,1024]{2,1,0:T(8,128)(2,1)S(1)}, u32[]{:S(2)}, u32[]{:S(2)}) collective-permute-start(bf16[13,56,1024]{2,1,0:T(8,128)(2,1)S(1)} %collective-permute-done.18), channel_id=1, source_target_pairs={{0,2},{2,0},{4,6},{6,4},{8,10},{10,8},{12,14},{14,12},{16,18},{18,... | collective-permute-start | bytes 4472840 | tf_op jit(solution)/shard_map/ppermute | solution.py:15
  247.2 2.6 copy-start
  267.1 1.2 copy-start.1
  268.3 70.8 %collective-permute-start.21 = (bf16[4,6,128,256]{3,2,1,0:T(8,128)(2,1)}, bf16[4,6,128,256]{3,2,1,0:T(8,128)(2,1)S(1)}, u32[]{:S(2)}, u32[]{:S(2)}) collective-permute-start(bf16[4,6,128,256]{3,2,1,0:T(8,128)(2,1)} %get-tuple-element.42), channel_id=1, source_target_pairs={{0,16},{2,18},{4,20},{6,22},{8,24},{10,26},{12,28},{14,30},{16,0},... | collective-permute-start | bytes 4718600 | tf_op jit(solution)/shard_map/ppermute | solution.py:15
  269.1 1.4 copy-start.2

commit v10 on v7

--- a/solution.py
+++ b/solution.py
@@ -233,57 +233,33 @@
     ready = [lower, *(slots[j, 4] for j in others), *taken_last]
     ready += [slots[j, r + 1] for j, r in keys]
 
-    cuts = (0, GROUP // 4, GROUP // 2, GROUP)
-    chunks = [lower[a:b] for a, b in zip(cuts, cuts[1:])]
-    received = [exchange(step(chunks[0]))]
+    received = exchange(step(lower))
     over_ch(2)
     slots[0, 6] = swap(step(slots[0, 4]), "img", 2)
     image = place(image, [(j, r + 1) for j, r in keys])
-    keys = [(j, 4) for j in others]
-    over_core(keys)
-    image = place(image, keys)
     raw = [filters[0]] + [
         jnp.concatenate([step(a), step(b)]) for a, b in zip(taken, taken_last)
     ]
-    by_rank = by_member(jnp.stack(raw), 0, parts)
-    ready = [*received[0], slots[0, 6], *(slots[j, 2] for j in others), image, by_rank]
-    ready += [slots[j, r + 1] for j, r in keys]
-
-    received.append(exchange(step(chunks[1])))
+    upper = share(by_member(jnp.stack(raw), 0, parts))
+    ready = []
     over_ch(6)
-    upper = share(step(by_rank))
-    image = place(image, [(j, r + 1) for j, r in keys])
-    keys = [(0, 6)] + [(j, 2) for j in others]
+    keys = [(0, 6)] + [(j, r) for r in (4, 2, 6) for j in others]
     over_core(keys)
-    image = place(image, keys)
-    image = place(image, [(j, r + 1) for j, r in keys])
-    ready = [*received[1], *(slots[j, 6] for j in others), image]
-
-    received.append(exchange(step(chunks[2])))
-    keys = [(j, 6) for j in others]
-    over_core(keys)
-    image = place(image, keys)
-    image = place(image, [(j, r + 1) for j, r in keys])
+    image = place(image, keys + [(j, r + 1) for j, r in keys])
 
     scalars = jnp.stack([group * GROUP * rows, group]).astype(jnp.int32)
     bias = lax.dynamic_slice_in_dim(channel_bias, rank * split, split)[None]
     which = [lambda s, j=j: s[1] ^ j for j in range(parts)]
     at_start = lambda s: (0, 0, 0, 0)
+    blocks = [(which[j], 0, array, array.shape, at_start, (1, 2))
+              for j, array in enumerate([lower, *received])]
     every = [
         (which[j], 0, upper, (GROUP, 3, shard, split), lambda s, j=j: (0, j, 0, 0), (0,))
         for j in range(parts)
     ]
-
-    def pieces(chosen):
-        return [
-            (which[j], cuts[c], array, array.shape, at_start, (1, 2))
-            for c in chosen
-            for j, array in enumerate(received[c], 1)
-        ]
-
-    acc = conv_call([(which[0], 0, lower, lower.shape, at_start, (1, 2))], scalars, image)
-    acc = conv_call(every + pieces((0, 1)), scalars, image, acc)
-    out = conv_call(pieces((2,)), scalars, image, acc, bias)
+    acc = conv_call(blocks[:1], scalars, image)
+    acc = conv_call(every, scalars, image, acc)
+    out = conv_call(blocks[1:], scalars, image, acc, bias)
     out = share(out).reshape(GROUP, rows, side, split)
     return jnp.moveaxis(out, 0, 2).reshape(rows, side, out_local)
 

time: 357 us -> 405 us (1.13)
  waiting for transfers between devices: 136 us -> 202 us
  local copies, waits for them, and re-layouts: 54.1 us -> 37.2 us
    ppermute x20 -> x18, waiting for transfers between devices: 135 us -> 201 us  [swap(): return lax.ppermute(array, axis, [(i, i ^ bit) for i in range(size)])]
    dynamic_update_slice x15, local copies, waits for them, and re-layouts: 33 us -> 12.4 us  [place(): lax.dynamic_update_slice(image, slots[j, r][None], (mine ^ j, start, 0, 0))]
    unnamed x30 -> x18, local copies, waits for them, and re-layouts: 7.17 us -> 14.4 us
    ppermute x20 -> x18, starting transfers between devices: 26.1 us -> 23.2 us  [swap(): return lax.ppermute(array, axis, [(i, i ^ bit) for i in range(size)])]
  transfers between devices with their start and end apart: 24 -> 22, of which waited for: 6 -> 8; matrix products, arithmetic and copies ran while one was open for 12% -> 4% of each run, Pallas kernels for 20% -> 14%
where the time goes in v10:
time: 405 us; the launch traced here: 404 us
  waiting for transfers between devices  202 us (50%)
  Pallas kernels  85.3 us (21%)
  starting transfers between devices  38.3 us (9%)
  local copies, waits for them, and re-layouts  37.2 us (9%)
  blocking collectives  36.4 us (9%)
  other arithmetic  4.16 us (1%)
    ppermute x18, waiting for transfers between devices, swap(): return lax.ppermute(array, axis, [(i, i ^ bit) for i in range(size)])  201 us
    pallas_call x3, Pallas kernels, conv_call(): pl.pallas_call(body, grid_spec=pltpu.PrefetchScalarGridSpec(num_scalar_pr...  74.7 us
    all_to_all x1, blocking collectives, share(): lax.all_to_all(taps, 'img', 0, 0, axis_index_groups=members, tiled=True)  36.4 us
    ppermute x18, starting transfers between devices, swap(): return lax.ppermute(array, axis, [(i, i ^ bit) for i in range(size)])  23.2 us
    unnamed x18, local copies, waits for them, and re-layouts  14.4 us
    dynamic_update_slice x15, local copies, waits for them, and re-layouts, place(): lax.dynamic_update_slice(image, slots[j, r][None], (mine ^ j, start, 0, 0))  12.4 us
    all_to_all x2, starting transfers between devices, share(): lax.all_to_all(taps, 'img', 0, 0, axis_index_groups=members, tiled=True)  10.8 us
    pallas_call x2, Pallas kernels, by_member(): pl.pallas_call(body, grid=(count, across), in_specs=[pl.BlockSpec((1, 1,...  10.6 us
  transfers between devices with their start and end apart: 22, of which 8 were waited for; matrix products, arithmetic and copies ran while one was open for 4% of the time, Pallas kernels for 14%

profile of v10, /device:TPU:0, one launch (start us, length us, event | category | flops | bytes accessed | tf_op | source)
XLA Modules:
  0.0 404.0 jit_solution(17490280216490553729)
XLA Ops:
  0.0 2.4 slice_bitcast_fusion
  2.4 1.0 fusion.1
  3.4 1.3 collective-permute-start
  4.7 3.0 collective-permute-start.1
  7.8 0.9 collective-permute-done.1
  8.9 7.6 %collective-permute-start.2 = (bf16[13,56,1024]{2,1,0:T(8,128)(2,1)S(1)}, bf16[13,56,1024]{2,1,0:T(8,128)(2,1)}, u32[]{:S(2)}, u32[]{:S(2)}) collective-permute-start(bf16[13,56,1024]{2,1,0:T(8,128)(2,1)S(1)} %maximum_select_fusion.1), channel_id=1, source_target_pairs={{0,8},{2,10},{4,12},{6,14},{8,0},{10,2},{12,4},{14,6},{16,24},{18,... | collective-permute-start | bytes 4472840 | tf_op jit(solution)/shard_map/ppermute | solution.py:15
  16.5 1.5 collective-permute-start.4
  18.0 2.6 collective-permute-start.5
  20.6 5.3 %shard_map.37 = bf16[8,6,128,256]{3,2,1,0:T(8,128)(2,1)} custom-call(bf16[3,3,128,2048]{3,2,1,0:T(8,128)(2,1)} %taps.1), custom_call_target="tpu_custom_call" | custom-call | tf_op jit(solution)/shard_map/pallas_call | solution.py:156
  25.9 42.9 %collective-permute-done.5 = bf16[2,128,2048]{2,1,0:T(8,128)(2,1)} collective-permute-done((bf16[2,128,2048]{2,1,0:T(8,128)(2,1)}, bf16[2,128,2048]{2,1,0:T(8,128)(2,1)}, u32[]{:S(2)}, u32[]{:S(2)}) %collective-permute-start.5) | collective-permute-done | bytes 1048608 | tf_op jit(solution)/shard_map/ppermute | solution.py:15
  68.8 0.9 collective-permute-done.2
  69.7 1.1 copy-done.4
  70.8 5.5 %all-to-all-start = ((bf16[8,6,128,256]{3,2,1,0:T(8,128)(2,1)}), bf16[8,6,128,256]{3,2,1,0:T(8,128)(2,1)}, u32[]{:S(2)}, u32[]{:S(2)}) async-start(bf16[8,6,128,256]{3,2,1,0:T(8,128)(2,1)} %shard_map.37), calls=%async_computation | async-start | bytes 6291456 | tf_op jit(solution)/shard_map/all_to_all | solution.py:178
  76.3 1.1 slice_bitcast_fusion.1
  77.4 1.5 collective-permute-start.11
  79.9 42.4 %collective-permute-done.11 = bf16[1,128,2048]{2,1,0:T(8,128)(2,1)S(1)} collective-permute-done((bf16[1,128,2048]{2,1,0:T(8,128)(2,1)S(1)}, bf16[1,128,2048]{2,1,0:T(8,128)(2,1)S(1)}, u32[]{:S(2)}, u32[]{:S(2)}) %collective-permute-start.11) | collective-permute-done | bytes 524320 | tf_op jit(solution)/shard_map/ppermute | solution.py:15
  122.4 0.8 copy-done.8
  123.2 1.5 collective-permute-start.10
  124.7 1.2 copy-done.6
  125.9 32.1 %collective-permute-done.10 = bf16[13,56,1024]{2,1,0:T(8,128)(2,1)} collective-permute-done((bf16[13,56,1024]{2,1,0:T(8,128)(2,1)}, bf16[13,56,1024]{2,1,0:T(8,128)(2,1)}, u32[]{:S(2)}, u32[]{:S(2)}) %collective-permute-start.10) | collective-permute-done | bytes 1490976 | tf_op jit(solution)/shard_map/ppermute | solution.py:15
  158.0 1.5 maximum_bitcast_fusion
  159.5 1.9 pad_maximum_fusion.taps
  161.4 5.3 %shard_map.38 = bf16[8,6,128,256]{3,2,1,0:T(8,128)(2,1)} custom-call(bf16[2,3,128,2048]{3,2,1,0:T(8,128)(2,1)} %pad_maximum_fusion.taps), custom_call_target="tpu_custom_call" | custom-call | tf_op jit(solution)/shard_map/pallas_call | solution.py:156
  166.7 5.3 %all-to-all-start.1 = ((bf16[8,6,128,256]{3,2,1,0:T(8,128)(2,1)}), bf16[8,6,128,256]{3,2,1,0:T(8,128)(2,1)S(1)}, u32[]{:S(2)}, u32[]{:S(2)}) async-start(bf16[8,6,128,256]{3,2,1,0:T(8,128)(2,1)} %shard_map.38), calls=%async_computation.1 | async-start | bytes 6291456 | tf_op jit(solution)/shard_map/all_to_all | solution.py:178
  172.0 2.0 collective-permute-start.12
  174.1 3.3 broadcast_in_dim.52
  177.9 1.6 bitcast_dynamic-update-slice_fusion.14
  179.7 1.6 collective-permute-start.13
  181.2 1.6 bitcast_dynamic-update-slice_fusion.12
  183.1 1.7 collective-permute-start.19
  184.7 56.3 %collective-permute-done.12 = bf16[13,56,1024]{2,1,0:T(8,128)(2,1)} collective-permute-done((bf16[13,56,1024]{2,1,0:T(8,128)(2,1)}, bf16[13,56,1024]{2,1,0:T(8,128)(2,1)}, u32[]{:S(2)}, u32[]{:S(2)}) %collective-permute-start.12) | collective-permute-done | bytes 1490976 | tf_op jit(solution)/shard_map/ppermute | solution.py:15
  241.0 1.5 collective-permute-start.14
  242.5 1.6 bitcast_dynamic-update-slice_fusion.10
  244.1 1.6 bitcast_dynamic-update-slice_fusion.9
  245.7 1.6 bitcast_dynamic-update-slice_fusion.8
  247.3 0.6 collective-permute-start.17
  247.8 1.6 bitcast_dynamic-update-slice_fusion.7
  249.4 1.6 bitcast_dynamic-update-slice_fusion.6
  251.0 24.4 %collective-permute-done.14 = bf16[13,56,1024]{2,1,0:T(8,128)(2,1)S(1)} collective-permute-done((bf16[13,56,1024]{2,1,0:T(8,128)(2,1)}, bf16[13,56,1024]{2,1,0:T(8,128)(2,1)S(1)}, u32[]{:S(2)}, u32[]{:S(2)}) %collective-permute-start.14) | collective-permute-done | bytes 1490976 | tf_op jit(solution)/shard_map/ppermute | solution.py:15
  276.4 2.3 collective-permute-done.18
  278.9 8.6 %copy-done.1 = bf16[2,99,64,1024]{3,2,1,0:T(8,128)(2,1)} copy-done((bf16[2,99,64,1024]{3,2,1,0:T(8,128)(2,1)}, bf16[2,99,64,1024]{3,2,1,0:T(8,128)(2,1)S(1)}, u32[]{:S(2)}) %copy-start.1) | copy-done | bytes 25952280
  287.5 0.8 dynamic_slice.3
  288.2 24.7 %shard_map.39.refs_6_ = f32[96,64,256]{2,1,0:T(8,128)S(1)} custom-call(s32[2]{0:T(128)S(1)} %pad_add_fusion.scalars_ref, bf16[2,99,64,1024]{3,2,1,0:T(8,128)(2,1)} %copy-done.1, bf16[2,99,64,1024]{3,2,1,0:T(8,128)(2,1)} %copy-done.1, bf16[8,6,128,256]{3,2,1,0:T(8,128)(2,1)} %all-to-all-done.refs_2_), custom_call_target="tpu_custom_call" | custom-call | flops 1024 | bytes 1024 | tf_op jit(solution)/shard_map/pallas_call | solution.py:129
  313.0 2.7 copy-done
  315.7 25.0 %shard_map.40.refs_3_ = f32[96,64,256]{2,1,0:T(8,128)S(1)} custom-call(s32[2]{0:T(128)S(1)} %pad_add_fusion.scalars_ref, bf16[2,99,64,1024]{3,2,1,0:T(8,128)(2,1)} %copy-done.1, bf16[2,99,64,1024]{3,2,1,0:T(8,128)(2,1)} %copy-done.1, bf16[2,99,64,1024]{3,2,1,0:T(8,128)(2,1)} %copy-done.1, bf16[2,99,64,1024]{3,2,1,0:T(8,128)(2,1)} %copy-done.1, ...), custom_call_target="tpu_custom_call" | custom-call | flops 1024 | bytes 1024 | tf_op jit(solution)/shard_map/pallas_call | solution.py:129
  340.7 24.9 %shard_map.41 = bf16[96,56,256]{2,1,0:T(8,128)(2,1)S(1)} custom-call(s32[2]{0:T(128)S(1)} %pad_add_fusion.scalars_ref, bf16[2,99,64,1024]{3,2,1,0:T(8,128)(2,1)} %copy-done.1, bf16[2,99,64,1024]{3,2,1,0:T(8,128)(2,1)} %copy-done.1, bf16[8,6,128,256]{3,2,1,0:T(8,128)(2,1)} %collective-permute-done.19.refs_2_, f32[96,64,256]{2,1,0:T(8,128)S(1)} %shard_map.40.refs_3_, ...), custom_call_target="tpu_custom_call" | custom-call | flops 1024 | bytes 1024 | tf_op jit(solution)/shard_map/pallas_call | solution.py:129
  365.7 36.4 %all_to_all.15 = bf16[96,56,256]{2,1,0:T(8,128)(2,1)S(1)} all-to-all(bf16[96,56,256]{2,1,0:T(8,128)(2,1)S(1)} %shard_map.41), channel_id=1, replica_groups={{0,2,4,6,8,10,12,14},{16,18,20,22,24,26,28,30},{1,3,5,7,9,11,13,15},{17..., dimensions={0} | all-to-all | bytes 5505024 | tf_op jit(solution)/shard_map/all_to_all | solution.py:178
  402.1 1.9 copy.5
  (48 shorter events, 3.5 us)
Async XLA Ops:
  0.0 8.7 %copy-start.2 = (bf16[12,56,1024]{2,1,0:T(8,128)(2,1)S(1)}, bf16[12,56,1024]{2,1,0:T(8,128)(2,1)}, u32[]{:S(2)}) copy-start(bf16[12,56,1024]{2,1,0:T(8,128)(2,1)} %param.3) | copy-start | bytes 4128772
  3.4 4.4 %collective-permute-start = (bf16[1,56,1024]{2,1,0:T(8,128)(2,1)S(1)}, bf16[1,56,1024]{2,1,0:T(8,128)(2,1)S(1)}, u32[]{:S(2)}, u32[]{:S(2)}) collective-permute-start(bf16[1,56,1024]{2,1,0:T(8,128)(2,1)S(1)} %get-tuple-element.32), channel_id=1, source_target_pairs={{2,0},{4,2},{6,4},{8,6},{10,8},{12,10},{14,12},{16,14},{18,16},{20... | collective-permute-start | bytes 344072 | tf_op jit(solution)/shard_map/ppermute | solution.py:192
  4.7 4.0 collective-permute-start.1
  8.9 60.8 %collective-permute-start.2 = (bf16[13,56,1024]{2,1,0:T(8,128)(2,1)S(1)}, bf16[13,56,1024]{2,1,0:T(8,128)(2,1)}, u32[]{:S(2)}, u32[]{:S(2)}) collective-permute-start(bf16[13,56,1024]{2,1,0:T(8,128)(2,1)S(1)} %maximum_select_fusion.1), channel_id=1, source_target_pairs={{0,8},{2,10},{4,12},{6,14},{8,0},{10,2},{12,4},{14,6},{16,24},{18,... | collective-permute-start | bytes 4472840 | tf_op jit(solution)/shard_map/ppermute | solution.py:15
  16.5 53.2 %collective-permute-start.3 = (bf16[13,56,1024]{2,1,0:T(8,128)(2,1)S(1)}, bf16[13,56,1024]{2,1,0:T(8,128)(2,1)S(1)}, u32[]{:S(2)}, u32[]{:S(2)}) collective-permute-start(bf16[13,56,1024]{2,1,0:T(8,128)(2,1)S(1)} %maximum_select_fusion.1), channel_id=1, source_target_pairs={{0,4},{2,6},{4,0},{6,2},{8,12},{10,14},{12,8},{14,10},{16,20},{18,... | collective-permute-start | bytes 4472840 | tf_op jit(solution)/shard_map/ppermute | solution.py:15
  16.5 53.2 %collective-permute-start.4 = (bf16[13,56,1024]{2,1,0:T(8,128)(2,1)S(1)}, bf16[13,56,1024]{2,1,0:T(8,128)(2,1)}, u32[]{:S(2)}, u32[]{:S(2)}) collective-permute-start(bf16[13,56,1024]{2,1,0:T(8,128)(2,1)S(1)} %maximum_select_fusion.1), channel_id=1, source_target_pairs={{0,1},{1,0},{2,3},{3,2},{4,5},{5,4},{6,7},{7,6},{8,9},{9,8},{10,11... | collective-permute-start | bytes 4472840 | tf_op jit(solution)/shard_map/ppermute | solution.py:15
  18.0 50.8 %collective-permute-start.5 = (bf16[2,128,2048]{2,1,0:T(8,128)(2,1)}, bf16[2,128,2048]{2,1,0:T(8,128)(2,1)}, u32[]{:S(2)}, u32[]{:S(2)}) collective-permute-start(bf16[2,128,2048]{2,1,0:T(8,128)(2,1)} %slice_bitcast_fusion), channel_id=1, source_target_pairs={{0,16},{2,18},{4,20},{6,22},{8,24},{10,26},{12,28},{14,30},{16,0},... | collective-permute-start | bytes 3145736 | tf_op jit(solution)/shard_map/ppermute | solution.py:15
  69.7 1.1 copy-start.4
  70.8 87.2 %all-to-all-start = ((bf16[8,6,128,256]{3,2,1,0:T(8,128)(2,1)}), bf16[8,6,128,256]{3,2,1,0:T(8,128)(2,1)}, u32[]{:S(2)}, u32[]{:S(2)}) async-start(bf16[8,6,128,256]{3,2,1,0:T(8,128)(2,1)} %shard_map.37), calls=%async_computation | async-start | bytes 6291456 | tf_op jit(solution)/shard_map/all_to_all | solution.py:178
  77.4 82.2 %slice-start = ((bf16[3,3,128,2048]{3,2,1,0:T(8,128)(2,1)}), bf16[1,3,128,2048]{3,2,1,0:T(8,128)(2,1)S(1)}, s32[]{:S(2)}) async-start(bf16[3,3,128,2048]{3,2,1,0:T(8,128)(2,1)} %taps.1), calls=%async_computation.3 | async-start | bytes 3145728 | tf_op jit(solution)/shard_map/slice | solution.py:240
  77.4 45.0 %collective-permute-start.11 = (bf16[1,128,2048]{2,1,0:T(8,128)(2,1)S(1)}, bf16[1,128,2048]{2,1,0:T(8,128)(2,1)S(1)}, u32[]{:S(2)}, u32[]{:S(2)}) collective-permute-start(bf16[1,128,2048]{2,1,0:T(8,128)(2,1)S(1)} %slice_bitcast_fusion.1), channel_id=1, source_target_pairs={{0,16},{2,18},{4,20},{6,22},{8,24},{10,26},{12,28},{14,30},{16,0},... | collective-permute-start | bytes 1572872 | tf_op jit(solution)/shard_map/ppermute | solution.py:15
  78.9 45.8 %collective-permute-start.6 = (bf16[13,56,1024]{2,1,0:T(8,128)(2,1)S(1)}, bf16[13,56,1024]{2,1,0:T(8,128)(2,1)S(1)}, u32[]{:S(2)}, u32[]{:S(2)}) collective-permute-start(bf16[13,56,1024]{2,1,0:T(8,128)(2,1)S(1)} %maximum_select_fusion.1), channel_id=1, source_target_pairs={{0,2},{2,0},{4,6},{6,4},{8,10},{10,8},{12,14},{14,12},{16,18},{18,... | collective-permute-start | bytes 4472840 | tf_op jit(solution)/shard_map/ppermute | solution.py:15
  79.0 46.9 %collective-permute-start.7 = (bf16[13,56,1024]{2,1,0:T(8,128)(2,1)}, bf16[13,56,1024]{2,1,0:T(8,128)(2,1)}, u32[]{:S(2)}, u32[]{:S(2)}) collective-permute-start(bf16[13,56,1024]{2,1,0:T(8,128)(2,1)} %collective-permute-done.2), channel_id=1, source_target_pairs={{0,2},{2,0},{4,6},{6,4},{8,10},{10,8},{12,14},{14,12},{16,18},{18,... | collective-permute-start | bytes 4472840 | tf_op jit(solution)/shard_map/ppermute | solution.py:15
  79.4 46.4 %collective-permute-start.8 = (bf16[13,56,1024]{2,1,0:T(8,128)(2,1)}, bf16[13,56,1024]{2,1,0:T(8,128)(2,1)}, u32[]{:S(2)}, u32[]{:S(2)}) collective-permute-start(bf16[13,56,1024]{2,1,0:T(8,128)(2,1)} %copy-done.4), channel_id=1, source_target_pairs={{0,2},{2,0},{4,6},{6,4},{8,10},{10,8},{12,14},{14,12},{16,18},{18,... | collective-permute-start | bytes 4472840 | tf_op jit(solution)/shard_map/ppermute | solution.py:15
  79.5 46.4 %collective-permute-start.9 = (bf16[13,56,1024]{2,1,0:T(8,128)(2,1)}, bf16[13,56,1024]{2,1,0:T(8,128)(2,1)}, u32[]{:S(2)}, u32[]{:S(2)}) collective-permute-start(bf16[13,56,1024]{2,1,0:T(8,128)(2,1)} %collective-permute-done.4), channel_id=1, source_target_pairs={{0,2},{2,0},{4,6},{6,4},{8,10},{10,8},{12,14},{14,12},{16,18},{18,... | collective-permute-start | bytes 4472840 | tf_op jit(solution)/shard_map/ppermute | solution.py:15
  122.4 0.8 copy-start.8
  123.2 34.8 %collective-permute-start.10 = (bf16[13,56,1024]{2,1,0:T(8,128)(2,1)}, bf16[13,56,1024]{2,1,0:T(8,128)(2,1)}, u32[]{:S(2)}, u32[]{:S(2)}) collective-permute-start(bf16[13,56,1024]{2,1,0:T(8,128)(2,1)} %collective-permute-done.2), channel_id=1, source_target_pairs={{0,1},{1,0},{2,3},{3,2},{4,5},{5,4},{6,7},{7,6},{8,9},{9,8},{10,11... | collective-permute-start | bytes 4472840 | tf_op jit(solution)/shard_map/ppermute | solution.py:15
  124.7 1.2 copy-start.6
  166.7 149.0 %all-to-all-start.1 = ((bf16[8,6,128,256]{3,2,1,0:T(8,128)(2,1)}), bf16[8,6,128,256]{3,2,1,0:T(8,128)(2,1)S(1)}, u32[]{:S(2)}, u32[]{:S(2)}) async-start(bf16[8,6,128,256]{3,2,1,0:T(8,128)(2,1)} %shard_map.38), calls=%async_computation.1 | async-start | bytes 6291456 | tf_op jit(solution)/shard_map/all_to_all | solution.py:178
  172.0 69.0 %collective-permute-start.12 = (bf16[13,56,1024]{2,1,0:T(8,128)(2,1)}, bf16[13,56,1024]{2,1,0:T(8,128)(2,1)}, u32[]{:S(2)}, u32[]{:S(2)}) collective-permute-start(bf16[13,56,1024]{2,1,0:T(8,128)(2,1)} %collective-permute-done.2), channel_id=1, source_target_pairs={{0,4},{2,6},{4,0},{6,2},{8,12},{10,14},{12,8},{14,10},{16,20},{18,... | collective-permute-start | bytes 4472840 | tf_op jit(solution)/shard_map/ppermute | solution.py:15
  174.1 3.3 copy-start.3
  177.4 2.0 copy-start.5
  179.5 3.4 copy-start.7
  179.7 67.6 %collective-permute-start.13 = (bf16[13,56,1024]{2,1,0:T(8,128)(2,1)S(1)}, bf16[13,56,1024]{2,1,0:T(8,128)(2,1)S(1)}, u32[]{:S(2)}, u32[]{:S(2)}) collective-permute-start(bf16[13,56,1024]{2,1,0:T(8,128)(2,1)S(1)} %copy-done.5), channel_id=1, source_target_pairs={{0,1},{1,0},{2,3},{3,2},{4,5},{5,4},{6,7},{7,6},{8,9},{9,8},{10,11... | collective-permute-start | bytes 4472840 | tf_op jit(solution)/shard_map/ppermute | solution.py:15
  182.8 93.2 %collective-permute-start.16 = (bf16[13,56,1024]{2,1,0:T(8,128)(2,1)}, bf16[13,56,1024]{2,1,0:T(8,128)(2,1)S(1)}, u32[]{:S(2)}, u32[]{:S(2)}) collective-permute-start(bf16[13,56,1024]{2,1,0:T(8,128)(2,1)} %collective-permute-done.10), channel_id=1, source_target_pairs={{0,2},{2,0},{4,6},{6,4},{8,10},{10,8},{12,14},{14,12},{16,18},{18,... | collective-permute-start | bytes 4472840 | tf_op jit(solution)/shard_map/ppermute | solution.py:15
  183.1 157.7 %collective-permute-start.19 = (bf16[8,6,128,256]{3,2,1,0:T(8,128)(2,1)}, bf16[8,6,128,256]{3,2,1,0:T(8,128)(2,1)}, u32[]{:S(2)}, u32[]{:S(2)}) collective-permute-start(bf16[8,6,128,256]{3,2,1,0:T(8,128)(2,1)} %all-to-all-done.refs_2_), channel_id=1, source_target_pairs={{0,16},{2,18},{4,20},{6,22},{8,24},{10,26},{12,28},{14,30},{16,0},... | collective-permute-start | bytes 9437192 | tf_op jit(solution)/shard_map/ppermute | solution.py:15
  241.0 34.4 %collective-permute-start.14 = (bf16[13,56,1024]{2,1,0:T(8,128)(2,1)}, bf16[13,56,1024]{2,1,0:T(8,128)(2,1)S(1)}, u32[]{:S(2)}, u32[]{:S(2)}) collective-permute-start(bf16[13,56,1024]{2,1,0:T(8,128)(2,1)} %collective-permute-done.12), channel_id=1, source_target_pairs={{0,1},{1,0},{2,3},{3,2},{4,5},{5,4},{6,7},{7,6},{8,9},{9,8},{10,11... | collective-permute-start | bytes 4472840 | tf_op jit(solution)/shard_map/ppermute | solution.py:15
  245.6 30.2 %collective-permute-start.15 = (bf16[13,56,1024]{2,1,0:T(8,128)(2,1)}, bf16[13,56,1024]{2,1,0:T(8,128)(2,1)S(1)}, u32[]{:S(2)}, u32[]{:S(2)}) collective-permute-start(bf16[13,56,1024]{2,1,0:T(8,128)(2,1)} %collective-permute-done.12), channel_id=1, source_target_pairs={{0,2},{2,0},{4,6},{6,4},{8,10},{10,8},{12,14},{14,12},{16,18},{18,... | collective-permute-start | bytes 4472840 | tf_op jit(solution)/shard_map/ppermute | solution.py:15
  247.3 28.9 %collective-permute-start.17 = (bf16[13,56,1024]{2,1,0:T(8,128)(2,1)S(1)}, bf16[13,56,1024]{2,1,0:T(8,128)(2,1)S(1)}, u32[]{:S(2)}, u32[]{:S(2)}) collective-permute-start(bf16[13,56,1024]{2,1,0:T(8,128)(2,1)S(1)} %collective-permute-done.13), channel_id=1, source_target_pairs={{0,2},{2,0},{4,6},{6,4},{8,10},{10,8},{12,14},{14,12},{16,18},{18,... | collective-permute-start | bytes 4472840 | tf_op jit(solution)/shard_map/ppermute | solution.py:15
  275.4 3.3 collective-permute-start.18
  278.9 8.6 %copy-start.1 = (bf16[2,99,64,1024]{3,2,1,0:T(8,128)(2,1)}, bf16[2,99,64,1024]{3,2,1,0:T(8,128)(2,1)S(1)}, u32[]{:S(2)}) copy-start(bf16[2,99,64,1024]{3,2,1,0:T(8,128)(2,1)S(1)} %bitcast_dynamic-update-slice_fusion.refs_0_.refs_1_.refs_2_.refs_3_) | copy-start | bytes 77856768
  313.0 2.7 copy-start

commit v11 on v7

--- a/solution.py
+++ b/solution.py
@@ -233,7 +233,7 @@
     ready = [lower, *(slots[j, 4] for j in others), *taken_last]
     ready += [slots[j, r + 1] for j, r in keys]
 
-    cuts = (0, GROUP // 4, GROUP // 2, GROUP)
+    cuts = (0, GROUP // 4, GROUP - GROUP // 4, GROUP)
     chunks = [lower[a:b] for a, b in zip(cuts, cuts[1:])]
     received = [exchange(step(chunks[0]))]
     over_ch(2)
@@ -257,9 +257,7 @@
     over_core(keys)
     image = place(image, keys)
     image = place(image, [(j, r + 1) for j, r in keys])
-    ready = [*received[1], *(slots[j, 6] for j in others), image]
-
-    received.append(exchange(step(chunks[2])))
+    ready = []
     keys = [(j, 6) for j in others]
     over_core(keys)
     image = place(image, keys)
@@ -282,6 +280,7 @@
         ]
 
     acc = conv_call([(which[0], 0, lower, lower.shape, at_start, (1, 2))], scalars, image)
+    received.append(exchange(after(chunks[2], *received[1], acc, upper)))
     acc = conv_call(every + pieces((0, 1)), scalars, image, acc)
     out = conv_call(pieces((2,)), scalars, image, acc, bias)
     out = share(out).reshape(GROUP, rows, side, split)

time: 357 us -> 348 us (0.975)
  waiting for transfers between devices: 136 us -> 130 us
    ppermute x20, waiting for transfers between devices: 135 us -> 129 us  [swap(): return lax.ppermute(array, axis, [(i, i ^ bit) for i in range(size)])]
  transfers between devices with their start and end apart: 24 -> 24, of which waited for: 6 -> 6; matrix products, arithmetic and copies ran while one was open for 12% -> 12% of each run, Pallas kernels for 20% -> 22%
where the time goes in v11:
time: 348 us; the launch traced here: 346 us
  waiting for transfers between devices  130 us (37%)
  Pallas kernels  86.3 us (25%)
  local copies, waits for them, and re-layouts  52.1 us (15%)
  starting transfers between devices  38 us (11%)
  blocking collectives  37.3 us (11%)
    ppermute x20, waiting for transfers between devices, swap(): return lax.ppermute(array, axis, [(i, i ^ bit) for i in range(size)])  129 us
    pallas_call x3, Pallas kernels, conv_call(): pl.pallas_call(body, grid_spec=pltpu.PrefetchScalarGridSpec(num_scalar_pr...  75.6 us
    all_to_all x1, blocking collectives, share(): lax.all_to_all(taps, 'img', 0, 0, axis_index_groups=members, tiled=True)  37.3 us
    dynamic_update_slice x15, local copies, waits for them, and re-layouts, place(): lax.dynamic_update_slice(image, slots[j, r][None], (mine ^ j, start, 0, 0))  31.7 us
    ppermute x20, starting transfers between devices, swap(): return lax.ppermute(array, axis, [(i, i ^ bit) for i in range(size)])  22.9 us
    all_to_all x2, starting transfers between devices, share(): lax.all_to_all(taps, 'img', 0, 0, axis_index_groups=members, tiled=True)  10.8 us
    pallas_call x2, Pallas kernels, by_member(): pl.pallas_call(body, grid=(count, across), in_specs=[pl.BlockSpec((1, 1,...  10.7 us
    unnamed x30, local copies, waits for them, and re-layouts  7.7 us
  transfers between devices with their start and end apart: 24, of which 6 were waited for; matrix products, arithmetic and copies ran while one was open for 12% of the time, Pallas kernels for 22%

profile of v11, /device:TPU:0, one launch (start us, length us, event | category | flops | bytes accessed | tf_op | source)
XLA Modules:
  0.0 346.3 jit_solution(3145681290026477614)
XLA Ops:
  0.0 2.4 slice_bitcast_fusion
  2.4 1.0 fusion.2
  3.4 1.3 collective-permute-start
  4.7 3.0 collective-permute-start.1
  7.8 0.9 collective-permute-done.1
  9.0 7.6 %collective-permute-start.2 = (bf16[13,56,1024]{2,1,0:T(8,128)(2,1)S(1)}, bf16[13,56,1024]{2,1,0:T(8,128)(2,1)}, u32[]{:S(2)}, u32[]{:S(2)}) collective-permute-start(bf16[13,56,1024]{2,1,0:T(8,128)(2,1)S(1)} %maximum_select_fusion.1), channel_id=1, source_target_pairs={{0,8},{2,10},{4,12},{6,14},{8,0},{10,2},{12,4},{14,6},{16,24},{18,... | collective-permute-start | bytes 4472840 | tf_op jit(solution)/shard_map/ppermute | solution.py:15
  16.5 1.5 collective-permute-start.4
  18.0 2.6 collective-permute-start.5
  20.6 5.3 %shard_map.37 = bf16[8,6,128,256]{3,2,1,0:T(8,128)(2,1)} custom-call(bf16[3,3,128,2048]{3,2,1,0:T(8,128)(2,1)} %taps.1), custom_call_target="tpu_custom_call" | custom-call | tf_op jit(solution)/shard_map/pallas_call | solution.py:156
  26.0 42.8 %collective-permute-done.5 = bf16[2,128,2048]{2,1,0:T(8,128)(2,1)S(1)} collective-permute-done((bf16[2,128,2048]{2,1,0:T(8,128)(2,1)}, bf16[2,128,2048]{2,1,0:T(8,128)(2,1)S(1)}, u32[]{:S(2)}, u32[]{:S(2)}) %collective-permute-start.5) | collective-permute-done | bytes 1048608 | tf_op jit(solution)/shard_map/ppermute | solution.py:15
  69.8 6.3 %all-to-all-start = ((bf16[8,6,128,256]{3,2,1,0:T(8,128)(2,1)}), bf16[8,6,128,256]{3,2,1,0:T(8,128)(2,1)S(1)}, u32[]{:S(2)}, u32[]{:S(2)}) async-start(bf16[8,6,128,256]{3,2,1,0:T(8,128)(2,1)} %shard_map.37), calls=%async_computation | async-start | bytes 6291456 | tf_op jit(solution)/shard_map/all_to_all | solution.py:178
  76.6 1.9 slice_bitcast_fusion.1
  78.5 3.3 broadcast_in_dim.52
  82.2 1.6 collective-permute-start.10
  84.3 1.6 bitcast_dynamic-update-slice_fusion.14
  85.8 1.6 bitcast_dynamic-update-slice_fusion.13
  87.4 1.6 bitcast_dynamic-update-slice_fusion.12
  89.8 1.6 bitcast_dynamic-update-slice_fusion.11
  91.4 1.6 bitcast_dynamic-update-slice_fusion.10
  92.9 29.2 %collective-permute-done.11 = bf16[1,128,2048]{2,1,0:T(8,128)(2,1)S(1)} collective-permute-done((bf16[1,128,2048]{2,1,0:T(8,128)(2,1)S(1)}, bf16[1,128,2048]{2,1,0:T(8,128)(2,1)S(1)}, u32[]{:S(2)}, u32[]{:S(2)}) %collective-permute-start.11) | collective-permute-done | bytes 524320 | tf_op jit(solution)/shard_map/ppermute | solution.py:15
  123.5 1.1 copy-done.8
  124.7 1.6 collective-permute-start.14
  126.2 1.6 collective-permute-start.13
  127.9 2.7 bitcast_dynamic-update-slice_fusion.9
  130.5 1.3 bitcast_dynamic-update-slice_fusion.8
  131.8 1.3 fusion.1
  133.1 3.4 collective-permute-start.15
  136.5 2.6 bitcast_dynamic-update-slice_fusion.7
  139.3 1.9 pad_maximum_fusion.taps
  141.2 5.3 %shard_map.38 = bf16[8,6,128,256]{3,2,1,0:T(8,128)(2,1)} custom-call(bf16[2,3,128,2048]{3,2,1,0:T(8,128)(2,1)} %pad_maximum_fusion.taps), custom_call_target="tpu_custom_call" | custom-call | tf_op jit(solution)/shard_map/pallas_call | solution.py:156
  146.5 24.6 %collective-permute-done.15.refs_7_ = bf16[2,6,128,256]{3,2,1,0:T(8,128)(2,1)} collective-permute-done((bf16[2,6,128,256]{3,2,1,0:T(8,128)(2,1)}, bf16[2,6,128,256]{3,2,1,0:T(8,128)(2,1)}, u32[]{:S(2)}, u32[]{:S(2)}) %collective-permute-start.15) | collective-permute-done | bytes 786464 | tf_op jit(solution)/shard_map/ppermute | solution.py:15
  171.2 4.5 %all-to-all-start.1 = ((bf16[8,6,128,256]{3,2,1,0:T(8,128)(2,1)}), bf16[8,6,128,256]{3,2,1,0:T(8,128)(2,1)}, u32[]{:S(2)}, u32[]{:S(2)}) async-start(bf16[8,6,128,256]{3,2,1,0:T(8,128)(2,1)} %shard_map.38), calls=%async_computation.1 | async-start | bytes 6291456 | tf_op jit(solution)/shard_map/all_to_all | solution.py:178
  177.1 2.7 bitcast_dynamic-update-slice_fusion.6
  179.8 31.1 %collective-permute-done.18 = bf16[13,56,1024]{2,1,0:T(8,128)(2,1)} collective-permute-done((bf16[13,56,1024]{2,1,0:T(8,128)(2,1)}, bf16[13,56,1024]{2,1,0:T(8,128)(2,1)}, u32[]{:S(2)}, u32[]{:S(2)}) %collective-permute-start.18) | collective-permute-done | bytes 1490976 | tf_op jit(solution)/shard_map/ppermute | solution.py:15
  210.9 2.6 bitcast_dynamic-update-slice_fusion.5
  213.5 2.7 bitcast_dynamic-update-slice_fusion.4
  216.2 2.7 bitcast_dynamic-update-slice_fusion.3
  218.9 2.7 bitcast_dynamic-update-slice_fusion.2
  221.6 2.6 bitcast_dynamic-update-slice_fusion.1
  224.2 1.3 bitcast_dynamic-update-slice_fusion.refs_0_.refs_1_.refs_2_.refs_3_.refs_4_
  225.5 23.7 %shard_map.39.refs_9_ = f32[96,64,256]{2,1,0:T(8,128)S(1)} custom-call(s32[2]{0:T(128)S(1)} %pad_add_fusion.scalars_ref, bf16[2,99,64,1024]{3,2,1,0:T(8,128)(2,1)} %bitcast_dynamic-update-slice_fusion.refs_0_.refs_1_.refs_2_.refs_3_.refs_4_, bf16[2,99,64,1024]{3,2,1,0:T(8,128)(2,1)} %bitcast_dynamic-update-slice_fusion.refs_0_.refs_1_.refs_2_.refs_3_.refs_4_, ...), custom_call_target="tpu_custom_call" | custom-call | flops 1024 | bytes 1024 | tf_op jit(solution)/shard_map/pallas_call | solution.py:129
  249.2 2.6 copy-done
  251.8 1.1 copy-done.1
  253.8 1.4 copy-done.2
  255.2 41.4 %shard_map.40.refs_3_ = f32[96,64,256]{2,1,0:T(8,128)S(1)} custom-call(s32[2]{0:T(128)S(1)} %pad_add_fusion.scalars_ref, bf16[2,99,64,1024]{3,2,1,0:T(8,128)(2,1)} %bitcast_dynamic-update-slice_fusion.refs_0_.refs_1_.refs_2_.refs_3_.refs_4_, bf16[2,99,64,1024]{3,2,1,0:T(8,128)(2,1)} %bitcast_dynamic-update-slice_fusion.refs_0_.refs_1_.refs_2_.refs_3_.refs_4_, ...), custom_call_target="tpu_custom_call" | custom-call | flops 1024 | bytes 1024 | tf_op jit(solution)/shard_map/pallas_call | solution.py:129
  296.6 10.5 %shard_map.41 = bf16[96,56,256]{2,1,0:T(8,128)(2,1)S(1)} custom-call(s32[2]{0:T(128)S(1)} %pad_add_fusion.scalars_ref, bf16[2,99,64,1024]{3,2,1,0:T(8,128)(2,1)} %bitcast_dynamic-update-slice_fusion.refs_0_.refs_1_.refs_2_.refs_3_.refs_4_, bf16[2,99,64,1024]{3,2,1,0:T(8,128)(2,1)} %bitcast_dynamic-update-slice_fusion.refs_0_.refs_1_.refs_2_.refs_3_.refs_4_, ...), custom_call_target="tpu_custom_call" | custom-call | flops 1024 | bytes 1024 | tf_op jit(solution)/shard_map/pallas_call | solution.py:129
  307.1 37.3 %all_to_all.15 = bf16[96,56,256]{2,1,0:T(8,128)(2,1)S(1)} all-to-all(bf16[96,56,256]{2,1,0:T(8,128)(2,1)S(1)} %shard_map.41), channel_id=1, replica_groups={{0,2,4,6,8,10,12,14},{16,18,20,22,24,26,28,30},{1,3,5,7,9,11,13,15},{17..., dimensions={0} | all-to-all | bytes 5505024 | tf_op jit(solution)/shard_map/all_to_all | solution.py:178
  344.4 1.9 copy.5
  (66 shorter events, 7.2 us)
Async XLA Ops:
  0.0 8.7 %copy-start.4 = (bf16[12,56,1024]{2,1,0:T(8,128)(2,1)S(1)}, bf16[12,56,1024]{2,1,0:T(8,128)(2,1)}, u32[]{:S(2)}) copy-start(bf16[12,56,1024]{2,1,0:T(8,128)(2,1)} %param.3) | copy-start | bytes 4128772
  3.4 4.4 %collective-permute-start = (bf16[1,56,1024]{2,1,0:T(8,128)(2,1)S(1)}, bf16[1,56,1024]{2,1,0:T(8,128)(2,1)S(1)}, u32[]{:S(2)}, u32[]{:S(2)}) collective-permute-start(bf16[1,56,1024]{2,1,0:T(8,128)(2,1)S(1)} %get-tuple-element.46), channel_id=1, source_target_pairs={{2,0},{4,2},{6,4},{8,6},{10,8},{12,10},{14,12},{16,14},{18,16},{20... | collective-permute-start | bytes 344072 | tf_op jit(solution)/shard_map/ppermute | solution.py:192
  4.7 4.0 %collective-permute-start.1 = (bf16[1,56,1024]{2,1,0:T(8,128)(2,1)S(1)}, bf16[1,56,1024]{2,1,0:T(8,128)(2,1)S(1)}, u32[]{:S(2)}, u32[]{:S(2)}) collective-permute-start(bf16[1,56,1024]{2,1,0:T(8,128)(2,1)S(1)} %get-tuple-element.45), channel_id=1, source_target_pairs={{0,2},{2,4},{4,6},{6,8},{8,10},{10,12},{12,14},{14,16},{16,18},{18... | collective-permute-start | bytes 344072 | tf_op jit(solution)/shard_map/ppermute | solution.py:191
  8.9 17.0 %copy-start.6 = (bf16[13,56,1024]{2,1,0:T(8,128)(2,1)}, bf16[13,56,1024]{2,1,0:T(8,128)(2,1)S(1)}, u32[]{:S(2)}) copy-start(bf16[13,56,1024]{2,1,0:T(8,128)(2,1)S(1)} %maximum_select_fusion.1) | copy-start | bytes 4472836
  9.0 60.8 %collective-permute-start.2 = (bf16[13,56,1024]{2,1,0:T(8,128)(2,1)S(1)}, bf16[13,56,1024]{2,1,0:T(8,128)(2,1)}, u32[]{:S(2)}, u32[]{:S(2)}) collective-permute-start(bf16[13,56,1024]{2,1,0:T(8,128)(2,1)S(1)} %maximum_select_fusion.1), channel_id=1, source_target_pairs={{0,8},{2,10},{4,12},{6,14},{8,0},{10,2},{12,4},{14,6},{16,24},{18,... | collective-permute-start | bytes 4472840 | tf_op jit(solution)/shard_map/ppermute | solution.py:15
  16.5 53.2 %collective-permute-start.3 = (bf16[13,56,1024]{2,1,0:T(8,128)(2,1)S(1)}, bf16[13,56,1024]{2,1,0:T(8,128)(2,1)}, u32[]{:S(2)}, u32[]{:S(2)}) collective-permute-start(bf16[13,56,1024]{2,1,0:T(8,128)(2,1)S(1)} %maximum_select_fusion.1), channel_id=1, source_target_pairs={{0,4},{2,6},{4,0},{6,2},{8,12},{10,14},{12,8},{14,10},{16,20},{18,... | collective-permute-start | bytes 4472840 | tf_op jit(solution)/shard_map/ppermute | solution.py:15
  16.5 53.2 %collective-permute-start.4 = (bf16[13,56,1024]{2,1,0:T(8,128)(2,1)S(1)}, bf16[13,56,1024]{2,1,0:T(8,128)(2,1)}, u32[]{:S(2)}, u32[]{:S(2)}) collective-permute-start(bf16[13,56,1024]{2,1,0:T(8,128)(2,1)S(1)} %maximum_select_fusion.1), channel_id=1, source_target_pairs={{0,1},{1,0},{2,3},{3,2},{4,5},{5,4},{6,7},{7,6},{8,9},{9,8},{10,11... | collective-permute-start | bytes 4472840 | tf_op jit(solution)/shard_map/ppermute | solution.py:15
  18.0 50.8 %collective-permute-start.5 = (bf16[2,128,2048]{2,1,0:T(8,128)(2,1)}, bf16[2,128,2048]{2,1,0:T(8,128)(2,1)S(1)}, u32[]{:S(2)}, u32[]{:S(2)}) collective-permute-start(bf16[2,128,2048]{2,1,0:T(8,128)(2,1)} %slice_bitcast_fusion), channel_id=1, source_target_pairs={{0,16},{2,18},{4,20},{6,22},{8,24},{10,26},{12,28},{14,30},{16,0},... | collective-permute-start | bytes 3145736 | tf_op jit(solution)/shard_map/ppermute | solution.py:15
  68.8 1.0 copy-start.10
  69.8 54.8 %all-to-all-start = ((bf16[8,6,128,256]{3,2,1,0:T(8,128)(2,1)}), bf16[8,6,128,256]{3,2,1,0:T(8,128)(2,1)S(1)}, u32[]{:S(2)}, u32[]{:S(2)}) async-start(bf16[8,6,128,256]{3,2,1,0:T(8,128)(2,1)} %shard_map.37), calls=%async_computation | async-start | bytes 6291456 | tf_op jit(solution)/shard_map/all_to_all | solution.py:178
  76.1 12.9 %collective-permute-start.6 = (bf16[13,56,1024]{2,1,0:T(8,128)(2,1)}, bf16[13,56,1024]{2,1,0:T(8,128)(2,1)}, u32[]{:S(2)}, u32[]{:S(2)}) collective-permute-start(bf16[13,56,1024]{2,1,0:T(8,128)(2,1)} %copy-done.6), channel_id=1, source_target_pairs={{0,2},{2,0},{4,6},{6,4},{8,10},{10,8},{12,14},{14,12},{16,18},{18,... | collective-permute-start | bytes 4472840 | tf_op jit(solution)/shard_map/ppermute | solution.py:15
  76.6 14.8 %collective-permute-start.7 = (bf16[13,56,1024]{2,1,0:T(8,128)(2,1)}, bf16[13,56,1024]{2,1,0:T(8,128)(2,1)}, u32[]{:S(2)}, u32[]{:S(2)}) collective-permute-start(bf16[13,56,1024]{2,1,0:T(8,128)(2,1)} %collective-permute-done.2), channel_id=1, source_target_pairs={{0,2},{2,0},{4,6},{6,4},{8,10},{10,8},{12,14},{14,12},{16,18},{18,... | collective-permute-start | bytes 4472840 | tf_op jit(solution)/shard_map/ppermute | solution.py:15
  78.5 3.3 copy-start.5
  82.2 42.4 %collective-permute-start.10 = (bf16[13,56,1024]{2,1,0:T(8,128)(2,1)}, bf16[13,56,1024]{2,1,0:T(8,128)(2,1)}, u32[]{:S(2)}, u32[]{:S(2)}) collective-permute-start(bf16[13,56,1024]{2,1,0:T(8,128)(2,1)} %collective-permute-done.2), channel_id=1, source_target_pairs={{0,1},{1,0},{2,3},{3,2},{4,5},{5,4},{6,7},{7,6},{8,9},{9,8},{10,11... | collective-permute-start | bytes 4472840 | tf_op jit(solution)/shard_map/ppermute | solution.py:15
  83.7 38.4 %collective-permute-start.8 = (bf16[13,56,1024]{2,1,0:T(8,128)(2,1)}, bf16[13,56,1024]{2,1,0:T(8,128)(2,1)S(1)}, u32[]{:S(2)}, u32[]{:S(2)}) collective-permute-start(bf16[13,56,1024]{2,1,0:T(8,128)(2,1)} %collective-permute-done.3), channel_id=1, source_target_pairs={{0,2},{2,0},{4,6},{6,4},{8,10},{10,8},{12,14},{14,12},{16,18},{18,... | collective-permute-start | bytes 4472840 | tf_op jit(solution)/shard_map/ppermute | solution.py:15
  84.0 38.2 %collective-permute-start.9 = (bf16[13,56,1024]{2,1,0:T(8,128)(2,1)}, bf16[13,56,1024]{2,1,0:T(8,128)(2,1)S(1)}, u32[]{:S(2)}, u32[]{:S(2)}) collective-permute-start(bf16[13,56,1024]{2,1,0:T(8,128)(2,1)} %collective-permute-done.4), channel_id=1, source_target_pairs={{0,2},{2,0},{4,6},{6,4},{8,10},{10,8},{12,14},{14,12},{16,18},{18,... | collective-permute-start | bytes 4472840 | tf_op jit(solution)/shard_map/ppermute | solution.py:15
  85.8 3.2 copy-start.12
  89.0 33.1 %collective-permute-start.11 = (bf16[1,128,2048]{2,1,0:T(8,128)(2,1)S(1)}, bf16[1,128,2048]{2,1,0:T(8,128)(2,1)S(1)}, u32[]{:S(2)}, u32[]{:S(2)}) collective-permute-start(bf16[1,128,2048]{2,1,0:T(8,128)(2,1)S(1)} %copy-done.12), channel_id=1, source_target_pairs={{0,16},{2,18},{4,20},{6,22},{8,24},{10,26},{12,28},{14,30},{16,0},... | collective-permute-start | bytes 1572872 | tf_op jit(solution)/shard_map/ppermute | solution.py:15
  92.9 29.2 %copy-start.3 = (bf16[2,99,64,1024]{3,2,1,0:T(8,128)(2,1)}, bf16[2,99,64,1024]{3,2,1,0:T(8,128)(2,1)S(1)}, u32[]{:S(2)}) copy-start(bf16[2,99,64,1024]{3,2,1,0:T(8,128)(2,1)S(1)} %bitcast_dynamic-update-slice_fusion.10) | copy-start | bytes 77856768
  122.2 0.8 copy-start.13
  122.2 1.3 copy-start.7
  123.5 1.1 copy-start.8
  124.6 5.9 %copy-start.9 = (bf16[13,56,1024]{2,1,0:T(8,128)(2,1)S(1)}, bf16[13,56,1024]{2,1,0:T(8,128)(2,1)}, u32[]{:S(2)}) copy-start(bf16[13,56,1024]{2,1,0:T(8,128)(2,1)} %copy-done.8) | copy-start | bytes 4472836
  124.6 46.5 %collective-permute-start.12 = (bf16[13,56,1024]{2,1,0:T(8,128)(2,1)}, bf16[13,56,1024]{2,1,0:T(8,128)(2,1)}, u32[]{:S(2)}, u32[]{:S(2)}) collective-permute-start(bf16[13,56,1024]{2,1,0:T(8,128)(2,1)} %collective-permute-done.10), channel_id=1, source_target_pairs={{0,2},{2,0},{4,6},{6,4},{8,10},{10,8},{12,14},{14,12},{16,18},{18,... | collective-permute-start | bytes 4472840 | tf_op jit(solution)/shard_map/ppermute | solution.py:15
  124.7 46.5 %collective-permute-start.14 = (bf16[13,56,1024]{2,1,0:T(8,128)(2,1)}, bf16[13,56,1024]{2,1,0:T(8,128)(2,1)}, u32[]{:S(2)}, u32[]{:S(2)}) collective-permute-start(bf16[13,56,1024]{2,1,0:T(8,128)(2,1)} %collective-permute-done.3), channel_id=1, source_target_pairs={{0,1},{1,0},{2,3},{3,2},{4,5},{5,4},{6,7},{7,6},{8,9},{9,8},{10,11... | collective-permute-start | bytes 4472840 | tf_op jit(solution)/shard_map/ppermute | solution.py:15
  126.2 44.9 %collective-permute-start.13 = (bf16[13,56,1024]{2,1,0:T(8,128)(2,1)}, bf16[13,56,1024]{2,1,0:T(8,128)(2,1)}, u32[]{:S(2)}, u32[]{:S(2)}) collective-permute-start(bf16[13,56,1024]{2,1,0:T(8,128)(2,1)} %collective-permute-done.2), channel_id=1, source_target_pairs={{0,4},{2,6},{4,0},{6,2},{8,12},{10,14},{12,8},{14,10},{16,20},{18,... | collective-permute-start | bytes 4472840 | tf_op jit(solution)/shard_map/ppermute | solution.py:15
  131.8 7.3 %copy-start.11 = (bf16[2,128,2048]{2,1,0:T(8,128)(2,1)S(1)}, bf16[2,128,2048]{2,1,0:T(8,128)(2,1)}, u32[]{:S(2)}) copy-start(bf16[2,128,2048]{2,1,0:T(8,128)(2,1)} %copy-done.10) | copy-start | bytes 3145732
  131.8 7.3 %copy-start.14 = (bf16[1,128,2048]{2,1,0:T(8,128)(2,1)S(1)}, bf16[1,128,2048]{2,1,0:T(8,128)(2,1)}, u32[]{:S(2)}) copy-start(bf16[1,128,2048]{2,1,0:T(8,128)(2,1)} %copy-done.13) | copy-start | bytes 1572868
  133.1 6.2 %slice-start = ((bf16[3,3,128,2048]{3,2,1,0:T(8,128)(2,1)}), bf16[1,3,128,2048]{3,2,1,0:T(8,128)(2,1)S(1)}, s32[]{:S(2)}) async-start(bf16[3,3,128,2048]{3,2,1,0:T(8,128)(2,1)} %taps.1), calls=%async_computation.3 | async-start | bytes 3145728 | tf_op jit(solution)/shard_map/slice | solution.py:245
  133.1 38.1 %collective-permute-start.15 = (bf16[2,6,128,256]{3,2,1,0:T(8,128)(2,1)}, bf16[2,6,128,256]{3,2,1,0:T(8,128)(2,1)}, u32[]{:S(2)}, u32[]{:S(2)}) collective-permute-start(bf16[2,6,128,256]{3,2,1,0:T(8,128)(2,1)} %get-tuple-element.35), channel_id=1, source_target_pairs={{0,16},{2,18},{4,20},{6,22},{8,24},{10,26},{12,28},{14,30},{16,0},... | collective-permute-start | bytes 2359304 | tf_op jit(solution)/shard_map/ppermute | solution.py:15
  171.2 81.8 %all-to-all-start.1 = ((bf16[8,6,128,256]{3,2,1,0:T(8,128)(2,1)}), bf16[8,6,128,256]{3,2,1,0:T(8,128)(2,1)}, u32[]{:S(2)}, u32[]{:S(2)}) async-start(bf16[8,6,128,256]{3,2,1,0:T(8,128)(2,1)} %shard_map.38), calls=%async_computation.1 | async-start | bytes 6291456 | tf_op jit(solution)/shard_map/all_to_all | solution.py:178
  175.6 35.2 %collective-permute-start.18 = (bf16[13,56,1024]{2,1,0:T(8,128)(2,1)}, bf16[13,56,1024]{2,1,0:T(8,128)(2,1)}, u32[]{:S(2)}, u32[]{:S(2)}) collective-permute-start(bf16[13,56,1024]{2,1,0:T(8,128)(2,1)} %collective-permute-done.13), channel_id=1, source_target_pairs={{0,1},{1,0},{2,3},{3,2},{4,5},{5,4},{6,7},{7,6},{8,9},{9,8},{10,11... | collective-permute-start | bytes 4472840 | tf_op jit(solution)/shard_map/ppermute | solution.py:15
  176.3 39.9 %collective-permute-start.16 = (bf16[13,56,1024]{2,1,0:T(8,128)(2,1)}, bf16[13,56,1024]{2,1,0:T(8,128)(2,1)}, u32[]{:S(2)}, u32[]{:S(2)}) collective-permute-start(bf16[13,56,1024]{2,1,0:T(8,128)(2,1)} %collective-permute-done.13), channel_id=1, source_target_pairs={{0,2},{2,0},{4,6},{6,4},{8,10},{10,8},{12,14},{14,12},{16,18},{18,... | collective-permute-start | bytes 4472840 | tf_op jit(solution)/shard_map/ppermute | solution.py:15
  176.3 42.6 %collective-permute-start.17 = (bf16[13,56,1024]{2,1,0:T(8,128)(2,1)}, bf16[13,56,1024]{2,1,0:T(8,128)(2,1)}, u32[]{:S(2)}, u32[]{:S(2)}) collective-permute-start(bf16[13,56,1024]{2,1,0:T(8,128)(2,1)} %collective-permute-done.14), channel_id=1, source_target_pairs={{0,2},{2,0},{4,6},{6,4},{8,10},{10,8},{12,14},{14,12},{16,18},{18,... | collective-permute-start | bytes 4472840 | tf_op jit(solution)/shard_map/ppermute | solution.py:15
  177.0 74.8 %collective-permute-start.20 = (bf16[4,6,128,256]{3,2,1,0:T(8,128)(2,1)S(1)}, bf16[4,6,128,256]{3,2,1,0:T(8,128)(2,1)S(1)}, u32[]{:S(2)}, u32[]{:S(2)}) collective-permute-start(bf16[4,6,128,256]{3,2,1,0:T(8,128)(2,1)S(1)} %slice.34), channel_id=1, source_target_pairs={{0,16},{2,18},{4,20},{6,22},{8,24},{10,26},{12,28},{14,30},{16,0},... | collective-permute-start | bytes 4718600 | tf_op jit(solution)/shard_map/ppermute | solution.py:15
  210.9 13.3 %collective-permute-start.19 = (bf16[13,56,1024]{2,1,0:T(8,128)(2,1)}, bf16[13,56,1024]{2,1,0:T(8,128)(2,1)S(1)}, u32[]{:S(2)}, u32[]{:S(2)}) collective-permute-start(bf16[13,56,1024]{2,1,0:T(8,128)(2,1)} %collective-permute-done.18), channel_id=1, source_target_pairs={{0,2},{2,0},{4,6},{6,4},{8,10},{10,8},{12,14},{14,12},{16,18},{18,... | collective-permute-start | bytes 4472840 | tf_op jit(solution)/shard_map/ppermute | solution.py:15
  249.2 2.7 copy-start
  251.8 1.1 copy-start.1
  253.0 43.6 %collective-permute-start.21 = (bf16[2,6,128,256]{3,2,1,0:T(8,128)(2,1)}, bf16[2,6,128,256]{3,2,1,0:T(8,128)(2,1)S(1)}, u32[]{:S(2)}, u32[]{:S(2)}) collective-permute-start(bf16[2,6,128,256]{3,2,1,0:T(8,128)(2,1)} %get-tuple-element.42), channel_id=1, source_target_pairs={{0,16},{2,18},{4,20},{6,22},{8,24},{10,26},{12,28},{14,30},{16,0},... | collective-permute-start | bytes 2359304 | tf_op jit(solution)/shard_map/ppermute | solution.py:15
  253.8 1.4 copy-start.2

commit v12 on v11

--- a/solution.py
+++ b/solution.py
@@ -246,10 +246,10 @@
         jnp.concatenate([step(a), step(b)]) for a, b in zip(taken, taken_last)
     ]
     by_rank = by_member(jnp.stack(raw), 0, parts)
-    ready = [*received[0], slots[0, 6], *(slots[j, 2] for j in others), image, by_rank]
+    ready = [slots[0, 6], *(slots[j, 2] for j in others), image, by_rank]
     ready += [slots[j, r + 1] for j, r in keys]
 
-    received.append(exchange(step(chunks[1])))
+    received.append(exchange(after(chunks[1], *ready, *received[0])))
     over_ch(6)
     upper = share(step(by_rank))
     image = place(image, [(j, r + 1) for j, r in keys])

time: 348 us -> 386 us (1.11)
  waiting for transfers between devices: 130 us -> 164 us
    ppermute x20, waiting for transfers between devices: 129 us -> 162 us  [swap(): return lax.ppermute(array, axis, [(i, i ^ bit) for i in range(size)])]
  transfers between devices with their start and end apart: 24 -> 24, of which waited for: 6 -> 9; matrix products, arithmetic and copies ran while one was open for 12% -> 12% of each run, Pallas kernels for 22% -> 20%
where the time goes in v12:
time: 386 us; the launch traced here: 385 us
  waiting for transfers between devices  164 us (42%)
  Pallas kernels  86.2 us (22%)
  local copies, waits for them, and re-layouts  53.1 us (14%)
  starting transfers between devices  39.5 us (10%)
  blocking collectives  39.2 us (10%)
    ppermute x20, waiting for transfers between devices, swap(): return lax.ppermute(array, axis, [(i, i ^ bit) for i in range(size)])  162 us
    pallas_call x3, Pallas kernels, conv_call(): pl.pallas_call(body, grid_spec=pltpu.PrefetchScalarGridSpec(num_scalar_pr...  75.6 us
    all_to_all x1, blocking collectives, share(): lax.all_to_all(taps, 'img', 0, 0, axis_index_groups=members, tiled=True)  39.2 us
    dynamic_update_slice x15, local copies, waits for them, and re-layouts, place(): lax.dynamic_update_slice(image, slots[j, r][None], (mine ^ j, start, 0, 0))  34.4 us
    ppermute x20, starting transfers between devices, swap(): return lax.ppermute(array, axis, [(i, i ^ bit) for i in range(size)])  24.5 us
    all_to_all x2, starting transfers between devices, share(): lax.all_to_all(taps, 'img', 0, 0, axis_index_groups=members, tiled=True)  10.8 us
    pallas_call x2, Pallas kernels, by_member(): pl.pallas_call(body, grid=(count, across), in_specs=[pl.BlockSpec((1, 1,...  10.6 us
  transfers between devices with their start and end apart: 24, of which 9 were waited for; matrix products, arithmetic and copies ran while one was open for 12% of the time, Pallas kernels for 20%

profile of v12, /device:TPU:0, one launch (start us, length us, event | category | flops | bytes accessed | tf_op | source)
XLA Modules:
  0.0 384.9 jit_solution(15708232790342456687)
XLA Ops:
  0.0 2.4 slice_bitcast_fusion
  3.4 1.3 collective-permute-start
  4.7 3.0 collective-permute-start.1
  8.9 7.6 %collective-permute-start.2 = (bf16[13,56,1024]{2,1,0:T(8,128)(2,1)S(1)}, bf16[13,56,1024]{2,1,0:T(8,128)(2,1)}, u32[]{:S(2)}, u32[]{:S(2)}) collective-permute-start(bf16[13,56,1024]{2,1,0:T(8,128)(2,1)S(1)} %maximum_select_fusion.1), channel_id=1, source_target_pairs={{0,8},{2,10},{4,12},{6,14},{8,0},{10,2},{12,4},{14,6},{16,24},{18,... | collective-permute-start | bytes 4472840 | tf_op jit(solution)/shard_map/ppermute | solution.py:15
  16.5 1.5 collective-permute-start.4
  18.0 2.6 collective-permute-start.5
  20.6 5.3 %shard_map.37 = bf16[8,6,128,256]{3,2,1,0:T(8,128)(2,1)} custom-call(bf16[3,3,128,2048]{3,2,1,0:T(8,128)(2,1)} %taps.1), custom_call_target="tpu_custom_call" | custom-call | tf_op jit(solution)/shard_map/pallas_call | solution.py:156
  25.9 42.9 %collective-permute-done.5 = bf16[2,128,2048]{2,1,0:T(8,128)(2,1)S(1)} collective-permute-done((bf16[2,128,2048]{2,1,0:T(8,128)(2,1)}, bf16[2,128,2048]{2,1,0:T(8,128)(2,1)S(1)}, u32[]{:S(2)}, u32[]{:S(2)}) %collective-permute-start.5) | collective-permute-done | bytes 1048608 | tf_op jit(solution)/shard_map/ppermute | solution.py:15
  69.8 6.3 %all-to-all-start = ((bf16[8,6,128,256]{3,2,1,0:T(8,128)(2,1)}), bf16[8,6,128,256]{3,2,1,0:T(8,128)(2,1)S(1)}, u32[]{:S(2)}, u32[]{:S(2)}) async-start(bf16[8,6,128,256]{3,2,1,0:T(8,128)(2,1)} %shard_map.37), calls=%async_computation | async-start | bytes 6291456 | tf_op jit(solution)/shard_map/all_to_all | solution.py:178
  76.6 1.5 collective-permute-start.10
  78.6 1.9 slice_bitcast_fusion.1
  80.5 3.3 broadcast_in_dim.52
  84.2 1.6 bitcast_dynamic-update-slice_fusion.14
  85.8 1.6 bitcast_dynamic-update-slice_fusion.13
  88.2 1.6 bitcast_dynamic-update-slice_fusion.12
  89.7 1.6 bitcast_dynamic-update-slice_fusion.11
  91.3 30.9 %collective-permute-done.11 = bf16[1,128,2048]{2,1,0:T(8,128)(2,1)S(1)} collective-permute-done((bf16[1,128,2048]{2,1,0:T(8,128)(2,1)S(1)}, bf16[1,128,2048]{2,1,0:T(8,128)(2,1)S(1)}, u32[]{:S(2)}, u32[]{:S(2)}) %collective-permute-start.11) | collective-permute-done | bytes 524320 | tf_op jit(solution)/shard_map/ppermute | solution.py:15
  123.0 1.3 all-to-all-done.refs_2_
  124.3 1.5 collective-permute-start.14
  125.8 1.5 collective-permute-start.13
  127.2 2.6 bitcast_dynamic-update-slice_fusion.10
  129.9 2.7 bitcast_dynamic-update-slice_fusion.9
  132.5 2.7 bitcast_dynamic-update-slice_fusion.8
  135.3 2.8 bitcast_dynamic-update-slice_fusion.7
  138.2 1.9 pad_maximum_fusion.taps
  140.1 5.3 %shard_map.38 = bf16[8,6,128,256]{3,2,1,0:T(8,128)(2,1)} custom-call(bf16[2,3,128,2048]{3,2,1,0:T(8,128)(2,1)} %pad_maximum_fusion.taps), custom_call_target="tpu_custom_call" | custom-call | tf_op jit(solution)/shard_map/pallas_call | solution.py:156
  145.4 14.2 %collective-permute-done.14 = bf16[13,56,1024]{2,1,0:T(8,128)(2,1)} collective-permute-done((bf16[13,56,1024]{2,1,0:T(8,128)(2,1)}, bf16[13,56,1024]{2,1,0:T(8,128)(2,1)}, u32[]{:S(2)}, u32[]{:S(2)}) %collective-permute-start.14) | collective-permute-done | bytes 1490976 | tf_op jit(solution)/shard_map/ppermute | solution.py:15
  159.7 1.2 collective-permute-done.13
  160.9 4.5 %all-to-all-start.1 = ((bf16[8,6,128,256]{3,2,1,0:T(8,128)(2,1)}), bf16[8,6,128,256]{3,2,1,0:T(8,128)(2,1)}, u32[]{:S(2)}, u32[]{:S(2)}) async-start(bf16[8,6,128,256]{3,2,1,0:T(8,128)(2,1)} %shard_map.38), calls=%async_computation.1 | async-start | bytes 6291456 | tf_op jit(solution)/shard_map/all_to_all | solution.py:178
  165.9 1.3 fusion.1
  167.2 2.1 collective-permute-start.19
  170.0 47.0 %collective-permute-done.19.refs_7_ = bf16[2,6,128,256]{3,2,1,0:T(8,128)(2,1)} collective-permute-done((bf16[2,6,128,256]{3,2,1,0:T(8,128)(2,1)}, bf16[2,6,128,256]{3,2,1,0:T(8,128)(2,1)}, u32[]{:S(2)}, u32[]{:S(2)}) %collective-permute-start.19) | collective-permute-done | bytes 786464 | tf_op jit(solution)/shard_map/ppermute | solution.py:15
  217.0 3.4 collective-permute-start.20
  220.4 2.7 bitcast_dynamic-update-slice_fusion.6
  223.1 2.7 bitcast_dynamic-update-slice_fusion.5
  225.7 2.7 bitcast_dynamic-update-slice_fusion.4
  228.4 2.8 bitcast_dynamic-update-slice_fusion.3
  231.2 2.7 bitcast_dynamic-update-slice_fusion.2
  233.8 2.6 bitcast_dynamic-update-slice_fusion.1
  236.5 1.3 bitcast_dynamic-update-slice_fusion.refs_0_.refs_1_.refs_2_.refs_3_.refs_4_
  237.7 23.7 %shard_map.39.refs_9_ = f32[96,64,256]{2,1,0:T(8,128)S(1)} custom-call(s32[2]{0:T(128)S(1)} %pad_add_fusion.scalars_ref, bf16[2,99,64,1024]{3,2,1,0:T(8,128)(2,1)} %bitcast_dynamic-update-slice_fusion.refs_0_.refs_1_.refs_2_.refs_3_.refs_4_, bf16[2,99,64,1024]{3,2,1,0:T(8,128)(2,1)} %bitcast_dynamic-update-slice_fusion.refs_0_.refs_1_.refs_2_.refs_3_.refs_4_, ...), custom_call_target="tpu_custom_call" | custom-call | flops 1024 | bytes 1024 | tf_op jit(solution)/shard_map/pallas_call | solution.py:129
  261.4 2.6 copy-done
  264.1 24.5 %collective-permute-done.20.refs_8_ = bf16[4,6,128,256]{3,2,1,0:T(8,128)(2,1)S(1)} collective-permute-done((bf16[4,6,128,256]{3,2,1,0:T(8,128)(2,1)S(1)}, bf16[4,6,128,256]{3,2,1,0:T(8,128)(2,1)S(1)}, u32[]{:S(2)}, u32[]{:S(2)}) %collective-permute-start.20) | collective-permute-done | bytes 1572896 | tf_op jit(solution)/shard_map/ppermute | solution.py:15
  290.5 1.4 copy-done.2
  291.9 41.4 %shard_map.40.refs_3_ = f32[96,64,256]{2,1,0:T(8,128)S(1)} custom-call(s32[2]{0:T(128)S(1)} %pad_add_fusion.scalars_ref, bf16[2,99,64,1024]{3,2,1,0:T(8,128)(2,1)} %bitcast_dynamic-update-slice_fusion.refs_0_.refs_1_.refs_2_.refs_3_.refs_4_, bf16[2,99,64,1024]{3,2,1,0:T(8,128)(2,1)} %bitcast_dynamic-update-slice_fusion.refs_0_.refs_1_.refs_2_.refs_3_.refs_4_, ...), custom_call_target="tpu_custom_call" | custom-call | flops 1024 | bytes 1024 | tf_op jit(solution)/shard_map/pallas_call | solution.py:129
  333.3 10.5 %shard_map.41 = bf16[96,56,256]{2,1,0:T(8,128)(2,1)S(1)} custom-call(s32[2]{0:T(128)S(1)} %pad_add_fusion.scalars_ref, bf16[2,99,64,1024]{3,2,1,0:T(8,128)(2,1)} %bitcast_dynamic-update-slice_fusion.refs_0_.refs_1_.refs_2_.refs_3_.refs_4_, bf16[2,99,64,1024]{3,2,1,0:T(8,128)(2,1)} %bitcast_dynamic-update-slice_fusion.refs_0_.refs_1_.refs_2_.refs_3_.refs_4_, ...), custom_call_target="tpu_custom_call" | custom-call | flops 1024 | bytes 1024 | tf_op jit(solution)/shard_map/pallas_call | solution.py:129
  343.8 39.2 %all_to_all.15 = bf16[96,56,256]{2,1,0:T(8,128)(2,1)S(1)} all-to-all(bf16[96,56,256]{2,1,0:T(8,128)(2,1)S(1)} %shard_map.41), channel_id=1, replica_groups={{0,2,4,6,8,10,12,14},{16,18,20,22,24,26,28,30},{1,3,5,7,9,11,13,15},{17..., dimensions={0} | all-to-all | bytes 5505024 | tf_op jit(solution)/shard_map/all_to_all | solution.py:178
  383.0 1.9 copy.5
  (60 shorter events, 9.5 us)
Async XLA Ops:
  0.0 8.7 %copy-start.4 = (bf16[12,56,1024]{2,1,0:T(8,128)(2,1)S(1)}, bf16[12,56,1024]{2,1,0:T(8,128)(2,1)}, u32[]{:S(2)}) copy-start(bf16[12,56,1024]{2,1,0:T(8,128)(2,1)} %param.3) | copy-start | bytes 4128772
  3.4 4.4 %collective-permute-start = (bf16[1,56,1024]{2,1,0:T(8,128)(2,1)S(1)}, bf16[1,56,1024]{2,1,0:T(8,128)(2,1)S(1)}, u32[]{:S(2)}, u32[]{:S(2)}) collective-permute-start(bf16[1,56,1024]{2,1,0:T(8,128)(2,1)S(1)} %get-tuple-element.46), channel_id=1, source_target_pairs={{2,0},{4,2},{6,4},{8,6},{10,8},{12,10},{14,12},{16,14},{18,16},{20... | collective-permute-start | bytes 344072 | tf_op jit(solution)/shard_map/ppermute | solution.py:192
  4.7 4.0 %collective-permute-start.1 = (bf16[1,56,1024]{2,1,0:T(8,128)(2,1)S(1)}, bf16[1,56,1024]{2,1,0:T(8,128)(2,1)S(1)}, u32[]{:S(2)}, u32[]{:S(2)}) collective-permute-start(bf16[1,56,1024]{2,1,0:T(8,128)(2,1)S(1)} %get-tuple-element.45), channel_id=1, source_target_pairs={{0,2},{2,4},{4,6},{6,8},{8,10},{10,12},{12,14},{14,16},{16,18},{18... | collective-permute-start | bytes 344072 | tf_op jit(solution)/shard_map/ppermute | solution.py:191
  8.9 17.0 %copy-start.6 = (bf16[13,56,1024]{2,1,0:T(8,128)(2,1)}, bf16[13,56,1024]{2,1,0:T(8,128)(2,1)S(1)}, u32[]{:S(2)}) copy-start(bf16[13,56,1024]{2,1,0:T(8,128)(2,1)S(1)} %maximum_select_fusion.1) | copy-start | bytes 4472836
  8.9 60.8 %collective-permute-start.2 = (bf16[13,56,1024]{2,1,0:T(8,128)(2,1)S(1)}, bf16[13,56,1024]{2,1,0:T(8,128)(2,1)}, u32[]{:S(2)}, u32[]{:S(2)}) collective-permute-start(bf16[13,56,1024]{2,1,0:T(8,128)(2,1)S(1)} %maximum_select_fusion.1), channel_id=1, source_target_pairs={{0,8},{2,10},{4,12},{6,14},{8,0},{10,2},{12,4},{14,6},{16,24},{18,... | collective-permute-start | bytes 4472840 | tf_op jit(solution)/shard_map/ppermute | solution.py:15
  16.5 53.2 %collective-permute-start.3 = (bf16[13,56,1024]{2,1,0:T(8,128)(2,1)S(1)}, bf16[13,56,1024]{2,1,0:T(8,128)(2,1)}, u32[]{:S(2)}, u32[]{:S(2)}) collective-permute-start(bf16[13,56,1024]{2,1,0:T(8,128)(2,1)S(1)} %maximum_select_fusion.1), channel_id=1, source_target_pairs={{0,4},{2,6},{4,0},{6,2},{8,12},{10,14},{12,8},{14,10},{16,20},{18,... | collective-permute-start | bytes 4472840 | tf_op jit(solution)/shard_map/ppermute | solution.py:15
  16.5 53.2 %collective-permute-start.4 = (bf16[13,56,1024]{2,1,0:T(8,128)(2,1)S(1)}, bf16[13,56,1024]{2,1,0:T(8,128)(2,1)}, u32[]{:S(2)}, u32[]{:S(2)}) collective-permute-start(bf16[13,56,1024]{2,1,0:T(8,128)(2,1)S(1)} %maximum_select_fusion.1), channel_id=1, source_target_pairs={{0,1},{1,0},{2,3},{3,2},{4,5},{5,4},{6,7},{7,6},{8,9},{9,8},{10,11... | collective-permute-start | bytes 4472840 | tf_op jit(solution)/shard_map/ppermute | solution.py:15
  18.0 50.8 %collective-permute-start.5 = (bf16[2,128,2048]{2,1,0:T(8,128)(2,1)}, bf16[2,128,2048]{2,1,0:T(8,128)(2,1)S(1)}, u32[]{:S(2)}, u32[]{:S(2)}) collective-permute-start(bf16[2,128,2048]{2,1,0:T(8,128)(2,1)} %slice_bitcast_fusion), channel_id=1, source_target_pairs={{0,16},{2,18},{4,20},{6,22},{8,24},{10,26},{12,28},{14,30},{16,0},... | collective-permute-start | bytes 3145736 | tf_op jit(solution)/shard_map/ppermute | solution.py:15
  68.8 1.0 copy-start.7
  69.8 54.5 %all-to-all-start = ((bf16[8,6,128,256]{3,2,1,0:T(8,128)(2,1)}), bf16[8,6,128,256]{3,2,1,0:T(8,128)(2,1)S(1)}, u32[]{:S(2)}, u32[]{:S(2)}) async-start(bf16[8,6,128,256]{3,2,1,0:T(8,128)(2,1)} %shard_map.37), calls=%async_computation | async-start | bytes 6291456 | tf_op jit(solution)/shard_map/all_to_all | solution.py:178
  76.1 11.3 %collective-permute-start.6 = (bf16[13,56,1024]{2,1,0:T(8,128)(2,1)}, bf16[13,56,1024]{2,1,0:T(8,128)(2,1)}, u32[]{:S(2)}, u32[]{:S(2)}) collective-permute-start(bf16[13,56,1024]{2,1,0:T(8,128)(2,1)} %copy-done.6), channel_id=1, source_target_pairs={{0,2},{2,0},{4,6},{6,4},{8,10},{10,8},{12,14},{14,12},{16,18},{18,... | collective-permute-start | bytes 4472840 | tf_op jit(solution)/shard_map/ppermute | solution.py:15
  76.6 45.6 %collective-permute-start.7 = (bf16[13,56,1024]{2,1,0:T(8,128)(2,1)}, bf16[13,56,1024]{2,1,0:T(8,128)(2,1)}, u32[]{:S(2)}, u32[]{:S(2)}) collective-permute-start(bf16[13,56,1024]{2,1,0:T(8,128)(2,1)} %collective-permute-done.2), channel_id=1, source_target_pairs={{0,2},{2,0},{4,6},{6,4},{8,10},{10,8},{12,14},{14,12},{16,18},{18,... | collective-permute-start | bytes 4472840 | tf_op jit(solution)/shard_map/ppermute | solution.py:15
  76.6 46.4 %collective-permute-start.10 = (bf16[13,56,1024]{2,1,0:T(8,128)(2,1)}, bf16[13,56,1024]{2,1,0:T(8,128)(2,1)}, u32[]{:S(2)}, u32[]{:S(2)}) collective-permute-start(bf16[13,56,1024]{2,1,0:T(8,128)(2,1)} %collective-permute-done.2), channel_id=1, source_target_pairs={{0,1},{1,0},{2,3},{3,2},{4,5},{5,4},{6,7},{7,6},{8,9},{9,8},{10,11... | collective-permute-start | bytes 4472840 | tf_op jit(solution)/shard_map/ppermute | solution.py:15
  78.1 44.1 %collective-permute-start.8 = (bf16[13,56,1024]{2,1,0:T(8,128)(2,1)}, bf16[13,56,1024]{2,1,0:T(8,128)(2,1)}, u32[]{:S(2)}, u32[]{:S(2)}) collective-permute-start(bf16[13,56,1024]{2,1,0:T(8,128)(2,1)} %collective-permute-done.3), channel_id=1, source_target_pairs={{0,2},{2,0},{4,6},{6,4},{8,10},{10,8},{12,14},{14,12},{16,18},{18,... | collective-permute-start | bytes 4472840 | tf_op jit(solution)/shard_map/ppermute | solution.py:15
  78.3 43.9 %collective-permute-start.9 = (bf16[13,56,1024]{2,1,0:T(8,128)(2,1)}, bf16[13,56,1024]{2,1,0:T(8,128)(2,1)}, u32[]{:S(2)}, u32[]{:S(2)}) collective-permute-start(bf16[13,56,1024]{2,1,0:T(8,128)(2,1)} %collective-permute-done.4), channel_id=1, source_target_pairs={{0,2},{2,0},{4,6},{6,4},{8,10},{10,8},{12,14},{14,12},{16,18},{18,... | collective-permute-start | bytes 4472840 | tf_op jit(solution)/shard_map/ppermute | solution.py:15
  80.5 3.3 copy-start.5
  84.2 3.2 copy-start.9
  87.4 34.8 %collective-permute-start.11 = (bf16[1,128,2048]{2,1,0:T(8,128)(2,1)S(1)}, bf16[1,128,2048]{2,1,0:T(8,128)(2,1)S(1)}, u32[]{:S(2)}, u32[]{:S(2)}) collective-permute-start(bf16[1,128,2048]{2,1,0:T(8,128)(2,1)S(1)} %copy-done.9), channel_id=1, source_target_pairs={{0,16},{2,18},{4,20},{6,22},{8,24},{10,26},{12,28},{14,30},{16,0},... | collective-permute-start | bytes 1572872 | tf_op jit(solution)/shard_map/ppermute | solution.py:15
  91.3 30.9 %copy-start.3 = (bf16[2,99,64,1024]{3,2,1,0:T(8,128)(2,1)}, bf16[2,99,64,1024]{3,2,1,0:T(8,128)(2,1)S(1)}, u32[]{:S(2)}) copy-start(bf16[2,99,64,1024]{3,2,1,0:T(8,128)(2,1)S(1)} %bitcast_dynamic-update-slice_fusion.11) | copy-start | bytes 77856768
  122.2 0.8 copy-start.10
  124.3 21.1 %collective-permute-start.12 = (bf16[13,56,1024]{2,1,0:T(8,128)(2,1)}, bf16[13,56,1024]{2,1,0:T(8,128)(2,1)}, u32[]{:S(2)}, u32[]{:S(2)}) collective-permute-start(bf16[13,56,1024]{2,1,0:T(8,128)(2,1)} %collective-permute-done.10), channel_id=1, source_target_pairs={{0,2},{2,0},{4,6},{6,4},{8,10},{10,8},{12,14},{14,12},{16,18},{18,... | collective-permute-start | bytes 4472840 | tf_op jit(solution)/shard_map/ppermute | solution.py:15
  124.3 35.4 %collective-permute-start.14 = (bf16[13,56,1024]{2,1,0:T(8,128)(2,1)}, bf16[13,56,1024]{2,1,0:T(8,128)(2,1)}, u32[]{:S(2)}, u32[]{:S(2)}) collective-permute-start(bf16[13,56,1024]{2,1,0:T(8,128)(2,1)} %collective-permute-done.3), channel_id=1, source_target_pairs={{0,1},{1,0},{2,3},{3,2},{4,5},{5,4},{6,7},{7,6},{8,9},{9,8},{10,11... | collective-permute-start | bytes 4472840 | tf_op jit(solution)/shard_map/ppermute | solution.py:15
  125.8 35.1 %collective-permute-start.13 = (bf16[13,56,1024]{2,1,0:T(8,128)(2,1)}, bf16[13,56,1024]{2,1,0:T(8,128)(2,1)}, u32[]{:S(2)}, u32[]{:S(2)}) collective-permute-start(bf16[13,56,1024]{2,1,0:T(8,128)(2,1)} %collective-permute-done.2), channel_id=1, source_target_pairs={{0,4},{2,6},{4,0},{6,2},{8,12},{10,14},{12,8},{14,10},{16,20},{18,... | collective-permute-start | bytes 4472840 | tf_op jit(solution)/shard_map/ppermute | solution.py:15
  132.5 5.5 %copy-start.8 = (bf16[2,128,2048]{2,1,0:T(8,128)(2,1)S(1)}, bf16[2,128,2048]{2,1,0:T(8,128)(2,1)}, u32[]{:S(2)}) copy-start(bf16[2,128,2048]{2,1,0:T(8,128)(2,1)} %copy-done.7) | copy-start | bytes 3145732
  132.5 5.5 %copy-start.11 = (bf16[1,128,2048]{2,1,0:T(8,128)(2,1)S(1)}, bf16[1,128,2048]{2,1,0:T(8,128)(2,1)}, u32[]{:S(2)}) copy-start(bf16[1,128,2048]{2,1,0:T(8,128)(2,1)} %copy-done.10) | copy-start | bytes 1572868
  135.3 2.9 slice-start
  160.9 128.8 %all-to-all-start.1 = ((bf16[8,6,128,256]{3,2,1,0:T(8,128)(2,1)}), bf16[8,6,128,256]{3,2,1,0:T(8,128)(2,1)}, u32[]{:S(2)}, u32[]{:S(2)}) async-start(bf16[8,6,128,256]{3,2,1,0:T(8,128)(2,1)} %shard_map.38), calls=%async_computation.1 | async-start | bytes 6291456 | tf_op jit(solution)/shard_map/all_to_all | solution.py:178
  165.3 57.8 %collective-permute-start.17 = (bf16[13,56,1024]{2,1,0:T(8,128)(2,1)}, bf16[13,56,1024]{2,1,0:T(8,128)(2,1)}, u32[]{:S(2)}, u32[]{:S(2)}) collective-permute-start(bf16[13,56,1024]{2,1,0:T(8,128)(2,1)} %collective-permute-done.13), channel_id=1, source_target_pairs={{0,1},{1,0},{2,3},{3,2},{4,5},{5,4},{6,7},{7,6},{8,9},{9,8},{10,11... | collective-permute-start | bytes 4472840 | tf_op jit(solution)/shard_map/ppermute | solution.py:15
  167.2 49.8 %collective-permute-start.19 = (bf16[2,6,128,256]{3,2,1,0:T(8,128)(2,1)}, bf16[2,6,128,256]{3,2,1,0:T(8,128)(2,1)}, u32[]{:S(2)}, u32[]{:S(2)}) collective-permute-start(bf16[2,6,128,256]{3,2,1,0:T(8,128)(2,1)} %get-tuple-element.39), channel_id=1, source_target_pairs={{0,16},{2,18},{4,20},{6,22},{8,24},{10,26},{12,28},{14,30},{16,0},... | collective-permute-start | bytes 2359304 | tf_op jit(solution)/shard_map/ppermute | solution.py:15
  169.3 59.1 %collective-permute-start.15 = (bf16[13,56,1024]{2,1,0:T(8,128)(2,1)}, bf16[13,56,1024]{2,1,0:T(8,128)(2,1)}, u32[]{:S(2)}, u32[]{:S(2)}) collective-permute-start(bf16[13,56,1024]{2,1,0:T(8,128)(2,1)} %collective-permute-done.13), channel_id=1, source_target_pairs={{0,2},{2,0},{4,6},{6,4},{8,10},{10,8},{12,14},{14,12},{16,18},{18,... | collective-permute-start | bytes 4472840 | tf_op jit(solution)/shard_map/ppermute | solution.py:15
  169.3 61.9 %collective-permute-start.16 = (bf16[13,56,1024]{2,1,0:T(8,128)(2,1)}, bf16[13,56,1024]{2,1,0:T(8,128)(2,1)}, u32[]{:S(2)}, u32[]{:S(2)}) collective-permute-start(bf16[13,56,1024]{2,1,0:T(8,128)(2,1)} %collective-permute-done.14), channel_id=1, source_target_pairs={{0,2},{2,0},{4,6},{6,4},{8,10},{10,8},{12,14},{14,12},{16,18},{18,... | collective-permute-start | bytes 4472840 | tf_op jit(solution)/shard_map/ppermute | solution.py:15
  217.0 71.5 %collective-permute-start.20 = (bf16[4,6,128,256]{3,2,1,0:T(8,128)(2,1)S(1)}, bf16[4,6,128,256]{3,2,1,0:T(8,128)(2,1)S(1)}, u32[]{:S(2)}, u32[]{:S(2)}) collective-permute-start(bf16[4,6,128,256]{3,2,1,0:T(8,128)(2,1)S(1)} %slice.33), channel_id=1, source_target_pairs={{0,16},{2,18},{4,20},{6,22},{8,24},{10,26},{12,28},{14,30},{16,0},... | collective-permute-start | bytes 4718600 | tf_op jit(solution)/shard_map/ppermute | solution.py:15
  223.1 13.4 %collective-permute-start.18 = (bf16[13,56,1024]{2,1,0:T(8,128)(2,1)}, bf16[13,56,1024]{2,1,0:T(8,128)(2,1)S(1)}, u32[]{:S(2)}, u32[]{:S(2)}) collective-permute-start(bf16[13,56,1024]{2,1,0:T(8,128)(2,1)} %collective-permute-done.17), channel_id=1, source_target_pairs={{0,2},{2,0},{4,6},{6,4},{8,10},{10,8},{12,14},{14,12},{16,18},{18,... | collective-permute-start | bytes 4472840 | tf_op jit(solution)/shard_map/ppermute | solution.py:15
  261.4 2.7 copy-start
  288.5 1.1 copy-start.1
  289.7 43.6 %collective-permute-start.21 = (bf16[2,6,128,256]{3,2,1,0:T(8,128)(2,1)}, bf16[2,6,128,256]{3,2,1,0:T(8,128)(2,1)S(1)}, u32[]{:S(2)}, u32[]{:S(2)}) collective-permute-start(bf16[2,6,128,256]{3,2,1,0:T(8,128)(2,1)} %get-tuple-element.42), channel_id=1, source_target_pairs={{0,16},{2,18},{4,20},{6,22},{8,24},{10,26},{12,28},{14,30},{16,0},... | collective-permute-start | bytes 2359304 | tf_op jit(solution)/shard_map/ppermute | solution.py:15
  290.4 1.4 copy-start.2
